TPU v7x, 256 devices: a whole 4x4x8 slice. The times are simulated.
256 devices in a mesh: node: 4 (over y_hi, core), dp: 64 (over x, y_lo, z).
Axes of the slice: x: 4, y: 4 (y_hi: 2, y_lo: 2; y = y_hi * 2 + y_lo), z: 8, core: 2. Of those that a mesh axis runs over, the one named last changes fastest.
Arguments:
- tokens: bfloat16 [2, 65536, 8192], P(None, ('node', 'dp')), may hold values from -24 to 24
- cotangent: bfloat16 [2, 65536, 512], P(None, ('node', 'dp')), may hold values from -0.0390625 to 0.0390625
- master: float32 [8192, 512], P(('node', 'dp')), may hold values from -0.0625 to 0.0625
- moment: float32 [8192, 512], P(('node', 'dp')), may hold values from -6 to 6
- second: float32 [8192, 512], P(('node', 'dp')), may hold values from 0.25 to 4
- gradient: float32 [8192, 512], P(('node', 'dp')), may hold values from -6 to 6
Outputs:
- new_master: float32 [8192, 512], P(('node', 'dp'))
- new_moment: float32 [8192, 512], P(('node', 'dp'))
- new_second: float32 [8192, 512], P(('node', 'dp'))
- values: bfloat16 [2, 65536, 512], P(None, ('node', 'dp'))
- weight_grad: float32 [8192, 512], P(('node', 'dp'))
All inputs are finite; a program needn't handle non-finite values.
Results may differ from a plain program's by a relative error of at most 0.0049.
Values may be sent and summed in bfloat16 or wider, within the bound.
No kernel may reach another device: no remote copies, remote signals or barrier semaphores. Data moves between devices by JAX's collectives and lax.ppermute only.
A program may use at most 128 MiB of HBM per device.

v0:
```python
import jax
import jax.numpy as jnp
from jax import lax
from jax.sharding import PartitionSpec as P


def body(tokens, cotangent, master, moment, second, gradient):
    new_moment = 0.9 * moment + 0.1 * gradient
    new_second = 0.95 * second + 0.05 * gradient * gradient
    first_fix = 1.0 - 0.9**10
    second_fix = 1.0 - 0.95**10
    update = new_moment / first_fix / (jnp.sqrt(new_second / second_fix) + 1e-08) + 0.1 * master
    new_master = master - 0.001 * update
    weight = new_master.astype(jnp.bfloat16)
    block = lax.all_gather(weight, "dp", axis=0, tiled=True)
    summed = jnp.einsum(
        "mtd,dv->mtv",
        tokens,
        lax.all_gather(block, "node", axis=0, tiled=True),
        preferred_element_type=jnp.float32,
    )
    values = summed.astype(jnp.bfloat16)
    local_term = jnp.einsum("mtd,mtv->dv", tokens, cotangent, preferred_element_type=jnp.float32)
    weight_grad = lax.psum_scatter(local_term, ("node", "dp"), scatter_dimension=0, tiled=True)
    return (new_master, new_moment, new_second, values, weight_grad)


def solution(mesh):
    return jax.shard_map(
        body,
        mesh=mesh,
        in_specs=(
            P(None, ("node", "dp"), None),
            P(None, ("node", "dp"), None),
            P(("node", "dp"), None),
            P(("node", "dp"), None),
            P(("node", "dp"), None),
            P(("node", "dp"), None),
        ),
        out_specs=(
            P(("node", "dp"), None),
            P(("node", "dp"), None),
            P(("node", "dp"), None),
            P(None, ("node", "dp"), None),
            P(("node", "dp"), None),
        ),
        check_vma=False,
    )
```

profile of v0, /device:TPU:0, one launch (start us, length us, event | category | flops | bytes accessed | tf_op | source)
XLA Modules:
  0.0 1632.7 jit_solution(12886021999073686935)
XLA Ops:
  8.0 0.0 copy-start
  8.0 0.0 all-gather.3.cloned.1.call-start
  8.1 1.7 fusion.9
  9.7 0.0 all-gather.3.cloned.1.call-update
  9.8 0.0 all-gather.5.cloned.1.call-start
  9.8 302.5 %all-gather.3.cloned.1.call-done = bf16[2048,512]{1,0:T(8,128)(2,1)} async-done(((bf16[32,512]{1,0:T(8,128)(2,1)}), bf16[2048,512]{1,0:T(8,128)(2,1)}) %all-gather.3.cloned.1.call-update) | async-done | bytes 2097168 | tf_op jit(solution)/shard_map/all_gather | solution.py:15
  312.3 3.9 copy.23
  316.2 0.0 all-gather.5.cloned.1.call-update
  316.3 0.0 reduce-scatter.2.cloned.1.call-start
  316.3 0.0 copy-done
  316.3 12.6 convolution_bitcast_fusion
  328.9 0.0 reduce-scatter.2.cloned.1.call-update
  329.0 58.6 %all-gather.5.cloned.1.call-done = bf16[8192,512]{0,1:T(8,128)(2,1)} async-done(((bf16[2048,512]{0,1:T(8,128)(2,1)}), bf16[8192,512]{0,1:T(8,128)(2,1)}) %all-gather.5.cloned.1.call-update) | async-done | bytes 8388624 | tf_op jit(solution)/shard_map/all_gather | solution.py:19
  387.6 10.3 fusion.5
  397.9 1.0 copy.25
  398.9 1226.4 %reduce-scatter.2.cloned.1.call-done = f32[32,512]{1,0:T(8,128)} async-done(((f32[8192,512]{1,0:T(8,128)}), f32[32,512]{1,0:T(8,128)}) %reduce-scatter.2.cloned.1.call-update) | async-done | bytes 65552 | tf_op jit(solution)/shard_map/reduce_scatter | solution.py:24
Async XLA Ops:
  8.0 308.3 %copy-start = (bf16[2,256,512]{2,1,0:T(8,128)(2,1)S(1)}, bf16[2,256,512]{2,1,0:T(8,128)(2,1)}, u32[]{:S(2)}) copy-start(bf16[2,256,512]{2,1,0:T(8,128)(2,1)} %param.7) | copy-start | bytes 1572868
  8.0 304.3 %all-gather.3.cloned.1.call-start = ((), (), s32[]{:S(2)}) async-start(), calls=%async_computation.1 | async-start | bytes 2129920 | tf_op jit(solution)/shard_map/all_gather | solution.py:15
  9.8 377.8 %all-gather.5.cloned.1.call-start = ((), (), s32[]{:S(2)}) async-start(), calls=%async_computation.2 | async-start | bytes 10485760 | tf_op jit(solution)/shard_map/all_gather | solution.py:19
  316.3 1309.0 %reduce-scatter.2.cloned.1.call-start = ((), (), s32[]{:S(2)}) async-start(), calls=%async_computation.3 | async-start | bytes 16842752 | tf_op jit(solution)/shard_map/reduce_scatter | solution.py:24
Sparse Core Ops, SparseCore 0:
  11.2 301.0 all-gather.2
  316.4 71.1 all-gather.4
Sparse Core Ops, SparseCore 1:
  329.1 1296.2 reduce-scatter.1
where the time goes:
time: 1630 us
  waiting for transfers between devices  1590 us (98%)
  matrix products  23 us (1%)
    reduce_scatter x1, waiting for transfers between devices, body(): lax.psum_scatter(local_term, ('node', 'dp'), scatter_dimension=0, tiled=T...  1230 us
    all_gather x1, waiting for transfers between devices, body(): block = lax.all_gather(weight, 'dp', axis=0, tiled=True)  302 us
    all_gather x1, waiting for transfers between devices, body(): lax.all_gather(block, 'node', axis=0, tiled=True)  58.6 us
  transfers between devices with their start and end apart: 3, of which 3 were waited for; matrix products, arithmetic and copies ran while one was open for 1% of the time, Pallas kernels for 0%

commit v1 on v0

v1 whole, which is shorter than its diff:
```python
import functools
import jax
import jax.numpy as jnp
from jax import lax
from jax.experimental import pallas as pl
from jax.experimental.pallas import tpu as pltpu
from jax.sharding import PartitionSpec as P

F32, BF16 = jnp.float32, jnp.bfloat16
ALL = ("node", "dp")
INTERPRET = False


def place(x, y, z, c):
    return ((((y // 2) * 2 + c) * 4 + x) * 2 + y % 2) * 8 + z


def devices():
    for c in range(2):
        for x in range(4):
            for y in range(4):
                for z in range(8):
                    yield x, y, z, c


def near_of(v, n, c):
    step = 1 - 2 * ((v + c) % 2)
    return (v + step) % n


def near(value, axis):
    pairs = []
    for x, y, z, c in devices():
        at = [x, y, z]
        at[axis] = near_of(at[axis], (4, 4, 8)[axis], c)
        pairs.append((place(x, y, z, c), place(*at, c)))
    return lax.ppermute(value, ALL, pairs)


def shift(value, dx, dy, dz):
    pairs = [
        (place(x, y, z, c), place((x + dx) % 4, (y + dy) % 4, (z + dz) % 8, c))
        for x, y, z, c in devices()
    ]
    return lax.ppermute(value, ALL, pairs)


def swap(value):
    pairs = [(place(x, y, z, c), place(x, y, z, 1 - c)) for x, y, z, c in devices()]
    return lax.ppermute(value, ALL, pairs)


def relative(u, v, n, c):
    p = lax.rem(u + v, 2)
    step = 1 - 2 * lax.rem(v + c, 2)
    d = lax.rem(u - v - p * step + 2 * n, n) // 2
    return p, d


def grad_kernel(me, own, r0, r1, cot, cotr, sx, sy, sz, kx, ky, kz):
    t = pl.program_id(0)
    yh, x = t // 4, lax.rem(t, 4)
    mx, my, mz, c = me[0], me[1], me[2], me[3]
    rows = own.shape[0] * own.shape[1]
    dims = (((0,), (0,)), ((), ()))

    def work(other):
        acc = lax.dot_general(
            own[...].reshape(rows, 512),
            cot[...].reshape(rows, 512),
            dims,
            preferred_element_type=F32,
        )
        acc += lax.dot_general(
            other[...].reshape(rows, 512),
            cotr[...].reshape(rows, 512),
            dims,
            preferred_element_type=F32,
        )
        px, dx = relative(x, mx, 4, c)
        ys = [relative(2 * yh + yl, my, 4, c) for yl in range(2)]
        zs = [relative(z, mz, 8, c) for z in range(8)]

        def part_x(block, yl, z):
            return block[0:16, 0:384], ys[yl][0] * 32 + zs[z][0] * 16 + dx * 8 + ys[yl][1] * 4 + zs[z][1]

        def part_y(block, yl, z):
            return block[16:32, 0:384], zs[z][0] * 32 + px * 16 + dx * 8 + ys[yl][1] * 4 + zs[z][1]

        def part_z(block, yl, z):
            return block[:, 384:512], px * 32 + ys[yl][0] * 16 + dx * 8 + ys[yl][1] * 4 + zs[z][1]

        def put(ref, part, yl, z):
            block = acc[(yl * 8 + z) * 32 : (yl * 8 + z) * 32 + 32]
            value, at = part(block, yl, z)
            ref[at] = value.astype(ref.dtype)

        everywhere = [(yl, z) for yl in range(2) for z in range(8)]
        for p, ref in ((0, kx), (1, sx)):

            @pl.when(px == p)
            def _(ref=ref):
                for yl, z in everywhere:
                    put(ref, part_x, yl, z)

        for yl in range(2):
            for p, ref in ((0, ky), (1, sy)):

                @pl.when(ys[yl][0] == p)
                def _(ref=ref, yl=yl):
                    for z in range(8):
                        put(ref, part_y, yl, z)

        for parity in range(2):

            @pl.when(lax.rem(mz, 2) == parity)
            def _(parity=parity):
                for yl, z in everywhere:
                    put(kz if z % 2 == parity else sz, part_z, yl, z)

    @pl.when(yh == 0)
    def _():
        work(r0)

    @pl.when(yh == 1)
    def _():
        work(r1)


def values_kernel(me, own0, own1, r0, r1, xa, xb, ya, yb, za, zb, keep, send, w):
    t = pl.program_id(0)
    mx, my, mz, c = me[0], me[1], me[2], me[3]

    @pl.when(t == 0)
    def _():
        def absolute(v, n, p, d):
            step = 1 - 2 * lax.rem(v + c, 2)
            return lax.rem(v + p * step + 2 * d + n, n)

        xs = [[absolute(mx, 4, p, d) * 512 for d in range(2)] for p in range(2)]
        ys = [[absolute(my, 4, p, d) for d in range(2)] for p in range(2)]
        ys = [[(y // 2) * 2048 + lax.rem(y, 2) * 256 for y in row] for row in ys]
        zs = [[absolute(mz, 8, p, d) * 32 for d in range(4)] for p in range(2)]
        far = [(dx, dy, dz) for dx in range(2) for dy in range(2) for dz in range(4)]
        for px in range(2):
            for py in range(2):
                for pz in range(2):
                    for i, (dx, dy, dz) in enumerate(far):
                        at = pl.multiple_of(xs[px][dx] + ys[py][dy] + zs[pz][dz], 32)
                        w[pl.ds(at, 16), 0:384] = (xa, xb)[px][py * 32 + pz * 16 + i]
                        w[pl.ds(at + 16, 16), 0:384] = (ya, yb)[py][pz * 32 + px * 16 + i]
                        w[pl.ds(at, 32), 384:512] = (za, zb)[pz][px * 32 + py * 16 + i]

    def product(a, b, out):
        out[0] = jnp.dot(a[0], w[0:2048], preferred_element_type=F32) + jnp.dot(
            b[0], w[2048:4096], preferred_element_type=F32
        )

    @pl.when(t < 2)
    def _():
        product(r0, r1, send)

    @pl.when(t >= 2)
    def _():
        product(own0, own1, keep)


def gradient_terms(me, tokens, r0, r1, cot, cotr):
    micro, rows, _ = tokens.shape
    block = (micro, rows, 512)
    vmem = pl.BlockSpec(memory_space=pltpu.VMEM)
    whole = pl.BlockSpec(block, lambda t, s: (0, 0, 0))
    shapes = [(64, 16, 384), (64, 16, 384), (64, 32, 128)]
    return pl.pallas_call(
        grad_kernel,
        grid_spec=pltpu.PrefetchScalarGridSpec(
            num_scalar_prefetch=1,
            grid=(8,),
            in_specs=[
                pl.BlockSpec(block, lambda t, s: (0, 0, (t // 4) * 8 + s[3] * 4 + t % 4)),
                pl.BlockSpec(block, lambda t, s: (0, 0, jnp.minimum(t, 3))),
                pl.BlockSpec(block, lambda t, s: (0, 0, jnp.maximum(t - 4, 0))),
                whole,
                whole,
            ],
            out_specs=[vmem] * 6,
        ),
        out_shape=[jax.ShapeDtypeStruct(s, BF16) for s in shapes]
        + [jax.ShapeDtypeStruct(s, F32) for s in shapes],
        compiler_params=pltpu.CompilerParams(vmem_limit_bytes=40 << 20),
        interpret=INTERPRET,
    )(me, tokens, r0, r1, cot, cotr)


def partial_values(me, tokens, r0, r1, halves):
    micro, rows, _ = tokens.shape
    vmem = pl.BlockSpec(memory_space=pltpu.VMEM)
    block = (1, rows, 2048)
    out = (1, rows, 512)
    shape = jax.ShapeDtypeStruct((micro, rows, 512), F32)
    return pl.pallas_call(
        values_kernel,
        grid_spec=pltpu.PrefetchScalarGridSpec(
            num_scalar_prefetch=1,
            grid=(4,),
            in_specs=[
                pl.BlockSpec(block, lambda t, s: (jnp.maximum(t - 2, 0), 0, s[3])),
                pl.BlockSpec(block, lambda t, s: (jnp.maximum(t - 2, 0), 0, 2 + s[3])),
                pl.BlockSpec(block, lambda t, s: (jnp.minimum(t, 1), 0, 0)),
                pl.BlockSpec(block, lambda t, s: (jnp.minimum(t, 1), 0, 0)),
            ]
            + [vmem] * 6,
            out_specs=[
                pl.BlockSpec(out, lambda t, s: (jnp.maximum(t - 2, 0), 0, 0)),
                pl.BlockSpec(out, lambda t, s: (jnp.minimum(t, 1), 0, 0)),
            ],
            scratch_shapes=[pltpu.VMEM((4096, 512), BF16)],
        ),
        out_shape=[shape, shape],
        compiler_params=pltpu.CompilerParams(vmem_limit_bytes=40 << 20),
        interpret=INTERPRET,
    )(me, tokens, tokens, r0, r1, *halves)


def gathered(weight):
    line = [weight] + [shift(weight, 0, 0, -2 * d) for d in (1, 2, 3)]
    line = jnp.stack(line)
    plane = [line] + [shift(line, 2 * (q // 2), 2 * (q % 2), 0) for q in (1, 2, 3)]

    def stream(cut, axes):
        held = jnp.concatenate([cut(part) for part in plane])
        for axis in axes[:2]:
            held = jnp.concatenate([held, near(held, axis)])
        return [held, near(held, axes[2])]

    return (
        stream(lambda a: a[:, 0:16, 0:384], (2, 1, 0))
        + stream(lambda a: a[:, 16:32, 0:384], (0, 2, 1))
        + stream(lambda a: a[:, :, 384:512], (1, 0, 2))
    )


def scattered(terms):
    def stream(send, keep, axes):
        for axis in axes:
            total = keep + near(send, axis).astype(F32)
            half = total.shape[0] // 2
            keep, send = total[:half], total[half:].astype(BF16)
        return total

    sx, sy, sz, kx, ky, kz = terms
    x = stream(sx, kx, (0, 1, 2))
    y = stream(sy, ky, (1, 2, 0))
    z = stream(sz, kz, (2, 0, 1))

    def joined(q):
        at = slice(4 * q, 4 * q + 4)
        return jnp.concatenate([jnp.concatenate([x[at], y[at]], axis=1), z[at]], axis=2)

    line = joined(0)
    for q in (1, 2, 3):
        line += shift(joined(q).astype(BF16), 2 * (q // 2), 2 * (q % 2), 0).astype(F32)
    total = line[0]
    for d in (1, 2, 3):
        total += shift(line[d].astype(BF16), 0, 0, 2 * d).astype(F32)
    return total


def body(tokens, cotangent, master, moment, second, gradient):
    node, dp = lax.axis_index("node"), lax.axis_index("dp")
    core = node % 2
    me = jnp.stack([dp // 16, (node // 2) * 2 + (dp // 8) % 2, dp % 8, core]).astype(jnp.int32)

    new_moment = 0.9 * moment + 0.1 * gradient
    new_second = 0.95 * second + 0.05 * gradient * gradient
    first_fix = 1.0 - 0.9**10
    second_fix = 1.0 - 0.95**10
    update = new_moment / first_fix / (jnp.sqrt(new_second / second_fix) + 1e-08) + 0.1 * master
    new_master = master - 0.001 * update
    weight = new_master.astype(BF16)

    far = 2048 * (1 - core)
    r0 = swap(lax.dynamic_slice_in_dim(tokens, far, 2048, 2))
    r1 = swap(lax.dynamic_slice_in_dim(tokens, far + 4096, 2048, 2))
    cotr = swap(cotangent)

    halves = gathered(weight)
    terms = gradient_terms(me, tokens, r0, r1, cotangent, cotr)
    weight_grad = scattered(terms)
    keep, send = partial_values(me, tokens, r0, r1, halves)
    values = (keep + swap(send)).astype(BF16)
    return (new_master, new_moment, new_second, values, weight_grad)


def solution(mesh):
    rows = P(("node", "dp"), None)
    tall = P(None, ("node", "dp"), None)
    return jax.shard_map(
        body,
        mesh=mesh,
        in_specs=(tall, tall, rows, rows, rows, rows),
        out_specs=(rows, rows, rows, tall, rows),
        check_vma=False,
    )
```

time: 1630 us -> 137 us (0.08)
  waiting for transfers between devices: 1590 us -> 43.1 us
  starting transfers between devices: 0.12 us -> 52.9 us
  matrix products: 23 us -> 0 us
  Pallas kernels: 0 us -> 18.8 us
    reduce_scatter x1 -> x0, waiting for transfers between devices: 1230 us -> none  [body(): lax.psum_scatter(local_term, ('node', 'dp'), scatter_dimension=0, tiled=T...]
    all_gather x2 -> x0, waiting for transfers between devices: 361 us -> none  [the longest x1 302 us: body(): block = lax.all_gather(weight, 'dp', axis=0, tiled=True)]
    ppermute x0 -> x34, starting transfers between devices: none -> 52.9 us  [the longest x12 31.1 us: shift(): return lax.ppermute(value, ALL, pairs)]
    ppermute x0 -> x34, waiting for transfers between devices: none -> 43.1 us  [the longest x12 22.3 us: shift(): return lax.ppermute(value, ALL, pairs)]
    dot_general x2 -> x0, matrix products: 23 us -> none  [the longest x1 12.6 us: body(): jnp.einsum('mtd,mtv->dv', tokens, cotangent, preferred_element_type=jnp.f...]
    pallas_call x0 -> x2, Pallas kernels: none -> 18.8 us  [the longest x1 10.2 us: gradient_terms(): pl.pallas_call(grad_kernel, grid_spec=pltpu.PrefetchScalarGridSpec(num_sc...]
  transfers between devices with their start and end apart: 3 -> 34, of which waited for: 3 -> 16; matrix products, arithmetic and copies ran while one was open for 1% -> 11% of each run, Pallas kernels for 0% -> 14%
where the time goes in v1:
time: 137 us; the launch traced here: 134 us
  starting transfers between devices  52.9 us (39%)
  waiting for transfers between devices  43.1 us (31%)
  Pallas kernels  18.8 us (14%)
  local copies, waits for them, and re-layouts  14 us (10%)
  other arithmetic  4.44 us (3%)
    ppermute x12, starting transfers between devices, shift(): return lax.ppermute(value, ALL, pairs)  31.1 us
    ppermute x12, waiting for transfers between devices, shift(): return lax.ppermute(value, ALL, pairs)  22.3 us
    ppermute x18, waiting for transfers between devices, near(): return lax.ppermute(value, ALL, pairs)  20.9 us
    ppermute x18, starting transfers between devices, near(): return lax.ppermute(value, ALL, pairs)  20.2 us
    pallas_call x1, Pallas kernels, gradient_terms(): pl.pallas_call(grad_kernel, grid_spec=pltpu.PrefetchScalarGridSpec(num_sc...  10.2 us
    pallas_call x1, Pallas kernels, partial_values(): pl.pallas_call(values_kernel, grid_spec=pltpu.PrefetchScalarGridSpec(num_...  8.56 us
    concatenate x6, local copies, waits for them, and re-layouts, stream(): held = jnp.concatenate([held, near(held, axis)])  5.05 us
    dynamic_slice x1, local copies, waits for them, and re-layouts, body(): r1 = swap(lax.dynamic_slice_in_dim(tokens, far + 4096, 2048, 2))  4.87 us
  transfers between devices with their start and end apart: 34, of which 16 were waited for; matrix products, arithmetic and copies ran while one was open for 11% of the time, Pallas kernels for 14%

profile of v1, /device:TPU:0, one launch (start us, length us, event | category | flops | bytes accessed | tf_op | source)
XLA Modules:
  0.0 134.2 jit_solution(4357960860603244077)
XLA Ops:
  0.6 1.6 %fusion.11 = (bf16[32,512]{1,0:T(8,128)(2,1)S(1)}, f32[32,512]{1,0:T(8,128)}, f32[32,512]{1,0:T(8,128)}, f32[32,512]{1,0:T(8,128)}) fusion(f32[32,512]{1,0:T(8,128)} %param.8, f32[32,512]{1,0:T(8,128)} %param.11, f32[32,512]{1,0:T(8,128)} %param.9, f32[32,512]{1,0:T(8,128)} %param.10), kind=kLoop, calls=%fused_computation.77 | loop fusion | flops 262144 | bytes 491520 | tf_op jit(solution)/shard_map/convert_element_type | solution.py:280
  2.3 1.5 %collective-permute-start.4 = (bf16[32,512]{1,0:T(8,128)(2,1)S(1)}, bf16[32,512]{1,0:T(8,128)(2,1)S(1)}, u32[]{:S(2)}, u32[]{:S(2)}) collective-permute-start(bf16[32,512]{1,0:T(8,128)(2,1)S(1)} %get-tuple-element.29), channel_id=1, source_target_pairs={{0,2},{1,3},{2,4},{3,5},{4,6},{5,7},{6,0},{7,1},{8,10},{9,11},{10,... | collective-permute-start | bytes 98312 | tf_op jit(solution)/shard_map/ppermute | solution.py:45
  3.8 5.4 %collective-permute-start.3 = (bf16[32,512]{1,0:T(8,128)(2,1)S(1)}, bf16[32,512]{1,0:T(8,128)(2,1)S(1)}, u32[]{:S(2)}, u32[]{:S(2)}) collective-permute-start(bf16[32,512]{1,0:T(8,128)(2,1)S(1)} %get-tuple-element.29), channel_id=1, source_target_pairs={{0,4},{1,5},{2,6},{3,7},{4,0},{5,1},{6,2},{7,3},{8,12},{9,13},{10,... | collective-permute-start | bytes 98312 | tf_op jit(solution)/shard_map/ppermute | solution.py:45
  9.2 2.7 %collective-permute-start.2 = (bf16[32,512]{1,0:T(8,128)(2,1)S(1)}, bf16[32,512]{1,0:T(8,128)(2,1)S(1)}, u32[]{:S(2)}, u32[]{:S(2)}) collective-permute-start(bf16[32,512]{1,0:T(8,128)(2,1)S(1)} %get-tuple-element.29), channel_id=1, source_target_pairs={{0,6},{1,7},{2,0},{3,1},{4,2},{5,3},{6,4},{7,5},{8,14},{9,15},{10,... | collective-permute-start | bytes 98312 | tf_op jit(solution)/shard_map/ppermute | solution.py:45
  11.9 4.9 %constant_dynamic-slice_fusion = (bf16[2,256,2048]{2,1,0:T(8,128)(2,1)}, bf16[2,256,2048]{2,1,0:T(8,128)(2,1)}) fusion(bf16[2,256,8192]{2,1,0:T(8,128)(2,1)} %own.1, s32[]{:T(128)S(6)} %select_n.38, s32[]{:T(128)S(6)} %select_n.37), kind=kLoop, calls=%fused_computation.71 | loop fusion | bytes 8388616 | tf_op jit(solution)/shard_map/dynamic_slice | solution.py:284
  17.4 5.7 %collective-permute-start.7 = (bf16[4,32,512]{2,1,0:T(8,128)(2,1)S(1)}, bf16[4,32,512]{2,1,0:T(8,128)(2,1)S(1)}, u32[]{:S(2)}, u32[]{:S(2)}) collective-permute-start(bf16[4,32,512]{2,1,0:T(8,128)(2,1)S(1)} %pad_maximum_fusion.2), channel_id=1, source_target_pairs={{0,160},{1,161},{2,162},{3,163},{4,164},{5,165},{6,166},{7,167},{8... | collective-permute-start | bytes 393224 | tf_op jit(solution)/shard_map/ppermute | solution.py:45
  24.1 6.1 %collective-permute-done.5 = bf16[4,32,512]{2,1,0:T(8,128)(2,1)S(1)} collective-permute-done((bf16[4,32,512]{2,1,0:T(8,128)(2,1)S(1)}, bf16[4,32,512]{2,1,0:T(8,128)(2,1)S(1)}, u32[]{:S(2)}, u32[]{:S(2)}) %collective-permute-start.5) | collective-permute-done | bytes 131104 | tf_op jit(solution)/shard_map/ppermute | solution.py:45
  30.2 2.9 %collective-permute-start.6 = (bf16[4,32,512]{2,1,0:T(8,128)(2,1)S(1)}, bf16[4,32,512]{2,1,0:T(8,128)(2,1)S(1)}, u32[]{:S(2)}, u32[]{:S(2)}) collective-permute-start(bf16[4,32,512]{2,1,0:T(8,128)(2,1)S(1)} %pad_maximum_fusion.2), channel_id=1, source_target_pairs={{0,32},{1,33},{2,34},{3,35},{4,36},{5,37},{6,38},{7,39},{8,40},{9,... | collective-permute-start | bytes 393224 | tf_op jit(solution)/shard_map/ppermute | solution.py:45
  33.7 3.0 %collective-permute-done.6 = bf16[4,32,512]{2,1,0:T(8,128)(2,1)S(1)} collective-permute-done((bf16[4,32,512]{2,1,0:T(8,128)(2,1)S(1)}, bf16[4,32,512]{2,1,0:T(8,128)(2,1)S(1)}, u32[]{:S(2)}, u32[]{:S(2)}) %collective-permute-start.6) | collective-permute-done | bytes 131104 | tf_op jit(solution)/shard_map/ppermute | solution.py:45
  38.1 1.1 collective-permute-start.8
  39.2 1.8 %collective-permute-start.11 = (bf16[16,16,384]{2,1,0:T(8,128)(2,1)S(1)}, bf16[16,16,384]{2,1,0:T(8,128)(2,1)S(1)}, u32[]{:S(2)}, u32[]{:S(2)}) collective-permute-start(bf16[16,16,384]{2,1,0:T(8,128)(2,1)S(1)} %pad_maximum_fusion.1), channel_id=1, source_target_pairs={{0,16},{1,17},{2,18},{3,19},{4,20},{5,21},{6,22},{7,23},{8,24},{9,... | collective-permute-start | bytes 589832 | tf_op jit(solution)/shard_map/ppermute | solution.py:37
  41.1 2.7 %collective-permute-done.8 = bf16[16,16,384]{2,1,0:T(8,128)(2,1)S(1)} collective-permute-done((bf16[16,16,384]{2,1,0:T(8,128)(2,1)S(1)}, bf16[16,16,384]{2,1,0:T(8,128)(2,1)S(1)}, u32[]{:S(2)}, u32[]{:S(2)}) %collective-permute-start.8) | collective-permute-done | bytes 196640 | tf_op jit(solution)/shard_map/ppermute | solution.py:37
  43.8 1.8 %collective-permute-start.14 = (bf16[16,32,128]{2,1,0:T(8,128)(2,1)S(1)}, bf16[16,32,128]{2,1,0:T(8,128)(2,1)S(1)}, u32[]{:S(2)}, u32[]{:S(2)}) collective-permute-start(bf16[16,32,128]{2,1,0:T(8,128)(2,1)S(1)} %pad_maximum_fusion.3), channel_id=1, source_target_pairs={{0,8},{1,9},{2,10},{3,11},{4,12},{5,13},{6,14},{7,15},{8,0},{9,1},... | collective-permute-start | bytes 393224 | tf_op jit(solution)/shard_map/ppermute | solution.py:37
  46.8 0.8 constant_dynamic-update-slice_fusion.11
  47.5 1.3 collective-permute-done.14
  48.8 1.0 collective-permute-start.12
  50.5 1.7 %collective-permute-start.15 = (bf16[32,32,128]{2,1,0:T(8,128)(2,1)}, bf16[32,32,128]{2,1,0:T(8,128)(2,1)S(1)}, u32[]{:S(2)}, u32[]{:S(2)}) collective-permute-start(bf16[32,32,128]{2,1,0:T(8,128)(2,1)} %get-tuple-element.51), channel_id=1, source_target_pairs={{0,16},{1,17},{2,18},{3,19},{4,20},{5,21},{6,22},{7,23},{8,24},{9,... | collective-permute-start | bytes 786440 | tf_op jit(solution)/shard_map/ppermute | solution.py:37
  52.3 1.0 copy-done
  53.4 10.2 %shard_map.102 = (bf16[64,16,384]{2,1,0:T(8,128)(2,1)S(1)}, bf16[64,16,384]{2,1,0:T(8,128)(2,1)S(1)}, bf16[64,32,128]{2,1,0:T(8,128)(2,1)S(1)}, f32[64,16,384]{2...) custom-call(s32[4]{0:T(128)S(1)} %pad_add_fusion.me, bf16[2,256,8192]{2,1,0:T(8,128)(2,1)} %own.1, ...), custom_call_target="tpu_custom_call" | custom-call | tf_op jit(solution)/shard_map/pallas_call | solution.py:174
  63.6 1.3 collective-permute-start.25
  64.9 1.1 constant_dynamic-update-slice_fusion.5.xa
  66.4 1.8 %constant_dynamic-update-slice_fusion.16.ya = bf16[64,16,384]{2,1,0:T(8,128)(2,1)} fusion(bf16[64,16,384]{2,1,0:T(8,128)(2,1)} %get-tuple-element.42, bf16[32,16,384]{2,1,0:T(8,128)(2,1)} %collective-permute-done.12), kind=kLoop, calls=%fused_computation.43 | loop fusion | bytes 786432 | tf_op jit(solution)/shard_map/concatenate | solution.py:233
  68.2 1.8 %collective-permute-start.13 = (bf16[64,16,384]{2,1,0:T(8,128)(2,1)}, bf16[64,16,384]{2,1,0:T(8,128)(2,1)S(1)}, u32[]{:S(2)}, u32[]{:S(2)}) collective-permute-start(bf16[64,16,384]{2,1,0:T(8,128)(2,1)} %constant_dynamic-update-slice_fusion.16.ya), channel_id=1, source_target_pairs={{0,8},{1,9},{2,10},{3,11},{4,12},{5,13},{6,14},{7,15},{8,0},{9,1},... | collective-permute-start | bytes 2359304 | tf_op jit(solution)/shard_map/ppermute | solution.py:37
  70.0 1.1 collective-permute-start.16
  71.1 1.5 %collective-permute-start.19 = (bf16[64,16,384]{2,1,0:T(8,128)(2,1)S(1)}, bf16[64,16,384]{2,1,0:T(8,128)(2,1)S(1)}, u32[]{:S(2)}, u32[]{:S(2)}) collective-permute-start(bf16[64,16,384]{2,1,0:T(8,128)(2,1)S(1)} %get-tuple-element.16), channel_id=1, source_target_pairs={{0,16},{1,17},{2,18},{3,19},{4,20},{5,21},{6,22},{7,23},{8,24},{9,... | collective-permute-start | bytes 2359304 | tf_op jit(solution)/shard_map/ppermute | solution.py:37
  73.7 5.6 %collective-permute-done.16.zb = bf16[64,32,128]{2,1,0:T(8,128)(2,1)S(1)} collective-permute-done((bf16[64,32,128]{2,1,0:T(8,128)(2,1)S(1)}, bf16[64,32,128]{2,1,0:T(8,128)(2,1)S(1)}, u32[]{:S(2)}, u32[]{:S(2)}) %collective-permute-start.16) | collective-permute-done | bytes 524320 | tf_op jit(solution)/shard_map/ppermute | solution.py:37
  79.3 1.0 collective-permute-start.22
  80.4 8.6 %shard_map.101 = (f32[2,256,512]{2,1,0:T(8,128)S(1)}, f32[2,256,512]{2,1,0:T(8,128)S(1)}) custom-call(s32[4]{0:T(128)S(1)} %pad_add_fusion.me, bf16[2,256,8192]{2,1,0:T(8,128)(2,1)} %own.1, bf16[2,256,8192]{2,1,0:T(8,128)(2,1)} %own.1, bf16[2,256,2048]{2,1,0:T(8,128)(2,1)} %collective-permute-done.r0, bf16[2,256,2048]{2,1,0:T(8,128)(2,1)S(1)} %collective-permute-done.1.r1, ...), custom_call_target="tpu_custom_call" | custom-call | tf_op jit(solution)/shard_map/pallas_call | solution.py:201
  88.9 1.1 collective-permute-start.17
  90.1 0.9 collective-permute-start.27
  91.3 1.3 collective-permute-start.20
  93.2 2.0 %collective-permute-done.27 = bf16[16,32,128]{2,1,0:T(8,128)(2,1)S(1)} collective-permute-done((bf16[16,32,128]{2,1,0:T(8,128)(2,1)S(1)}, bf16[16,32,128]{2,1,0:T(8,128)(2,1)S(1)}, u32[]{:S(2)}, u32[]{:S(2)}) %collective-permute-start.27) | collective-permute-done | bytes 131104 | tf_op jit(solution)/shard_map/ppermute | solution.py:37
  95.2 4.1 %collective-permute-done.20 = bf16[32,16,384]{2,1,0:T(8,128)(2,1)S(1)} collective-permute-done((bf16[32,16,384]{2,1,0:T(8,128)(2,1)S(1)}, bf16[32,16,384]{2,1,0:T(8,128)(2,1)S(1)}, u32[]{:S(2)}, u32[]{:S(2)}) %collective-permute-start.20) | collective-permute-done | bytes 393248 | tf_op jit(solution)/shard_map/ppermute | solution.py:37
  99.5 0.9 collective-permute-start.21
  100.8 1.3 collective-permute-start.24
  102.1 3.2 %collective-permute-done.21 = bf16[16,16,384]{2,1,0:T(8,128)(2,1)S(1)} collective-permute-done((bf16[16,16,384]{2,1,0:T(8,128)(2,1)S(1)}, bf16[16,16,384]{2,1,0:T(8,128)(2,1)S(1)}, u32[]{:S(2)}, u32[]{:S(2)}) %collective-permute-start.21) | collective-permute-done | bytes 196640 | tf_op jit(solution)/shard_map/ppermute | solution.py:37
  105.3 1.3 collective-permute-done.24
  106.7 2.5 %collective-permute-start.29 = (bf16[4,32,512]{2,1,0:T(8,128)(2,1)S(1)}, bf16[4,32,512]{2,1,0:T(8,128)(2,1)S(1)}, u32[]{:S(2)}, u32[]{:S(2)}) collective-permute-start(bf16[4,32,512]{2,1,0:T(8,128)(2,1)S(1)} %pad_maximum_fusion.5), channel_id=1, source_target_pairs={{0,32},{1,33},{2,34},{3,35},{4,36},{5,37},{6,38},{7,39},{8,40},{9,... | collective-permute-start | bytes 393224 | tf_op jit(solution)/shard_map/ppermute | solution.py:45
  109.2 3.2 %collective-permute-start.30 = (bf16[4,32,512]{2,1,0:T(8,128)(2,1)S(1)}, bf16[4,32,512]{2,1,0:T(8,128)(2,1)S(1)}, u32[]{:S(2)}, u32[]{:S(2)}) collective-permute-start(bf16[4,32,512]{2,1,0:T(8,128)(2,1)S(1)} %pad_maximum_fusion.6), channel_id=1, source_target_pairs={{0,160},{1,161},{2,162},{3,163},{4,164},{5,165},{6,166},{7,167},{8... | collective-permute-start | bytes 393224 | tf_op jit(solution)/shard_map/ppermute | solution.py:45
  112.5 1.0 collective-permute-start.28
  113.5 1.0 collective-permute-done.29
  114.5 4.0 %collective-permute-done.30 = bf16[4,32,512]{2,1,0:T(8,128)(2,1)S(1)} collective-permute-done((bf16[4,32,512]{2,1,0:T(8,128)(2,1)S(1)}, bf16[4,32,512]{2,1,0:T(8,128)(2,1)S(1)}, u32[]{:S(2)}, u32[]{:S(2)}) %collective-permute-start.30) | collective-permute-done | bytes 131104 | tf_op jit(solution)/shard_map/ppermute | solution.py:45
  118.5 2.7 %collective-permute-done.28 = bf16[4,32,512]{2,1,0:T(8,128)(2,1)S(1)} collective-permute-done((bf16[4,32,512]{2,1,0:T(8,128)(2,1)S(1)}, bf16[4,32,512]{2,1,0:T(8,128)(2,1)S(1)}, u32[]{:S(2)}, u32[]{:S(2)}) %collective-permute-start.28) | collective-permute-done | bytes 131104 | tf_op jit(solution)/shard_map/ppermute | solution.py:45
  121.3 0.8 collective-permute-start.31
  122.1 3.4 %collective-permute-start.33 = (bf16[32,512]{1,0:T(8,128)(2,1)S(1)}, bf16[32,512]{1,0:T(8,128)(2,1)S(1)}, u32[]{:S(2)}, u32[]{:S(2)}) collective-permute-start(bf16[32,512]{1,0:T(8,128)(2,1)S(1)} %get-tuple-element.46), channel_id=1, source_target_pairs={{0,6},{1,7},{2,0},{3,1},{4,2},{5,3},{6,4},{7,5},{8,14},{9,15},{10,... | collective-permute-start | bytes 98312 | tf_op jit(solution)/shard_map/ppermute | solution.py:45
  125.5 1.6 %collective-permute-start.32 = (bf16[32,512]{1,0:T(8,128)(2,1)S(1)}, bf16[32,512]{1,0:T(8,128)(2,1)S(1)}, u32[]{:S(2)}, u32[]{:S(2)}) collective-permute-start(bf16[32,512]{1,0:T(8,128)(2,1)S(1)} %get-tuple-element.47), channel_id=1, source_target_pairs={{0,4},{1,5},{2,6},{3,7},{4,0},{5,1},{6,2},{7,3},{8,12},{9,13},{10,... | collective-permute-start | bytes 98312 | tf_op jit(solution)/shard_map/ppermute | solution.py:45
  127.2 0.9 add_convert_fusion
  128.1 5.4 %collective-permute-done.32 = bf16[32,512]{1,0:T(8,128)(2,1)S(1)} collective-permute-done((bf16[32,512]{1,0:T(8,128)(2,1)S(1)}, bf16[32,512]{1,0:T(8,128)(2,1)S(1)}, u32[]{:S(2)}, u32[]{:S(2)}) %collective-permute-start.32) | collective-permute-done | bytes 32800 | tf_op jit(solution)/shard_map/ppermute | solution.py:45
  (74 shorter events, 9.8 us)
Async XLA Ops:
  2.3 15.0 %collective-permute-start.4 = (bf16[32,512]{1,0:T(8,128)(2,1)S(1)}, bf16[32,512]{1,0:T(8,128)(2,1)S(1)}, u32[]{:S(2)}, u32[]{:S(2)}) collective-permute-start(bf16[32,512]{1,0:T(8,128)(2,1)S(1)} %get-tuple-element.29), channel_id=1, source_target_pairs={{0,2},{1,3},{2,4},{3,5},{4,6},{5,7},{6,0},{7,1},{8,10},{9,11},{10,... | collective-permute-start | bytes 98312 | tf_op jit(solution)/shard_map/ppermute | solution.py:45
  3.8 13.5 %collective-permute-start.3 = (bf16[32,512]{1,0:T(8,128)(2,1)S(1)}, bf16[32,512]{1,0:T(8,128)(2,1)S(1)}, u32[]{:S(2)}, u32[]{:S(2)}) collective-permute-start(bf16[32,512]{1,0:T(8,128)(2,1)S(1)} %get-tuple-element.29), channel_id=1, source_target_pairs={{0,4},{1,5},{2,6},{3,7},{4,0},{5,1},{6,2},{7,3},{8,12},{9,13},{10,... | collective-permute-start | bytes 98312 | tf_op jit(solution)/shard_map/ppermute | solution.py:45
  9.2 8.1 %collective-permute-start.2 = (bf16[32,512]{1,0:T(8,128)(2,1)S(1)}, bf16[32,512]{1,0:T(8,128)(2,1)S(1)}, u32[]{:S(2)}, u32[]{:S(2)}) collective-permute-start(bf16[32,512]{1,0:T(8,128)(2,1)S(1)} %get-tuple-element.29), channel_id=1, source_target_pairs={{0,6},{1,7},{2,0},{3,1},{4,2},{5,3},{6,4},{7,5},{8,14},{9,15},{10,... | collective-permute-start | bytes 98312 | tf_op jit(solution)/shard_map/ppermute | solution.py:45
  11.9 38.7 %collective-permute-start.18 = (bf16[2,256,512]{2,1,0:T(8,128)(2,1)}, bf16[2,256,512]{2,1,0:T(8,128)(2,1)}, u32[]{:S(2)}, u32[]{:S(2)}) collective-permute-start(bf16[2,256,512]{2,1,0:T(8,128)(2,1)} %cot.1), channel_id=1, source_target_pairs={{0,64},{1,65},{2,66},{3,67},{4,68},{5,69},{6,70},{7,71},{8,72},{9,... | collective-permute-start | bytes 1572872 | tf_op jit(solution)/shard_map/ppermute | solution.py:50
  16.7 35.6 %collective-permute-start.1 = (bf16[2,256,2048]{2,1,0:T(8,128)(2,1)}, bf16[2,256,2048]{2,1,0:T(8,128)(2,1)S(1)}, u32[]{:S(2)}, u32[]{:S(2)}) collective-permute-start(bf16[2,256,2048]{2,1,0:T(8,128)(2,1)} %get-tuple-element.33), channel_id=1, source_target_pairs={{0,64},{1,65},{2,66},{3,67},{4,68},{5,69},{6,70},{7,71},{8,72},{9,... | collective-permute-start | bytes 6291464 | tf_op jit(solution)/shard_map/ppermute | solution.py:50
  17.2 35.1 %collective-permute-start = (bf16[2,256,2048]{2,1,0:T(8,128)(2,1)}, bf16[2,256,2048]{2,1,0:T(8,128)(2,1)}, u32[]{:S(2)}, u32[]{:S(2)}) collective-permute-start(bf16[2,256,2048]{2,1,0:T(8,128)(2,1)} %get-tuple-element.34), channel_id=1, source_target_pairs={{0,64},{1,65},{2,66},{3,67},{4,68},{5,69},{6,70},{7,71},{8,72},{9,... | collective-permute-start | bytes 6291464 | tf_op jit(solution)/shard_map/ppermute | solution.py:50
  17.4 20.0 %collective-permute-start.7 = (bf16[4,32,512]{2,1,0:T(8,128)(2,1)S(1)}, bf16[4,32,512]{2,1,0:T(8,128)(2,1)S(1)}, u32[]{:S(2)}, u32[]{:S(2)}) collective-permute-start(bf16[4,32,512]{2,1,0:T(8,128)(2,1)S(1)} %pad_maximum_fusion.2), channel_id=1, source_target_pairs={{0,160},{1,161},{2,162},{3,163},{4,164},{5,165},{6,166},{7,167},{8... | collective-permute-start | bytes 393224 | tf_op jit(solution)/shard_map/ppermute | solution.py:45
  23.1 7.1 %collective-permute-start.5 = (bf16[4,32,512]{2,1,0:T(8,128)(2,1)S(1)}, bf16[4,32,512]{2,1,0:T(8,128)(2,1)S(1)}, u32[]{:S(2)}, u32[]{:S(2)}) collective-permute-start(bf16[4,32,512]{2,1,0:T(8,128)(2,1)S(1)} %pad_maximum_fusion.2), channel_id=1, source_target_pairs={{0,128},{1,129},{2,130},{3,131},{4,132},{5,133},{6,134},{7,135},{8... | collective-permute-start | bytes 393224 | tf_op jit(solution)/shard_map/ppermute | solution.py:45
  30.2 6.6 %collective-permute-start.6 = (bf16[4,32,512]{2,1,0:T(8,128)(2,1)S(1)}, bf16[4,32,512]{2,1,0:T(8,128)(2,1)S(1)}, u32[]{:S(2)}, u32[]{:S(2)}) collective-permute-start(bf16[4,32,512]{2,1,0:T(8,128)(2,1)S(1)} %pad_maximum_fusion.2), channel_id=1, source_target_pairs={{0,32},{1,33},{2,34},{3,35},{4,36},{5,37},{6,38},{7,39},{8,40},{9,... | collective-permute-start | bytes 393224 | tf_op jit(solution)/shard_map/ppermute | solution.py:45
  38.1 5.8 %collective-permute-start.8 = (bf16[16,16,384]{2,1,0:T(8,128)(2,1)S(1)}, bf16[16,16,384]{2,1,0:T(8,128)(2,1)S(1)}, u32[]{:S(2)}, u32[]{:S(2)}) collective-permute-start(bf16[16,16,384]{2,1,0:T(8,128)(2,1)S(1)} %pad_maximum_fusion), channel_id=1, source_target_pairs={{0,1},{1,0},{2,3},{3,2},{4,5},{5,4},{6,7},{7,6},{8,9},{9,8},{10,11... | collective-permute-start | bytes 589832 | tf_op jit(solution)/shard_map/ppermute | solution.py:37
  39.2 7.1 %collective-permute-start.11 = (bf16[16,16,384]{2,1,0:T(8,128)(2,1)S(1)}, bf16[16,16,384]{2,1,0:T(8,128)(2,1)S(1)}, u32[]{:S(2)}, u32[]{:S(2)}) collective-permute-start(bf16[16,16,384]{2,1,0:T(8,128)(2,1)S(1)} %pad_maximum_fusion.1), channel_id=1, source_target_pairs={{0,16},{1,17},{2,18},{3,19},{4,20},{5,21},{6,22},{7,23},{8,24},{9,... | collective-permute-start | bytes 589832 | tf_op jit(solution)/shard_map/ppermute | solution.py:37
  41.1 7.7 %copy-start.1 = (bf16[32,32,128]{2,1,0:T(8,128)(2,1)}, bf16[32,32,128]{2,1,0:T(8,128)(2,1)S(1)}, u32[]{:S(2)}) copy-start(bf16[32,32,128]{2,1,0:T(8,128)(2,1)S(1)} %get-tuple-element.53) | copy-start | bytes 786436
  43.8 5.0 %collective-permute-start.14 = (bf16[16,32,128]{2,1,0:T(8,128)(2,1)S(1)}, bf16[16,32,128]{2,1,0:T(8,128)(2,1)S(1)}, u32[]{:S(2)}, u32[]{:S(2)}) collective-permute-start(bf16[16,32,128]{2,1,0:T(8,128)(2,1)S(1)} %pad_maximum_fusion.3), channel_id=1, source_target_pairs={{0,8},{1,9},{2,10},{3,11},{4,12},{5,13},{6,14},{7,15},{8,0},{9,1},... | collective-permute-start | bytes 393224 | tf_op jit(solution)/shard_map/ppermute | solution.py:37
  46.4 18.5 %collective-permute-start.9 = (bf16[32,16,384]{2,1,0:T(8,128)(2,1)}, bf16[32,16,384]{2,1,0:T(8,128)(2,1)}, u32[]{:S(2)}, u32[]{:S(2)}) collective-permute-start(bf16[32,16,384]{2,1,0:T(8,128)(2,1)} %get-tuple-element.43), channel_id=1, source_target_pairs={{0,8},{1,9},{2,10},{3,11},{4,12},{5,13},{6,14},{7,15},{8,0},{9,1},... | collective-permute-start | bytes 1179656 | tf_op jit(solution)/shard_map/ppermute | solution.py:37
  48.8 17.6 %collective-permute-start.12 = (bf16[32,16,384]{2,1,0:T(8,128)(2,1)}, bf16[32,16,384]{2,1,0:T(8,128)(2,1)}, u32[]{:S(2)}, u32[]{:S(2)}) collective-permute-start(bf16[32,16,384]{2,1,0:T(8,128)(2,1)} %get-tuple-element.41), channel_id=1, source_target_pairs={{0,1},{1,0},{2,3},{3,2},{4,5},{5,4},{6,7},{7,6},{8,9},{9,8},{10,11... | collective-permute-start | bytes 1179656 | tf_op jit(solution)/shard_map/ppermute | solution.py:37
  50.5 19.4 %collective-permute-start.15 = (bf16[32,32,128]{2,1,0:T(8,128)(2,1)}, bf16[32,32,128]{2,1,0:T(8,128)(2,1)S(1)}, u32[]{:S(2)}, u32[]{:S(2)}) collective-permute-start(bf16[32,32,128]{2,1,0:T(8,128)(2,1)} %get-tuple-element.51), channel_id=1, source_target_pairs={{0,16},{1,17},{2,18},{3,19},{4,20},{5,21},{6,22},{7,23},{8,24},{9,... | collective-permute-start | bytes 786440 | tf_op jit(solution)/shard_map/ppermute | solution.py:37
  52.3 1.0 copy-start
  63.6 9.4 %collective-permute-start.25 = (bf16[64,32,128]{2,1,0:T(8,128)(2,1)S(1)}, bf16[64,32,128]{2,1,0:T(8,128)(2,1)S(1)}, u32[]{:S(2)}, u32[]{:S(2)}) collective-permute-start(bf16[64,32,128]{2,1,0:T(8,128)(2,1)S(1)} %get-tuple-element.20), channel_id=1, source_target_pairs={{0,1},{1,0},{2,3},{3,2},{4,5},{5,4},{6,7},{7,6},{8,9},{9,8},{10,11... | collective-permute-start | bytes 1572872 | tf_op jit(solution)/shard_map/ppermute | solution.py:37
  66.0 14.3 %collective-permute-start.10 = (bf16[64,16,384]{2,1,0:T(8,128)(2,1)S(1)}, bf16[64,16,384]{2,1,0:T(8,128)(2,1)S(1)}, u32[]{:S(2)}, u32[]{:S(2)}) collective-permute-start(bf16[64,16,384]{2,1,0:T(8,128)(2,1)S(1)} %constant_dynamic-update-slice_fusion.5.xa), channel_id=1, source_target_pairs={{0,16},{1,17},{2,18},{3,19},{4,20},{5,21},{6,22},{7,23},{8,24},{9,... | collective-permute-start | bytes 2359304 | tf_op jit(solution)/shard_map/ppermute | solution.py:37
  68.2 12.2 %collective-permute-start.13 = (bf16[64,16,384]{2,1,0:T(8,128)(2,1)}, bf16[64,16,384]{2,1,0:T(8,128)(2,1)S(1)}, u32[]{:S(2)}, u32[]{:S(2)}) collective-permute-start(bf16[64,16,384]{2,1,0:T(8,128)(2,1)} %constant_dynamic-update-slice_fusion.16.ya), channel_id=1, source_target_pairs={{0,8},{1,9},{2,10},{3,11},{4,12},{5,13},{6,14},{7,15},{8,0},{9,1},... | collective-permute-start | bytes 2359304 | tf_op jit(solution)/shard_map/ppermute | solution.py:37
  70.0 9.3 %collective-permute-start.16 = (bf16[64,32,128]{2,1,0:T(8,128)(2,1)S(1)}, bf16[64,32,128]{2,1,0:T(8,128)(2,1)S(1)}, u32[]{:S(2)}, u32[]{:S(2)}) collective-permute-start(bf16[64,32,128]{2,1,0:T(8,128)(2,1)S(1)} %constant_dynamic-update-slice_fusion.27.za), channel_id=1, source_target_pairs={{0,1},{1,0},{2,3},{3,2},{4,5},{5,4},{6,7},{7,6},{8,9},{9,8},{10,11... | collective-permute-start | bytes 1572872 | tf_op jit(solution)/shard_map/ppermute | solution.py:37
  71.1 19.9 %collective-permute-start.19 = (bf16[64,16,384]{2,1,0:T(8,128)(2,1)S(1)}, bf16[64,16,384]{2,1,0:T(8,128)(2,1)S(1)}, u32[]{:S(2)}, u32[]{:S(2)}) collective-permute-start(bf16[64,16,384]{2,1,0:T(8,128)(2,1)S(1)} %get-tuple-element.16), channel_id=1, source_target_pairs={{0,16},{1,17},{2,18},{3,19},{4,20},{5,21},{6,22},{7,23},{8,24},{9,... | collective-permute-start | bytes 2359304 | tf_op jit(solution)/shard_map/ppermute | solution.py:37
  73.3 16.7 %collective-permute-start.26 = (bf16[32,32,128]{2,1,0:T(8,128)(2,1)S(1)}, bf16[32,32,128]{2,1,0:T(8,128)(2,1)S(1)}, u32[]{:S(2)}, u32[]{:S(2)}) collective-permute-start(bf16[32,32,128]{2,1,0:T(8,128)(2,1)S(1)} %slice.266), channel_id=1, source_target_pairs={{0,16},{1,17},{2,18},{3,19},{4,20},{5,21},{6,22},{7,23},{8,24},{9,... | collective-permute-start | bytes 786440 | tf_op jit(solution)/shard_map/ppermute | solution.py:37
  79.3 13.3 %collective-permute-start.22 = (bf16[64,16,384]{2,1,0:T(8,128)(2,1)S(1)}, bf16[64,16,384]{2,1,0:T(8,128)(2,1)S(1)}, u32[]{:S(2)}, u32[]{:S(2)}) collective-permute-start(bf16[64,16,384]{2,1,0:T(8,128)(2,1)S(1)} %get-tuple-element.18), channel_id=1, source_target_pairs={{0,8},{1,9},{2,10},{3,11},{4,12},{5,13},{6,14},{7,15},{8,0},{9,1},... | collective-permute-start | bytes 2359304 | tf_op jit(solution)/shard_map/ppermute | solution.py:37
  88.9 38.2 %collective-permute-start.17 = (f32[2,256,512]{2,1,0:T(8,128)S(1)}, f32[2,256,512]{2,1,0:T(8,128)S(1)}, u32[]{:S(2)}, u32[]{:S(2)}) collective-permute-start(f32[2,256,512]{2,1,0:T(8,128)S(1)} %get-tuple-element.14), channel_id=1, source_target_pairs={{0,64},{1,65},{2,66},{3,67},{4,68},{5,69},{6,70},{7,71},{8,72},{9,... | collective-permute-start | bytes 3145736 | tf_op jit(solution)/shard_map/ppermute | solution.py:50
  90.1 5.1 %collective-permute-start.27 = (bf16[16,32,128]{2,1,0:T(8,128)(2,1)S(1)}, bf16[16,32,128]{2,1,0:T(8,128)(2,1)S(1)}, u32[]{:S(2)}, u32[]{:S(2)}) collective-permute-start(bf16[16,32,128]{2,1,0:T(8,128)(2,1)S(1)} %slice.269), channel_id=1, source_target_pairs={{0,8},{1,9},{2,10},{3,11},{4,12},{5,13},{6,14},{7,15},{8,0},{9,1},... | collective-permute-start | bytes 393224 | tf_op jit(solution)/shard_map/ppermute | solution.py:37
  91.3 8.1 %collective-permute-start.20 = (bf16[32,16,384]{2,1,0:T(8,128)(2,1)S(1)}, bf16[32,16,384]{2,1,0:T(8,128)(2,1)S(1)}, u32[]{:S(2)}, u32[]{:S(2)}) collective-permute-start(bf16[32,16,384]{2,1,0:T(8,128)(2,1)S(1)} %slice.265), channel_id=1, source_target_pairs={{0,8},{1,9},{2,10},{3,11},{4,12},{5,13},{6,14},{7,15},{8,0},{9,1},... | collective-permute-start | bytes 1179656 | tf_op jit(solution)/shard_map/ppermute | solution.py:37
  92.8 7.9 %collective-permute-start.23 = (bf16[32,16,384]{2,1,0:T(8,128)(2,1)S(1)}, bf16[32,16,384]{2,1,0:T(8,128)(2,1)S(1)}, u32[]{:S(2)}, u32[]{:S(2)}) collective-permute-start(bf16[32,16,384]{2,1,0:T(8,128)(2,1)S(1)} %slice.264), channel_id=1, source_target_pairs={{0,1},{1,0},{2,3},{3,2},{4,5},{5,4},{6,7},{7,6},{8,9},{9,8},{10,11... | collective-permute-start | bytes 1179656 | tf_op jit(solution)/shard_map/ppermute | solution.py:37
  99.5 5.8 %collective-permute-start.21 = (bf16[16,16,384]{2,1,0:T(8,128)(2,1)S(1)}, bf16[16,16,384]{2,1,0:T(8,128)(2,1)S(1)}, u32[]{:S(2)}, u32[]{:S(2)}) collective-permute-start(bf16[16,16,384]{2,1,0:T(8,128)(2,1)S(1)} %slice.268), channel_id=1, source_target_pairs={{0,1},{1,0},{2,3},{3,2},{4,5},{5,4},{6,7},{7,6},{8,9},{9,8},{10,11... | collective-permute-start | bytes 589832 | tf_op jit(solution)/shard_map/ppermute | solution.py:37
  100.8 5.8 %collective-permute-start.24 = (bf16[16,16,384]{2,1,0:T(8,128)(2,1)S(1)}, bf16[16,16,384]{2,1,0:T(8,128)(2,1)S(1)}, u32[]{:S(2)}, u32[]{:S(2)}) collective-permute-start(bf16[16,16,384]{2,1,0:T(8,128)(2,1)S(1)} %slice.267), channel_id=1, source_target_pairs={{0,16},{1,17},{2,18},{3,19},{4,20},{5,21},{6,22},{7,23},{8,24},{9,... | collective-permute-start | bytes 589832 | tf_op jit(solution)/shard_map/ppermute | solution.py:37
  106.7 7.9 %collective-permute-start.29 = (bf16[4,32,512]{2,1,0:T(8,128)(2,1)S(1)}, bf16[4,32,512]{2,1,0:T(8,128)(2,1)S(1)}, u32[]{:S(2)}, u32[]{:S(2)}) collective-permute-start(bf16[4,32,512]{2,1,0:T(8,128)(2,1)S(1)} %pad_maximum_fusion.5), channel_id=1, source_target_pairs={{0,32},{1,33},{2,34},{3,35},{4,36},{5,37},{6,38},{7,39},{8,40},{9,... | collective-permute-start | bytes 393224 | tf_op jit(solution)/shard_map/ppermute | solution.py:45
  109.2 9.3 %collective-permute-start.30 = (bf16[4,32,512]{2,1,0:T(8,128)(2,1)S(1)}, bf16[4,32,512]{2,1,0:T(8,128)(2,1)S(1)}, u32[]{:S(2)}, u32[]{:S(2)}) collective-permute-start(bf16[4,32,512]{2,1,0:T(8,128)(2,1)S(1)} %pad_maximum_fusion.6), channel_id=1, source_target_pairs={{0,160},{1,161},{2,162},{3,163},{4,164},{5,165},{6,166},{7,167},{8... | collective-permute-start | bytes 393224 | tf_op jit(solution)/shard_map/ppermute | solution.py:45
  112.5 8.8 %collective-permute-start.28 = (bf16[4,32,512]{2,1,0:T(8,128)(2,1)S(1)}, bf16[4,32,512]{2,1,0:T(8,128)(2,1)S(1)}, u32[]{:S(2)}, u32[]{:S(2)}) collective-permute-start(bf16[4,32,512]{2,1,0:T(8,128)(2,1)S(1)} %pad_maximum_fusion.4), channel_id=1, source_target_pairs={{0,128},{1,129},{2,130},{3,131},{4,132},{5,133},{6,134},{7,135},{8... | collective-permute-start | bytes 393224 | tf_op jit(solution)/shard_map/ppermute | solution.py:45
  121.3 6.8 %collective-permute-start.31 = (bf16[32,512]{1,0:T(8,128)(2,1)S(1)}, bf16[32,512]{1,0:T(8,128)(2,1)S(1)}, u32[]{:S(2)}, u32[]{:S(2)}) collective-permute-start(bf16[32,512]{1,0:T(8,128)(2,1)S(1)} %get-tuple-element.45), channel_id=1, source_target_pairs={{0,2},{1,3},{2,4},{3,5},{4,6},{5,7},{6,0},{7,1},{8,10},{9,11},{10,... | collective-permute-start | bytes 98312 | tf_op jit(solution)/shard_map/ppermute | solution.py:45
  122.1 6.0 %collective-permute-start.33 = (bf16[32,512]{1,0:T(8,128)(2,1)S(1)}, bf16[32,512]{1,0:T(8,128)(2,1)S(1)}, u32[]{:S(2)}, u32[]{:S(2)}) collective-permute-start(bf16[32,512]{1,0:T(8,128)(2,1)S(1)} %get-tuple-element.46), channel_id=1, source_target_pairs={{0,6},{1,7},{2,0},{3,1},{4,2},{5,3},{6,4},{7,5},{8,14},{9,15},{10,... | collective-permute-start | bytes 98312 | tf_op jit(solution)/shard_map/ppermute | solution.py:45
  125.5 8.0 %collective-permute-start.32 = (bf16[32,512]{1,0:T(8,128)(2,1)S(1)}, bf16[32,512]{1,0:T(8,128)(2,1)S(1)}, u32[]{:S(2)}, u32[]{:S(2)}) collective-permute-start(bf16[32,512]{1,0:T(8,128)(2,1)S(1)} %get-tuple-element.47), channel_id=1, source_target_pairs={{0,4},{1,5},{2,6},{3,7},{4,0},{5,1},{6,2},{7,3},{8,12},{9,13},{10,... | collective-permute-start | bytes 98312 | tf_op jit(solution)/shard_map/ppermute | solution.py:45

commit v2 on v0

v2 whole, which is shorter than its diff:
```python
import jax
import jax.numpy as jnp
from jax import lax
from jax.experimental import pallas as pl
from jax.experimental.pallas import tpu as pltpu
from jax.sharding import PartitionSpec as P

F32, BF16 = jnp.float32, jnp.bfloat16
ALL = ("node", "dp")
INTERPRET = False
VMEM = pl.BlockSpec(memory_space=pltpu.VMEM)
PARAMS = pltpu.CompilerParams(vmem_limit_bytes=40 << 20)


STREAMS = ((16, 384), (16, 384), (32, 128))
AXES = ((0, 1, 2), (1, 2, 0), (2, 0, 1))


def place(x, y, z, c):
    return ((((y // 2) * 2 + c) * 4 + x) * 2 + y % 2) * 8 + z


def permute(value, move):
    pairs = []
    for c in range(2):
        for x in range(4):
            for y in range(4):
                for z in range(8):
                    pairs.append((place(x, y, z, c), place(*move(x, y, z, c))))
    return lax.ppermute(value, ALL, pairs)


def neighbour(v, n, c):
    return (v + 1 - 2 * ((v + c) % 2)) % n


def near(value, axis):
    def move(x, y, z, c):
        at = [x, y, z]
        at[axis] = neighbour(at[axis], (4, 4, 8)[axis], c)
        return (*at, c)

    return permute(value, move)


def plane_step(value, xb, yb):
    def move(x, y, z, c):
        return (neighbour(x, 4, 1 - c) if xb else x, neighbour(y, 4, 1 - c) if yb else y, z, c)

    return permute(value, move)


def line_step(value, d):
    return permute(value, lambda x, y, z, c: (x, y, (z + d) % 8, c))


def swap(value):
    return permute(value, lambda x, y, z, c: (x, y, z, 1 - c))


def as_int(flag):
    return jnp.where(flag, 1, 0)


def label4(u, v, c):
    step = 1 - 2 * lax.rem(v + c, 2)
    delta = lax.rem(u - v + 4, 4)
    far = delta == 2
    return as_int(far | (delta == lax.rem(step + 4, 4))), as_int(far | (delta == lax.rem(4 - step, 4)))


def label8(u, v, c):
    p = lax.rem(u + v, 2)
    step = 1 - 2 * lax.rem(v + c, 2)
    return p, lax.rem(u - v - p * step + 16, 8) // 2


def reached4(v, c, a, b):
    step = 1 - 2 * lax.rem(v + c, 2)
    return lax.rem(v + (2 if a and b else a * step - b * step) + 4, 4)


def reached8(v, c, a, d):
    step = 1 - 2 * lax.rem(v + c, 2)
    return lax.rem(v + a * step + 2 * d + 8, 8)


def call(kernel, outs, *args, **more):
    return pl.pallas_call(
        kernel,
        out_shape=[jax.ShapeDtypeStruct(*o) for o in outs],
        in_specs=[VMEM] * len(args),
        out_specs=[VMEM] * len(outs),
        compiler_params=PARAMS,
        interpret=INTERPRET,
        **more,
    )(*args)


def first_kernel(me, tokens, master, moment, second, gradient, r0, r1, weight, out_master, out_moment, out_second, sems):
    far = pl.multiple_of(2048 * (1 - me[3]), 2048)
    copies = [
        pltpu.make_async_copy(tokens.at[:, :, pl.ds(far + 4096 * i, 2048)], ref, sems.at[i])
        for i, ref in enumerate((r0, r1))
    ]
    for copy in copies:
        copy.start()
    new_moment = 0.9 * moment[...] + 0.1 * gradient[...]
    new_second = 0.95 * second[...] + 0.05 * gradient[...] * gradient[...]
    first_fix = 1.0 - 0.9**10
    second_fix = 1.0 - 0.95**10
    update = new_moment / first_fix / (jnp.sqrt(new_second / second_fix) + 1e-08) + 0.1 * master[...]
    new_master = master[...] - 0.001 * update
    out_master[...] = new_master
    out_moment[...] = new_moment
    out_second[...] = new_second
    weight[...] = new_master.astype(BF16)
    for copy in copies:
        copy.wait()


def first(me, tokens, master, moment, second, gradient):
    half = jax.ShapeDtypeStruct((*tokens.shape[:2], 2048), BF16)
    rows = jax.ShapeDtypeStruct(master.shape, F32)
    return pl.pallas_call(
        first_kernel,
        in_specs=[pl.BlockSpec(memory_space=pltpu.SMEM), pl.BlockSpec(memory_space=pl.ANY)] + [VMEM] * 4,
        out_specs=[VMEM] * 6,
        out_shape=[half, half, jax.ShapeDtypeStruct(master.shape, BF16), rows, rows, rows],
        scratch_shapes=[pltpu.SemaphoreType.DMA((2,))],
        compiler_params=PARAMS,
        interpret=INTERPRET,
    )(me, tokens, master, moment, second, gradient)


def dot_rows(a, b):
    rows = a.shape[0] * a.shape[1]
    return lax.dot_general(
        a[...].reshape(rows, 512), b[...].reshape(rows, 512), (((0,), (0,)), ((), ())), preferred_element_type=F32
    )


def own_kernel(me, own, cot, out):
    out[pl.program_id(0)] = dot_rows(own, cot)


def own_terms(me, tokens, cot):
    block = (*tokens.shape[:2], 512)
    return pl.pallas_call(
        own_kernel,
        grid_spec=pltpu.PrefetchScalarGridSpec(
            num_scalar_prefetch=1,
            grid=(8,),
            in_specs=[
                pl.BlockSpec(block, lambda t, s: (0, 0, (t // 4) * 8 + s[3] * 4 + t % 4)),
                pl.BlockSpec(block, lambda t, s: (0, 0, 0)),
            ],
            out_specs=VMEM,
        ),
        out_shape=jax.ShapeDtypeStruct((8, 512, 512), F32),
        compiler_params=PARAMS,
        interpret=INTERPRET,
    )(me, tokens, cot)


def terms_kernel(me, r0, r1, cot, mine, sx, sy, sz, kx, ky, kz):
    t = pl.program_id(0)
    yh, x = t // 4, lax.rem(t, 4)
    mx, my, mz, c = me[0], me[1], me[2], me[3]

    def work(other):
        acc = mine[t] + dot_rows(other, cot)
        xa, xb = label4(x, mx, c)
        ys = [label4(2 * yh + yl, my, c) for yl in range(2)]
        zs = [label8(z, mz, c) for z in range(8)]

        def put(ref, stream, yl, z):
            near_at = (xa, ys[yl][0], zs[z][0])
            _, second, third = AXES[stream]
            at = near_at[second] * 32 + near_at[third] * 16 + xb * 8 + ys[yl][1] * 4 + zs[z][1]
            row = (yl * 8 + z) * 32
            part = (
                acc[row : row + 16, 0:384],
                acc[row + 16 : row + 32, 0:384],
                acc[row : row + 32, 384:512],
            )[stream]
            ref[at] = part.astype(ref.dtype)

        everywhere = [(yl, z) for yl in range(2) for z in range(8)]
        for sent, ref in ((0, kx), (1, sx)):

            @pl.when(xa == sent)
            def _(ref=ref):
                for yl, z in everywhere:
                    put(ref, 0, yl, z)

        for yl in range(2):
            for sent, ref in ((0, ky), (1, sy)):

                @pl.when(ys[yl][0] == sent)
                def _(ref=ref, yl=yl):
                    for z in range(8):
                        put(ref, 1, yl, z)

        for parity in range(2):

            @pl.when(lax.rem(mz, 2) == parity)
            def _(parity=parity):
                for yl, z in everywhere:
                    put(kz if z % 2 == parity else sz, 2, yl, z)

    @pl.when(yh == 0)
    def _():
        work(r0)

    @pl.when(yh == 1)
    def _():
        work(r1)


def all_terms(me, r0, r1, cot, mine):
    block = (*r0.shape[:2], 512)
    return pl.pallas_call(
        terms_kernel,
        grid_spec=pltpu.PrefetchScalarGridSpec(
            num_scalar_prefetch=1,
            grid=(8,),
            in_specs=[
                pl.BlockSpec(block, lambda t, s: (0, 0, jnp.minimum(t, 3))),
                pl.BlockSpec(block, lambda t, s: (0, 0, jnp.maximum(t - 4, 0))),
                pl.BlockSpec(block, lambda t, s: (0, 0, 0)),
                VMEM,
            ],
            out_specs=[VMEM] * 6,
        ),
        out_shape=[jax.ShapeDtypeStruct((80, *s), BF16) for s in STREAMS]
        + [jax.ShapeDtypeStruct((64, *s), F32) for s in STREAMS],
        compiler_params=PARAMS,
        interpret=INTERPRET,
    )(me, r0, r1, cot, mine)


def cut(stream, block):
    return (block[..., 0:16, 0:384], block[..., 16:32, 0:384], block[..., :, 384:512])[stream]


def pack_kernel(*refs):
    plane, outs = refs[3:7], refs[7:10]
    for stream, out in enumerate(outs):
        for q, part in enumerate(plane):
            out[64 + 4 * q : 68 + 4 * q] = cut(stream, part[...])


def second_kernel(sent, got, keep, send, kept):
    send[0:32] = (keep[32:64] + got[32:64].astype(F32)).astype(BF16)
    send[32:48] = sent[64:80]
    send[48:64] = got[64:80]
    kept[...] = keep[0:32] + got[0:32].astype(F32)


def third_kernel(sent, got, keep, send, kept):
    send[0:16] = (keep[16:32] + got[16:32].astype(F32)).astype(BF16)
    send[16:48] = sent[32:64]
    send[48:80] = got[32:64]
    kept[...] = keep[0:16] + got[0:16].astype(F32)


def far_kernel(gx, gy, gz, kx, ky, kz, own, s1, s2, s3):
    for q, out in enumerate((own, s1, s2, s3)):
        at = slice(4 * q, 4 * q + 4)
        out[:, 0:16, 0:384] = (kx[at] + gx[at].astype(F32)).astype(out.dtype)
        out[:, 16:32, 0:384] = (ky[at] + gy[at].astype(F32)).astype(out.dtype)
        out[:, :, 384:512] = (kz[at] + gz[at].astype(F32)).astype(out.dtype)


def last_kernel(own, g1, g2, g3, kept, s1, s2, s3):
    for d, out in enumerate((kept, s1, s2, s3)):
        total = own[d] + g1[d].astype(F32) + g2[d].astype(F32) + g3[d].astype(F32)
        out[...] = total.astype(out.dtype)


def sum_kernel(own, g1, g2, g3, out):
    out[...] = own[...] + g1[...].astype(F32) + g2[...].astype(F32) + g3[...].astype(F32)


def assemble(me, sx, sy, sz, gx, gy, gz, w):
    mx, my, mz, c = me[0], me[1], me[2], me[3]
    xs = [[reached4(mx, c, a, b) * 512 for b in range(2)] for a in range(2)]
    ys = [[reached4(my, c, a, b) for b in range(2)] for a in range(2)]
    ys = [[(y // 2) * 2048 + lax.rem(y, 2) * 256 for y in row] for row in ys]
    zs = [[reached8(mz, c, a, d) * 32 for d in range(4)] for a in range(2)]
    for xa in range(2):
        for ya in range(2):
            for za in range(2):
                for i in range(16):
                    at = pl.multiple_of(xs[xa][i // 8] + ys[ya][(i // 4) % 2] + zs[za][i % 4], 32)
                    label = (xa, ya, za)

                    def part(stream, sent, got):
                        first, second, third = (label[axis] for axis in AXES[stream])
                        return (got if third else sent)[16 + second * 32 + first * 16 + i]

                    w[pl.ds(at, 16), 0:384] = part(0, sx, gx)
                    w[pl.ds(at + 16, 16), 0:384] = part(1, sy, gy)
                    w[pl.ds(at, 32), 384:512] = part(2, sz, gz)


def product(a, b, w):
    return jnp.dot(a[0], w[0:2048], preferred_element_type=F32) + jnp.dot(
        b[0], w[2048:4096], preferred_element_type=F32
    )


def other_kernel(me, r0, r1, sx, sy, sz, gx, gy, gz, out, w):
    @pl.when(pl.program_id(0) == 0)
    def _():
        assemble(me, sx, sy, sz, gx, gy, gz, w)

    out[0] = product(r0, r1, w)


def mine_kernel(me, own0, own1, w, out):
    out[0] = product(own0, own1, w)


def other_values(me, r0, r1, messages):
    micro, rows, _ = r0.shape
    block = (1, rows, 2048)
    return pl.pallas_call(
        other_kernel,
        grid_spec=pltpu.PrefetchScalarGridSpec(
            num_scalar_prefetch=1,
            grid=(micro,),
            in_specs=[pl.BlockSpec(block, lambda t, s: (t, 0, 0))] * 2 + [VMEM] * 6,
            out_specs=[pl.BlockSpec((1, rows, 512), lambda t, s: (t, 0, 0)), VMEM],
        ),
        out_shape=[
            jax.ShapeDtypeStruct((micro, rows, 512), F32),
            jax.ShapeDtypeStruct((4096, 512), BF16),
        ],
        compiler_params=PARAMS,
        interpret=INTERPRET,
    )(me, r0, r1, *messages)


def my_values(me, tokens, w):
    micro, rows, _ = tokens.shape
    block = (1, rows, 2048)
    return pl.pallas_call(
        mine_kernel,
        grid_spec=pltpu.PrefetchScalarGridSpec(
            num_scalar_prefetch=1,
            grid=(micro,),
            in_specs=[
                pl.BlockSpec(block, lambda t, s: (t, 0, s[3])),
                pl.BlockSpec(block, lambda t, s: (t, 0, 2 + s[3])),
                VMEM,
            ],
            out_specs=pl.BlockSpec((1, rows, 512), lambda t, s: (t, 0, 0)),
        ),
        out_shape=jax.ShapeDtypeStruct((micro, rows, 512), F32),
        compiler_params=PARAMS,
        interpret=INTERPRET,
    )(me, tokens, tokens, w)


def after(value, *others):
    return lax.optimization_barrier((value, *others))[0]


def body(tokens, cotangent, master, moment, second, gradient):
    node, dp = lax.axis_index("node"), lax.axis_index("dp")
    me = jnp.stack([dp // 16, (node // 2) * 2 + (dp // 8) % 2, dp % 8, node % 2]).astype(jnp.int32)

    r0, r1, weight, new_master, new_moment, new_second = first(me, tokens, master, moment, second, gradient)
    r0, r1, cotr = swap(r0), swap(r1), swap(cotangent)
    line = jnp.stack([weight] + [line_step(weight, -2 * d) for d in (1, 2, 3)])
    mine = own_terms(me, tokens, cotangent)
    line = after(line, mine)
    plane = [line] + [plane_step(line, q // 2, q % 2) for q in (1, 2, 3)]
    terms = all_terms(me, r0, r1, cotr, mine)
    send, keep = terms[:3], terms[3:]

    send = call(
        pack_kernel,
        [((80, *s), BF16) for s in STREAMS],
        *send,
        *plane,
        input_output_aliases={0: 0, 1: 1, 2: 2},
    )
    got = [near(send[i], AXES[i][0]) for i in range(3)]
    for step, kernel, size, rest in ((1, second_kernel, 64, 32), (2, third_kernel, 80, 16)):
        new = [
            call(kernel, [((size, *STREAMS[i]), BF16), ((rest, *STREAMS[i]), F32)], send[i], got[i], keep[i])
            for i in range(3)
        ]
        send, keep = [n[0] for n in new], [n[1] for n in new]
        got = [near(send[i], AXES[i][step]) for i in range(3)]

    block = (4, 32, 512)
    own, *parts = call(far_kernel, [(block, F32)] + [(block, BF16)] * 3, *got, *keep)
    parts = [plane_step(part, q // 2, q % 2) for q, part in zip((1, 2, 3), parts)]

    other, w = other_values(me, r0, r1, [*send, *got])

    own, *parts = call(last_kernel, [(block[1:], F32)] + [(block[1:], BF16)] * 3, own, *parts)
    parts = [line_step(part, 2 * d) for d, part in zip((1, 2, 3), parts)]
    (weight_grad,) = call(sum_kernel, [(block[1:], F32)], own, *parts)

    ours = my_values(me, tokens, w)
    values = (ours + swap(other)).astype(BF16)
    return (new_master, new_moment, new_second, values, weight_grad)


def solution(mesh):
    rows = P(("node", "dp"), None)
    tall = P(None, ("node", "dp"), None)
    return jax.shard_map(
        body,
        mesh=mesh,
        in_specs=(tall, tall, rows, rows, rows, rows),
        out_specs=(rows, rows, rows, tall, rows),
        check_vma=False,
    )
```

time: 1630 us -> 123 us (0.08)
  waiting for transfers between devices: 1590 us -> 40.7 us
  starting transfers between devices: 0.12 us -> 38.3 us
  Pallas kernels: 0 us -> 29.1 us
  matrix products: 23 us -> 0 us
    reduce_scatter x1 -> x0, waiting for transfers between devices: 1230 us -> none  [body(): lax.psum_scatter(local_term, ('node', 'dp'), scatter_dimension=0, tiled=T...]
    all_gather x2 -> x0, waiting for transfers between devices: 361 us -> none  [the longest x1 302 us: body(): block = lax.all_gather(weight, 'dp', axis=0, tiled=True)]
    ppermute x0 -> x25, waiting for transfers between devices: none -> 40.7 us  [permute(): return lax.ppermute(value, ALL, pairs)]
    ppermute x0 -> x25, starting transfers between devices: none -> 38.3 us  [permute(): return lax.ppermute(value, ALL, pairs)]
    pallas_call x0 -> x15, Pallas kernels: none -> 29.1 us  [the longest x1 9.86 us: all_terms(): pl.pallas_call(terms_kernel, grid_spec=pltpu.PrefetchScalarGridSpec(num_s...]
    dot_general x2 -> x0, matrix products: 23 us -> none  [the longest x1 12.6 us: body(): jnp.einsum('mtd,mtv->dv', tokens, cotangent, preferred_element_type=jnp.f...]
  transfers between devices with their start and end apart: 3 -> 25, of which waited for: 3 -> 9; matrix products, arithmetic and copies ran while one was open for 1% -> 0% of each run, Pallas kernels for 0% -> 18%
where the time goes in v2:
time: 123 us; the launch traced here: 121 us
  waiting for transfers between devices  40.7 us (33%)
  starting transfers between devices  38.3 us (31%)
  Pallas kernels  29.1 us (24%)
  local copies, waits for them, and re-layouts  11.3 us (9%)
    ppermute x25, waiting for transfers between devices, permute(): return lax.ppermute(value, ALL, pairs)  40.7 us
    ppermute x25, starting transfers between devices, permute(): return lax.ppermute(value, ALL, pairs)  38.3 us
    unnamed x24, local copies, waits for them, and re-layouts  11.3 us
    pallas_call x1, Pallas kernels, all_terms(): pl.pallas_call(terms_kernel, grid_spec=pltpu.PrefetchScalarGridSpec(num_s...  9.86 us
    pallas_call x1, Pallas kernels, own_terms(): pl.pallas_call(own_kernel, grid_spec=pltpu.PrefetchScalarGridSpec(num_sca...  7.3 us
    pallas_call x1, Pallas kernels, other_values(): pl.pallas_call(other_kernel, grid_spec=pltpu.PrefetchScalarGridSpec(num_s...  4.56 us
    pallas_call x1, Pallas kernels, my_values(): pl.pallas_call(mine_kernel, grid_spec=pltpu.PrefetchScalarGridSpec(num_sc...  3.37 us
  transfers between devices with their start and end apart: 25, of which 9 were waited for; matrix products, arithmetic and copies ran while one was open for 0% of the time, Pallas kernels for 18%

profile of v2, /device:TPU:0, one launch (start us, length us, event | category | flops | bytes accessed | tf_op | source)
XLA Modules:
  0.0 121.3 jit_solution(9507880752418136152)
XLA Ops:
  0.8 3.4 %copy-done = bf16[2,256,8192]{2,1,0:T(8,128)(2,1)S(1)} copy-done((bf16[2,256,8192]{2,1,0:T(8,128)(2,1)S(1)}, bf16[2,256,8192]{2,1,0:T(8,128)(2,1)}, u32[]{:S(2)}) %copy-start) | copy-done | bytes 8388632
  4.2 0.8 copy-done.6
  5.0 0.8 copy-done.7
  5.8 0.8 copy-done.8
  6.7 0.8 copy-done.9
  7.5 2.3 %shard_map.101 = (bf16[2,256,2048]{2,1,0:T(8,128)(2,1)S(1)}, bf16[2,256,2048]{2,1,0:T(8,128)(2,1)S(1)}, bf16[32,512]{1,0:T(8,128)(2,1)S(1)}, f32[32,512]{1,0:T(8...) custom-call(s32[4]{0:T(128)S(1)} %pad_add_fusion.me, bf16[2,256,8192]{2,1,0:T(8,128)(2,1)S(1)} %copy-done, ...), custom_call_target="tpu_custom_call" | custom-call | tf_op jit(solution)/shard_map/pallas_call | solution.py:125
  9.9 0.5 collective-permute-start.1
  10.5 1.5 %collective-permute-start.5 = (bf16[32,512]{1,0:T(8,128)(2,1)S(1)}, bf16[32,512]{1,0:T(8,128)(2,1)S(1)}, u32[]{:S(2)}, u32[]{:S(2)}) collective-permute-start(bf16[32,512]{1,0:T(8,128)(2,1)S(1)} %get-tuple-element.51), channel_id=1, source_target_pairs={{0,2},{1,3},{2,4},{3,5},{4,6},{5,7},{6,0},{7,1},{8,10},{9,11},{10,... | collective-permute-start | bytes 98312 | tf_op jit(solution)/shard_map/ppermute | solution.py:30
  12.1 5.4 %collective-permute-start.4 = (bf16[32,512]{1,0:T(8,128)(2,1)S(1)}, bf16[32,512]{1,0:T(8,128)(2,1)S(1)}, u32[]{:S(2)}, u32[]{:S(2)}) collective-permute-start(bf16[32,512]{1,0:T(8,128)(2,1)S(1)} %get-tuple-element.51), channel_id=1, source_target_pairs={{0,4},{1,5},{2,6},{3,7},{4,0},{5,1},{6,2},{7,3},{8,12},{9,13},{10,... | collective-permute-start | bytes 98312 | tf_op jit(solution)/shard_map/ppermute | solution.py:30
  17.5 2.7 %collective-permute-start.3 = (bf16[32,512]{1,0:T(8,128)(2,1)S(1)}, bf16[32,512]{1,0:T(8,128)(2,1)S(1)}, u32[]{:S(2)}, u32[]{:S(2)}) collective-permute-start(bf16[32,512]{1,0:T(8,128)(2,1)S(1)} %get-tuple-element.51), channel_id=1, source_target_pairs={{0,6},{1,7},{2,0},{3,1},{4,2},{5,3},{6,4},{7,5},{8,14},{9,15},{10,... | collective-permute-start | bytes 98312 | tf_op jit(solution)/shard_map/ppermute | solution.py:30
  20.2 7.3 %shard_map.102.mine = f32[8,512,512]{2,1,0:T(8,128)S(1)} custom-call(s32[4]{0:T(128)S(1)} %pad_add_fusion.me, bf16[2,256,8192]{2,1,0:T(8,128)(2,1)} %own1.1, bf16[2,256,512]{2,1,0:T(8,128)(2,1)S(1)} %copy-done.5), custom_call_target="tpu_custom_call" | custom-call | tf_op jit(solution)/shard_map/pallas_call | solution.py:149
  27.5 3.3 %copy-done.1 = f32[8,512,512]{2,1,0:T(8,128)} copy-done((f32[8,512,512]{2,1,0:T(8,128)}, f32[8,512,512]{2,1,0:T(8,128)S(1)}, u32[]{:S(2)}) %copy-start.1) | copy-done | bytes 8388632
  30.8 3.1 %collective-permute-start.6 = (bf16[4,32,512]{2,1,0:T(8,128)(2,1)S(1)}, bf16[4,32,512]{2,1,0:T(8,128)(2,1)S(1)}, u32[]{:S(2)}, u32[]{:S(2)}) collective-permute-start(bf16[4,32,512]{2,1,0:T(8,128)(2,1)S(1)} %pad_maximum_fusion.refs_3_), channel_id=1, source_target_pairs={{0,136},{1,137},{2,138},{3,139},{4,140},{5,141},{6,142},{7,143},{8... | collective-permute-start | bytes 393224 | tf_op jit(solution)/shard_map/ppermute | solution.py:30
  33.9 2.8 %collective-permute-start.7 = (bf16[4,32,512]{2,1,0:T(8,128)(2,1)S(1)}, bf16[4,32,512]{2,1,0:T(8,128)(2,1)S(1)}, u32[]{:S(2)}, u32[]{:S(2)}) collective-permute-start(bf16[4,32,512]{2,1,0:T(8,128)(2,1)S(1)} %pad_maximum_fusion.refs_3_), channel_id=1, source_target_pairs={{0,48},{1,49},{2,50},{3,51},{4,52},{5,53},{6,54},{7,55},{8,56},{9,... | collective-permute-start | bytes 393224 | tf_op jit(solution)/shard_map/ppermute | solution.py:30
  36.7 0.1 collective-permute-start.8
  36.8 9.9 %shard_map.103 = (bf16[80,16,384]{2,1,0:T(8,128)(2,1)S(1)}, bf16[80,16,384]{2,1,0:T(8,128)(2,1)S(1)}, bf16[80,32,128]{2,1,0:T(8,128)(2,1)S(1)}, f32[64,16,384]{2...) custom-call(s32[4]{0:T(128)S(1)} %pad_add_fusion.me, ...), custom_call_target="tpu_custom_call" | custom-call | tf_op jit(solution)/shard_map/pallas_call | solution.py:223
  46.8 0.4 collective-permute-start.9
  47.1 0.4 collective-permute-start.11
  47.5 2.1 %collective-permute-start.13 = (bf16[80,32,128]{2,1,0:T(8,128)(2,1)S(1)}, bf16[80,32,128]{2,1,0:T(8,128)(2,1)S(1)}, u32[]{:S(2)}, u32[]{:S(2)}) collective-permute-start(bf16[80,32,128]{2,1,0:T(8,128)(2,1)S(1)} %get-tuple-element.63.sent), channel_id=1, source_target_pairs={{0,1},{1,0},{2,3},{3,2},{4,5},{5,4},{6,7},{7,6},{8,9},{9,8},{10,11... | collective-permute-start | bytes 1966088 | tf_op jit(solution)/shard_map/ppermute | solution.py:30
  49.6 11.4 %collective-permute-done.9.got = bf16[80,16,384]{2,1,0:T(8,128)(2,1)S(1)} collective-permute-done((bf16[80,16,384]{2,1,0:T(8,128)(2,1)S(1)}, bf16[80,16,384]{2,1,0:T(8,128)(2,1)S(1)}, u32[]{:S(2)}, u32[]{:S(2)}) %collective-permute-start.9) | collective-permute-done | bytes 983072 | tf_op jit(solution)/shard_map/ppermute | solution.py:30
  61.0 0.2 shard_map.105
  61.1 0.5 collective-permute-start.10
  61.6 0.2 shard_map.107
  61.8 2.1 %collective-permute-start.12 = (bf16[64,16,384]{2,1,0:T(8,128)(2,1)S(1)}, bf16[64,16,384]{2,1,0:T(8,128)(2,1)S(1)}, u32[]{:S(2)}, u32[]{:S(2)}) collective-permute-start(bf16[64,16,384]{2,1,0:T(8,128)(2,1)S(1)} %get-tuple-element.60.sent), channel_id=1, source_target_pairs={{0,1},{1,0},{2,3},{3,2},{4,5},{5,4},{6,7},{7,6},{8,9},{9,8},{10,11... | collective-permute-start | bytes 2359304 | tf_op jit(solution)/shard_map/ppermute | solution.py:30
  64.1 1.5 %collective-permute-start.14 = (bf16[64,32,128]{2,1,0:T(8,128)(2,1)S(1)}, bf16[64,32,128]{2,1,0:T(8,128)(2,1)S(1)}, u32[]{:S(2)}, u32[]{:S(2)}) collective-permute-start(bf16[64,32,128]{2,1,0:T(8,128)(2,1)S(1)} %get-tuple-element.65.sent), channel_id=1, source_target_pairs={{0,16},{1,17},{2,18},{3,19},{4,20},{5,21},{6,22},{7,23},{8,24},{9,... | collective-permute-start | bytes 1572872 | tf_op jit(solution)/shard_map/ppermute | solution.py:30
  65.5 7.7 %collective-permute-done.10.got = bf16[64,16,384]{2,1,0:T(8,128)(2,1)S(1)} collective-permute-done((bf16[64,16,384]{2,1,0:T(8,128)(2,1)S(1)}, bf16[64,16,384]{2,1,0:T(8,128)(2,1)S(1)}, u32[]{:S(2)}, u32[]{:S(2)}) %collective-permute-start.10) | collective-permute-done | bytes 786464 | tf_op jit(solution)/shard_map/ppermute | solution.py:30
  73.2 0.1 shard_map.106
  73.4 2.3 %collective-permute-start.15 = (bf16[80,16,384]{2,1,0:T(8,128)(2,1)S(1)}, bf16[80,16,384]{2,1,0:T(8,128)(2,1)S(1)}, u32[]{:S(2)}, u32[]{:S(2)}) collective-permute-start(bf16[80,16,384]{2,1,0:T(8,128)(2,1)S(1)} %get-tuple-element.57.sx), channel_id=1, source_target_pairs={{0,1},{1,0},{2,3},{3,2},{4,5},{5,4},{6,7},{7,6},{8,9},{9,8},{10,11... | collective-permute-start | bytes 2949128 | tf_op jit(solution)/shard_map/ppermute | solution.py:30
  75.7 0.2 shard_map.108
  75.8 0.4 collective-permute-start.16
  76.3 0.5 collective-permute-start.17
  76.8 10.2 %collective-permute-done.17.gz = bf16[80,32,128]{2,1,0:T(8,128)(2,1)S(1)} collective-permute-done((bf16[80,32,128]{2,1,0:T(8,128)(2,1)S(1)}, bf16[80,32,128]{2,1,0:T(8,128)(2,1)S(1)}, u32[]{:S(2)}, u32[]{:S(2)}) %collective-permute-start.17) | collective-permute-done | bytes 655392 | tf_op jit(solution)/shard_map/ppermute | solution.py:30
  87.0 0.8 collective-permute-done.15.gx
  87.8 2.3 %collective-permute-done.16.gy = bf16[80,16,384]{2,1,0:T(8,128)(2,1)S(1)} collective-permute-done((bf16[80,16,384]{2,1,0:T(8,128)(2,1)S(1)}, bf16[80,16,384]{2,1,0:T(8,128)(2,1)S(1)}, u32[]{:S(2)}, u32[]{:S(2)}) %collective-permute-start.16) | collective-permute-done | bytes 983072 | tf_op jit(solution)/shard_map/ppermute | solution.py:30
  90.0 4.6 %shard_map.111 = (f32[2,256,512]{2,1,0:T(8,128)S(1)}, bf16[4096,512]{1,0:T(8,128)(2,1)}) custom-call(s32[4]{0:T(128)S(1)} %pad_add_fusion.me, bf16[2,256,2048]{2,1,0:T(8,128)(2,1)S(1)} %collective-permute-done.r0, bf16[2,256,2048]{2,1,0:T(8,128)(2,1)S(1)} %collective-permute-done.1.r1, bf16[80,16,384]{2,1,0:T(8,128)(2,1)S(1)} %get-tuple-element.57.sx, ...), custom_call_target="tpu_custom_call" | custom-call | tf_op jit(solution)/shard_map/pallas_call | solution.py:329
  94.6 1.2 copy-done.4
  95.9 3.1 %collective-permute-start.19 = (bf16[4,32,512]{2,1,0:T(8,128)(2,1)S(1)}, bf16[4,32,512]{2,1,0:T(8,128)(2,1)S(1)}, u32[]{:S(2)}, u32[]{:S(2)}) collective-permute-start(bf16[4,32,512]{2,1,0:T(8,128)(2,1)S(1)} %get-tuple-element.74), channel_id=1, source_target_pairs={{0,136},{1,137},{2,138},{3,139},{4,140},{5,141},{6,142},{7,143},{8... | collective-permute-start | bytes 393224 | tf_op jit(solution)/shard_map/ppermute | solution.py:30
  99.0 2.8 %collective-permute-start.20 = (bf16[4,32,512]{2,1,0:T(8,128)(2,1)S(1)}, bf16[4,32,512]{2,1,0:T(8,128)(2,1)S(1)}, u32[]{:S(2)}, u32[]{:S(2)}) collective-permute-start(bf16[4,32,512]{2,1,0:T(8,128)(2,1)S(1)} %get-tuple-element.75), channel_id=1, source_target_pairs={{0,48},{1,49},{2,50},{3,51},{4,52},{5,53},{6,54},{7,55},{8,56},{9,... | collective-permute-start | bytes 393224 | tf_op jit(solution)/shard_map/ppermute | solution.py:30
  101.8 0.1 collective-permute-start.21
  101.9 0.3 collective-permute-done.19.g1
  102.2 3.0 %collective-permute-done.20.g2 = bf16[4,32,512]{2,1,0:T(8,128)(2,1)S(1)} collective-permute-done((bf16[4,32,512]{2,1,0:T(8,128)(2,1)S(1)}, bf16[4,32,512]{2,1,0:T(8,128)(2,1)S(1)}, u32[]{:S(2)}, u32[]{:S(2)}) %collective-permute-start.20) | collective-permute-done | bytes 131104 | tf_op jit(solution)/shard_map/ppermute | solution.py:30
  105.2 4.9 %collective-permute-done.21.g3 = bf16[4,32,512]{2,1,0:T(8,128)(2,1)S(1)} collective-permute-done((bf16[4,32,512]{2,1,0:T(8,128)(2,1)S(1)}, bf16[4,32,512]{2,1,0:T(8,128)(2,1)S(1)}, u32[]{:S(2)}, u32[]{:S(2)}) %collective-permute-start.21) | collective-permute-done | bytes 131104 | tf_op jit(solution)/shard_map/ppermute | solution.py:30
  110.2 4.7 %collective-permute-start.23 = (bf16[32,512]{1,0:T(8,128)(2,1)S(1)}, bf16[32,512]{1,0:T(8,128)(2,1)S(1)}, u32[]{:S(2)}, u32[]{:S(2)}) collective-permute-start(bf16[32,512]{1,0:T(8,128)(2,1)S(1)} %get-tuple-element.79), channel_id=1, source_target_pairs={{0,4},{1,5},{2,6},{3,7},{4,0},{5,1},{6,2},{7,3},{8,12},{9,13},{10,... | collective-permute-start | bytes 98312 | tf_op jit(solution)/shard_map/ppermute | solution.py:30
  114.9 1.2 %collective-permute-start.24 = (bf16[32,512]{1,0:T(8,128)(2,1)S(1)}, bf16[32,512]{1,0:T(8,128)(2,1)S(1)}, u32[]{:S(2)}, u32[]{:S(2)}) collective-permute-start(bf16[32,512]{1,0:T(8,128)(2,1)S(1)} %get-tuple-element.80), channel_id=1, source_target_pairs={{0,6},{1,7},{2,0},{3,1},{4,2},{5,3},{6,4},{7,5},{8,14},{9,15},{10,... | collective-permute-start | bytes 98312 | tf_op jit(solution)/shard_map/ppermute | solution.py:30
  116.1 3.4 %shard_map.112 = f32[2,256,512]{2,1,0:T(8,128)S(1)} custom-call(s32[4]{0:T(128)S(1)} %pad_add_fusion.me, bf16[2,256,8192]{2,1,0:T(8,128)(2,1)S(1)} %bitcast.9, bf16[2,256,8192]{2,1,0:T(8,128)(2,1)S(1)} %bitcast.9, bf16[4096,512]{1,0:T(8,128)(2,1)S(1)} %copy-done.2), custom_call_target="tpu_custom_call" | custom-call | tf_op jit(solution)/shard_map/pallas_call | solution.py:349
  119.5 0.2 collective-permute-done.24.g3
  119.7 0.6 shard_map.115
  120.3 0.9 add_convert_fusion
  (45 shorter events, 0.9 us)
Async XLA Ops:
  0.8 3.4 %copy-start = (bf16[2,256,8192]{2,1,0:T(8,128)(2,1)S(1)}, bf16[2,256,8192]{2,1,0:T(8,128)(2,1)}, u32[]{:S(2)}) copy-start(bf16[2,256,8192]{2,1,0:T(8,128)(2,1)} %own1.1) | copy-start | bytes 25165828
  4.2 0.8 copy-start.6
  5.0 0.8 copy-start.7
  5.8 0.8 copy-start.8
  6.7 0.8 copy-start.9
  7.5 2.9 %copy-start.5 = (bf16[2,256,512]{2,1,0:T(8,128)(2,1)S(1)}, bf16[2,256,512]{2,1,0:T(8,128)(2,1)}, u32[]{:S(2)}) copy-start(bf16[2,256,512]{2,1,0:T(8,128)(2,1)} %cot.1) | copy-start | bytes 1572868
  9.8 27.0 %collective-permute-start = (bf16[2,256,2048]{2,1,0:T(8,128)(2,1)S(1)}, bf16[2,256,2048]{2,1,0:T(8,128)(2,1)S(1)}, u32[]{:S(2)}, u32[]{:S(2)}) collective-permute-start(bf16[2,256,2048]{2,1,0:T(8,128)(2,1)S(1)} %get-tuple-element.46), channel_id=1, source_target_pairs={{0,64},{1,65},{2,66},{3,67},{4,68},{5,69},{6,70},{7,71},{8,72},{9,... | collective-permute-start | bytes 6291464 | tf_op jit(solution)/shard_map/ppermute | solution.py:30
  9.9 26.9 %collective-permute-start.1 = (bf16[2,256,2048]{2,1,0:T(8,128)(2,1)S(1)}, bf16[2,256,2048]{2,1,0:T(8,128)(2,1)S(1)}, u32[]{:S(2)}, u32[]{:S(2)}) collective-permute-start(bf16[2,256,2048]{2,1,0:T(8,128)(2,1)S(1)} %get-tuple-element.47), channel_id=1, source_target_pairs={{0,64},{1,65},{2,66},{3,67},{4,68},{5,69},{6,70},{7,71},{8,72},{9,... | collective-permute-start | bytes 6291464 | tf_op jit(solution)/shard_map/ppermute | solution.py:30
  10.4 26.2 %collective-permute-start.2 = (bf16[2,256,512]{2,1,0:T(8,128)(2,1)S(1)}, bf16[2,256,512]{2,1,0:T(8,128)(2,1)S(1)}, u32[]{:S(2)}, u32[]{:S(2)}) collective-permute-start(bf16[2,256,512]{2,1,0:T(8,128)(2,1)S(1)} %copy-done.5), channel_id=1, source_target_pairs={{0,64},{1,65},{2,66},{3,67},{4,68},{5,69},{6,70},{7,71},{8,72},{9,... | collective-permute-start | bytes 1572872 | tf_op jit(solution)/shard_map/ppermute | solution.py:30
  10.5 6.9 %collective-permute-start.5 = (bf16[32,512]{1,0:T(8,128)(2,1)S(1)}, bf16[32,512]{1,0:T(8,128)(2,1)S(1)}, u32[]{:S(2)}, u32[]{:S(2)}) collective-permute-start(bf16[32,512]{1,0:T(8,128)(2,1)S(1)} %get-tuple-element.51), channel_id=1, source_target_pairs={{0,2},{1,3},{2,4},{3,5},{4,6},{5,7},{6,0},{7,1},{8,10},{9,11},{10,... | collective-permute-start | bytes 98312 | tf_op jit(solution)/shard_map/ppermute | solution.py:30
  12.1 18.7 %collective-permute-start.4 = (bf16[32,512]{1,0:T(8,128)(2,1)S(1)}, bf16[32,512]{1,0:T(8,128)(2,1)S(1)}, u32[]{:S(2)}, u32[]{:S(2)}) collective-permute-start(bf16[32,512]{1,0:T(8,128)(2,1)S(1)} %get-tuple-element.51), channel_id=1, source_target_pairs={{0,4},{1,5},{2,6},{3,7},{4,0},{5,1},{6,2},{7,3},{8,12},{9,13},{10,... | collective-permute-start | bytes 98312 | tf_op jit(solution)/shard_map/ppermute | solution.py:30
  17.5 13.3 %collective-permute-start.3 = (bf16[32,512]{1,0:T(8,128)(2,1)S(1)}, bf16[32,512]{1,0:T(8,128)(2,1)S(1)}, u32[]{:S(2)}, u32[]{:S(2)}) collective-permute-start(bf16[32,512]{1,0:T(8,128)(2,1)S(1)} %get-tuple-element.51), channel_id=1, source_target_pairs={{0,6},{1,7},{2,0},{3,1},{4,2},{5,3},{6,4},{7,5},{8,14},{9,15},{10,... | collective-permute-start | bytes 98312 | tf_op jit(solution)/shard_map/ppermute | solution.py:30
  27.5 3.3 %copy-start.1 = (f32[8,512,512]{2,1,0:T(8,128)}, f32[8,512,512]{2,1,0:T(8,128)S(1)}, u32[]{:S(2)}) copy-start(f32[8,512,512]{2,1,0:T(8,128)S(1)} %shard_map.102.mine) | copy-start | bytes 25165828
  30.8 15.9 %collective-permute-start.6 = (bf16[4,32,512]{2,1,0:T(8,128)(2,1)S(1)}, bf16[4,32,512]{2,1,0:T(8,128)(2,1)S(1)}, u32[]{:S(2)}, u32[]{:S(2)}) collective-permute-start(bf16[4,32,512]{2,1,0:T(8,128)(2,1)S(1)} %pad_maximum_fusion.refs_3_), channel_id=1, source_target_pairs={{0,136},{1,137},{2,138},{3,139},{4,140},{5,141},{6,142},{7,143},{8... | collective-permute-start | bytes 393224 | tf_op jit(solution)/shard_map/ppermute | solution.py:30
  33.9 12.8 %collective-permute-start.7 = (bf16[4,32,512]{2,1,0:T(8,128)(2,1)S(1)}, bf16[4,32,512]{2,1,0:T(8,128)(2,1)S(1)}, u32[]{:S(2)}, u32[]{:S(2)}) collective-permute-start(bf16[4,32,512]{2,1,0:T(8,128)(2,1)S(1)} %pad_maximum_fusion.refs_3_), channel_id=1, source_target_pairs={{0,48},{1,49},{2,50},{3,51},{4,52},{5,53},{6,54},{7,55},{8,56},{9,... | collective-permute-start | bytes 393224 | tf_op jit(solution)/shard_map/ppermute | solution.py:30
  36.7 10.0 %collective-permute-start.8 = (bf16[4,32,512]{2,1,0:T(8,128)(2,1)S(1)}, bf16[4,32,512]{2,1,0:T(8,128)(2,1)S(1)}, u32[]{:S(2)}, u32[]{:S(2)}) collective-permute-start(bf16[4,32,512]{2,1,0:T(8,128)(2,1)S(1)} %pad_maximum_fusion.refs_3_), channel_id=1, source_target_pairs={{0,184},{1,185},{2,186},{3,187},{4,188},{5,189},{6,190},{7,191},{8... | collective-permute-start | bytes 393224 | tf_op jit(solution)/shard_map/ppermute | solution.py:30
  46.8 14.2 %collective-permute-start.9 = (bf16[80,16,384]{2,1,0:T(8,128)(2,1)S(1)}, bf16[80,16,384]{2,1,0:T(8,128)(2,1)S(1)}, u32[]{:S(2)}, u32[]{:S(2)}) collective-permute-start(bf16[80,16,384]{2,1,0:T(8,128)(2,1)S(1)} %get-tuple-element.53.sent), channel_id=1, source_target_pairs={{0,16},{1,17},{2,18},{3,19},{4,20},{5,21},{6,22},{7,23},{8,24},{9,... | collective-permute-start | bytes 2949128 | tf_op jit(solution)/shard_map/ppermute | solution.py:30
  47.1 14.4 %collective-permute-start.11 = (bf16[80,16,384]{2,1,0:T(8,128)(2,1)S(1)}, bf16[80,16,384]{2,1,0:T(8,128)(2,1)S(1)}, u32[]{:S(2)}, u32[]{:S(2)}) collective-permute-start(bf16[80,16,384]{2,1,0:T(8,128)(2,1)S(1)} %get-tuple-element.58.sent), channel_id=1, source_target_pairs={{0,8},{1,9},{2,10},{3,11},{4,12},{5,13},{6,14},{7,15},{8,0},{9,1},... | collective-permute-start | bytes 2949128 | tf_op jit(solution)/shard_map/ppermute | solution.py:30
  47.5 16.4 %collective-permute-start.13 = (bf16[80,32,128]{2,1,0:T(8,128)(2,1)S(1)}, bf16[80,32,128]{2,1,0:T(8,128)(2,1)S(1)}, u32[]{:S(2)}, u32[]{:S(2)}) collective-permute-start(bf16[80,32,128]{2,1,0:T(8,128)(2,1)S(1)} %get-tuple-element.63.sent), channel_id=1, source_target_pairs={{0,1},{1,0},{2,3},{3,2},{4,5},{5,4},{6,7},{7,6},{8,9},{9,8},{10,11... | collective-permute-start | bytes 1966088 | tf_op jit(solution)/shard_map/ppermute | solution.py:30
  61.1 12.1 %collective-permute-start.10 = (bf16[64,16,384]{2,1,0:T(8,128)(2,1)S(1)}, bf16[64,16,384]{2,1,0:T(8,128)(2,1)S(1)}, u32[]{:S(2)}, u32[]{:S(2)}) collective-permute-start(bf16[64,16,384]{2,1,0:T(8,128)(2,1)S(1)} %get-tuple-element.55.sent), channel_id=1, source_target_pairs={{0,8},{1,9},{2,10},{3,11},{4,12},{5,13},{6,14},{7,15},{8,0},{9,1},... | collective-permute-start | bytes 2359304 | tf_op jit(solution)/shard_map/ppermute | solution.py:30
  61.8 13.9 %collective-permute-start.12 = (bf16[64,16,384]{2,1,0:T(8,128)(2,1)S(1)}, bf16[64,16,384]{2,1,0:T(8,128)(2,1)S(1)}, u32[]{:S(2)}, u32[]{:S(2)}) collective-permute-start(bf16[64,16,384]{2,1,0:T(8,128)(2,1)S(1)} %get-tuple-element.60.sent), channel_id=1, source_target_pairs={{0,1},{1,0},{2,3},{3,2},{4,5},{5,4},{6,7},{7,6},{8,9},{9,8},{10,11... | collective-permute-start | bytes 2359304 | tf_op jit(solution)/shard_map/ppermute | solution.py:30
  64.1 12.2 %collective-permute-start.14 = (bf16[64,32,128]{2,1,0:T(8,128)(2,1)S(1)}, bf16[64,32,128]{2,1,0:T(8,128)(2,1)S(1)}, u32[]{:S(2)}, u32[]{:S(2)}) collective-permute-start(bf16[64,32,128]{2,1,0:T(8,128)(2,1)S(1)} %get-tuple-element.65.sent), channel_id=1, source_target_pairs={{0,16},{1,17},{2,18},{3,19},{4,20},{5,21},{6,22},{7,23},{8,24},{9,... | collective-permute-start | bytes 1572872 | tf_op jit(solution)/shard_map/ppermute | solution.py:30
  73.4 14.4 %collective-permute-start.15 = (bf16[80,16,384]{2,1,0:T(8,128)(2,1)S(1)}, bf16[80,16,384]{2,1,0:T(8,128)(2,1)S(1)}, u32[]{:S(2)}, u32[]{:S(2)}) collective-permute-start(bf16[80,16,384]{2,1,0:T(8,128)(2,1)S(1)} %get-tuple-element.57.sx), channel_id=1, source_target_pairs={{0,1},{1,0},{2,3},{3,2},{4,5},{5,4},{6,7},{7,6},{8,9},{9,8},{10,11... | collective-permute-start | bytes 2949128 | tf_op jit(solution)/shard_map/ppermute | solution.py:30
  75.8 14.2 %collective-permute-start.16 = (bf16[80,16,384]{2,1,0:T(8,128)(2,1)S(1)}, bf16[80,16,384]{2,1,0:T(8,128)(2,1)S(1)}, u32[]{:S(2)}, u32[]{:S(2)}) collective-permute-start(bf16[80,16,384]{2,1,0:T(8,128)(2,1)S(1)} %get-tuple-element.62.sy), channel_id=1, source_target_pairs={{0,16},{1,17},{2,18},{3,19},{4,20},{5,21},{6,22},{7,23},{8,24},{9,... | collective-permute-start | bytes 2949128 | tf_op jit(solution)/shard_map/ppermute | solution.py:30
  76.2 39.9 %slice-start = ((s8[8388608]{0:T(1024)(128)(4,1)}), s8[4194304]{0:T(1024)(128)(4,1)S(1)}, s32[]{:S(2)}) async-start(s8[8388608]{0:T(1024)(128)(4,1)} %bitcast.8), calls=%async_computation | async-start | bytes 8388608
  76.3 39.8 %slice-start.1 = ((s8[8388608]{0:T(1024)(128)(4,1)}), s8[4194304]{0:T(1024)(128)(4,1)S(1)}, s32[]{:S(2)}) async-start(s8[8388608]{0:T(1024)(128)(4,1)} %bitcast.8), calls=%async_computation.1 | async-start | bytes 8388608
  76.3 10.7 %collective-permute-start.17 = (bf16[80,32,128]{2,1,0:T(8,128)(2,1)S(1)}, bf16[80,32,128]{2,1,0:T(8,128)(2,1)S(1)}, u32[]{:S(2)}, u32[]{:S(2)}) collective-permute-start(bf16[80,32,128]{2,1,0:T(8,128)(2,1)S(1)} %get-tuple-element.67.sz), channel_id=1, source_target_pairs={{0,8},{1,9},{2,10},{3,11},{4,12},{5,13},{6,14},{7,15},{8,0},{9,1},... | collective-permute-start | bytes 1966088 | tf_op jit(solution)/shard_map/ppermute | solution.py:30
  90.0 4.6 %copy-start.3 = (bf16[80,16,384]{2,1,0:T(8,128)(2,1)}, bf16[80,16,384]{2,1,0:T(8,128)(2,1)S(1)}, u32[]{:S(2)}) copy-start(bf16[80,16,384]{2,1,0:T(8,128)(2,1)S(1)} %collective-permute-done.16.gy) | copy-start | bytes 2949124
  94.6 25.7 %collective-permute-start.18 = (f32[2,256,512]{2,1,0:T(8,128)S(1)}, f32[2,256,512]{2,1,0:T(8,128)S(1)}, u32[]{:S(2)}, u32[]{:S(2)}) collective-permute-start(f32[2,256,512]{2,1,0:T(8,128)S(1)} %get-tuple-element.69), channel_id=1, source_target_pairs={{0,64},{1,65},{2,66},{3,67},{4,68},{5,69},{6,70},{7,71},{8,72},{9,... | collective-permute-start | bytes 3145736 | tf_op jit(solution)/shard_map/ppermute | solution.py:30
  94.6 1.2 copy-start.4
  95.8 20.3 %copy-start.2 = (bf16[4096,512]{1,0:T(8,128)(2,1)S(1)}, bf16[4096,512]{1,0:T(8,128)(2,1)}, u32[]{:S(2)}) copy-start(bf16[4096,512]{1,0:T(8,128)(2,1)} %get-tuple-element.68.w) | copy-start | bytes 12582916
  95.9 6.3 %collective-permute-start.19 = (bf16[4,32,512]{2,1,0:T(8,128)(2,1)S(1)}, bf16[4,32,512]{2,1,0:T(8,128)(2,1)S(1)}, u32[]{:S(2)}, u32[]{:S(2)}) collective-permute-start(bf16[4,32,512]{2,1,0:T(8,128)(2,1)S(1)} %get-tuple-element.74), channel_id=1, source_target_pairs={{0,136},{1,137},{2,138},{3,139},{4,140},{5,141},{6,142},{7,143},{8... | collective-permute-start | bytes 393224 | tf_op jit(solution)/shard_map/ppermute | solution.py:30
  99.0 6.2 %collective-permute-start.20 = (bf16[4,32,512]{2,1,0:T(8,128)(2,1)S(1)}, bf16[4,32,512]{2,1,0:T(8,128)(2,1)S(1)}, u32[]{:S(2)}, u32[]{:S(2)}) collective-permute-start(bf16[4,32,512]{2,1,0:T(8,128)(2,1)S(1)} %get-tuple-element.75), channel_id=1, source_target_pairs={{0,48},{1,49},{2,50},{3,51},{4,52},{5,53},{6,54},{7,55},{8,56},{9,... | collective-permute-start | bytes 393224 | tf_op jit(solution)/shard_map/ppermute | solution.py:30
  101.8 8.3 %collective-permute-start.21 = (bf16[4,32,512]{2,1,0:T(8,128)(2,1)S(1)}, bf16[4,32,512]{2,1,0:T(8,128)(2,1)S(1)}, u32[]{:S(2)}, u32[]{:S(2)}) collective-permute-start(bf16[4,32,512]{2,1,0:T(8,128)(2,1)S(1)} %get-tuple-element.76), channel_id=1, source_target_pairs={{0,184},{1,185},{2,186},{3,187},{4,188},{5,189},{6,190},{7,191},{8... | collective-permute-start | bytes 393224 | tf_op jit(solution)/shard_map/ppermute | solution.py:30
  110.1 9.4 %collective-permute-start.22 = (bf16[32,512]{1,0:T(8,128)(2,1)S(1)}, bf16[32,512]{1,0:T(8,128)(2,1)S(1)}, u32[]{:S(2)}, u32[]{:S(2)}) collective-permute-start(bf16[32,512]{1,0:T(8,128)(2,1)S(1)} %get-tuple-element.78), channel_id=1, source_target_pairs={{0,2},{1,3},{2,4},{3,5},{4,6},{5,7},{6,0},{7,1},{8,10},{9,11},{10,... | collective-permute-start | bytes 98312 | tf_op jit(solution)/shard_map/ppermute | solution.py:30
  110.2 9.3 %collective-permute-start.23 = (bf16[32,512]{1,0:T(8,128)(2,1)S(1)}, bf16[32,512]{1,0:T(8,128)(2,1)S(1)}, u32[]{:S(2)}, u32[]{:S(2)}) collective-permute-start(bf16[32,512]{1,0:T(8,128)(2,1)S(1)} %get-tuple-element.79), channel_id=1, source_target_pairs={{0,4},{1,5},{2,6},{3,7},{4,0},{5,1},{6,2},{7,3},{8,12},{9,13},{10,... | collective-permute-start | bytes 98312 | tf_op jit(solution)/shard_map/ppermute | solution.py:30
  114.9 4.8 %collective-permute-start.24 = (bf16[32,512]{1,0:T(8,128)(2,1)S(1)}, bf16[32,512]{1,0:T(8,128)(2,1)S(1)}, u32[]{:S(2)}, u32[]{:S(2)}) collective-permute-start(bf16[32,512]{1,0:T(8,128)(2,1)S(1)} %get-tuple-element.80), channel_id=1, source_target_pairs={{0,6},{1,7},{2,0},{3,1},{4,2},{5,3},{6,4},{7,5},{8,14},{9,15},{10,... | collective-permute-start | bytes 98312 | tf_op jit(solution)/shard_map/ppermute | solution.py:30

commit v3 on v2

v3 whole, which is shorter than its diff:
```python
import jax
import jax.numpy as jnp
from jax import lax
from jax.experimental import pallas as pl
from jax.experimental.pallas import tpu as pltpu
from jax.sharding import PartitionSpec as P

F32, BF16 = jnp.float32, jnp.bfloat16
ALL = ("node", "dp")
INTERPRET = False
VMEM = pl.BlockSpec(memory_space=pltpu.VMEM)
SMEM = pl.BlockSpec(memory_space=pltpu.SMEM)
HBM = pl.BlockSpec(memory_space=pltpu.HBM)
PARAMS = pltpu.CompilerParams(vmem_limit_bytes=40 << 20)


STREAMS = ((16, 384), (16, 384), (32, 128))
AXES = ((0, 1, 2), (1, 2, 0), (2, 0, 1))


def place(x, y, z, c):
    return ((((y // 2) * 2 + c) * 4 + x) * 2 + y % 2) * 8 + z


def permute(value, move):
    pairs = []
    for c in range(2):
        for x in range(4):
            for y in range(4):
                for z in range(8):
                    pairs.append((place(x, y, z, c), place(*move(x, y, z, c))))
    return lax.ppermute(value, ALL, pairs)


def neighbour(v, n, c):
    return (v + 1 - 2 * ((v + c) % 2)) % n


def near(value, axis):
    def move(x, y, z, c):
        at = [x, y, z]
        at[axis] = neighbour(at[axis], (4, 4, 8)[axis], c)
        return (*at, c)

    return permute(value, move)


def plane_step(value, xb, yb):
    def move(x, y, z, c):
        return (neighbour(x, 4, 1 - c) if xb else x, neighbour(y, 4, 1 - c) if yb else y, z, c)

    return permute(value, move)


def line_step(value, d):
    return permute(value, lambda x, y, z, c: (x, y, (z + d) % 8, c))


def swap(value):
    return permute(value, lambda x, y, z, c: (x, y, z, 1 - c))


def as_int(flag):
    return jnp.where(flag, 1, 0)


def label4(u, v, c):
    step = 1 - 2 * lax.rem(v + c, 2)
    delta = lax.rem(u - v + 4, 4)
    far = delta == 2
    return as_int(far | (delta == lax.rem(step + 4, 4))), as_int(far | (delta == lax.rem(4 - step, 4)))


def label8(u, v, c):
    p = lax.rem(u + v, 2)
    step = 1 - 2 * lax.rem(v + c, 2)
    return p, lax.rem(u - v - p * step + 16, 8) // 2


def reached4(v, c, a, b):
    step = 1 - 2 * lax.rem(v + c, 2)
    return lax.rem(v + (2 if a and b else a * step - b * step) + 4, 4)


def reached8(v, c, a, d):
    step = 1 - 2 * lax.rem(v + c, 2)
    return lax.rem(v + a * step + 2 * d + 8, 8)


def call(kernel, outs, *args, **more):
    return pl.pallas_call(
        kernel,
        out_shape=[jax.ShapeDtypeStruct(*o) for o in outs],
        in_specs=[VMEM] * len(args),
        out_specs=[VMEM] * len(outs),
        compiler_params=PARAMS,
        interpret=INTERPRET,
        **more,
    )(*args)


def first_kernel(me, tokens, master, moment, second, gradient, r0, r1, weight, out_master, out_moment, out_second, rows, sems):
    far = pl.multiple_of(2048 * (1 - me[3]), 2048)
    loads = [
        pltpu.make_async_copy(ref, rows.at[i], sems.at[i]) for i, ref in enumerate((master, moment, second, gradient))
    ]
    copies = [
        pltpu.make_async_copy(tokens.at[:, :, pl.ds(far + 4096 * i, 2048)], ref, sems.at[4 + i])
        for i, ref in enumerate((r0, r1))
    ]
    for copy in loads + copies:
        copy.start()
    for copy in loads:
        copy.wait()
    new_moment = 0.9 * rows[1] + 0.1 * rows[3]
    new_second = 0.95 * rows[2] + 0.05 * rows[3] * rows[3]
    first_fix = 1.0 - 0.9**10
    second_fix = 1.0 - 0.95**10
    update = new_moment / first_fix / (jnp.sqrt(new_second / second_fix) + 1e-08) + 0.1 * rows[0]
    new_master = rows[0] - 0.001 * update
    out_master[...] = new_master
    out_moment[...] = new_moment
    out_second[...] = new_second
    weight[...] = new_master.astype(BF16)
    for copy in copies:
        copy.wait()


def first(me, tokens, master, moment, second, gradient):
    half = jax.ShapeDtypeStruct((*tokens.shape[:2], 2048), BF16)
    rows = jax.ShapeDtypeStruct(master.shape, F32)
    return pl.pallas_call(
        first_kernel,
        in_specs=[SMEM] + [HBM] * 5,
        out_specs=[VMEM] * 6,
        out_shape=[half, half, jax.ShapeDtypeStruct(master.shape, BF16), rows, rows, rows],
        scratch_shapes=[pltpu.VMEM((4, *master.shape), F32), pltpu.SemaphoreType.DMA((6,))],
        compiler_params=PARAMS,
        interpret=INTERPRET,
    )(me, tokens, master, moment, second, gradient)


def terms_kernel(me, tokens, r0, r1, cot, cotr, sx, sy, sz, kx, ky, kz, own, sems):
    mx, my, mz, c = me[0], me[1], me[2], me[3]
    mine = pl.multiple_of(2048 * c, 2048)
    loads = [
        pltpu.make_async_copy(tokens.at[:, :, pl.ds(mine + 4096 * (t // 4) + 512 * (t % 4), 512)], own.at[t], sems.at[t])
        for t in range(8)
    ]
    for load in loads:
        load.start()
    flat = cot.shape[0] * cot.shape[1]
    ours, theirs = cot[...].reshape(flat, 512), cotr[...].reshape(flat, 512)
    xs = [label4(x, mx, c) for x in range(4)]
    ys = [label4(y, my, c) for y in range(4)]
    zs = [label8(z, mz, c) for z in range(8)]

    def product(a, b):
        return lax.dot_general(a.reshape(flat, 512), b, (((0,), (0,)), ((), ())), preferred_element_type=F32)

    for t in range(8):
        other = (r0, r1)[t // 4][:, :, 512 * (t % 4) : 512 * (t % 4) + 512]
        acc = product(other, theirs)
        loads[t].wait()
        acc += product(own[t], ours)
        for j in range(16):
            x, y, z = xs[t % 4], ys[2 * (t // 4) + j // 8], zs[j % 8]
            far = x[1] * 8 + y[1] * 4 + z[1]
            axes = (x[0], y[0], z[0])
            block = acc[32 * j : 32 * j + 32]
            for stream, (send, keep) in enumerate(((sx, kx), (sy, ky), (sz, kz))):
                first_, second_, third_ = (axes[axis] for axis in AXES[stream])
                at = second_ * 32 + third_ * 16 + far
                part = cut(stream, block)
                send[jnp.where(first_ == 1, at, 64)] = part.astype(BF16)
                keep[jnp.where(first_ == 1, 64, at)] = part


def all_terms(me, tokens, r0, r1, cot, cotr):
    return pl.pallas_call(
        terms_kernel,
        in_specs=[SMEM, HBM] + [VMEM] * 4,
        out_specs=[VMEM] * 6,
        out_shape=[jax.ShapeDtypeStruct((80, *s), BF16) for s in STREAMS]
        + [jax.ShapeDtypeStruct((65, *s), F32) for s in STREAMS],
        scratch_shapes=[pltpu.VMEM((8, *tokens.shape[:2], 512), BF16), pltpu.SemaphoreType.DMA((8,))],
        compiler_params=PARAMS,
        interpret=INTERPRET,
    )(me, tokens, r0, r1, cot, cotr)


def cut(stream, block):
    return (block[..., 0:16, 0:384], block[..., 16:32, 0:384], block[..., :, 384:512])[stream]


def pack_kernel(*refs):
    plane, outs = refs[3:7], refs[7:10]
    for stream, out in enumerate(outs):
        for q, part in enumerate(plane):
            out[64 + 4 * q : 68 + 4 * q] = cut(stream, part[...])


def second_kernel(sent, got, keep, send, kept):
    send[0:32] = (keep[32:64] + got[32:64].astype(F32)).astype(BF16)
    send[32:48] = sent[64:80]
    send[48:64] = got[64:80]
    kept[...] = keep[0:32] + got[0:32].astype(F32)


def third_kernel(sent, got, keep, send, kept):
    send[0:16] = (keep[16:32] + got[16:32].astype(F32)).astype(BF16)
    send[16:48] = sent[32:64]
    send[48:80] = got[32:64]
    kept[...] = keep[0:16] + got[0:16].astype(F32)


def far_kernel(gx, gy, gz, kx, ky, kz, own, s1, s2, s3):
    for q, out in enumerate((own, s1, s2, s3)):
        at = slice(4 * q, 4 * q + 4)
        out[:, 0:16, 0:384] = (kx[at] + gx[at].astype(F32)).astype(out.dtype)
        out[:, 16:32, 0:384] = (ky[at] + gy[at].astype(F32)).astype(out.dtype)
        out[:, :, 384:512] = (kz[at] + gz[at].astype(F32)).astype(out.dtype)


def last_kernel(own, g1, g2, g3, kept, s1, s2, s3):
    for d, out in enumerate((kept, s1, s2, s3)):
        total = own[d] + g1[d].astype(F32) + g2[d].astype(F32) + g3[d].astype(F32)
        out[...] = total.astype(out.dtype)


def sum_kernel(own, g1, g2, g3, out):
    out[...] = own[...] + g1[...].astype(F32) + g2[...].astype(F32) + g3[...].astype(F32)


def assemble(me, sx, sy, sz, gx, gy, gz, w):
    mx, my, mz, c = me[0], me[1], me[2], me[3]
    xs = [[reached4(mx, c, a, b) * 512 for b in range(2)] for a in range(2)]
    ys = [[reached4(my, c, a, b) for b in range(2)] for a in range(2)]
    ys = [[(y // 2) * 2048 + lax.rem(y, 2) * 256 for y in row] for row in ys]
    zs = [[reached8(mz, c, a, d) * 32 for d in range(4)] for a in range(2)]
    for xa in range(2):
        for ya in range(2):
            for za in range(2):
                for i in range(16):
                    at = pl.multiple_of(xs[xa][i // 8] + ys[ya][(i // 4) % 2] + zs[za][i % 4], 32)
                    label = (xa, ya, za)

                    def part(stream, sent, got):
                        first, second, third = (label[axis] for axis in AXES[stream])
                        return (got if third else sent)[16 + second * 32 + first * 16 + i]

                    w[pl.ds(at, 16), 0:384] = part(0, sx, gx)
                    w[pl.ds(at + 16, 16), 0:384] = part(1, sy, gy)
                    w[pl.ds(at, 32), 384:512] = part(2, sz, gz)


def other_kernel(me, r0, r1, sx, sy, sz, gx, gy, gz, out, w):
    assemble(me, sx, sy, sz, gx, gy, gz, w)
    for m in range(out.shape[0]):
        out[m] = jnp.dot(r0[m], w[0:2048], preferred_element_type=F32) + jnp.dot(
            r1[m], w[2048:4096], preferred_element_type=F32
        )


def mine_kernel(me, tokens, w, other, out, own, sems):
    mine = pl.multiple_of(2048 * me[3], 2048)
    loads = [
        [
            pltpu.make_async_copy(tokens.at[m, :, pl.ds(mine + 4096 * i, 2048)], own.at[2 * m + i], sems.at[2 * m + i])
            for i in range(2)
        ]
        for m in range(2)
    ]
    for load in loads[0] + loads[1]:
        load.start()
    for m in range(2):
        total = other[m]
        for i in range(2):
            loads[m][i].wait()
            total += jnp.dot(own[2 * m + i], w[2048 * i : 2048 * i + 2048], preferred_element_type=F32)
        out[m] = total.astype(BF16)


def other_values(me, r0, r1, messages):
    return pl.pallas_call(
        other_kernel,
        in_specs=[SMEM] + [VMEM] * 8,
        out_specs=[VMEM] * 2,
        out_shape=[
            jax.ShapeDtypeStruct((*r0.shape[:2], 512), F32),
            jax.ShapeDtypeStruct((4096, 512), BF16),
        ],
        compiler_params=PARAMS,
        interpret=INTERPRET,
    )(me, r0, r1, *messages)


def my_values(me, tokens, w, other):
    micro, rows, _ = tokens.shape
    return pl.pallas_call(
        mine_kernel,
        in_specs=[SMEM, HBM, VMEM, VMEM],
        out_specs=VMEM,
        out_shape=jax.ShapeDtypeStruct((micro, rows, 512), BF16),
        scratch_shapes=[pltpu.VMEM((2 * micro, rows, 2048), BF16), pltpu.SemaphoreType.DMA((2 * micro,))],
        compiler_params=PARAMS,
        interpret=INTERPRET,
    )(me, tokens, w, other)


def after(value, *others):
    return lax.optimization_barrier((value, *others))[0]


def body(tokens, cotangent, master, moment, second, gradient):
    node, dp = lax.axis_index("node"), lax.axis_index("dp")
    me = jnp.stack([dp // 16, (node // 2) * 2 + (dp // 8) % 2, dp % 8, node % 2]).astype(jnp.int32)

    tokens, master, moment, second, gradient = (
        pltpu.with_memory_space_constraint(a, pltpu.HBM) for a in (tokens, master, moment, second, gradient)
    )
    r0, r1, weight, new_master, new_moment, new_second = first(me, tokens, master, moment, second, gradient)
    r0, r1, cotr = swap(r0), swap(r1), swap(cotangent)
    line = jnp.stack([weight] + [line_step(weight, -2 * d) for d in (1, 2, 3)])
    plane = [line] + [plane_step(line, q // 2, q % 2) for q in (1, 2, 3)]
    terms = all_terms(me, tokens, r0, r1, cotangent, cotr)
    send, keep = terms[:3], terms[3:]

    send = call(
        pack_kernel,
        [((80, *s), BF16) for s in STREAMS],
        *send,
        *plane,
        input_output_aliases={0: 0, 1: 1, 2: 2},
    )
    got = [near(send[i], AXES[i][0]) for i in range(3)]
    for step, kernel, size, rest in ((1, second_kernel, 64, 32), (2, third_kernel, 80, 16)):
        new = [
            call(kernel, [((size, *STREAMS[i]), BF16), ((rest, *STREAMS[i]), F32)], send[i], got[i], keep[i])
            for i in range(3)
        ]
        send, keep = [n[0] for n in new], [n[1] for n in new]
        got = [near(send[i], AXES[i][step]) for i in range(3)]

    block = (4, 32, 512)
    own, *parts = call(far_kernel, [(block, F32)] + [(block, BF16)] * 3, *got, *keep)
    parts = [plane_step(part, q // 2, q % 2) for q, part in zip((1, 2, 3), parts)]

    other, w = other_values(after(me, own), r0, r1, [*send, *got])
    other = swap(after(other, *parts))

    own, *parts = call(last_kernel, [(block[1:], F32)] + [(block[1:], BF16)] * 3, after(own, w), *parts)
    parts = [line_step(part, 2 * d) for d, part in zip((1, 2, 3), parts)]
    values = my_values(me, tokens, w, other)
    (weight_grad,) = call(sum_kernel, [(block[1:], F32)], after(own, values), *parts)
    return (new_master, new_moment, new_second, values, weight_grad)


def solution(mesh):
    rows = P(("node", "dp"), None)
    tall = P(None, ("node", "dp"), None)
    return jax.shard_map(
        body,
        mesh=mesh,
        in_specs=(tall, tall, rows, rows, rows, rows),
        out_specs=(rows, rows, rows, tall, rows),
        check_vma=False,
    )
```

time: 123 us -> 111 us (0.902)
  the two profiles are of different devices: /device:TPU:0 before, /device:TPU:1 now
where the time goes in v3:
time: 111 us; the launch traced here: 110 us
  starting transfers between devices  64.3 us (58%)
  Pallas kernels  22.3 us (20%)
  waiting for transfers between devices  20.7 us (19%)
  local copies, waits for them, and re-layouts  2.19 us (2%)
    ppermute x25, starting transfers between devices, permute(): return lax.ppermute(value, ALL, pairs)  64.3 us
    ppermute x25, waiting for transfers between devices, permute(): return lax.ppermute(value, ALL, pairs)  20.7 us
    pallas_call x1, Pallas kernels, all_terms(): pl.pallas_call(terms_kernel, in_specs=[SMEM, HBM] + [VMEM] * 4, out_specs...  8.09 us
    pallas_call x1, Pallas kernels, my_values(): pl.pallas_call(mine_kernel, in_specs=[SMEM, HBM, VMEM, VMEM], out_specs=V...  5.28 us
    pallas_call x1, Pallas kernels, first(): pl.pallas_call(first_kernel, in_specs=[SMEM] + [HBM] * 5, out_specs=[VMEM...  3.65 us
    pallas_call x1, Pallas kernels, other_values(): pl.pallas_call(other_kernel, in_specs=[SMEM] + [VMEM] * 8, out_specs=[VME...  3.51 us
  transfers between devices with their start and end apart: 25, of which 7 were waited for; matrix products, arithmetic and copies ran while one was open for 0% of the time, Pallas kernels for 16%

profile of v3, /device:TPU:1, one launch (start us, length us, event | category | flops | bytes accessed | tf_op | source)
XLA Modules:
  0.0 110.4 jit_solution(10475947170784179589)
XLA Ops:
  0.7 0.1 pad_add_fusion.me
  0.8 3.6 %shard_map.101 = (bf16[2,256,2048]{2,1,0:T(8,128)(2,1)S(1)}, bf16[2,256,2048]{2,1,0:T(8,128)(2,1)S(1)}, bf16[32,512]{1,0:T(8,128)(2,1)S(1)}, f32[32,512]{1,0:T(8...) custom-call(s32[4]{0:T(128)S(1)} %pad_add_fusion.me, bf16[2,256,8192]{2,1,0:T(8,128)(2,1)} %tokens.5, f32[32,512]{1,0:T(8,128)} %master.1, ...), custom_call_target="tpu_custom_call" | custom-call | tf_op jit(solution)/shard_map/pallas_call | solution.py:132
  4.4 3.3 %collective-permute-start = (bf16[2,256,2048]{2,1,0:T(8,128)(2,1)S(1)}, bf16[2,256,2048]{2,1,0:T(8,128)(2,1)S(1)}, u32[]{:S(2)}, u32[]{:S(2)}) collective-permute-start(bf16[2,256,2048]{2,1,0:T(8,128)(2,1)S(1)} %get-tuple-element.49), channel_id=1, source_target_pairs={{0,64},{1,65},{2,66},{3,67},{4,68},{5,69},{6,70},{7,71},{8,72},{9,... | collective-permute-start | bytes 6291464 | tf_op jit(solution)/shard_map/ppermute | solution.py:32
  7.8 0.1 collective-permute-start.1
  7.9 0.4 collective-permute-start.2
  8.3 1.3 %collective-permute-start.5 = (bf16[32,512]{1,0:T(8,128)(2,1)S(1)}, bf16[32,512]{1,0:T(8,128)(2,1)S(1)}, u32[]{:S(2)}, u32[]{:S(2)}) collective-permute-start(bf16[32,512]{1,0:T(8,128)(2,1)S(1)} %get-tuple-element.54), channel_id=1, source_target_pairs={{0,2},{1,3},{2,4},{3,5},{4,6},{5,7},{6,0},{7,1},{8,10},{9,11},{10,... | collective-permute-start | bytes 98312 | tf_op jit(solution)/shard_map/ppermute | solution.py:32
  9.5 5.1 %collective-permute-start.4 = (bf16[32,512]{1,0:T(8,128)(2,1)S(1)}, bf16[32,512]{1,0:T(8,128)(2,1)S(1)}, u32[]{:S(2)}, u32[]{:S(2)}) collective-permute-start(bf16[32,512]{1,0:T(8,128)(2,1)S(1)} %get-tuple-element.54), channel_id=1, source_target_pairs={{0,4},{1,5},{2,6},{3,7},{4,0},{5,1},{6,2},{7,3},{8,12},{9,13},{10,... | collective-permute-start | bytes 98312 | tf_op jit(solution)/shard_map/ppermute | solution.py:32
  14.7 0.0 collective-permute-done.5
  14.7 2.4 %collective-permute-start.3 = (bf16[32,512]{1,0:T(8,128)(2,1)S(1)}, bf16[32,512]{1,0:T(8,128)(2,1)S(1)}, u32[]{:S(2)}, u32[]{:S(2)}) collective-permute-start(bf16[32,512]{1,0:T(8,128)(2,1)S(1)} %get-tuple-element.54), channel_id=1, source_target_pairs={{0,6},{1,7},{2,0},{3,1},{4,2},{5,3},{6,4},{7,5},{8,14},{9,15},{10,... | collective-permute-start | bytes 98312 | tf_op jit(solution)/shard_map/ppermute | solution.py:32
  17.0 2.1 %collective-permute-done.3 = bf16[32,512]{1,0:T(8,128)(2,1)S(1)} collective-permute-done((bf16[32,512]{1,0:T(8,128)(2,1)S(1)}, bf16[32,512]{1,0:T(8,128)(2,1)S(1)}, u32[]{:S(2)}, u32[]{:S(2)}) %collective-permute-start.3) | collective-permute-done | bytes 32800 | tf_op jit(solution)/shard_map/ppermute | solution.py:32
  19.1 2.3 %collective-permute-start.8 = (bf16[4,32,512]{2,1,0:T(8,128)(2,1)S(1)}, bf16[4,32,512]{2,1,0:T(8,128)(2,1)S(1)}, u32[]{:S(2)}, u32[]{:S(2)}) collective-permute-start(bf16[4,32,512]{2,1,0:T(8,128)(2,1)S(1)} %pad_maximum_fusion.refs_3_), channel_id=1, source_target_pairs={{0,184},{1,185},{2,186},{3,187},{4,188},{5,189},{6,190},{7,191},{8... | collective-permute-start | bytes 393224 | tf_op jit(solution)/shard_map/ppermute | solution.py:32
  21.5 0.3 collective-permute-start.7
  21.7 0.2 collective-permute-start.6
  21.9 8.1 %shard_map.102 = (bf16[80,16,384]{2,1,0:T(8,128)(2,1)S(1)}, bf16[80,16,384]{2,1,0:T(8,128)(2,1)S(1)}, bf16[80,32,128]{2,1,0:T(8,128)(2,1)S(1)}, f32[65,16,384]{2...) custom-call(s32[4]{0:T(128)S(1)} %pad_add_fusion.me, bf16[2,256,8192]{2,1,0:T(8,128)(2,1)} %tokens.5, ...), custom_call_target="tpu_custom_call" | custom-call | tf_op jit(solution)/shard_map/pallas_call | solution.py:180
  30.0 0.1 shard_map.103
  30.1 2.6 %collective-permute-start.9 = (bf16[80,16,384]{2,1,0:T(8,128)(2,1)S(1)}, bf16[80,16,384]{2,1,0:T(8,128)(2,1)S(1)}, u32[]{:S(2)}, u32[]{:S(2)}) collective-permute-start(bf16[80,16,384]{2,1,0:T(8,128)(2,1)S(1)} %get-tuple-element.55.sent), channel_id=1, source_target_pairs={{0,16},{1,17},{2,18},{3,19},{4,20},{5,21},{6,22},{7,23},{8,24},{9,... | collective-permute-start | bytes 2949128 | tf_op jit(solution)/shard_map/ppermute | solution.py:32
  32.6 2.7 %collective-permute-start.12 = (bf16[80,16,384]{2,1,0:T(8,128)(2,1)S(1)}, bf16[80,16,384]{2,1,0:T(8,128)(2,1)S(1)}, u32[]{:S(2)}, u32[]{:S(2)}) collective-permute-start(bf16[80,16,384]{2,1,0:T(8,128)(2,1)S(1)} %get-tuple-element.60.sent), channel_id=1, source_target_pairs={{0,8},{1,9},{2,10},{3,11},{4,12},{5,13},{6,14},{7,15},{8,0},{9,1},... | collective-permute-start | bytes 2949128 | tf_op jit(solution)/shard_map/ppermute | solution.py:32
  35.4 3.0 %collective-permute-start.15 = (bf16[80,32,128]{2,1,0:T(8,128)(2,1)S(1)}, bf16[80,32,128]{2,1,0:T(8,128)(2,1)S(1)}, u32[]{:S(2)}, u32[]{:S(2)}) collective-permute-start(bf16[80,32,128]{2,1,0:T(8,128)(2,1)S(1)} %get-tuple-element.65.sent), channel_id=1, source_target_pairs={{0,1},{1,0},{2,3},{3,2},{4,5},{5,4},{6,7},{7,6},{8,9},{9,8},{10,11... | collective-permute-start | bytes 1966088 | tf_op jit(solution)/shard_map/ppermute | solution.py:32
  38.4 6.0 %collective-permute-done.9.got = bf16[80,16,384]{2,1,0:T(8,128)(2,1)S(1)} collective-permute-done((bf16[80,16,384]{2,1,0:T(8,128)(2,1)S(1)}, bf16[80,16,384]{2,1,0:T(8,128)(2,1)S(1)}, u32[]{:S(2)}, u32[]{:S(2)}) %collective-permute-start.9) | collective-permute-done | bytes 983072 | tf_op jit(solution)/shard_map/ppermute | solution.py:32
  44.3 0.2 shard_map.104
  44.5 2.8 %collective-permute-start.10 = (bf16[64,16,384]{2,1,0:T(8,128)(2,1)S(1)}, bf16[64,16,384]{2,1,0:T(8,128)(2,1)S(1)}, u32[]{:S(2)}, u32[]{:S(2)}) collective-permute-start(bf16[64,16,384]{2,1,0:T(8,128)(2,1)S(1)} %get-tuple-element.57.sent), channel_id=1, source_target_pairs={{0,8},{1,9},{2,10},{3,11},{4,12},{5,13},{6,14},{7,15},{8,0},{9,1},... | collective-permute-start | bytes 2359304 | tf_op jit(solution)/shard_map/ppermute | solution.py:32
  47.4 0.2 shard_map.106
  47.6 3.1 %collective-permute-start.13 = (bf16[64,16,384]{2,1,0:T(8,128)(2,1)S(1)}, bf16[64,16,384]{2,1,0:T(8,128)(2,1)S(1)}, u32[]{:S(2)}, u32[]{:S(2)}) collective-permute-start(bf16[64,16,384]{2,1,0:T(8,128)(2,1)S(1)} %get-tuple-element.62.sent), channel_id=1, source_target_pairs={{0,1},{1,0},{2,3},{3,2},{4,5},{5,4},{6,7},{7,6},{8,9},{9,8},{10,11... | collective-permute-start | bytes 2359304 | tf_op jit(solution)/shard_map/ppermute | solution.py:32
  50.6 0.1 shard_map.108
  50.7 2.6 %collective-permute-start.16 = (bf16[64,32,128]{2,1,0:T(8,128)(2,1)S(1)}, bf16[64,32,128]{2,1,0:T(8,128)(2,1)S(1)}, u32[]{:S(2)}, u32[]{:S(2)}) collective-permute-start(bf16[64,32,128]{2,1,0:T(8,128)(2,1)S(1)} %get-tuple-element.67.sent), channel_id=1, source_target_pairs={{0,16},{1,17},{2,18},{3,19},{4,20},{5,21},{6,22},{7,23},{8,24},{9,... | collective-permute-start | bytes 1572872 | tf_op jit(solution)/shard_map/ppermute | solution.py:32
  53.3 3.4 %collective-permute-done.10.got = bf16[64,16,384]{2,1,0:T(8,128)(2,1)S(1)} collective-permute-done((bf16[64,16,384]{2,1,0:T(8,128)(2,1)S(1)}, bf16[64,16,384]{2,1,0:T(8,128)(2,1)S(1)}, u32[]{:S(2)}, u32[]{:S(2)}) %collective-permute-start.10) | collective-permute-done | bytes 786464 | tf_op jit(solution)/shard_map/ppermute | solution.py:32
  56.7 0.1 shard_map.105
  56.9 3.1 %collective-permute-start.11 = (bf16[80,16,384]{2,1,0:T(8,128)(2,1)S(1)}, bf16[80,16,384]{2,1,0:T(8,128)(2,1)S(1)}, u32[]{:S(2)}, u32[]{:S(2)}) collective-permute-start(bf16[80,16,384]{2,1,0:T(8,128)(2,1)S(1)} %get-tuple-element.59.sx), channel_id=1, source_target_pairs={{0,1},{1,0},{2,3},{3,2},{4,5},{5,4},{6,7},{7,6},{8,9},{9,8},{10,11... | collective-permute-start | bytes 2949128 | tf_op jit(solution)/shard_map/ppermute | solution.py:32
  59.9 0.1 collective-permute-done.13.got
  60.0 0.2 shard_map.107
  60.2 2.6 %collective-permute-start.14 = (bf16[80,16,384]{2,1,0:T(8,128)(2,1)S(1)}, bf16[80,16,384]{2,1,0:T(8,128)(2,1)S(1)}, u32[]{:S(2)}, u32[]{:S(2)}) collective-permute-start(bf16[80,16,384]{2,1,0:T(8,128)(2,1)S(1)} %get-tuple-element.64.sy), channel_id=1, source_target_pairs={{0,16},{1,17},{2,18},{3,19},{4,20},{5,21},{6,22},{7,23},{8,24},{9,... | collective-permute-start | bytes 2949128 | tf_op jit(solution)/shard_map/ppermute | solution.py:32
  62.7 0.1 shard_map.109
  62.8 2.7 %collective-permute-start.17 = (bf16[80,32,128]{2,1,0:T(8,128)(2,1)S(1)}, bf16[80,32,128]{2,1,0:T(8,128)(2,1)S(1)}, u32[]{:S(2)}, u32[]{:S(2)}) collective-permute-start(bf16[80,32,128]{2,1,0:T(8,128)(2,1)S(1)} %get-tuple-element.69.sz), channel_id=1, source_target_pairs={{0,8},{1,9},{2,10},{3,11},{4,12},{5,13},{6,14},{7,15},{8,0},{9,1},... | collective-permute-start | bytes 1966088 | tf_op jit(solution)/shard_map/ppermute | solution.py:32
  65.5 8.0 %collective-permute-done.17.gz = bf16[80,32,128]{2,1,0:T(8,128)(2,1)S(1)} collective-permute-done((bf16[80,32,128]{2,1,0:T(8,128)(2,1)S(1)}, bf16[80,32,128]{2,1,0:T(8,128)(2,1)S(1)}, u32[]{:S(2)}, u32[]{:S(2)}) %collective-permute-start.17) | collective-permute-done | bytes 655392 | tf_op jit(solution)/shard_map/ppermute | solution.py:32
  73.6 0.9 collective-permute-done.14.gy
  74.4 0.1 shard_map.110
  74.5 0.3 collective-permute-start.18
  74.9 2.4 %collective-permute-start.20 = (bf16[4,32,512]{2,1,0:T(8,128)(2,1)S(1)}, bf16[4,32,512]{2,1,0:T(8,128)(2,1)S(1)}, u32[]{:S(2)}, u32[]{:S(2)}) collective-permute-start(bf16[4,32,512]{2,1,0:T(8,128)(2,1)S(1)} %get-tuple-element.79), channel_id=1, source_target_pairs={{0,184},{1,185},{2,186},{3,187},{4,188},{5,189},{6,190},{7,191},{8... | collective-permute-start | bytes 393224 | tf_op jit(solution)/shard_map/ppermute | solution.py:32
  77.3 3.5 %shard_map.111 = (f32[2,256,512]{2,1,0:T(8,128)S(1)}, bf16[4096,512]{1,0:T(8,128)(2,1)}) custom-call(s32[4]{0:T(128)S(1)} %pad_add_fusion.me, bf16[2,256,2048]{2,1,0:T(8,128)(2,1)S(1)} %collective-permute-done.r0, bf16[2,256,2048]{2,1,0:T(8,128)(2,1)S(1)} %collective-permute-done.1.r1, bf16[80,16,384]{2,1,0:T(8,128)(2,1)S(1)} %get-tuple-element.59.sx, ...), custom_call_target="tpu_custom_call" | custom-call | tf_op jit(solution)/shard_map/pallas_call | solution.py:285
  80.8 0.2 collective-permute-done.20.g3
  81.0 10.2 %collective-permute-start.21 = (f32[2,256,512]{2,1,0:T(8,128)S(1)}, f32[2,256,512]{2,1,0:T(8,128)S(1)}, u32[]{:S(2)}, u32[]{:S(2)}) collective-permute-start(f32[2,256,512]{2,1,0:T(8,128)S(1)} %get-tuple-element.80), channel_id=1, source_target_pairs={{0,64},{1,65},{2,66},{3,67},{4,68},{5,69},{6,70},{7,71},{8,72},{9,... | collective-permute-start | bytes 3145736 | tf_op jit(solution)/shard_map/ppermute | solution.py:32
  91.2 0.1 shard_map.113
  91.3 5.2 %collective-permute-start.22 = (bf16[32,512]{1,0:T(8,128)(2,1)S(1)}, bf16[32,512]{1,0:T(8,128)(2,1)S(1)}, u32[]{:S(2)}, u32[]{:S(2)}) collective-permute-start(bf16[32,512]{1,0:T(8,128)(2,1)S(1)} %get-tuple-element.84), channel_id=1, source_target_pairs={{0,2},{1,3},{2,4},{3,5},{4,6},{5,7},{6,0},{7,1},{8,10},{9,11},{10,... | collective-permute-start | bytes 98312 | tf_op jit(solution)/shard_map/ppermute | solution.py:32
  96.5 3.9 %collective-permute-start.23 = (bf16[32,512]{1,0:T(8,128)(2,1)S(1)}, bf16[32,512]{1,0:T(8,128)(2,1)S(1)}, u32[]{:S(2)}, u32[]{:S(2)}) collective-permute-start(bf16[32,512]{1,0:T(8,128)(2,1)S(1)} %get-tuple-element.85), channel_id=1, source_target_pairs={{0,4},{1,5},{2,6},{3,7},{4,0},{5,1},{6,2},{7,3},{8,12},{9,13},{10,... | collective-permute-start | bytes 98312 | tf_op jit(solution)/shard_map/ppermute | solution.py:32
  100.4 1.9 %collective-permute-start.24 = (bf16[32,512]{1,0:T(8,128)(2,1)S(1)}, bf16[32,512]{1,0:T(8,128)(2,1)S(1)}, u32[]{:S(2)}, u32[]{:S(2)}) collective-permute-start(bf16[32,512]{1,0:T(8,128)(2,1)S(1)} %get-tuple-element.86), channel_id=1, source_target_pairs={{0,6},{1,7},{2,0},{3,1},{4,2},{5,3},{6,4},{7,5},{8,14},{9,15},{10,... | collective-permute-start | bytes 98312 | tf_op jit(solution)/shard_map/ppermute | solution.py:32
  102.3 2.2 %copy-done = bf16[4096,512]{1,0:T(8,128)(2,1)S(1)} copy-done((bf16[4096,512]{1,0:T(8,128)(2,1)S(1)}, bf16[4096,512]{1,0:T(8,128)(2,1)}, u32[]{:S(2)}) %copy-start) | copy-done | bytes 4194328
  104.4 5.3 %shard_map.112 = bf16[2,256,512]{2,1,0:T(8,128)(2,1)} custom-call(s32[4]{0:T(128)S(1)} %pad_add_fusion.me, bf16[2,256,8192]{2,1,0:T(8,128)(2,1)} %tokens.5, bf16[4096,512]{1,0:T(8,128)(2,1)S(1)} %copy-done, f32[2,256,512]{2,1,0:T(8,128)S(1)} %collective-permute-done.21.other), custom_call_target="tpu_custom_call" | custom-call | tf_op jit(solution)/shard_map/pallas_call | solution.py:300
  109.8 0.6 shard_map.114
  (22 shorter events, 0.1 us)
Async XLA Ops:
  0.8 7.1 %copy-start.1 = (bf16[2,256,512]{2,1,0:T(8,128)(2,1)S(1)}, bf16[2,256,512]{2,1,0:T(8,128)(2,1)}, u32[]{:S(2)}) copy-start(bf16[2,256,512]{2,1,0:T(8,128)(2,1)} %cot.1) | copy-start | bytes 1572868
  4.4 17.5 %collective-permute-start = (bf16[2,256,2048]{2,1,0:T(8,128)(2,1)S(1)}, bf16[2,256,2048]{2,1,0:T(8,128)(2,1)S(1)}, u32[]{:S(2)}, u32[]{:S(2)}) collective-permute-start(bf16[2,256,2048]{2,1,0:T(8,128)(2,1)S(1)} %get-tuple-element.49), channel_id=1, source_target_pairs={{0,64},{1,65},{2,66},{3,67},{4,68},{5,69},{6,70},{7,71},{8,72},{9,... | collective-permute-start | bytes 6291464 | tf_op jit(solution)/shard_map/ppermute | solution.py:32
  7.8 14.1 %collective-permute-start.1 = (bf16[2,256,2048]{2,1,0:T(8,128)(2,1)S(1)}, bf16[2,256,2048]{2,1,0:T(8,128)(2,1)S(1)}, u32[]{:S(2)}, u32[]{:S(2)}) collective-permute-start(bf16[2,256,2048]{2,1,0:T(8,128)(2,1)S(1)} %get-tuple-element.50), channel_id=1, source_target_pairs={{0,64},{1,65},{2,66},{3,67},{4,68},{5,69},{6,70},{7,71},{8,72},{9,... | collective-permute-start | bytes 6291464 | tf_op jit(solution)/shard_map/ppermute | solution.py:32
  7.9 13.9 %collective-permute-start.2 = (bf16[2,256,512]{2,1,0:T(8,128)(2,1)S(1)}, bf16[2,256,512]{2,1,0:T(8,128)(2,1)S(1)}, u32[]{:S(2)}, u32[]{:S(2)}) collective-permute-start(bf16[2,256,512]{2,1,0:T(8,128)(2,1)S(1)} %copy-done.1), channel_id=1, source_target_pairs={{0,64},{1,65},{2,66},{3,67},{4,68},{5,69},{6,70},{7,71},{8,72},{9,... | collective-permute-start | bytes 1572872 | tf_op jit(solution)/shard_map/ppermute | solution.py:32
  8.3 6.4 %collective-permute-start.5 = (bf16[32,512]{1,0:T(8,128)(2,1)S(1)}, bf16[32,512]{1,0:T(8,128)(2,1)S(1)}, u32[]{:S(2)}, u32[]{:S(2)}) collective-permute-start(bf16[32,512]{1,0:T(8,128)(2,1)S(1)} %get-tuple-element.54), channel_id=1, source_target_pairs={{0,2},{1,3},{2,4},{3,5},{4,6},{5,7},{6,0},{7,1},{8,10},{9,11},{10,... | collective-permute-start | bytes 98312 | tf_op jit(solution)/shard_map/ppermute | solution.py:32
  9.5 7.5 %collective-permute-start.4 = (bf16[32,512]{1,0:T(8,128)(2,1)S(1)}, bf16[32,512]{1,0:T(8,128)(2,1)S(1)}, u32[]{:S(2)}, u32[]{:S(2)}) collective-permute-start(bf16[32,512]{1,0:T(8,128)(2,1)S(1)} %get-tuple-element.54), channel_id=1, source_target_pairs={{0,4},{1,5},{2,6},{3,7},{4,0},{5,1},{6,2},{7,3},{8,12},{9,13},{10,... | collective-permute-start | bytes 98312 | tf_op jit(solution)/shard_map/ppermute | solution.py:32
  14.7 4.5 %collective-permute-start.3 = (bf16[32,512]{1,0:T(8,128)(2,1)S(1)}, bf16[32,512]{1,0:T(8,128)(2,1)S(1)}, u32[]{:S(2)}, u32[]{:S(2)}) collective-permute-start(bf16[32,512]{1,0:T(8,128)(2,1)S(1)} %get-tuple-element.54), channel_id=1, source_target_pairs={{0,6},{1,7},{2,0},{3,1},{4,2},{5,3},{6,4},{7,5},{8,14},{9,15},{10,... | collective-permute-start | bytes 98312 | tf_op jit(solution)/shard_map/ppermute | solution.py:32
  19.1 10.8 %collective-permute-start.8 = (bf16[4,32,512]{2,1,0:T(8,128)(2,1)S(1)}, bf16[4,32,512]{2,1,0:T(8,128)(2,1)S(1)}, u32[]{:S(2)}, u32[]{:S(2)}) collective-permute-start(bf16[4,32,512]{2,1,0:T(8,128)(2,1)S(1)} %pad_maximum_fusion.refs_3_), channel_id=1, source_target_pairs={{0,184},{1,185},{2,186},{3,187},{4,188},{5,189},{6,190},{7,191},{8... | collective-permute-start | bytes 393224 | tf_op jit(solution)/shard_map/ppermute | solution.py:32
  21.5 8.5 %collective-permute-start.7 = (bf16[4,32,512]{2,1,0:T(8,128)(2,1)S(1)}, bf16[4,32,512]{2,1,0:T(8,128)(2,1)S(1)}, u32[]{:S(2)}, u32[]{:S(2)}) collective-permute-start(bf16[4,32,512]{2,1,0:T(8,128)(2,1)S(1)} %pad_maximum_fusion.refs_3_), channel_id=1, source_target_pairs={{0,48},{1,49},{2,50},{3,51},{4,52},{5,53},{6,54},{7,55},{8,56},{9,... | collective-permute-start | bytes 393224 | tf_op jit(solution)/shard_map/ppermute | solution.py:32
  21.7 8.3 %collective-permute-start.6 = (bf16[4,32,512]{2,1,0:T(8,128)(2,1)S(1)}, bf16[4,32,512]{2,1,0:T(8,128)(2,1)S(1)}, u32[]{:S(2)}, u32[]{:S(2)}) collective-permute-start(bf16[4,32,512]{2,1,0:T(8,128)(2,1)S(1)} %pad_maximum_fusion.refs_3_), channel_id=1, source_target_pairs={{0,136},{1,137},{2,138},{3,139},{4,140},{5,141},{6,142},{7,143},{8... | collective-permute-start | bytes 393224 | tf_op jit(solution)/shard_map/ppermute | solution.py:32
  30.1 14.2 %collective-permute-start.9 = (bf16[80,16,384]{2,1,0:T(8,128)(2,1)S(1)}, bf16[80,16,384]{2,1,0:T(8,128)(2,1)S(1)}, u32[]{:S(2)}, u32[]{:S(2)}) collective-permute-start(bf16[80,16,384]{2,1,0:T(8,128)(2,1)S(1)} %get-tuple-element.55.sent), channel_id=1, source_target_pairs={{0,16},{1,17},{2,18},{3,19},{4,20},{5,21},{6,22},{7,23},{8,24},{9,... | collective-permute-start | bytes 2949128 | tf_op jit(solution)/shard_map/ppermute | solution.py:32
  32.6 14.7 %collective-permute-start.12 = (bf16[80,16,384]{2,1,0:T(8,128)(2,1)S(1)}, bf16[80,16,384]{2,1,0:T(8,128)(2,1)S(1)}, u32[]{:S(2)}, u32[]{:S(2)}) collective-permute-start(bf16[80,16,384]{2,1,0:T(8,128)(2,1)S(1)} %get-tuple-element.60.sent), channel_id=1, source_target_pairs={{0,8},{1,9},{2,10},{3,11},{4,12},{5,13},{6,14},{7,15},{8,0},{9,1},... | collective-permute-start | bytes 2949128 | tf_op jit(solution)/shard_map/ppermute | solution.py:32
  35.4 15.2 %collective-permute-start.15 = (bf16[80,32,128]{2,1,0:T(8,128)(2,1)S(1)}, bf16[80,32,128]{2,1,0:T(8,128)(2,1)S(1)}, u32[]{:S(2)}, u32[]{:S(2)}) collective-permute-start(bf16[80,32,128]{2,1,0:T(8,128)(2,1)S(1)} %get-tuple-element.65.sent), channel_id=1, source_target_pairs={{0,1},{1,0},{2,3},{3,2},{4,5},{5,4},{6,7},{7,6},{8,9},{9,8},{10,11... | collective-permute-start | bytes 1966088 | tf_op jit(solution)/shard_map/ppermute | solution.py:32
  44.5 12.2 %collective-permute-start.10 = (bf16[64,16,384]{2,1,0:T(8,128)(2,1)S(1)}, bf16[64,16,384]{2,1,0:T(8,128)(2,1)S(1)}, u32[]{:S(2)}, u32[]{:S(2)}) collective-permute-start(bf16[64,16,384]{2,1,0:T(8,128)(2,1)S(1)} %get-tuple-element.57.sent), channel_id=1, source_target_pairs={{0,8},{1,9},{2,10},{3,11},{4,12},{5,13},{6,14},{7,15},{8,0},{9,1},... | collective-permute-start | bytes 2359304 | tf_op jit(solution)/shard_map/ppermute | solution.py:32
  47.6 12.4 %collective-permute-start.13 = (bf16[64,16,384]{2,1,0:T(8,128)(2,1)S(1)}, bf16[64,16,384]{2,1,0:T(8,128)(2,1)S(1)}, u32[]{:S(2)}, u32[]{:S(2)}) collective-permute-start(bf16[64,16,384]{2,1,0:T(8,128)(2,1)S(1)} %get-tuple-element.62.sent), channel_id=1, source_target_pairs={{0,1},{1,0},{2,3},{3,2},{4,5},{5,4},{6,7},{7,6},{8,9},{9,8},{10,11... | collective-permute-start | bytes 2359304 | tf_op jit(solution)/shard_map/ppermute | solution.py:32
  50.7 12.0 %collective-permute-start.16 = (bf16[64,32,128]{2,1,0:T(8,128)(2,1)S(1)}, bf16[64,32,128]{2,1,0:T(8,128)(2,1)S(1)}, u32[]{:S(2)}, u32[]{:S(2)}) collective-permute-start(bf16[64,32,128]{2,1,0:T(8,128)(2,1)S(1)} %get-tuple-element.67.sent), channel_id=1, source_target_pairs={{0,16},{1,17},{2,18},{3,19},{4,20},{5,21},{6,22},{7,23},{8,24},{9,... | collective-permute-start | bytes 1572872 | tf_op jit(solution)/shard_map/ppermute | solution.py:32
  56.9 16.7 %collective-permute-start.11 = (bf16[80,16,384]{2,1,0:T(8,128)(2,1)S(1)}, bf16[80,16,384]{2,1,0:T(8,128)(2,1)S(1)}, u32[]{:S(2)}, u32[]{:S(2)}) collective-permute-start(bf16[80,16,384]{2,1,0:T(8,128)(2,1)S(1)} %get-tuple-element.59.sx), channel_id=1, source_target_pairs={{0,1},{1,0},{2,3},{3,2},{4,5},{5,4},{6,7},{7,6},{8,9},{9,8},{10,11... | collective-permute-start | bytes 2949128 | tf_op jit(solution)/shard_map/ppermute | solution.py:32
  60.2 14.2 %collective-permute-start.14 = (bf16[80,16,384]{2,1,0:T(8,128)(2,1)S(1)}, bf16[80,16,384]{2,1,0:T(8,128)(2,1)S(1)}, u32[]{:S(2)}, u32[]{:S(2)}) collective-permute-start(bf16[80,16,384]{2,1,0:T(8,128)(2,1)S(1)} %get-tuple-element.64.sy), channel_id=1, source_target_pairs={{0,16},{1,17},{2,18},{3,19},{4,20},{5,21},{6,22},{7,23},{8,24},{9,... | collective-permute-start | bytes 2949128 | tf_op jit(solution)/shard_map/ppermute | solution.py:32
  62.8 10.7 %collective-permute-start.17 = (bf16[80,32,128]{2,1,0:T(8,128)(2,1)S(1)}, bf16[80,32,128]{2,1,0:T(8,128)(2,1)S(1)}, u32[]{:S(2)}, u32[]{:S(2)}) collective-permute-start(bf16[80,32,128]{2,1,0:T(8,128)(2,1)S(1)} %get-tuple-element.69.sz), channel_id=1, source_target_pairs={{0,8},{1,9},{2,10},{3,11},{4,12},{5,13},{6,14},{7,15},{8,0},{9,1},... | collective-permute-start | bytes 1966088 | tf_op jit(solution)/shard_map/ppermute | solution.py:32
  74.5 6.3 %collective-permute-start.18 = (bf16[4,32,512]{2,1,0:T(8,128)(2,1)S(1)}, bf16[4,32,512]{2,1,0:T(8,128)(2,1)S(1)}, u32[]{:S(2)}, u32[]{:S(2)}) collective-permute-start(bf16[4,32,512]{2,1,0:T(8,128)(2,1)S(1)} %get-tuple-element.77), channel_id=1, source_target_pairs={{0,136},{1,137},{2,138},{3,139},{4,140},{5,141},{6,142},{7,143},{8... | collective-permute-start | bytes 393224 | tf_op jit(solution)/shard_map/ppermute | solution.py:32
  74.9 5.9 %collective-permute-start.19 = (bf16[4,32,512]{2,1,0:T(8,128)(2,1)S(1)}, bf16[4,32,512]{2,1,0:T(8,128)(2,1)S(1)}, u32[]{:S(2)}, u32[]{:S(2)}) collective-permute-start(bf16[4,32,512]{2,1,0:T(8,128)(2,1)S(1)} %get-tuple-element.78), channel_id=1, source_target_pairs={{0,48},{1,49},{2,50},{3,51},{4,52},{5,53},{6,54},{7,55},{8,56},{9,... | collective-permute-start | bytes 393224 | tf_op jit(solution)/shard_map/ppermute | solution.py:32
  74.9 6.2 %collective-permute-start.20 = (bf16[4,32,512]{2,1,0:T(8,128)(2,1)S(1)}, bf16[4,32,512]{2,1,0:T(8,128)(2,1)S(1)}, u32[]{:S(2)}, u32[]{:S(2)}) collective-permute-start(bf16[4,32,512]{2,1,0:T(8,128)(2,1)S(1)} %get-tuple-element.79), channel_id=1, source_target_pairs={{0,184},{1,185},{2,186},{3,187},{4,188},{5,189},{6,190},{7,191},{8... | collective-permute-start | bytes 393224 | tf_op jit(solution)/shard_map/ppermute | solution.py:32
  81.0 21.2 %collective-permute-start.21 = (f32[2,256,512]{2,1,0:T(8,128)S(1)}, f32[2,256,512]{2,1,0:T(8,128)S(1)}, u32[]{:S(2)}, u32[]{:S(2)}) collective-permute-start(f32[2,256,512]{2,1,0:T(8,128)S(1)} %get-tuple-element.80), channel_id=1, source_target_pairs={{0,64},{1,65},{2,66},{3,67},{4,68},{5,69},{6,70},{7,71},{8,72},{9,... | collective-permute-start | bytes 3145736 | tf_op jit(solution)/shard_map/ppermute | solution.py:32
  91.3 18.5 %collective-permute-start.22 = (bf16[32,512]{1,0:T(8,128)(2,1)S(1)}, bf16[32,512]{1,0:T(8,128)(2,1)S(1)}, u32[]{:S(2)}, u32[]{:S(2)}) collective-permute-start(bf16[32,512]{1,0:T(8,128)(2,1)S(1)} %get-tuple-element.84), channel_id=1, source_target_pairs={{0,2},{1,3},{2,4},{3,5},{4,6},{5,7},{6,0},{7,1},{8,10},{9,11},{10,... | collective-permute-start | bytes 98312 | tf_op jit(solution)/shard_map/ppermute | solution.py:32
  96.5 13.3 %collective-permute-start.23 = (bf16[32,512]{1,0:T(8,128)(2,1)S(1)}, bf16[32,512]{1,0:T(8,128)(2,1)S(1)}, u32[]{:S(2)}, u32[]{:S(2)}) collective-permute-start(bf16[32,512]{1,0:T(8,128)(2,1)S(1)} %get-tuple-element.85), channel_id=1, source_target_pairs={{0,4},{1,5},{2,6},{3,7},{4,0},{5,1},{6,2},{7,3},{8,12},{9,13},{10,... | collective-permute-start | bytes 98312 | tf_op jit(solution)/shard_map/ppermute | solution.py:32
  100.4 9.4 %collective-permute-start.24 = (bf16[32,512]{1,0:T(8,128)(2,1)S(1)}, bf16[32,512]{1,0:T(8,128)(2,1)S(1)}, u32[]{:S(2)}, u32[]{:S(2)}) collective-permute-start(bf16[32,512]{1,0:T(8,128)(2,1)S(1)} %get-tuple-element.86), channel_id=1, source_target_pairs={{0,6},{1,7},{2,0},{3,1},{4,2},{5,3},{6,4},{7,5},{8,14},{9,15},{10,... | collective-permute-start | bytes 98312 | tf_op jit(solution)/shard_map/ppermute | solution.py:32
  102.3 2.2 %copy-start = (bf16[4096,512]{1,0:T(8,128)(2,1)S(1)}, bf16[4096,512]{1,0:T(8,128)(2,1)}, u32[]{:S(2)}) copy-start(bf16[4096,512]{1,0:T(8,128)(2,1)} %get-tuple-element.75.w) | copy-start | bytes 12582916

commit v4 on v3

--- a/solution.py
+++ b/solution.py
@@ -1,3 +1,4 @@
+import functools
 import jax
 import jax.numpy as jnp
 from jax import lax
@@ -11,11 +12,15 @@
 VMEM = pl.BlockSpec(memory_space=pltpu.VMEM)
 SMEM = pl.BlockSpec(memory_space=pltpu.SMEM)
 HBM = pl.BlockSpec(memory_space=pltpu.HBM)
-PARAMS = pltpu.CompilerParams(vmem_limit_bytes=40 << 20)
+PARAMS = pltpu.CompilerParams(vmem_limit_bytes=28 << 20)
 
 
 STREAMS = ((16, 384), (16, 384), (32, 128))
 AXES = ((0, 1, 2), (1, 2, 0), (2, 0, 1))
+
+
+def message(n, stream):
+    return (n + n // 2 if stream == 2 else n, *STREAMS[stream]), BF16
 
 
 def place(x, y, z, c):
@@ -45,15 +50,17 @@
     return permute(value, move)
 
 
-def plane_step(value, xb, yb):
+def far_step(value, axis, second):
     def move(x, y, z, c):
-        return (neighbour(x, 4, 1 - c) if xb else x, neighbour(y, 4, 1 - c) if yb else y, z, c)
+        at = [x, y, z]
+        if axis < 2:
+            at[axis] = neighbour(at[axis], 4, 1 - c)
+        else:
+            w = neighbour((z + c) // 2 % 4, 4, (1 - c) if second else c)
+            at[2] = (2 * w + (z % 2) * (1 - 2 * c)) % 8
+        return (*at, c)
 
     return permute(value, move)
-
-
-def line_step(value, d):
-    return permute(value, lambda x, y, z, c: (x, y, (z + d) % 8, c))
 
 
 def swap(value):
@@ -72,9 +79,8 @@
 
 
 def label8(u, v, c):
-    p = lax.rem(u + v, 2)
-    step = 1 - 2 * lax.rem(v + c, 2)
-    return p, lax.rem(u - v - p * step + 16, 8) // 2
+    b, d = label4(lax.rem((u + c) // 2, 4), lax.rem((v + c) // 2, 4), c)
+    return lax.rem(u + v, 2), b * 2 + d
 
 
 def reached4(v, c, a, b):
@@ -83,8 +89,9 @@
 
 
 def reached8(v, c, a, d):
-    step = 1 - 2 * lax.rem(v + c, 2)
-    return lax.rem(v + a * step + 2 * d + 8, 8)
+    w = reached4(lax.rem((v + c) // 2, 4), c, d // 2, d % 2)
+    p = lax.rem(v + a, 2)
+    return lax.rem(2 * w + p * (1 - 2 * c) + 8, 8)
 
 
 def call(kernel, outs, *args, **more):
@@ -181,7 +188,7 @@
         terms_kernel,
         in_specs=[SMEM, HBM] + [VMEM] * 4,
         out_specs=[VMEM] * 6,
-        out_shape=[jax.ShapeDtypeStruct((80, *s), BF16) for s in STREAMS]
+        out_shape=[jax.ShapeDtypeStruct(*message(65, i)) for i in range(3)]
         + [jax.ShapeDtypeStruct((65, *s), F32) for s in STREAMS],
         scratch_shapes=[pltpu.VMEM((8, *tokens.shape[:2], 512), BF16), pltpu.SemaphoreType.DMA((8,))],
         compiler_params=PARAMS,
@@ -193,43 +200,51 @@
     return (block[..., 0:16, 0:384], block[..., 16:32, 0:384], block[..., :, 384:512])[stream]
 
 
-def pack_kernel(*refs):
-    plane, outs = refs[3:7], refs[7:10]
-    for stream, out in enumerate(outs):
-        for q, part in enumerate(plane):
-            out[64 + 4 * q : 68 + 4 * q] = cut(stream, part[...])
-
-
-def second_kernel(sent, got, keep, send, kept):
+def second_kernel(stream, got, keep, plane, send, kept):
     send[0:32] = (keep[32:64] + got[32:64].astype(F32)).astype(BF16)
-    send[32:48] = sent[64:80]
-    send[48:64] = got[64:80]
+    send[32:48] = cut(stream, plane[...])
     kept[...] = keep[0:32] + got[0:32].astype(F32)
 
 
-def third_kernel(sent, got, keep, send, kept):
+def third_kernel(got, keep, sent, send, kept):
     send[0:16] = (keep[16:32] + got[16:32].astype(F32)).astype(BF16)
-    send[16:48] = sent[32:64]
-    send[48:80] = got[32:64]
+    send[16:32] = sent[32:48]
+    send[32:48] = got[32:48]
     kept[...] = keep[0:16] + got[0:16].astype(F32)
 
 
-def far_kernel(gx, gy, gz, kx, ky, kz, own, s1, s2, s3):
-    for q, out in enumerate((own, s1, s2, s3)):
-        at = slice(4 * q, 4 * q + 4)
-        out[:, 0:16, 0:384] = (kx[at] + gx[at].astype(F32)).astype(out.dtype)
-        out[:, 16:32, 0:384] = (ky[at] + gy[at].astype(F32)).astype(out.dtype)
-        out[:, :, 384:512] = (kz[at] + gz[at].astype(F32)).astype(out.dtype)
-
-
-def last_kernel(own, g1, g2, g3, kept, s1, s2, s3):
-    for d, out in enumerate((kept, s1, s2, s3)):
-        total = own[d] + g1[d].astype(F32) + g2[d].astype(F32) + g3[d].astype(F32)
-        out[...] = total.astype(out.dtype)
-
-
-def sum_kernel(own, g1, g2, g3, out):
-    out[...] = own[...] + g1[...].astype(F32) + g2[...].astype(F32) + g3[...].astype(F32)
+def fourth_kernel(got, sent, send):
+    send[0:32] = sent[16:48]
+    send[32:64] = got[16:48]
+
+
+def far_kernel(gx, gy, gz, kx, ky, kz, s0, s1, k0, k1):
+    for out, start, stride in ((s0, 8, 4), (k0, 0, 4), (s1, 6, 8), (k1, 2, 8)):
+        for i in range(2):
+            at, to = slice(start + stride * i, start + stride * i + 2), slice(2 * i, 2 * i + 2)
+            out[to, 0:16, 0:384] = (kx[at] + gx[at].astype(F32)).astype(out.dtype)
+            out[to, 16:32, 0:384] = (ky[at] + gy[at].astype(F32)).astype(out.dtype)
+            out[to, :, 384:512] = (kz[at] + gz[at].astype(F32)).astype(out.dtype)
+
+
+def across_kernel(g0, g1, k0, k1, s0, s1, kept):
+    for i, (got, keep, send) in enumerate(((g0, k0, s0), (g1, k1, s1))):
+        send[...] = (keep[2:4] + got[2:4].astype(F32)).astype(BF16)
+        kept[2 * i : 2 * i + 2] = keep[0:2] + got[0:2].astype(F32)
+
+
+def line_kernel(g0, g1, keep, send, kept):
+    send[...] = (keep[2:4] + g1[...].astype(F32)).astype(BF16)
+    kept[...] = keep[0:2] + g0[...].astype(F32)
+
+
+def last_kernel(got, keep, send, kept):
+    send[...] = (keep[1] + got[1].astype(F32)).astype(BF16)
+    kept[...] = keep[0] + got[0].astype(F32)
+
+
+def sum_kernel(got, keep, out):
+    out[...] = keep[...] + got[...].astype(F32)
 
 
 def assemble(me, sx, sy, sz, gx, gy, gz, w):
@@ -247,65 +262,53 @@
 
                     def part(stream, sent, got):
                         first, second, third = (label[axis] for axis in AXES[stream])
-                        return (got if third else sent)[16 + second * 32 + first * 16 + i]
+                        return (got if first else sent)[third * 32 + second * 16 + i]
 
                     w[pl.ds(at, 16), 0:384] = part(0, sx, gx)
                     w[pl.ds(at + 16, 16), 0:384] = part(1, sy, gy)
                     w[pl.ds(at, 32), 384:512] = part(2, sz, gz)
 
 
-def other_kernel(me, r0, r1, sx, sy, sz, gx, gy, gz, out, w):
+def other_kernel(me, tokens, r0, r1, sx, sy, sz, gx, gy, gz, out, w, own, sems):
+    mine = pl.multiple_of(2048 * me[3], 2048)
+    loads = [
+        pltpu.make_async_copy(tokens.at[:, :, pl.ds(mine + 4096 * i, 2048)], own.at[i], sems.at[i]) for i in range(2)
+    ]
+    for load in loads:
+        load.start()
     assemble(me, sx, sy, sz, gx, gy, gz, w)
     for m in range(out.shape[0]):
         out[m] = jnp.dot(r0[m], w[0:2048], preferred_element_type=F32) + jnp.dot(
             r1[m], w[2048:4096], preferred_element_type=F32
         )
-
-
-def mine_kernel(me, tokens, w, other, out, own, sems):
-    mine = pl.multiple_of(2048 * me[3], 2048)
-    loads = [
-        [
-            pltpu.make_async_copy(tokens.at[m, :, pl.ds(mine + 4096 * i, 2048)], own.at[2 * m + i], sems.at[2 * m + i])
-            for i in range(2)
-        ]
-        for m in range(2)
-    ]
-    for load in loads[0] + loads[1]:
-        load.start()
-    for m in range(2):
-        total = other[m]
-        for i in range(2):
-            loads[m][i].wait()
-            total += jnp.dot(own[2 * m + i], w[2048 * i : 2048 * i + 2048], preferred_element_type=F32)
+    for load in loads:
+        load.wait()
+
+
+def mine_kernel(own, w, other, out):
+    for m in range(out.shape[0]):
+        total = (
+            other[m]
+            + jnp.dot(own[0, m], w[0:2048], preferred_element_type=F32)
+            + jnp.dot(own[1, m], w[2048:4096], preferred_element_type=F32)
+        )
         out[m] = total.astype(BF16)
 
 
-def other_values(me, r0, r1, messages):
+def other_values(me, tokens, r0, r1, messages):
     return pl.pallas_call(
         other_kernel,
-        in_specs=[SMEM] + [VMEM] * 8,
-        out_specs=[VMEM] * 2,
+        in_specs=[SMEM, HBM] + [VMEM] * 8,
+        out_specs=[VMEM] * 3,
         out_shape=[
             jax.ShapeDtypeStruct((*r0.shape[:2], 512), F32),
             jax.ShapeDtypeStruct((4096, 512), BF16),
+            jax.ShapeDtypeStruct((2, *r0.shape), BF16),
         ],
+        scratch_shapes=[pltpu.SemaphoreType.DMA((2,))],
         compiler_params=PARAMS,
         interpret=INTERPRET,
-    )(me, r0, r1, *messages)
-
-
-def my_values(me, tokens, w, other):
-    micro, rows, _ = tokens.shape
-    return pl.pallas_call(
-        mine_kernel,
-        in_specs=[SMEM, HBM, VMEM, VMEM],
-        out_specs=VMEM,
-        out_shape=jax.ShapeDtypeStruct((micro, rows, 512), BF16),
-        scratch_shapes=[pltpu.VMEM((2 * micro, rows, 2048), BF16), pltpu.SemaphoreType.DMA((2 * micro,))],
-        compiler_params=PARAMS,
-        interpret=INTERPRET,
-    )(me, tokens, w, other)
+    )(me, tokens, r0, r1, *messages)
 
 
 def after(value, *others):
@@ -321,38 +324,52 @@
     )
     r0, r1, weight, new_master, new_moment, new_second = first(me, tokens, master, moment, second, gradient)
     r0, r1, cotr = swap(r0), swap(r1), swap(cotangent)
-    line = jnp.stack([weight] + [line_step(weight, -2 * d) for d in (1, 2, 3)])
-    plane = [line] + [plane_step(line, q // 2, q % 2) for q in (1, 2, 3)]
+    line = jnp.stack([weight, far_step(weight, 2, True)])
+    line = jnp.concatenate([line, far_step(line, 2, False)])
     terms = all_terms(me, tokens, r0, r1, cotangent, cotr)
     send, keep = terms[:3], terms[3:]
 
-    send = call(
-        pack_kernel,
-        [((80, *s), BF16) for s in STREAMS],
-        *send,
-        *plane,
-        input_output_aliases={0: 0, 1: 1, 2: 2},
-    )
     got = [near(send[i], AXES[i][0]) for i in range(3)]
-    for step, kernel, size, rest in ((1, second_kernel, 64, 32), (2, third_kernel, 80, 16)):
-        new = [
-            call(kernel, [((size, *STREAMS[i]), BF16), ((rest, *STREAMS[i]), F32)], send[i], got[i], keep[i])
-            for i in range(3)
-        ]
-        send, keep = [n[0] for n in new], [n[1] for n in new]
-        got = [near(send[i], AXES[i][step]) for i in range(3)]
-
-    block = (4, 32, 512)
-    own, *parts = call(far_kernel, [(block, F32)] + [(block, BF16)] * 3, *got, *keep)
-    parts = [plane_step(part, q // 2, q % 2) for q, part in zip((1, 2, 3), parts)]
-
-    other, w = other_values(after(me, own), r0, r1, [*send, *got])
-    other = swap(after(other, *parts))
-
-    own, *parts = call(last_kernel, [(block[1:], F32)] + [(block[1:], BF16)] * 3, after(own, w), *parts)
-    parts = [line_step(part, 2 * d) for d, part in zip((1, 2, 3), parts)]
-    values = my_values(me, tokens, w, other)
-    (weight_grad,) = call(sum_kernel, [(block[1:], F32)], after(own, values), *parts)
+    line = after(line, send[0])
+    plane = jnp.concatenate([line, far_step(line, 1, False)])
+    plane = jnp.concatenate([plane, far_step(plane, 0, False)])
+
+    *got, plane = lax.optimization_barrier((*got, plane))
+    new = [
+        call(
+            functools.partial(second_kernel, i),
+            [message(48, i), ((32, *STREAMS[i]), F32)],
+            got[i],
+            keep[i],
+            plane,
+        )
+        for i in range(3)
+    ]
+    send, keep = [n[0] for n in new], [n[1] for n in new]
+    got = [near(send[i], AXES[i][1]) for i in range(3)]
+
+    new = [
+        call(third_kernel, [message(48, i), ((16, *STREAMS[i]), F32)], got[i], keep[i], send[i])
+        for i in range(3)
+    ]
+    send, keep = [n[0] for n in new], [n[1] for n in new]
+    got = [near(send[i], AXES[i][2]) for i in range(3)]
+
+    block = (32, 512)
+    s0, s1, k0, k1 = call(far_kernel, [((4, *block), BF16)] * 2 + [((4, *block), F32)] * 2, *got, *keep)
+    half = [call(fourth_kernel, [message(64, i)], got[i], send[i])[0] for i in range(3)]
+    g0, g1 = far_step(s0, 0, False), far_step(s1, 1, False)
+    rest = [near(half[i], AXES[i][0]) for i in range(3)]
+    s0, s1, kept = call(across_kernel, [((2, *block), BF16)] * 2 + [((4, *block), F32)], g0, g1, k0, k1)
+    g0, g1 = far_step(s0, 1, False), far_step(s1, 0, False)
+    s, kept = call(line_kernel, [((2, *block), BF16), ((2, *block), F32)], g0, g1, kept)
+    got = far_step(s, 2, False)
+
+    other, w, own = other_values(after(me, kept), tokens, r0, r1, [*half, *rest])
+    s, kept = call(last_kernel, [(block, BF16), (block, F32)], got, after(kept, w))
+    got = far_step(s, 2, True)
+    (values,) = call(mine_kernel, [((*r0.shape[:2], 512), BF16)], own, w, swap(after(other, kept)))
+    (weight_grad,) = call(sum_kernel, [(block, F32)], got, after(kept, values))
     return (new_master, new_moment, new_second, values, weight_grad)
 
 

time: 111 us -> 99.5 us (0.90)
  the two profiles are of different devices: /device:TPU:1 before, /device:TPU:0 now
where the time goes in v4:
time: 99.5 us; the launch traced here: 98.3 us
  waiting for transfers between devices  38.3 us (38%)
  starting transfers between devices  36.8 us (37%)
  Pallas kernels  22.1 us (22%)
    ppermute x26, waiting for transfers between devices, permute(): return lax.ppermute(value, ALL, pairs)  38.3 us
    ppermute x26, starting transfers between devices, permute(): return lax.ppermute(value, ALL, pairs)  36.8 us
    pallas_call x1, Pallas kernels, all_terms(): pl.pallas_call(terms_kernel, in_specs=[SMEM, HBM] + [VMEM] * 4, out_specs...  8.1 us
    pallas_call x1, Pallas kernels, other_values(): pl.pallas_call(other_kernel, in_specs=[SMEM, HBM] + [VMEM] * 8, out_specs...  5.47 us
    pallas_call x15, Pallas kernels, call(): pl.pallas_call(kernel, out_shape=[jax.ShapeDtypeStruct(*o) for o in outs]...  4.92 us
    pallas_call x1, Pallas kernels, first(): pl.pallas_call(first_kernel, in_specs=[SMEM] + [HBM] * 5, out_specs=[VMEM...  3.65 us
  transfers between devices with their start and end apart: 26, of which 10 were waited for; matrix products, arithmetic and copies ran while one was open for 0% of the time, Pallas kernels for 18%

profile of v4, /device:TPU:0, one launch (start us, length us, event | category | flops | bytes accessed | tf_op | source)
XLA Modules:
  0.0 98.3 jit_solution(14731364204769959208)
XLA Ops:
  0.7 0.1 pad_add_fusion.me
  0.8 3.6 %shard_map.101 = (bf16[2,256,2048]{2,1,0:T(8,128)(2,1)S(1)}, bf16[2,256,2048]{2,1,0:T(8,128)(2,1)S(1)}, bf16[32,512]{1,0:T(8,128)(2,1)S(1)}, f32[32,512]{1,0:T(8...) custom-call(s32[4]{0:T(128)S(1)} %pad_add_fusion.me, bf16[2,256,8192]{2,1,0:T(8,128)(2,1)} %tokens.5, f32[32,512]{1,0:T(8,128)} %master.1, ...), custom_call_target="tpu_custom_call" | custom-call | tf_op jit(solution)/shard_map/pallas_call | solution.py:139
  4.4 0.1 collective-permute-start
  4.5 0.5 collective-permute-start.1
  5.0 0.1 collective-permute-start.2
  5.1 4.6 %collective-permute-start.6 = (bf16[32,512]{1,0:T(8,128)(2,1)S(1)}, bf16[32,512]{1,0:T(8,128)(2,1)S(1)}, u32[]{:S(2)}, u32[]{:S(2)}) collective-permute-start(bf16[32,512]{1,0:T(8,128)(2,1)S(1)} %get-tuple-element.60), channel_id=1, source_target_pairs={{0,6},{1,7},{2,4},{3,5},{4,2},{5,3},{6,0},{7,1},{8,14},{9,15},{10,... | collective-permute-start | bytes 98312 | tf_op jit(solution)/shard_map/ppermute | solution.py:37
  9.7 1.9 %collective-permute-done.6 = bf16[32,512]{1,0:T(8,128)(2,1)S(1)} collective-permute-done((bf16[32,512]{1,0:T(8,128)(2,1)S(1)}, bf16[32,512]{1,0:T(8,128)(2,1)S(1)}, u32[]{:S(2)}, u32[]{:S(2)}) %collective-permute-start.6) | collective-permute-done | bytes 32800 | tf_op jit(solution)/shard_map/ppermute | solution.py:37
  11.6 1.5 %collective-permute-start.7 = (bf16[2,32,512]{2,1,0:T(8,128)(2,1)S(1)}, bf16[2,32,512]{2,1,0:T(8,128)(2,1)S(1)}, u32[]{:S(2)}, u32[]{:S(2)}) collective-permute-start(bf16[2,32,512]{2,1,0:T(8,128)(2,1)S(1)} %pad_maximum_fusion.3), channel_id=1, source_target_pairs={{0,2},{1,3},{2,0},{3,1},{4,6},{5,7},{6,4},{7,5},{8,10},{9,11},{10,... | collective-permute-start | bytes 196616 | tf_op jit(solution)/shard_map/ppermute | solution.py:37
  13.1 8.1 %shard_map.102 = (bf16[65,16,384]{2,1,0:T(8,128)(2,1)S(1)}, bf16[65,16,384]{2,1,0:T(8,128)(2,1)S(1)}, bf16[97,32,128]{2,1,0:T(8,128)(2,1)S(1)}, f32[65,16,384]{2...) custom-call(s32[4]{0:T(128)S(1)} %pad_add_fusion.me, bf16[2,256,8192]{2,1,0:T(8,128)(2,1)} %tokens.5, ...), custom_call_target="tpu_custom_call" | custom-call | tf_op jit(solution)/shard_map/pallas_call | solution.py:187
  21.2 1.7 %collective-permute-start.4 = (bf16[65,16,384]{2,1,0:T(8,128)(2,1)S(1)}, bf16[65,16,384]{2,1,0:T(8,128)(2,1)S(1)}, u32[]{:S(2)}, u32[]{:S(2)}) collective-permute-start(bf16[65,16,384]{2,1,0:T(8,128)(2,1)S(1)} %get-tuple-element.58), channel_id=1, source_target_pairs={{0,8},{1,9},{2,10},{3,11},{4,12},{5,13},{6,14},{7,15},{8,0},{9,1},... | collective-permute-start | bytes 2396168 | tf_op jit(solution)/shard_map/ppermute | solution.py:37
  22.9 1.5 %collective-permute-start.3 = (bf16[65,16,384]{2,1,0:T(8,128)(2,1)S(1)}, bf16[65,16,384]{2,1,0:T(8,128)(2,1)S(1)}, u32[]{:S(2)}, u32[]{:S(2)}) collective-permute-start(bf16[65,16,384]{2,1,0:T(8,128)(2,1)S(1)} %get-tuple-element.57), channel_id=1, source_target_pairs={{0,16},{1,17},{2,18},{3,19},{4,20},{5,21},{6,22},{7,23},{8,24},{9,... | collective-permute-start | bytes 2396168 | tf_op jit(solution)/shard_map/ppermute | solution.py:37
  24.4 1.6 %collective-permute-start.5 = (bf16[97,32,128]{2,1,0:T(8,128)(2,1)S(1)}, bf16[97,32,128]{2,1,0:T(8,128)(2,1)S(1)}, u32[]{:S(2)}, u32[]{:S(2)}) collective-permute-start(bf16[97,32,128]{2,1,0:T(8,128)(2,1)S(1)} %get-tuple-element.59), channel_id=1, source_target_pairs={{0,1},{1,0},{2,3},{3,2},{4,5},{5,4},{6,7},{7,6},{8,9},{9,8},{10,11... | collective-permute-start | bytes 2383880 | tf_op jit(solution)/shard_map/ppermute | solution.py:37
  26.0 2.3 %collective-permute-start.8 = (bf16[4,32,512]{2,1,0:T(8,128)(2,1)S(1)}, bf16[4,32,512]{2,1,0:T(8,128)(2,1)S(1)}, u32[]{:S(2)}, u32[]{:S(2)}) collective-permute-start(bf16[4,32,512]{2,1,0:T(8,128)(2,1)S(1)} %pad_maximum_fusion.2), channel_id=1, source_target_pairs={{0,136},{1,137},{2,138},{3,139},{4,140},{5,141},{6,142},{7,143},{8... | collective-permute-start | bytes 393224 | tf_op jit(solution)/shard_map/ppermute | solution.py:37
  28.3 5.5 %collective-permute-done.8 = bf16[4,32,512]{2,1,0:T(8,128)(2,1)S(1)} collective-permute-done((bf16[4,32,512]{2,1,0:T(8,128)(2,1)S(1)}, bf16[4,32,512]{2,1,0:T(8,128)(2,1)S(1)}, u32[]{:S(2)}, u32[]{:S(2)}) %collective-permute-start.8) | collective-permute-done | bytes 131104 | tf_op jit(solution)/shard_map/ppermute | solution.py:37
  33.8 2.2 %collective-permute-start.9 = (bf16[8,32,512]{2,1,0:T(8,128)(2,1)S(1)}, bf16[8,32,512]{2,1,0:T(8,128)(2,1)S(1)}, u32[]{:S(2)}, u32[]{:S(2)}) collective-permute-start(bf16[8,32,512]{2,1,0:T(8,128)(2,1)S(1)} %pad_maximum_fusion.1), channel_id=1, source_target_pairs={{0,48},{1,49},{2,50},{3,51},{4,52},{5,53},{6,54},{7,55},{8,56},{9,... | collective-permute-start | bytes 786440 | tf_op jit(solution)/shard_map/ppermute | solution.py:37
  35.9 5.5 %collective-permute-done.9 = bf16[8,32,512]{2,1,0:T(8,128)(2,1)S(1)} collective-permute-done((bf16[8,32,512]{2,1,0:T(8,128)(2,1)S(1)}, bf16[8,32,512]{2,1,0:T(8,128)(2,1)S(1)}, u32[]{:S(2)}, u32[]{:S(2)}) %collective-permute-start.9) | collective-permute-done | bytes 262176 | tf_op jit(solution)/shard_map/ppermute | solution.py:37
  41.5 0.1 shard_map.107
  41.6 0.1 collective-permute-start.14
  41.7 0.2 shard_map.103
  41.9 0.3 collective-permute-start.10
  42.2 0.2 shard_map.105
  42.4 0.6 collective-permute-start.12
  43.0 8.6 %collective-permute-done.14.got = bf16[72,32,128]{2,1,0:T(8,128)(2,1)S(1)} collective-permute-done((bf16[72,32,128]{2,1,0:T(8,128)(2,1)S(1)}, bf16[72,32,128]{2,1,0:T(8,128)(2,1)S(1)}, u32[]{:S(2)}, u32[]{:S(2)}) %collective-permute-start.14) | collective-permute-done | bytes 589856 | tf_op jit(solution)/shard_map/ppermute | solution.py:37
  51.7 0.1 collective-permute-start.15
  51.8 0.3 collective-permute-done.10.got
  52.1 0.1 shard_map.104
  52.2 0.6 collective-permute-start.11
  52.7 0.1 shard_map.106
  52.9 2.1 %collective-permute-start.13 = (bf16[48,16,384]{2,1,0:T(8,128)(2,1)S(1)}, bf16[48,16,384]{2,1,0:T(8,128)(2,1)S(1)}, u32[]{:S(2)}, u32[]{:S(2)}) collective-permute-start(bf16[48,16,384]{2,1,0:T(8,128)(2,1)S(1)} %get-tuple-element.72.sent), channel_id=1, source_target_pairs={{0,16},{1,17},{2,18},{3,19},{4,20},{5,21},{6,22},{7,23},{8,24},{9,... | collective-permute-start | bytes 1769480 | tf_op jit(solution)/shard_map/ppermute | solution.py:37
  55.0 6.7 %collective-permute-done.15.gz.got = bf16[72,32,128]{2,1,0:T(8,128)(2,1)S(1)} collective-permute-done((bf16[72,32,128]{2,1,0:T(8,128)(2,1)S(1)}, bf16[72,32,128]{2,1,0:T(8,128)(2,1)S(1)}, u32[]{:S(2)}, u32[]{:S(2)}) %collective-permute-start.15) | collective-permute-done | bytes 589856 | tf_op jit(solution)/shard_map/ppermute | solution.py:37
  61.7 0.6 collective-permute-start.22
  62.3 2.0 %collective-permute-start.20 = (bf16[64,16,384]{2,1,0:T(8,128)(2,1)S(1)}, bf16[64,16,384]{2,1,0:T(8,128)(2,1)S(1)}, u32[]{:S(2)}, u32[]{:S(2)}) collective-permute-start(bf16[64,16,384]{2,1,0:T(8,128)(2,1)S(1)} %shard_map.112.sx), channel_id=1, source_target_pairs={{0,16},{1,17},{2,18},{3,19},{4,20},{5,21},{6,22},{7,23},{8,24},{9,... | collective-permute-start | bytes 2359304 | tf_op jit(solution)/shard_map/ppermute | solution.py:37
  64.4 0.3 collective-permute-start.21
  64.7 0.1 shard_map.109
  64.8 2.2 %collective-permute-start.16 = (bf16[4,32,512]{2,1,0:T(8,128)(2,1)S(1)}, bf16[4,32,512]{2,1,0:T(8,128)(2,1)S(1)}, u32[]{:S(2)}, u32[]{:S(2)}) collective-permute-start(bf16[4,32,512]{2,1,0:T(8,128)(2,1)S(1)} %get-tuple-element.81), channel_id=1, source_target_pairs={{0,48},{1,49},{2,50},{3,51},{4,52},{5,53},{6,54},{7,55},{8,56},{9,... | collective-permute-start | bytes 393224 | tf_op jit(solution)/shard_map/ppermute | solution.py:37
  67.0 2.2 %collective-permute-start.17 = (bf16[4,32,512]{2,1,0:T(8,128)(2,1)S(1)}, bf16[4,32,512]{2,1,0:T(8,128)(2,1)S(1)}, u32[]{:S(2)}, u32[]{:S(2)}) collective-permute-start(bf16[4,32,512]{2,1,0:T(8,128)(2,1)S(1)} %get-tuple-element.82), channel_id=1, source_target_pairs={{0,136},{1,137},{2,138},{3,139},{4,140},{5,141},{6,142},{7,143},{8... | collective-permute-start | bytes 393224 | tf_op jit(solution)/shard_map/ppermute | solution.py:37
  69.2 3.4 %collective-permute-done.16.g0 = bf16[4,32,512]{2,1,0:T(8,128)(2,1)S(1)} collective-permute-done((bf16[4,32,512]{2,1,0:T(8,128)(2,1)S(1)}, bf16[4,32,512]{2,1,0:T(8,128)(2,1)S(1)}, u32[]{:S(2)}, u32[]{:S(2)}) %collective-permute-start.16) | collective-permute-done | bytes 131104 | tf_op jit(solution)/shard_map/ppermute | solution.py:37
  72.5 2.1 %collective-permute-done.17.g1 = bf16[4,32,512]{2,1,0:T(8,128)(2,1)S(1)} collective-permute-done((bf16[4,32,512]{2,1,0:T(8,128)(2,1)S(1)}, bf16[4,32,512]{2,1,0:T(8,128)(2,1)S(1)}, u32[]{:S(2)}, u32[]{:S(2)}) %collective-permute-start.17) | collective-permute-done | bytes 131104 | tf_op jit(solution)/shard_map/ppermute | solution.py:37
  74.7 2.3 %collective-permute-start.18 = (bf16[2,32,512]{2,1,0:T(8,128)(2,1)S(1)}, bf16[2,32,512]{2,1,0:T(8,128)(2,1)S(1)}, u32[]{:S(2)}, u32[]{:S(2)}) collective-permute-start(bf16[2,32,512]{2,1,0:T(8,128)(2,1)S(1)} %get-tuple-element.85), channel_id=1, source_target_pairs={{0,136},{1,137},{2,138},{3,139},{4,140},{5,141},{6,142},{7,143},{8... | collective-permute-start | bytes 196616 | tf_op jit(solution)/shard_map/ppermute | solution.py:37
  76.9 1.1 %collective-permute-start.19 = (bf16[2,32,512]{2,1,0:T(8,128)(2,1)S(1)}, bf16[2,32,512]{2,1,0:T(8,128)(2,1)S(1)}, u32[]{:S(2)}, u32[]{:S(2)}) collective-permute-start(bf16[2,32,512]{2,1,0:T(8,128)(2,1)S(1)} %get-tuple-element.86), channel_id=1, source_target_pairs={{0,48},{1,49},{2,50},{3,51},{4,52},{5,53},{6,54},{7,55},{8,56},{9,... | collective-permute-start | bytes 196616 | tf_op jit(solution)/shard_map/ppermute | solution.py:37
  78.1 2.2 %collective-permute-done.18.g0 = bf16[2,32,512]{2,1,0:T(8,128)(2,1)S(1)} collective-permute-done((bf16[2,32,512]{2,1,0:T(8,128)(2,1)S(1)}, bf16[2,32,512]{2,1,0:T(8,128)(2,1)S(1)}, u32[]{:S(2)}, u32[]{:S(2)}) %collective-permute-start.18) | collective-permute-done | bytes 65568 | tf_op jit(solution)/shard_map/ppermute | solution.py:37
  80.2 2.2 %collective-permute-done.19.g1 = bf16[2,32,512]{2,1,0:T(8,128)(2,1)S(1)} collective-permute-done((bf16[2,32,512]{2,1,0:T(8,128)(2,1)S(1)}, bf16[2,32,512]{2,1,0:T(8,128)(2,1)S(1)}, u32[]{:S(2)}, u32[]{:S(2)}) %collective-permute-start.19) | collective-permute-done | bytes 65568 | tf_op jit(solution)/shard_map/ppermute | solution.py:37
  82.5 1.6 %collective-permute-start.23 = (bf16[2,32,512]{2,1,0:T(8,128)(2,1)S(1)}, bf16[2,32,512]{2,1,0:T(8,128)(2,1)S(1)}, u32[]{:S(2)}, u32[]{:S(2)}) collective-permute-start(bf16[2,32,512]{2,1,0:T(8,128)(2,1)S(1)} %get-tuple-element.93), channel_id=1, source_target_pairs={{0,2},{1,3},{2,0},{3,1},{4,6},{5,7},{6,4},{7,5},{8,10},{9,11},{10,... | collective-permute-start | bytes 196616 | tf_op jit(solution)/shard_map/ppermute | solution.py:37
  84.0 5.5 %shard_map.115 = (f32[2,256,512]{2,1,0:T(8,128)S(1)}, bf16[4096,512]{1,0:T(8,128)(2,1)S(1)}, bf16[2,2,256,2048]{3,2,1,0:T(8,128)(2,1)S(1)}) custom-call(s32[4]{0:T(128)S(1)} %pad_add_fusion.me, bf16[2,256,8192]{2,1,0:T(8,128)(2,1)} %tokens.5, bf16[2,256,2048]{2,1,0:T(8,128)(2,1)S(1)} %collective-permute-done.r0, ...), custom_call_target="tpu_custom_call" | custom-call | tf_op jit(solution)/shard_map/pallas_call | solution.py:299
  89.5 0.1 collective-permute-start.24
  89.6 4.8 %collective-permute-start.25 = (bf16[32,512]{1,0:T(8,128)(2,1)S(1)}, bf16[32,512]{1,0:T(8,128)(2,1)S(1)}, u32[]{:S(2)}, u32[]{:S(2)}) collective-permute-start(bf16[32,512]{1,0:T(8,128)(2,1)S(1)} %get-tuple-element.97), channel_id=1, source_target_pairs={{0,6},{1,7},{2,4},{3,5},{4,2},{5,3},{6,0},{7,1},{8,14},{9,15},{10,... | collective-permute-start | bytes 98312 | tf_op jit(solution)/shard_map/ppermute | solution.py:37
  94.5 3.1 %shard_map.117 = bf16[2,256,512]{2,1,0:T(8,128)(2,1)} custom-call(bf16[2,2,256,2048]{3,2,1,0:T(8,128)(2,1)S(1)} %get-tuple-element.90.own, bf16[4096,512]{1,0:T(8,128)(2,1)S(1)} %get-tuple-element.91.w, f32[2,256,512]{2,1,0:T(8,128)S(1)} %collective-permute-done.24.other), custom_call_target="tpu_custom_call" | custom-call | tf_op jit(solution)/shard_map/pallas_call | solution.py:98
  97.6 0.6 shard_map.118
  (29 shorter events, 0.5 us)
Async XLA Ops:
  0.8 4.3 %copy-start = (bf16[2,256,512]{2,1,0:T(8,128)(2,1)S(1)}, bf16[2,256,512]{2,1,0:T(8,128)(2,1)}, u32[]{:S(2)}) copy-start(bf16[2,256,512]{2,1,0:T(8,128)(2,1)} %cot.1) | copy-start | bytes 1572868
  4.4 8.7 %collective-permute-start = (bf16[2,256,2048]{2,1,0:T(8,128)(2,1)S(1)}, bf16[2,256,2048]{2,1,0:T(8,128)(2,1)S(1)}, u32[]{:S(2)}, u32[]{:S(2)}) collective-permute-start(bf16[2,256,2048]{2,1,0:T(8,128)(2,1)S(1)} %get-tuple-element.55), channel_id=1, source_target_pairs={{0,64},{1,65},{2,66},{3,67},{4,68},{5,69},{6,70},{7,71},{8,72},{9,... | collective-permute-start | bytes 6291464 | tf_op jit(solution)/shard_map/ppermute | solution.py:37
  4.5 8.6 %collective-permute-start.1 = (bf16[2,256,2048]{2,1,0:T(8,128)(2,1)S(1)}, bf16[2,256,2048]{2,1,0:T(8,128)(2,1)S(1)}, u32[]{:S(2)}, u32[]{:S(2)}) collective-permute-start(bf16[2,256,2048]{2,1,0:T(8,128)(2,1)S(1)} %get-tuple-element.56), channel_id=1, source_target_pairs={{0,64},{1,65},{2,66},{3,67},{4,68},{5,69},{6,70},{7,71},{8,72},{9,... | collective-permute-start | bytes 6291464 | tf_op jit(solution)/shard_map/ppermute | solution.py:37
  5.0 8.1 %collective-permute-start.2 = (bf16[2,256,512]{2,1,0:T(8,128)(2,1)S(1)}, bf16[2,256,512]{2,1,0:T(8,128)(2,1)S(1)}, u32[]{:S(2)}, u32[]{:S(2)}) collective-permute-start(bf16[2,256,512]{2,1,0:T(8,128)(2,1)S(1)} %copy-done), channel_id=1, source_target_pairs={{0,64},{1,65},{2,66},{3,67},{4,68},{5,69},{6,70},{7,71},{8,72},{9,... | collective-permute-start | bytes 1572872 | tf_op jit(solution)/shard_map/ppermute | solution.py:37
  5.1 6.5 %collective-permute-start.6 = (bf16[32,512]{1,0:T(8,128)(2,1)S(1)}, bf16[32,512]{1,0:T(8,128)(2,1)S(1)}, u32[]{:S(2)}, u32[]{:S(2)}) collective-permute-start(bf16[32,512]{1,0:T(8,128)(2,1)S(1)} %get-tuple-element.60), channel_id=1, source_target_pairs={{0,6},{1,7},{2,4},{3,5},{4,2},{5,3},{6,0},{7,1},{8,14},{9,15},{10,... | collective-permute-start | bytes 98312 | tf_op jit(solution)/shard_map/ppermute | solution.py:37
  11.6 14.4 %collective-permute-start.7 = (bf16[2,32,512]{2,1,0:T(8,128)(2,1)S(1)}, bf16[2,32,512]{2,1,0:T(8,128)(2,1)S(1)}, u32[]{:S(2)}, u32[]{:S(2)}) collective-permute-start(bf16[2,32,512]{2,1,0:T(8,128)(2,1)S(1)} %pad_maximum_fusion.3), channel_id=1, source_target_pairs={{0,2},{1,3},{2,0},{3,1},{4,6},{5,7},{6,4},{7,5},{8,10},{9,11},{10,... | collective-permute-start | bytes 196616 | tf_op jit(solution)/shard_map/ppermute | solution.py:37
  21.2 20.2 %collective-permute-start.4 = (bf16[65,16,384]{2,1,0:T(8,128)(2,1)S(1)}, bf16[65,16,384]{2,1,0:T(8,128)(2,1)S(1)}, u32[]{:S(2)}, u32[]{:S(2)}) collective-permute-start(bf16[65,16,384]{2,1,0:T(8,128)(2,1)S(1)} %get-tuple-element.58), channel_id=1, source_target_pairs={{0,8},{1,9},{2,10},{3,11},{4,12},{5,13},{6,14},{7,15},{8,0},{9,1},... | collective-permute-start | bytes 2396168 | tf_op jit(solution)/shard_map/ppermute | solution.py:37
  22.9 18.6 %collective-permute-start.3 = (bf16[65,16,384]{2,1,0:T(8,128)(2,1)S(1)}, bf16[65,16,384]{2,1,0:T(8,128)(2,1)S(1)}, u32[]{:S(2)}, u32[]{:S(2)}) collective-permute-start(bf16[65,16,384]{2,1,0:T(8,128)(2,1)S(1)} %get-tuple-element.57), channel_id=1, source_target_pairs={{0,16},{1,17},{2,18},{3,19},{4,20},{5,21},{6,22},{7,23},{8,24},{9,... | collective-permute-start | bytes 2396168 | tf_op jit(solution)/shard_map/ppermute | solution.py:37
  24.4 17.1 %collective-permute-start.5 = (bf16[97,32,128]{2,1,0:T(8,128)(2,1)S(1)}, bf16[97,32,128]{2,1,0:T(8,128)(2,1)S(1)}, u32[]{:S(2)}, u32[]{:S(2)}) collective-permute-start(bf16[97,32,128]{2,1,0:T(8,128)(2,1)S(1)} %get-tuple-element.59), channel_id=1, source_target_pairs={{0,1},{1,0},{2,3},{3,2},{4,5},{5,4},{6,7},{7,6},{8,9},{9,8},{10,11... | collective-permute-start | bytes 2383880 | tf_op jit(solution)/shard_map/ppermute | solution.py:37
  26.0 7.7 %collective-permute-start.8 = (bf16[4,32,512]{2,1,0:T(8,128)(2,1)S(1)}, bf16[4,32,512]{2,1,0:T(8,128)(2,1)S(1)}, u32[]{:S(2)}, u32[]{:S(2)}) collective-permute-start(bf16[4,32,512]{2,1,0:T(8,128)(2,1)S(1)} %pad_maximum_fusion.2), channel_id=1, source_target_pairs={{0,136},{1,137},{2,138},{3,139},{4,140},{5,141},{6,142},{7,143},{8... | collective-permute-start | bytes 393224 | tf_op jit(solution)/shard_map/ppermute | solution.py:37
  33.8 7.7 %collective-permute-start.9 = (bf16[8,32,512]{2,1,0:T(8,128)(2,1)S(1)}, bf16[8,32,512]{2,1,0:T(8,128)(2,1)S(1)}, u32[]{:S(2)}, u32[]{:S(2)}) collective-permute-start(bf16[8,32,512]{2,1,0:T(8,128)(2,1)S(1)} %pad_maximum_fusion.1), channel_id=1, source_target_pairs={{0,48},{1,49},{2,50},{3,51},{4,52},{5,53},{6,54},{7,55},{8,56},{9,... | collective-permute-start | bytes 786440 | tf_op jit(solution)/shard_map/ppermute | solution.py:37
  41.6 10.0 %collective-permute-start.14 = (bf16[72,32,128]{2,1,0:T(8,128)(2,1)S(1)}, bf16[72,32,128]{2,1,0:T(8,128)(2,1)S(1)}, u32[]{:S(2)}, u32[]{:S(2)}) collective-permute-start(bf16[72,32,128]{2,1,0:T(8,128)(2,1)S(1)} %get-tuple-element.75.sent), channel_id=1, source_target_pairs={{0,16},{1,17},{2,18},{3,19},{4,20},{5,21},{6,22},{7,23},{8,24},{9,... | collective-permute-start | bytes 1769480 | tf_op jit(solution)/shard_map/ppermute | solution.py:37
  41.9 10.2 %collective-permute-start.10 = (bf16[48,16,384]{2,1,0:T(8,128)(2,1)S(1)}, bf16[48,16,384]{2,1,0:T(8,128)(2,1)S(1)}, u32[]{:S(2)}, u32[]{:S(2)}) collective-permute-start(bf16[48,16,384]{2,1,0:T(8,128)(2,1)S(1)} %get-tuple-element.65.sent), channel_id=1, source_target_pairs={{0,8},{1,9},{2,10},{3,11},{4,12},{5,13},{6,14},{7,15},{8,0},{9,1},... | collective-permute-start | bytes 1769480 | tf_op jit(solution)/shard_map/ppermute | solution.py:37
  42.4 10.3 %collective-permute-start.12 = (bf16[48,16,384]{2,1,0:T(8,128)(2,1)S(1)}, bf16[48,16,384]{2,1,0:T(8,128)(2,1)S(1)}, u32[]{:S(2)}, u32[]{:S(2)}) collective-permute-start(bf16[48,16,384]{2,1,0:T(8,128)(2,1)S(1)} %get-tuple-element.70.sent), channel_id=1, source_target_pairs={{0,1},{1,0},{2,3},{3,2},{4,5},{5,4},{6,7},{7,6},{8,9},{9,8},{10,11... | collective-permute-start | bytes 1769480 | tf_op jit(solution)/shard_map/ppermute | solution.py:37
  51.7 10.0 %collective-permute-start.15 = (bf16[72,32,128]{2,1,0:T(8,128)(2,1)S(1)}, bf16[72,32,128]{2,1,0:T(8,128)(2,1)S(1)}, u32[]{:S(2)}, u32[]{:S(2)}) collective-permute-start(bf16[72,32,128]{2,1,0:T(8,128)(2,1)S(1)} %get-tuple-element.77.sent), channel_id=1, source_target_pairs={{0,8},{1,9},{2,10},{3,11},{4,12},{5,13},{6,14},{7,15},{8,0},{9,1},... | collective-permute-start | bytes 1769480 | tf_op jit(solution)/shard_map/ppermute | solution.py:37
  52.2 10.1 %collective-permute-start.11 = (bf16[48,16,384]{2,1,0:T(8,128)(2,1)S(1)}, bf16[48,16,384]{2,1,0:T(8,128)(2,1)S(1)}, u32[]{:S(2)}, u32[]{:S(2)}) collective-permute-start(bf16[48,16,384]{2,1,0:T(8,128)(2,1)S(1)} %get-tuple-element.67.sent), channel_id=1, source_target_pairs={{0,1},{1,0},{2,3},{3,2},{4,5},{5,4},{6,7},{7,6},{8,9},{9,8},{10,11... | collective-permute-start | bytes 1769480 | tf_op jit(solution)/shard_map/ppermute | solution.py:37
  52.9 11.5 %collective-permute-start.13 = (bf16[48,16,384]{2,1,0:T(8,128)(2,1)S(1)}, bf16[48,16,384]{2,1,0:T(8,128)(2,1)S(1)}, u32[]{:S(2)}, u32[]{:S(2)}) collective-permute-start(bf16[48,16,384]{2,1,0:T(8,128)(2,1)S(1)} %get-tuple-element.72.sent), channel_id=1, source_target_pairs={{0,16},{1,17},{2,18},{3,19},{4,20},{5,21},{6,22},{7,23},{8,24},{9,... | collective-permute-start | bytes 1769480 | tf_op jit(solution)/shard_map/ppermute | solution.py:37
  61.7 22.3 %collective-permute-start.22 = (bf16[96,32,128]{2,1,0:T(8,128)(2,1)S(1)}, bf16[96,32,128]{2,1,0:T(8,128)(2,1)S(1)}, u32[]{:S(2)}, u32[]{:S(2)}) collective-permute-start(bf16[96,32,128]{2,1,0:T(8,128)(2,1)S(1)} %shard_map.114.sz), channel_id=1, source_target_pairs={{0,1},{1,0},{2,3},{3,2},{4,5},{5,4},{6,7},{7,6},{8,9},{9,8},{10,11... | collective-permute-start | bytes 2359304 | tf_op jit(solution)/shard_map/ppermute | solution.py:37
  62.3 21.7 %collective-permute-start.20 = (bf16[64,16,384]{2,1,0:T(8,128)(2,1)S(1)}, bf16[64,16,384]{2,1,0:T(8,128)(2,1)S(1)}, u32[]{:S(2)}, u32[]{:S(2)}) collective-permute-start(bf16[64,16,384]{2,1,0:T(8,128)(2,1)S(1)} %shard_map.112.sx), channel_id=1, source_target_pairs={{0,16},{1,17},{2,18},{3,19},{4,20},{5,21},{6,22},{7,23},{8,24},{9,... | collective-permute-start | bytes 2359304 | tf_op jit(solution)/shard_map/ppermute | solution.py:37
  64.4 19.6 %collective-permute-start.21 = (bf16[64,16,384]{2,1,0:T(8,128)(2,1)S(1)}, bf16[64,16,384]{2,1,0:T(8,128)(2,1)S(1)}, u32[]{:S(2)}, u32[]{:S(2)}) collective-permute-start(bf16[64,16,384]{2,1,0:T(8,128)(2,1)S(1)} %shard_map.113.sy), channel_id=1, source_target_pairs={{0,8},{1,9},{2,10},{3,11},{4,12},{5,13},{6,14},{7,15},{8,0},{9,1},... | collective-permute-start | bytes 2359304 | tf_op jit(solution)/shard_map/ppermute | solution.py:37
  64.8 7.7 %collective-permute-start.16 = (bf16[4,32,512]{2,1,0:T(8,128)(2,1)S(1)}, bf16[4,32,512]{2,1,0:T(8,128)(2,1)S(1)}, u32[]{:S(2)}, u32[]{:S(2)}) collective-permute-start(bf16[4,32,512]{2,1,0:T(8,128)(2,1)S(1)} %get-tuple-element.81), channel_id=1, source_target_pairs={{0,48},{1,49},{2,50},{3,51},{4,52},{5,53},{6,54},{7,55},{8,56},{9,... | collective-permute-start | bytes 393224 | tf_op jit(solution)/shard_map/ppermute | solution.py:37
  67.0 7.6 %collective-permute-start.17 = (bf16[4,32,512]{2,1,0:T(8,128)(2,1)S(1)}, bf16[4,32,512]{2,1,0:T(8,128)(2,1)S(1)}, u32[]{:S(2)}, u32[]{:S(2)}) collective-permute-start(bf16[4,32,512]{2,1,0:T(8,128)(2,1)S(1)} %get-tuple-element.82), channel_id=1, source_target_pairs={{0,136},{1,137},{2,138},{3,139},{4,140},{5,141},{6,142},{7,143},{8... | collective-permute-start | bytes 393224 | tf_op jit(solution)/shard_map/ppermute | solution.py:37
  74.7 5.6 %collective-permute-start.18 = (bf16[2,32,512]{2,1,0:T(8,128)(2,1)S(1)}, bf16[2,32,512]{2,1,0:T(8,128)(2,1)S(1)}, u32[]{:S(2)}, u32[]{:S(2)}) collective-permute-start(bf16[2,32,512]{2,1,0:T(8,128)(2,1)S(1)} %get-tuple-element.85), channel_id=1, source_target_pairs={{0,136},{1,137},{2,138},{3,139},{4,140},{5,141},{6,142},{7,143},{8... | collective-permute-start | bytes 196616 | tf_op jit(solution)/shard_map/ppermute | solution.py:37
  76.9 5.5 %collective-permute-start.19 = (bf16[2,32,512]{2,1,0:T(8,128)(2,1)S(1)}, bf16[2,32,512]{2,1,0:T(8,128)(2,1)S(1)}, u32[]{:S(2)}, u32[]{:S(2)}) collective-permute-start(bf16[2,32,512]{2,1,0:T(8,128)(2,1)S(1)} %get-tuple-element.86), channel_id=1, source_target_pairs={{0,48},{1,49},{2,50},{3,51},{4,52},{5,53},{6,54},{7,55},{8,56},{9,... | collective-permute-start | bytes 196616 | tf_op jit(solution)/shard_map/ppermute | solution.py:37
  82.5 7.0 %collective-permute-start.23 = (bf16[2,32,512]{2,1,0:T(8,128)(2,1)S(1)}, bf16[2,32,512]{2,1,0:T(8,128)(2,1)S(1)}, u32[]{:S(2)}, u32[]{:S(2)}) collective-permute-start(bf16[2,32,512]{2,1,0:T(8,128)(2,1)S(1)} %get-tuple-element.93), channel_id=1, source_target_pairs={{0,2},{1,3},{2,0},{3,1},{4,6},{5,7},{6,4},{7,5},{8,10},{9,11},{10,... | collective-permute-start | bytes 196616 | tf_op jit(solution)/shard_map/ppermute | solution.py:37
  89.5 5.0 %collective-permute-start.24 = (f32[2,256,512]{2,1,0:T(8,128)S(1)}, f32[2,256,512]{2,1,0:T(8,128)S(1)}, u32[]{:S(2)}, u32[]{:S(2)}) collective-permute-start(f32[2,256,512]{2,1,0:T(8,128)S(1)} %get-tuple-element.96), channel_id=1, source_target_pairs={{0,64},{1,65},{2,66},{3,67},{4,68},{5,69},{6,70},{7,71},{8,72},{9,... | collective-permute-start | bytes 3145736 | tf_op jit(solution)/shard_map/ppermute | solution.py:37
  89.6 8.0 %collective-permute-start.25 = (bf16[32,512]{1,0:T(8,128)(2,1)S(1)}, bf16[32,512]{1,0:T(8,128)(2,1)S(1)}, u32[]{:S(2)}, u32[]{:S(2)}) collective-permute-start(bf16[32,512]{1,0:T(8,128)(2,1)S(1)} %get-tuple-element.97), channel_id=1, source_target_pairs={{0,6},{1,7},{2,4},{3,5},{4,2},{5,3},{6,0},{7,1},{8,14},{9,15},{10,... | collective-permute-start | bytes 98312 | tf_op jit(solution)/shard_map/ppermute | solution.py:37

commit v5 on v4

--- a/solution.py
+++ b/solution.py
@@ -106,15 +106,25 @@
     )(*args)
 
 
+def load_half(tokens, column, to, sems, at):
+    half = tokens.shape[1] // 2
+    pieces = [(i, m, h) for i in range(2) for m in range(2) for h in range(2)]
+    return [
+        pltpu.make_async_copy(
+            tokens.at[m, pl.ds(half * h, half), pl.ds(column + 4096 * i, 2048)],
+            to[i].at[m, pl.ds(half * h, half)],
+            sems.at[at + n],
+        )
+        for n, (i, m, h) in enumerate(pieces)
+    ]
+
+
 def first_kernel(me, tokens, master, moment, second, gradient, r0, r1, weight, out_master, out_moment, out_second, rows, sems):
     far = pl.multiple_of(2048 * (1 - me[3]), 2048)
     loads = [
         pltpu.make_async_copy(ref, rows.at[i], sems.at[i]) for i, ref in enumerate((master, moment, second, gradient))
     ]
-    copies = [
-        pltpu.make_async_copy(tokens.at[:, :, pl.ds(far + 4096 * i, 2048)], ref, sems.at[4 + i])
-        for i, ref in enumerate((r0, r1))
-    ]
+    copies = load_half(tokens, far, (r0, r1), sems, 4)
     for copy in loads + copies:
         copy.start()
     for copy in loads:
@@ -141,59 +151,60 @@
         in_specs=[SMEM] + [HBM] * 5,
         out_specs=[VMEM] * 6,
         out_shape=[half, half, jax.ShapeDtypeStruct(master.shape, BF16), rows, rows, rows],
-        scratch_shapes=[pltpu.VMEM((4, *master.shape), F32), pltpu.SemaphoreType.DMA((6,))],
+        scratch_shapes=[pltpu.VMEM((4, *master.shape), F32), pltpu.SemaphoreType.DMA((12,))],
         compiler_params=PARAMS,
         interpret=INTERPRET,
     )(me, tokens, master, moment, second, gradient)
 
 
-def terms_kernel(me, tokens, r0, r1, cot, cotr, sx, sy, sz, kx, ky, kz, own, sems):
+def terms_kernel(part, me, tokens, other, cot, cotr, *refs):
+    sx, sy, sz, kx, ky, kz, own, sems = refs[-8:]
     mx, my, mz, c = me[0], me[1], me[2], me[3]
     mine = pl.multiple_of(2048 * c, 2048)
     loads = [
-        pltpu.make_async_copy(tokens.at[:, :, pl.ds(mine + 4096 * (t // 4) + 512 * (t % 4), 512)], own.at[t], sems.at[t])
-        for t in range(8)
+        pltpu.make_async_copy(tokens.at[:, :, pl.ds(mine + 4096 * part + 512 * x, 512)], own.at[x], sems.at[x])
+        for x in range(4)
     ]
     for load in loads:
         load.start()
     flat = cot.shape[0] * cot.shape[1]
     ours, theirs = cot[...].reshape(flat, 512), cotr[...].reshape(flat, 512)
     xs = [label4(x, mx, c) for x in range(4)]
-    ys = [label4(y, my, c) for y in range(4)]
+    ys = [label4(2 * part + y, my, c) for y in range(2)]
     zs = [label8(z, mz, c) for z in range(8)]
 
     def product(a, b):
         return lax.dot_general(a.reshape(flat, 512), b, (((0,), (0,)), ((), ())), preferred_element_type=F32)
 
-    for t in range(8):
-        other = (r0, r1)[t // 4][:, :, 512 * (t % 4) : 512 * (t % 4) + 512]
-        acc = product(other, theirs)
+    for t in range(4):
+        acc = product(other[:, :, 512 * t : 512 * t + 512], theirs)
         loads[t].wait()
         acc += product(own[t], ours)
         for j in range(16):
-            x, y, z = xs[t % 4], ys[2 * (t // 4) + j // 8], zs[j % 8]
+            x, y, z = xs[t], ys[j // 8], zs[j % 8]
             far = x[1] * 8 + y[1] * 4 + z[1]
             axes = (x[0], y[0], z[0])
             block = acc[32 * j : 32 * j + 32]
             for stream, (send, keep) in enumerate(((sx, kx), (sy, ky), (sz, kz))):
                 first_, second_, third_ = (axes[axis] for axis in AXES[stream])
                 at = second_ * 32 + third_ * 16 + far
-                part = cut(stream, block)
-                send[jnp.where(first_ == 1, at, 64)] = part.astype(BF16)
-                keep[jnp.where(first_ == 1, 64, at)] = part
-
-
-def all_terms(me, tokens, r0, r1, cot, cotr):
+                piece = cut(stream, block)
+                send[jnp.where(first_ == 1, at, 64)] = piece.astype(BF16)
+                keep[jnp.where(first_ == 1, 64, at)] = piece
+
+
+def terms(part, me, tokens, other, cot, cotr, held=()):
     return pl.pallas_call(
-        terms_kernel,
-        in_specs=[SMEM, HBM] + [VMEM] * 4,
+        functools.partial(terms_kernel, part),
+        in_specs=[SMEM, HBM] + [VMEM] * (3 + len(held)),
         out_specs=[VMEM] * 6,
         out_shape=[jax.ShapeDtypeStruct(*message(65, i)) for i in range(3)]
         + [jax.ShapeDtypeStruct((65, *s), F32) for s in STREAMS],
-        scratch_shapes=[pltpu.VMEM((8, *tokens.shape[:2], 512), BF16), pltpu.SemaphoreType.DMA((8,))],
+        scratch_shapes=[pltpu.VMEM((4, *tokens.shape[:2], 512), BF16), pltpu.SemaphoreType.DMA((4,))],
+        input_output_aliases={5 + i: i for i in range(len(held))},
         compiler_params=PARAMS,
         interpret=INTERPRET,
-    )(me, tokens, r0, r1, cot, cotr)
+    )(me, tokens, other, cot, cotr, *held)
 
 
 def cut(stream, block):
@@ -271,9 +282,7 @@
 
 def other_kernel(me, tokens, r0, r1, sx, sy, sz, gx, gy, gz, out, w, own, sems):
     mine = pl.multiple_of(2048 * me[3], 2048)
-    loads = [
-        pltpu.make_async_copy(tokens.at[:, :, pl.ds(mine + 4096 * i, 2048)], own.at[i], sems.at[i]) for i in range(2)
-    ]
+    loads = load_half(tokens, mine, (own.at[0], own.at[1]), sems, 0)
     for load in loads:
         load.start()
     assemble(me, sx, sy, sz, gx, gy, gz, w)
@@ -285,14 +294,15 @@
         load.wait()
 
 
-def mine_kernel(own, w, other, out):
+def mine_kernel(own, w, out):
     for m in range(out.shape[0]):
-        total = (
-            other[m]
-            + jnp.dot(own[0, m], w[0:2048], preferred_element_type=F32)
-            + jnp.dot(own[1, m], w[2048:4096], preferred_element_type=F32)
+        out[m] = jnp.dot(own[0, m], w[0:2048], preferred_element_type=F32) + jnp.dot(
+            own[1, m], w[2048:4096], preferred_element_type=F32
         )
-        out[m] = total.astype(BF16)
+
+
+def add_kernel(mine, other, out):
+    out[...] = (mine[...] + other[...]).astype(BF16)
 
 
 def other_values(me, tokens, r0, r1, messages):
@@ -305,7 +315,7 @@
             jax.ShapeDtypeStruct((4096, 512), BF16),
             jax.ShapeDtypeStruct((2, *r0.shape), BF16),
         ],
-        scratch_shapes=[pltpu.SemaphoreType.DMA((2,))],
+        scratch_shapes=[pltpu.SemaphoreType.DMA((8,))],
         compiler_params=PARAMS,
         interpret=INTERPRET,
     )(me, tokens, r0, r1, *messages)
@@ -313,6 +323,10 @@
 
 def after(value, *others):
     return lax.optimization_barrier((value, *others))[0]
+
+
+def joined(a, b, other):
+    return jnp.concatenate(lax.optimization_barrier((a, b, other))[:2])
 
 
 def body(tokens, cotangent, master, moment, second, gradient):
@@ -323,16 +337,16 @@
         pltpu.with_memory_space_constraint(a, pltpu.HBM) for a in (tokens, master, moment, second, gradient)
     )
     r0, r1, weight, new_master, new_moment, new_second = first(me, tokens, master, moment, second, gradient)
-    r0, r1, cotr = swap(r0), swap(r1), swap(cotangent)
+    cotr, r0, r1 = swap(cotangent), swap(r0), swap(r1)
     line = jnp.stack([weight, far_step(weight, 2, True)])
-    line = jnp.concatenate([line, far_step(line, 2, False)])
-    terms = all_terms(me, tokens, r0, r1, cotangent, cotr)
-    send, keep = terms[:3], terms[3:]
-
+    held = terms(0, me, tokens, r0, cotangent, cotr)
+    line = joined(line, far_step(line, 2, False), held[0])
+    far = far_step(line, 1, False)
+    held = terms(1, me, tokens, r1, cotangent, cotr, held)
+    send, keep = held[:3], held[3:]
+    plane = joined(line, far, send[0])
+    plane = jnp.concatenate([plane, far_step(plane, 0, False)])
     got = [near(send[i], AXES[i][0]) for i in range(3)]
-    line = after(line, send[0])
-    plane = jnp.concatenate([line, far_step(line, 1, False)])
-    plane = jnp.concatenate([plane, far_step(plane, 0, False)])
 
     *got, plane = lax.optimization_barrier((*got, plane))
     new = [
@@ -357,8 +371,8 @@
 
     block = (32, 512)
     s0, s1, k0, k1 = call(far_kernel, [((4, *block), BF16)] * 2 + [((4, *block), F32)] * 2, *got, *keep)
+    g0, g1 = far_step(s0, 0, False), far_step(s1, 1, False)
     half = [call(fourth_kernel, [message(64, i)], got[i], send[i])[0] for i in range(3)]
-    g0, g1 = far_step(s0, 0, False), far_step(s1, 1, False)
     rest = [near(half[i], AXES[i][0]) for i in range(3)]
     s0, s1, kept = call(across_kernel, [((2, *block), BF16)] * 2 + [((4, *block), F32)], g0, g1, k0, k1)
     g0, g1 = far_step(s0, 1, False), far_step(s1, 0, False)
@@ -368,8 +382,10 @@
     other, w, own = other_values(after(me, kept), tokens, r0, r1, [*half, *rest])
     s, kept = call(last_kernel, [(block, BF16), (block, F32)], got, after(kept, w))
     got = far_step(s, 2, True)
-    (values,) = call(mine_kernel, [((*r0.shape[:2], 512), BF16)], own, w, swap(after(other, kept)))
-    (weight_grad,) = call(sum_kernel, [(block, F32)], got, after(kept, values))
+    other = swap(after(other, kept))
+    (mine,) = call(mine_kernel, [((*r0.shape[:2], 512), F32)], own, after(w, kept))
+    (weight_grad,) = call(sum_kernel, [(block, F32)], got, after(kept, mine))
+    (values,) = call(add_kernel, [((*r0.shape[:2], 512), BF16)], mine, other)
     return (new_master, new_moment, new_second, values, weight_grad)
 
 

time: 99.5 us -> 101 us (1.015)
  starting transfers between devices: 36.8 us -> 32.8 us
  waiting for transfers between devices: 38.3 us -> 42.3 us
  Pallas kernels: 22.1 us -> 23.9 us
    ppermute x26, waiting for transfers between devices: 38.3 us -> 42.3 us  [permute(): return lax.ppermute(value, ALL, pairs)]
    ppermute x26, starting transfers between devices: 36.8 us -> 32.8 us  [permute(): return lax.ppermute(value, ALL, pairs)]
    pallas_call x1 -> x2, Pallas kernels: 8.1 us -> 9.83 us  [terms(): pl.pallas_call(functools.partial(terms_kernel, part), in_specs=[SMEM, HBM...]
    pallas_call x15 -> x16, Pallas kernels: 4.92 us -> 4.97 us  [call(): pl.pallas_call(kernel, out_shape=[jax.ShapeDtypeStruct(*o) for o in outs]...]
  transfers between devices with their start and end apart: 26 -> 26, of which waited for: 10 -> 12; matrix products, arithmetic and copies ran while one was open for 0% -> 0% of each run, Pallas kernels for 18% -> 14%
where the time goes in v5:
time: 101 us; the launch traced here: 100 us
  waiting for transfers between devices  42.3 us (42%)
  starting transfers between devices  32.8 us (32%)
  Pallas kernels  23.9 us (24%)
    ppermute x26, waiting for transfers between devices, permute(): return lax.ppermute(value, ALL, pairs)  42.3 us
    ppermute x26, starting transfers between devices, permute(): return lax.ppermute(value, ALL, pairs)  32.8 us
    pallas_call x2, Pallas kernels, terms(): pl.pallas_call(functools.partial(terms_kernel, part), in_specs=[SMEM, HBM...  9.83 us
    pallas_call x1, Pallas kernels, other_values(): pl.pallas_call(other_kernel, in_specs=[SMEM, HBM] + [VMEM] * 8, out_specs...  5.45 us
    pallas_call x16, Pallas kernels, call(): pl.pallas_call(kernel, out_shape=[jax.ShapeDtypeStruct(*o) for o in outs]...  4.97 us
    pallas_call x1, Pallas kernels, first(): pl.pallas_call(first_kernel, in_specs=[SMEM] + [HBM] * 5, out_specs=[VMEM...  3.62 us
  transfers between devices with their start and end apart: 26, of which 12 were waited for; matrix products, arithmetic and copies ran while one was open for 0% of the time, Pallas kernels for 14%

profile of v5, /device:TPU:0, one launch (start us, length us, event | category | flops | bytes accessed | tf_op | source)
XLA Modules:
  0.0 100.1 jit_solution(9778885008607400088)
XLA Ops:
  0.8 3.6 %shard_map.101 = (bf16[2,256,2048]{2,1,0:T(8,128)(2,1)S(1)}, bf16[2,256,2048]{2,1,0:T(8,128)(2,1)S(1)}, bf16[32,512]{1,0:T(8,128)(2,1)S(1)}, f32[32,512]{1,0:T(8...) custom-call(s32[4]{0:T(128)S(1)} %pad_add_fusion.me, bf16[2,256,8192]{2,1,0:T(8,128)(2,1)} %tokens.7, f32[32,512]{1,0:T(8,128)} %master.1, ...), custom_call_target="tpu_custom_call" | custom-call | tf_op jit(solution)/shard_map/pallas_call | solution.py:149
  4.5 0.5 collective-permute-start
  5.0 0.1 collective-permute-start.1
  5.1 4.6 %collective-permute-start.6 = (bf16[32,512]{1,0:T(8,128)(2,1)S(1)}, bf16[32,512]{1,0:T(8,128)(2,1)S(1)}, u32[]{:S(2)}, u32[]{:S(2)}) collective-permute-start(bf16[32,512]{1,0:T(8,128)(2,1)S(1)} %get-tuple-element.76), channel_id=1, source_target_pairs={{0,6},{1,7},{2,4},{3,5},{4,2},{5,3},{6,0},{7,1},{8,14},{9,15},{10,... | collective-permute-start | bytes 98312 | tf_op jit(solution)/shard_map/ppermute | solution.py:37
  9.7 1.9 %collective-permute-done.6 = bf16[32,512]{1,0:T(8,128)(2,1)S(1)} collective-permute-done((bf16[32,512]{1,0:T(8,128)(2,1)S(1)}, bf16[32,512]{1,0:T(8,128)(2,1)S(1)}, u32[]{:S(2)}, u32[]{:S(2)}) %collective-permute-start.6) | collective-permute-done | bytes 32800 | tf_op jit(solution)/shard_map/ppermute | solution.py:37
  11.6 1.5 %collective-permute-start.7 = (bf16[2,32,512]{2,1,0:T(8,128)(2,1)S(1)}, bf16[2,32,512]{2,1,0:T(8,128)(2,1)S(1)}, u32[]{:S(2)}, u32[]{:S(2)}) collective-permute-start(bf16[2,32,512]{2,1,0:T(8,128)(2,1)S(1)} %pad_maximum_fusion.2), channel_id=1, source_target_pairs={{0,2},{1,3},{2,0},{3,1},{4,6},{5,7},{6,4},{7,5},{8,10},{9,11},{10,... | collective-permute-start | bytes 196616 | tf_op jit(solution)/shard_map/ppermute | solution.py:37
  13.1 4.9 %shard_map.102 = (bf16[65,16,384]{2,1,0:T(8,128)(2,1)S(1)}, bf16[65,16,384]{2,1,0:T(8,128)(2,1)S(1)}, bf16[97,32,128]{2,1,0:T(8,128)(2,1)S(1)}, f32[65,16,384]{2...) custom-call(s32[4]{0:T(128)S(1)} %pad_add_fusion.me, bf16[2,256,8192]{2,1,0:T(8,128)(2,1)} %tokens.7, ...), custom_call_target="tpu_custom_call" | custom-call | tf_op jit(solution)/shard_map/pallas_call | solution.py:197
  18.0 4.9 %shard_map.103 = (bf16[65,16,384]{2,1,0:T(8,128)(2,1)S(1)}, bf16[65,16,384]{2,1,0:T(8,128)(2,1)S(1)}, bf16[97,32,128]{2,1,0:T(8,128)(2,1)S(1)}, f32[65,16,384]{2...) custom-call(s32[4]{0:T(128)S(1)} %pad_add_fusion.me, ...), custom_call_target="tpu_custom_call", output_to_operand_aliasing={{0}: (5, {}), {1}: (6, {}), {2}: (7, {}), {3}: (8, {}), {4}... | custom-call | tf_op jit(solution)/shard_map/pallas_call | solution.py:197
  23.0 1.6 %collective-permute-start.5 = (bf16[97,32,128]{2,1,0:T(8,128)(2,1)S(1)}, bf16[97,32,128]{2,1,0:T(8,128)(2,1)S(1)}, u32[]{:S(2)}, u32[]{:S(2)}) collective-permute-start(bf16[97,32,128]{2,1,0:T(8,128)(2,1)S(1)} %get-tuple-element.75), channel_id=1, source_target_pairs={{0,1},{1,0},{2,3},{3,2},{4,5},{5,4},{6,7},{7,6},{8,9},{9,8},{10,11... | collective-permute-start | bytes 2383880 | tf_op jit(solution)/shard_map/ppermute | solution.py:37
  24.6 1.6 %collective-permute-start.4 = (bf16[65,16,384]{2,1,0:T(8,128)(2,1)S(1)}, bf16[65,16,384]{2,1,0:T(8,128)(2,1)S(1)}, u32[]{:S(2)}, u32[]{:S(2)}) collective-permute-start(bf16[65,16,384]{2,1,0:T(8,128)(2,1)S(1)} %get-tuple-element.74), channel_id=1, source_target_pairs={{0,8},{1,9},{2,10},{3,11},{4,12},{5,13},{6,14},{7,15},{8,0},{9,1},... | collective-permute-start | bytes 2396168 | tf_op jit(solution)/shard_map/ppermute | solution.py:37
  26.2 1.5 %collective-permute-start.3 = (bf16[65,16,384]{2,1,0:T(8,128)(2,1)S(1)}, bf16[65,16,384]{2,1,0:T(8,128)(2,1)S(1)}, u32[]{:S(2)}, u32[]{:S(2)}) collective-permute-start(bf16[65,16,384]{2,1,0:T(8,128)(2,1)S(1)} %get-tuple-element.73), channel_id=1, source_target_pairs={{0,16},{1,17},{2,18},{3,19},{4,20},{5,21},{6,22},{7,23},{8,24},{9,... | collective-permute-start | bytes 2396168 | tf_op jit(solution)/shard_map/ppermute | solution.py:37
  27.7 2.3 %collective-permute-start.8 = (bf16[4,32,512]{2,1,0:T(8,128)(2,1)S(1)}, bf16[4,32,512]{2,1,0:T(8,128)(2,1)S(1)}, u32[]{:S(2)}, u32[]{:S(2)}) collective-permute-start(bf16[4,32,512]{2,1,0:T(8,128)(2,1)S(1)} %constant_dynamic-update-slice_fusion), channel_id=1, source_target_pairs={{0,136},{1,137},{2,138},{3,139},{4,140},{5,141},{6,142},{7,143},{8... | collective-permute-start | bytes 393224 | tf_op jit(solution)/shard_map/ppermute | solution.py:37
  30.0 5.5 %collective-permute-done.8 = bf16[4,32,512]{2,1,0:T(8,128)(2,1)S(1)} collective-permute-done((bf16[4,32,512]{2,1,0:T(8,128)(2,1)S(1)}, bf16[4,32,512]{2,1,0:T(8,128)(2,1)S(1)}, u32[]{:S(2)}, u32[]{:S(2)}) %collective-permute-start.8) | collective-permute-done | bytes 131104 | tf_op jit(solution)/shard_map/ppermute | solution.py:37
  35.5 2.2 %collective-permute-start.9 = (bf16[8,32,512]{2,1,0:T(8,128)(2,1)S(1)}, bf16[8,32,512]{2,1,0:T(8,128)(2,1)S(1)}, u32[]{:S(2)}, u32[]{:S(2)}) collective-permute-start(bf16[8,32,512]{2,1,0:T(8,128)(2,1)S(1)} %pad_maximum_fusion.1), channel_id=1, source_target_pairs={{0,48},{1,49},{2,50},{3,51},{4,52},{5,53},{6,54},{7,55},{8,56},{9,... | collective-permute-start | bytes 786440 | tf_op jit(solution)/shard_map/ppermute | solution.py:37
  37.7 6.6 %collective-permute-done.9 = bf16[8,32,512]{2,1,0:T(8,128)(2,1)S(1)} collective-permute-done((bf16[8,32,512]{2,1,0:T(8,128)(2,1)S(1)}, bf16[8,32,512]{2,1,0:T(8,128)(2,1)S(1)}, u32[]{:S(2)}, u32[]{:S(2)}) %collective-permute-start.9) | collective-permute-done | bytes 262176 | tf_op jit(solution)/shard_map/ppermute | solution.py:37
  44.3 0.1 shard_map.108
  44.5 0.4 collective-permute-start.14
  44.8 0.1 shard_map.104
  45.0 0.4 collective-permute-start.10
  45.4 0.2 shard_map.106
  45.6 0.1 collective-permute-start.12
  45.7 8.8 %collective-permute-done.14.got = bf16[72,32,128]{2,1,0:T(8,128)(2,1)S(1)} collective-permute-done((bf16[72,32,128]{2,1,0:T(8,128)(2,1)S(1)}, bf16[72,32,128]{2,1,0:T(8,128)(2,1)S(1)}, u32[]{:S(2)}, u32[]{:S(2)}) %collective-permute-start.14) | collective-permute-done | bytes 589856 | tf_op jit(solution)/shard_map/ppermute | solution.py:37
  54.5 0.2 collective-permute-start.15
  54.7 0.4 collective-permute-done.10.got
  55.1 0.1 shard_map.105
  55.2 0.1 collective-permute-start.11
  55.3 0.2 collective-permute-done.12.got
  55.5 0.1 shard_map.107
  55.6 1.8 %collective-permute-start.13 = (bf16[48,16,384]{2,1,0:T(8,128)(2,1)S(1)}, bf16[48,16,384]{2,1,0:T(8,128)(2,1)S(1)}, u32[]{:S(2)}, u32[]{:S(2)}) collective-permute-start(bf16[48,16,384]{2,1,0:T(8,128)(2,1)S(1)} %get-tuple-element.91.sent), channel_id=1, source_target_pairs={{0,16},{1,17},{2,18},{3,19},{4,20},{5,21},{6,22},{7,23},{8,24},{9,... | collective-permute-start | bytes 1769480 | tf_op jit(solution)/shard_map/ppermute | solution.py:37
  57.5 7.0 %collective-permute-done.15.gz.got = bf16[72,32,128]{2,1,0:T(8,128)(2,1)S(1)} collective-permute-done((bf16[72,32,128]{2,1,0:T(8,128)(2,1)S(1)}, bf16[72,32,128]{2,1,0:T(8,128)(2,1)S(1)}, u32[]{:S(2)}, u32[]{:S(2)}) %collective-permute-start.15) | collective-permute-done | bytes 589856 | tf_op jit(solution)/shard_map/ppermute | solution.py:37
  64.6 0.6 collective-permute-done.11.gx.got
  65.3 1.8 %collective-permute-start.20 = (bf16[64,16,384]{2,1,0:T(8,128)(2,1)S(1)}, bf16[64,16,384]{2,1,0:T(8,128)(2,1)S(1)}, u32[]{:S(2)}, u32[]{:S(2)}) collective-permute-start(bf16[64,16,384]{2,1,0:T(8,128)(2,1)S(1)} %shard_map.113.sx), channel_id=1, source_target_pairs={{0,16},{1,17},{2,18},{3,19},{4,20},{5,21},{6,22},{7,23},{8,24},{9,... | collective-permute-start | bytes 2359304 | tf_op jit(solution)/shard_map/ppermute | solution.py:37
  67.2 0.5 collective-permute-start.21
  67.7 0.1 shard_map.110
  67.8 2.6 %collective-permute-start.16 = (bf16[4,32,512]{2,1,0:T(8,128)(2,1)S(1)}, bf16[4,32,512]{2,1,0:T(8,128)(2,1)S(1)}, u32[]{:S(2)}, u32[]{:S(2)}) collective-permute-start(bf16[4,32,512]{2,1,0:T(8,128)(2,1)S(1)} %get-tuple-element.100), channel_id=1, source_target_pairs={{0,48},{1,49},{2,50},{3,51},{4,52},{5,53},{6,54},{7,55},{8,56},{9,... | collective-permute-start | bytes 393224 | tf_op jit(solution)/shard_map/ppermute | solution.py:37
  70.4 1.1 %collective-permute-start.17 = (bf16[4,32,512]{2,1,0:T(8,128)(2,1)S(1)}, bf16[4,32,512]{2,1,0:T(8,128)(2,1)S(1)}, u32[]{:S(2)}, u32[]{:S(2)}) collective-permute-start(bf16[4,32,512]{2,1,0:T(8,128)(2,1)S(1)} %get-tuple-element.101), channel_id=1, source_target_pairs={{0,136},{1,137},{2,138},{3,139},{4,140},{5,141},{6,142},{7,143},{8... | collective-permute-start | bytes 393224 | tf_op jit(solution)/shard_map/ppermute | solution.py:37
  71.4 4.1 %collective-permute-done.16.g0 = bf16[4,32,512]{2,1,0:T(8,128)(2,1)S(1)} collective-permute-done((bf16[4,32,512]{2,1,0:T(8,128)(2,1)S(1)}, bf16[4,32,512]{2,1,0:T(8,128)(2,1)S(1)}, u32[]{:S(2)}, u32[]{:S(2)}) %collective-permute-start.16) | collective-permute-done | bytes 131104 | tf_op jit(solution)/shard_map/ppermute | solution.py:37
  75.5 2.5 %collective-permute-done.17.g1 = bf16[4,32,512]{2,1,0:T(8,128)(2,1)S(1)} collective-permute-done((bf16[4,32,512]{2,1,0:T(8,128)(2,1)S(1)}, bf16[4,32,512]{2,1,0:T(8,128)(2,1)S(1)}, u32[]{:S(2)}, u32[]{:S(2)}) %collective-permute-start.17) | collective-permute-done | bytes 131104 | tf_op jit(solution)/shard_map/ppermute | solution.py:37
  78.1 1.1 %collective-permute-start.18 = (bf16[2,32,512]{2,1,0:T(8,128)(2,1)S(1)}, bf16[2,32,512]{2,1,0:T(8,128)(2,1)S(1)}, u32[]{:S(2)}, u32[]{:S(2)}) collective-permute-start(bf16[2,32,512]{2,1,0:T(8,128)(2,1)S(1)} %get-tuple-element.104), channel_id=1, source_target_pairs={{0,136},{1,137},{2,138},{3,139},{4,140},{5,141},{6,142},{7,143},{8... | collective-permute-start | bytes 196616 | tf_op jit(solution)/shard_map/ppermute | solution.py:37
  79.2 0.6 collective-permute-start.19
  79.8 3.8 %collective-permute-done.18.g0 = bf16[2,32,512]{2,1,0:T(8,128)(2,1)S(1)} collective-permute-done((bf16[2,32,512]{2,1,0:T(8,128)(2,1)S(1)}, bf16[2,32,512]{2,1,0:T(8,128)(2,1)S(1)}, u32[]{:S(2)}, u32[]{:S(2)}) %collective-permute-start.18) | collective-permute-done | bytes 65568 | tf_op jit(solution)/shard_map/ppermute | solution.py:37
  83.6 1.1 %collective-permute-done.19.g1 = bf16[2,32,512]{2,1,0:T(8,128)(2,1)S(1)} collective-permute-done((bf16[2,32,512]{2,1,0:T(8,128)(2,1)S(1)}, bf16[2,32,512]{2,1,0:T(8,128)(2,1)S(1)}, u32[]{:S(2)}, u32[]{:S(2)}) %collective-permute-start.19) | collective-permute-done | bytes 65568 | tf_op jit(solution)/shard_map/ppermute | solution.py:37
  84.7 1.7 %collective-permute-start.23 = (bf16[2,32,512]{2,1,0:T(8,128)(2,1)S(1)}, bf16[2,32,512]{2,1,0:T(8,128)(2,1)S(1)}, u32[]{:S(2)}, u32[]{:S(2)}) collective-permute-start(bf16[2,32,512]{2,1,0:T(8,128)(2,1)S(1)} %get-tuple-element.111), channel_id=1, source_target_pairs={{0,2},{1,3},{2,0},{3,1},{4,6},{5,7},{6,4},{7,5},{8,10},{9,11},{10,... | collective-permute-start | bytes 196616 | tf_op jit(solution)/shard_map/ppermute | solution.py:37
  86.4 5.4 %shard_map.116 = (f32[2,256,512]{2,1,0:T(8,128)S(1)}, bf16[4096,512]{1,0:T(8,128)(2,1)S(1)}, bf16[2,2,256,2048]{3,2,1,0:T(8,128)(2,1)S(1)}) custom-call(s32[4]{0:T(128)S(1)} %pad_add_fusion.me, bf16[2,256,8192]{2,1,0:T(8,128)(2,1)} %tokens.7, bf16[2,256,2048]{2,1,0:T(8,128)(2,1)S(1)} %collective-permute-done.2.other.r0, ...), custom_call_target="tpu_custom_call" | custom-call | tf_op jit(solution)/shard_map/pallas_call | solution.py:309
  92.0 4.2 %collective-permute-start.25 = (bf16[32,512]{1,0:T(8,128)(2,1)S(1)}, bf16[32,512]{1,0:T(8,128)(2,1)S(1)}, u32[]{:S(2)}, u32[]{:S(2)}) collective-permute-start(bf16[32,512]{1,0:T(8,128)(2,1)S(1)} %get-tuple-element.117), channel_id=1, source_target_pairs={{0,6},{1,7},{2,4},{3,5},{4,2},{5,3},{6,0},{7,1},{8,14},{9,15},{10,... | collective-permute-start | bytes 98312 | tf_op jit(solution)/shard_map/ppermute | solution.py:37
  96.2 2.3 %shard_map.118.mine = f32[2,256,512]{2,1,0:T(8,128)S(1)} custom-call(bf16[2,2,256,2048]{3,2,1,0:T(8,128)(2,1)S(1)} %get-tuple-element.109.own, bf16[4096,512]{1,0:T(8,128)(2,1)S(1)} %get-tuple-element.114.w), custom_call_target="tpu_custom_call" | custom-call | tf_op jit(solution)/shard_map/pallas_call | solution.py:98
  98.5 0.6 shard_map.120
  99.2 0.9 shard_map.119
  (32 shorter events, 0.8 us)
Async XLA Ops:
  0.8 4.2 %copy-start = (bf16[2,256,512]{2,1,0:T(8,128)(2,1)S(1)}, bf16[2,256,512]{2,1,0:T(8,128)(2,1)}, u32[]{:S(2)}) copy-start(bf16[2,256,512]{2,1,0:T(8,128)(2,1)} %cot.3) | copy-start | bytes 1572868
  4.4 8.7 %collective-permute-start.2 = (bf16[2,256,2048]{2,1,0:T(8,128)(2,1)S(1)}, bf16[2,256,2048]{2,1,0:T(8,128)(2,1)S(1)}, u32[]{:S(2)}, u32[]{:S(2)}) collective-permute-start(bf16[2,256,2048]{2,1,0:T(8,128)(2,1)S(1)} %get-tuple-element.66), channel_id=1, source_target_pairs={{0,64},{1,65},{2,66},{3,67},{4,68},{5,69},{6,70},{7,71},{8,72},{9,... | collective-permute-start | bytes 6291464 | tf_op jit(solution)/shard_map/ppermute | solution.py:37
  4.5 13.6 %collective-permute-start = (bf16[2,256,2048]{2,1,0:T(8,128)(2,1)S(1)}, bf16[2,256,2048]{2,1,0:T(8,128)(2,1)S(1)}, u32[]{:S(2)}, u32[]{:S(2)}) collective-permute-start(bf16[2,256,2048]{2,1,0:T(8,128)(2,1)S(1)} %get-tuple-element.65), channel_id=1, source_target_pairs={{0,64},{1,65},{2,66},{3,67},{4,68},{5,69},{6,70},{7,71},{8,72},{9,... | collective-permute-start | bytes 6291464 | tf_op jit(solution)/shard_map/ppermute | solution.py:37
  5.0 8.1 %collective-permute-start.1 = (bf16[2,256,512]{2,1,0:T(8,128)(2,1)S(1)}, bf16[2,256,512]{2,1,0:T(8,128)(2,1)S(1)}, u32[]{:S(2)}, u32[]{:S(2)}) collective-permute-start(bf16[2,256,512]{2,1,0:T(8,128)(2,1)S(1)} %copy-done), channel_id=1, source_target_pairs={{0,64},{1,65},{2,66},{3,67},{4,68},{5,69},{6,70},{7,71},{8,72},{9,... | collective-permute-start | bytes 1572872 | tf_op jit(solution)/shard_map/ppermute | solution.py:37
  5.1 6.5 %collective-permute-start.6 = (bf16[32,512]{1,0:T(8,128)(2,1)S(1)}, bf16[32,512]{1,0:T(8,128)(2,1)S(1)}, u32[]{:S(2)}, u32[]{:S(2)}) collective-permute-start(bf16[32,512]{1,0:T(8,128)(2,1)S(1)} %get-tuple-element.76), channel_id=1, source_target_pairs={{0,6},{1,7},{2,4},{3,5},{4,2},{5,3},{6,0},{7,1},{8,14},{9,15},{10,... | collective-permute-start | bytes 98312 | tf_op jit(solution)/shard_map/ppermute | solution.py:37
  11.6 6.5 %collective-permute-start.7 = (bf16[2,32,512]{2,1,0:T(8,128)(2,1)S(1)}, bf16[2,32,512]{2,1,0:T(8,128)(2,1)S(1)}, u32[]{:S(2)}, u32[]{:S(2)}) collective-permute-start(bf16[2,32,512]{2,1,0:T(8,128)(2,1)S(1)} %pad_maximum_fusion.2), channel_id=1, source_target_pairs={{0,2},{1,3},{2,0},{3,1},{4,6},{5,7},{6,4},{7,5},{8,10},{9,11},{10,... | collective-permute-start | bytes 196616 | tf_op jit(solution)/shard_map/ppermute | solution.py:37
  23.0 21.3 %collective-permute-start.5 = (bf16[97,32,128]{2,1,0:T(8,128)(2,1)S(1)}, bf16[97,32,128]{2,1,0:T(8,128)(2,1)S(1)}, u32[]{:S(2)}, u32[]{:S(2)}) collective-permute-start(bf16[97,32,128]{2,1,0:T(8,128)(2,1)S(1)} %get-tuple-element.75), channel_id=1, source_target_pairs={{0,1},{1,0},{2,3},{3,2},{4,5},{5,4},{6,7},{7,6},{8,9},{9,8},{10,11... | collective-permute-start | bytes 2383880 | tf_op jit(solution)/shard_map/ppermute | solution.py:37
  24.6 19.7 %collective-permute-start.4 = (bf16[65,16,384]{2,1,0:T(8,128)(2,1)S(1)}, bf16[65,16,384]{2,1,0:T(8,128)(2,1)S(1)}, u32[]{:S(2)}, u32[]{:S(2)}) collective-permute-start(bf16[65,16,384]{2,1,0:T(8,128)(2,1)S(1)} %get-tuple-element.74), channel_id=1, source_target_pairs={{0,8},{1,9},{2,10},{3,11},{4,12},{5,13},{6,14},{7,15},{8,0},{9,1},... | collective-permute-start | bytes 2396168 | tf_op jit(solution)/shard_map/ppermute | solution.py:37
  26.2 18.1 %collective-permute-start.3 = (bf16[65,16,384]{2,1,0:T(8,128)(2,1)S(1)}, bf16[65,16,384]{2,1,0:T(8,128)(2,1)S(1)}, u32[]{:S(2)}, u32[]{:S(2)}) collective-permute-start(bf16[65,16,384]{2,1,0:T(8,128)(2,1)S(1)} %get-tuple-element.73), channel_id=1, source_target_pairs={{0,16},{1,17},{2,18},{3,19},{4,20},{5,21},{6,22},{7,23},{8,24},{9,... | collective-permute-start | bytes 2396168 | tf_op jit(solution)/shard_map/ppermute | solution.py:37
  27.7 7.7 %collective-permute-start.8 = (bf16[4,32,512]{2,1,0:T(8,128)(2,1)S(1)}, bf16[4,32,512]{2,1,0:T(8,128)(2,1)S(1)}, u32[]{:S(2)}, u32[]{:S(2)}) collective-permute-start(bf16[4,32,512]{2,1,0:T(8,128)(2,1)S(1)} %constant_dynamic-update-slice_fusion), channel_id=1, source_target_pairs={{0,136},{1,137},{2,138},{3,139},{4,140},{5,141},{6,142},{7,143},{8... | collective-permute-start | bytes 393224 | tf_op jit(solution)/shard_map/ppermute | solution.py:37
  35.5 8.8 %collective-permute-start.9 = (bf16[8,32,512]{2,1,0:T(8,128)(2,1)S(1)}, bf16[8,32,512]{2,1,0:T(8,128)(2,1)S(1)}, u32[]{:S(2)}, u32[]{:S(2)}) collective-permute-start(bf16[8,32,512]{2,1,0:T(8,128)(2,1)S(1)} %pad_maximum_fusion.1), channel_id=1, source_target_pairs={{0,48},{1,49},{2,50},{3,51},{4,52},{5,53},{6,54},{7,55},{8,56},{9,... | collective-permute-start | bytes 786440 | tf_op jit(solution)/shard_map/ppermute | solution.py:37
  44.5 10.0 %collective-permute-start.14 = (bf16[72,32,128]{2,1,0:T(8,128)(2,1)S(1)}, bf16[72,32,128]{2,1,0:T(8,128)(2,1)S(1)}, u32[]{:S(2)}, u32[]{:S(2)}) collective-permute-start(bf16[72,32,128]{2,1,0:T(8,128)(2,1)S(1)} %get-tuple-element.94.sent), channel_id=1, source_target_pairs={{0,16},{1,17},{2,18},{3,19},{4,20},{5,21},{6,22},{7,23},{8,24},{9,... | collective-permute-start | bytes 1769480 | tf_op jit(solution)/shard_map/ppermute | solution.py:37
  45.0 10.2 %collective-permute-start.10 = (bf16[48,16,384]{2,1,0:T(8,128)(2,1)S(1)}, bf16[48,16,384]{2,1,0:T(8,128)(2,1)S(1)}, u32[]{:S(2)}, u32[]{:S(2)}) collective-permute-start(bf16[48,16,384]{2,1,0:T(8,128)(2,1)S(1)} %get-tuple-element.84.sent), channel_id=1, source_target_pairs={{0,8},{1,9},{2,10},{3,11},{4,12},{5,13},{6,14},{7,15},{8,0},{9,1},... | collective-permute-start | bytes 1769480 | tf_op jit(solution)/shard_map/ppermute | solution.py:37
  45.6 10.0 %collective-permute-start.12 = (bf16[48,16,384]{2,1,0:T(8,128)(2,1)S(1)}, bf16[48,16,384]{2,1,0:T(8,128)(2,1)S(1)}, u32[]{:S(2)}, u32[]{:S(2)}) collective-permute-start(bf16[48,16,384]{2,1,0:T(8,128)(2,1)S(1)} %get-tuple-element.89.sent), channel_id=1, source_target_pairs={{0,1},{1,0},{2,3},{3,2},{4,5},{5,4},{6,7},{7,6},{8,9},{9,8},{10,11... | collective-permute-start | bytes 1769480 | tf_op jit(solution)/shard_map/ppermute | solution.py:37
  54.5 10.0 %collective-permute-start.15 = (bf16[72,32,128]{2,1,0:T(8,128)(2,1)S(1)}, bf16[72,32,128]{2,1,0:T(8,128)(2,1)S(1)}, u32[]{:S(2)}, u32[]{:S(2)}) collective-permute-start(bf16[72,32,128]{2,1,0:T(8,128)(2,1)S(1)} %get-tuple-element.96.sent), channel_id=1, source_target_pairs={{0,8},{1,9},{2,10},{3,11},{4,12},{5,13},{6,14},{7,15},{8,0},{9,1},... | collective-permute-start | bytes 1769480 | tf_op jit(solution)/shard_map/ppermute | solution.py:37
  55.2 10.0 %collective-permute-start.11 = (bf16[48,16,384]{2,1,0:T(8,128)(2,1)S(1)}, bf16[48,16,384]{2,1,0:T(8,128)(2,1)S(1)}, u32[]{:S(2)}, u32[]{:S(2)}) collective-permute-start(bf16[48,16,384]{2,1,0:T(8,128)(2,1)S(1)} %get-tuple-element.86.sent), channel_id=1, source_target_pairs={{0,1},{1,0},{2,3},{3,2},{4,5},{5,4},{6,7},{7,6},{8,9},{9,8},{10,11... | collective-permute-start | bytes 1769480 | tf_op jit(solution)/shard_map/ppermute | solution.py:37
  55.6 11.5 %collective-permute-start.13 = (bf16[48,16,384]{2,1,0:T(8,128)(2,1)S(1)}, bf16[48,16,384]{2,1,0:T(8,128)(2,1)S(1)}, u32[]{:S(2)}, u32[]{:S(2)}) collective-permute-start(bf16[48,16,384]{2,1,0:T(8,128)(2,1)S(1)} %get-tuple-element.91.sent), channel_id=1, source_target_pairs={{0,16},{1,17},{2,18},{3,19},{4,20},{5,21},{6,22},{7,23},{8,24},{9,... | collective-permute-start | bytes 1769480 | tf_op jit(solution)/shard_map/ppermute | solution.py:37
  64.5 21.9 %collective-permute-start.22 = (bf16[96,32,128]{2,1,0:T(8,128)(2,1)S(1)}, bf16[96,32,128]{2,1,0:T(8,128)(2,1)S(1)}, u32[]{:S(2)}, u32[]{:S(2)}) collective-permute-start(bf16[96,32,128]{2,1,0:T(8,128)(2,1)S(1)} %shard_map.115.sz), channel_id=1, source_target_pairs={{0,1},{1,0},{2,3},{3,2},{4,5},{5,4},{6,7},{7,6},{8,9},{9,8},{10,11... | collective-permute-start | bytes 2359304 | tf_op jit(solution)/shard_map/ppermute | solution.py:37
  65.3 21.1 %collective-permute-start.20 = (bf16[64,16,384]{2,1,0:T(8,128)(2,1)S(1)}, bf16[64,16,384]{2,1,0:T(8,128)(2,1)S(1)}, u32[]{:S(2)}, u32[]{:S(2)}) collective-permute-start(bf16[64,16,384]{2,1,0:T(8,128)(2,1)S(1)} %shard_map.113.sx), channel_id=1, source_target_pairs={{0,16},{1,17},{2,18},{3,19},{4,20},{5,21},{6,22},{7,23},{8,24},{9,... | collective-permute-start | bytes 2359304 | tf_op jit(solution)/shard_map/ppermute | solution.py:37
  67.2 19.2 %collective-permute-start.21 = (bf16[64,16,384]{2,1,0:T(8,128)(2,1)S(1)}, bf16[64,16,384]{2,1,0:T(8,128)(2,1)S(1)}, u32[]{:S(2)}, u32[]{:S(2)}) collective-permute-start(bf16[64,16,384]{2,1,0:T(8,128)(2,1)S(1)} %shard_map.114.sy), channel_id=1, source_target_pairs={{0,8},{1,9},{2,10},{3,11},{4,12},{5,13},{6,14},{7,15},{8,0},{9,1},... | collective-permute-start | bytes 2359304 | tf_op jit(solution)/shard_map/ppermute | solution.py:37
  67.8 7.7 %collective-permute-start.16 = (bf16[4,32,512]{2,1,0:T(8,128)(2,1)S(1)}, bf16[4,32,512]{2,1,0:T(8,128)(2,1)S(1)}, u32[]{:S(2)}, u32[]{:S(2)}) collective-permute-start(bf16[4,32,512]{2,1,0:T(8,128)(2,1)S(1)} %get-tuple-element.100), channel_id=1, source_target_pairs={{0,48},{1,49},{2,50},{3,51},{4,52},{5,53},{6,54},{7,55},{8,56},{9,... | collective-permute-start | bytes 393224 | tf_op jit(solution)/shard_map/ppermute | solution.py:37
  70.4 7.6 %collective-permute-start.17 = (bf16[4,32,512]{2,1,0:T(8,128)(2,1)S(1)}, bf16[4,32,512]{2,1,0:T(8,128)(2,1)S(1)}, u32[]{:S(2)}, u32[]{:S(2)}) collective-permute-start(bf16[4,32,512]{2,1,0:T(8,128)(2,1)S(1)} %get-tuple-element.101), channel_id=1, source_target_pairs={{0,136},{1,137},{2,138},{3,139},{4,140},{5,141},{6,142},{7,143},{8... | collective-permute-start | bytes 393224 | tf_op jit(solution)/shard_map/ppermute | solution.py:37
  78.1 5.6 %collective-permute-start.18 = (bf16[2,32,512]{2,1,0:T(8,128)(2,1)S(1)}, bf16[2,32,512]{2,1,0:T(8,128)(2,1)S(1)}, u32[]{:S(2)}, u32[]{:S(2)}) collective-permute-start(bf16[2,32,512]{2,1,0:T(8,128)(2,1)S(1)} %get-tuple-element.104), channel_id=1, source_target_pairs={{0,136},{1,137},{2,138},{3,139},{4,140},{5,141},{6,142},{7,143},{8... | collective-permute-start | bytes 196616 | tf_op jit(solution)/shard_map/ppermute | solution.py:37
  79.2 5.5 %collective-permute-start.19 = (bf16[2,32,512]{2,1,0:T(8,128)(2,1)S(1)}, bf16[2,32,512]{2,1,0:T(8,128)(2,1)S(1)}, u32[]{:S(2)}, u32[]{:S(2)}) collective-permute-start(bf16[2,32,512]{2,1,0:T(8,128)(2,1)S(1)} %get-tuple-element.105), channel_id=1, source_target_pairs={{0,48},{1,49},{2,50},{3,51},{4,52},{5,53},{6,54},{7,55},{8,56},{9,... | collective-permute-start | bytes 196616 | tf_op jit(solution)/shard_map/ppermute | solution.py:37
  84.7 7.2 %collective-permute-start.23 = (bf16[2,32,512]{2,1,0:T(8,128)(2,1)S(1)}, bf16[2,32,512]{2,1,0:T(8,128)(2,1)S(1)}, u32[]{:S(2)}, u32[]{:S(2)}) collective-permute-start(bf16[2,32,512]{2,1,0:T(8,128)(2,1)S(1)} %get-tuple-element.111), channel_id=1, source_target_pairs={{0,2},{1,3},{2,0},{3,1},{4,6},{5,7},{6,4},{7,5},{8,10},{9,11},{10,... | collective-permute-start | bytes 196616 | tf_op jit(solution)/shard_map/ppermute | solution.py:37
  91.9 7.2 %collective-permute-start.24 = (f32[2,256,512]{2,1,0:T(8,128)S(1)}, f32[2,256,512]{2,1,0:T(8,128)S(1)}, u32[]{:S(2)}, u32[]{:S(2)}) collective-permute-start(f32[2,256,512]{2,1,0:T(8,128)S(1)} %get-tuple-element.116), channel_id=1, source_target_pairs={{0,64},{1,65},{2,66},{3,67},{4,68},{5,69},{6,70},{7,71},{8,72},{9,... | collective-permute-start | bytes 3145736 | tf_op jit(solution)/shard_map/ppermute | solution.py:37
  92.0 6.5 %collective-permute-start.25 = (bf16[32,512]{1,0:T(8,128)(2,1)S(1)}, bf16[32,512]{1,0:T(8,128)(2,1)S(1)}, u32[]{:S(2)}, u32[]{:S(2)}) collective-permute-start(bf16[32,512]{1,0:T(8,128)(2,1)S(1)} %get-tuple-element.117), channel_id=1, source_target_pairs={{0,6},{1,7},{2,4},{3,5},{4,2},{5,3},{6,0},{7,1},{8,14},{9,15},{10,... | collective-permute-start | bytes 98312 | tf_op jit(solution)/shard_map/ppermute | solution.py:37

commit v6 on v5

--- a/solution.py
+++ b/solution.py
@@ -157,31 +157,52 @@
     )(me, tokens, master, moment, second, gradient)
 
 
-def terms_kernel(part, me, tokens, other, cot, cotr, *refs):
-    sx, sy, sz, kx, ky, kz, own, sems = refs[-8:]
-    mx, my, mz, c = me[0], me[1], me[2], me[3]
-    mine = pl.multiple_of(2048 * c, 2048)
+def product(a, b):
+    flat = b.shape[0] * b.shape[1]
+    return lax.dot_general(
+        a.reshape(flat, 512), b[...].reshape(flat, 512), (((0,), (0,)), ((), ())), preferred_element_type=F32
+    )
+
+
+def own_kernel(me, tokens, cot, out, own, sems):
+    column = pl.multiple_of(2048 * me[3], 2048)
     loads = [
-        pltpu.make_async_copy(tokens.at[:, :, pl.ds(mine + 4096 * part + 512 * x, 512)], own.at[x], sems.at[x])
-        for x in range(4)
+        pltpu.make_async_copy(
+            tokens.at[:, :, pl.ds(column + 4096 * (t // 4) + 512 * (t % 4), 512)], own.at[t], sems.at[t]
+        )
+        for t in range(8)
     ]
     for load in loads:
         load.start()
-    flat = cot.shape[0] * cot.shape[1]
-    ours, theirs = cot[...].reshape(flat, 512), cotr[...].reshape(flat, 512)
+    for t in range(8):
+        loads[t].wait()
+        out[t] = product(own[t], cot)
+
+
+def own_terms(me, tokens, cot):
+    return pl.pallas_call(
+        own_kernel,
+        in_specs=[SMEM, HBM, VMEM],
+        out_specs=[VMEM] * 2,
+        out_shape=[
+            jax.ShapeDtypeStruct((8, 512, 512), F32),
+            jax.ShapeDtypeStruct((8, *tokens.shape[:2], 512), BF16),
+        ],
+        scratch_shapes=[pltpu.SemaphoreType.DMA((8,))],
+        compiler_params=PARAMS,
+        interpret=INTERPRET,
+    )(me, tokens, cot)
+
+
+def terms_kernel(me, r0, r1, cot, mine, sx, sy, sz, kx, ky, kz):
+    mx, my, mz, c = me[0], me[1], me[2], me[3]
     xs = [label4(x, mx, c) for x in range(4)]
-    ys = [label4(2 * part + y, my, c) for y in range(2)]
+    ys = [label4(y, my, c) for y in range(4)]
     zs = [label8(z, mz, c) for z in range(8)]
-
-    def product(a, b):
-        return lax.dot_general(a.reshape(flat, 512), b, (((0,), (0,)), ((), ())), preferred_element_type=F32)
-
-    for t in range(4):
-        acc = product(other[:, :, 512 * t : 512 * t + 512], theirs)
-        loads[t].wait()
-        acc += product(own[t], ours)
+    for t in range(8):
+        acc = mine[t] + product((r0, r1)[t // 4][:, :, 512 * (t % 4) : 512 * (t % 4) + 512], cot)
         for j in range(16):
-            x, y, z = xs[t], ys[j // 8], zs[j % 8]
+            x, y, z = xs[t % 4], ys[2 * (t // 4) + j // 8], zs[j % 8]
             far = x[1] * 8 + y[1] * 4 + z[1]
             axes = (x[0], y[0], z[0])
             block = acc[32 * j : 32 * j + 32]
@@ -193,18 +214,16 @@
                 keep[jnp.where(first_ == 1, 64, at)] = piece
 
 
-def terms(part, me, tokens, other, cot, cotr, held=()):
+def all_terms(me, r0, r1, cot, mine):
     return pl.pallas_call(
-        functools.partial(terms_kernel, part),
-        in_specs=[SMEM, HBM] + [VMEM] * (3 + len(held)),
+        terms_kernel,
+        in_specs=[SMEM] + [VMEM] * 4,
         out_specs=[VMEM] * 6,
         out_shape=[jax.ShapeDtypeStruct(*message(65, i)) for i in range(3)]
         + [jax.ShapeDtypeStruct((65, *s), F32) for s in STREAMS],
-        scratch_shapes=[pltpu.VMEM((4, *tokens.shape[:2], 512), BF16), pltpu.SemaphoreType.DMA((4,))],
-        input_output_aliases={5 + i: i for i in range(len(held))},
         compiler_params=PARAMS,
         interpret=INTERPRET,
-    )(me, tokens, other, cot, cotr, *held)
+    )(me, r0, r1, cot, mine)
 
 
 def cut(stream, block):
@@ -252,10 +271,6 @@
 def last_kernel(got, keep, send, kept):
     send[...] = (keep[1] + got[1].astype(F32)).astype(BF16)
     kept[...] = keep[0] + got[0].astype(F32)
-
-
-def sum_kernel(got, keep, out):
-    out[...] = keep[...] + got[...].astype(F32)
 
 
 def assemble(me, sx, sy, sz, gx, gy, gz, w):
@@ -280,53 +295,43 @@
                     w[pl.ds(at, 32), 384:512] = part(2, sz, gz)
 
 
-def other_kernel(me, tokens, r0, r1, sx, sy, sz, gx, gy, gz, out, w, own, sems):
-    mine = pl.multiple_of(2048 * me[3], 2048)
-    loads = load_half(tokens, mine, (own.at[0], own.at[1]), sems, 0)
-    for load in loads:
-        load.start()
+def other_kernel(me, r0, r1, sx, sy, sz, gx, gy, gz, out, w):
     assemble(me, sx, sy, sz, gx, gy, gz, w)
     for m in range(out.shape[0]):
         out[m] = jnp.dot(r0[m], w[0:2048], preferred_element_type=F32) + jnp.dot(
             r1[m], w[2048:4096], preferred_element_type=F32
         )
-    for load in loads:
-        load.wait()
 
 
 def mine_kernel(own, w, out):
-    for m in range(out.shape[0]):
-        out[m] = jnp.dot(own[0, m], w[0:2048], preferred_element_type=F32) + jnp.dot(
-            own[1, m], w[2048:4096], preferred_element_type=F32
-        )
-
-
-def add_kernel(mine, other, out):
-    out[...] = (mine[...] + other[...]).astype(BF16)
-
-
-def other_values(me, tokens, r0, r1, messages):
+    flat = out.shape[0] * out.shape[1]
+    total = jnp.dot(own[0].reshape(flat, 512), w[0:512], preferred_element_type=F32)
+    for t in range(1, 8):
+        total += jnp.dot(own[t].reshape(flat, 512), w[512 * t : 512 * t + 512], preferred_element_type=F32)
+    out[...] = total.reshape(out.shape)
+
+
+def end_kernel(got, keep, mine, other, grad, values):
+    grad[...] = keep[...] + got[...].astype(F32)
+    values[...] = (mine[...] + other[...]).astype(BF16)
+
+
+def other_values(me, r0, r1, messages):
     return pl.pallas_call(
         other_kernel,
-        in_specs=[SMEM, HBM] + [VMEM] * 8,
-        out_specs=[VMEM] * 3,
+        in_specs=[SMEM] + [VMEM] * 8,
+        out_specs=[VMEM] * 2,
         out_shape=[
             jax.ShapeDtypeStruct((*r0.shape[:2], 512), F32),
             jax.ShapeDtypeStruct((4096, 512), BF16),
-            jax.ShapeDtypeStruct((2, *r0.shape), BF16),
         ],
-        scratch_shapes=[pltpu.SemaphoreType.DMA((8,))],
         compiler_params=PARAMS,
         interpret=INTERPRET,
-    )(me, tokens, r0, r1, *messages)
+    )(me, r0, r1, *messages)
 
 
 def after(value, *others):
     return lax.optimization_barrier((value, *others))[0]
-
-
-def joined(a, b, other):
-    return jnp.concatenate(lax.optimization_barrier((a, b, other))[:2])
 
 
 def body(tokens, cotangent, master, moment, second, gradient):
@@ -338,15 +343,17 @@
     )
     r0, r1, weight, new_master, new_moment, new_second = first(me, tokens, master, moment, second, gradient)
     cotr, r0, r1 = swap(cotangent), swap(r0), swap(r1)
-    line = jnp.stack([weight, far_step(weight, 2, True)])
-    held = terms(0, me, tokens, r0, cotangent, cotr)
-    line = joined(line, far_step(line, 2, False), held[0])
-    far = far_step(line, 1, False)
-    held = terms(1, me, tokens, r1, cotangent, cotr, held)
+    far = far_step(weight, 2, True)
+    mine, own = own_terms(me, tokens, cotangent)
+    line = jnp.stack(lax.optimization_barrier((weight, far, mine))[:2])
+    line = jnp.concatenate([line, far_step(line, 2, False)])
+    held = all_terms(me, r0, r1, cotr, mine)
     send, keep = held[:3], held[3:]
-    plane = joined(line, far, send[0])
+
+    got = [near(send[i], AXES[i][0]) for i in range(3)]
+    line = after(line, send[0])
+    plane = jnp.concatenate([line, far_step(line, 1, False)])
     plane = jnp.concatenate([plane, far_step(plane, 0, False)])
-    got = [near(send[i], AXES[i][0]) for i in range(3)]
 
     *got, plane = lax.optimization_barrier((*got, plane))
     new = [
@@ -379,13 +386,14 @@
     s, kept = call(line_kernel, [((2, *block), BF16), ((2, *block), F32)], g0, g1, kept)
     got = far_step(s, 2, False)
 
-    other, w, own = other_values(after(me, kept), tokens, r0, r1, [*half, *rest])
+    other, w = other_values(after(me, kept), r0, r1, [*half, *rest])
     s, kept = call(last_kernel, [(block, BF16), (block, F32)], got, after(kept, w))
     got = far_step(s, 2, True)
     other = swap(after(other, kept))
     (mine,) = call(mine_kernel, [((*r0.shape[:2], 512), F32)], own, after(w, kept))
-    (weight_grad,) = call(sum_kernel, [(block, F32)], got, after(kept, mine))
-    (values,) = call(add_kernel, [((*r0.shape[:2], 512), BF16)], mine, other)
+    weight_grad, values = call(
+        end_kernel, [(block, F32), ((*r0.shape[:2], 512), BF16)], got, kept, mine, other
+    )
     return (new_master, new_moment, new_second, values, weight_grad)
 
 

time: 101 us -> 95.1 us (0.942)
  waiting for transfers between devices: 42.3 us -> 38.3 us
  Pallas kernels: 23.9 us -> 20 us
  starting transfers between devices: 32.8 us -> 34.3 us
    ppermute x26, waiting for transfers between devices: 42.3 us -> 38.3 us  [permute(): return lax.ppermute(value, ALL, pairs)]
    pallas_call x3, Pallas kernels: 15.3 us -> 12.1 us  [the longest x1 5.39 us: own_terms(): pl.pallas_call(own_kernel, in_specs=[SMEM, HBM, VMEM], out_specs=[VMEM] *...]
    ppermute x26, starting transfers between devices: 32.8 us -> 34.3 us  [permute(): return lax.ppermute(value, ALL, pairs)]
    pallas_call x16 -> x15, Pallas kernels: 4.97 us -> 4.35 us  [call(): pl.pallas_call(kernel, out_shape=[jax.ShapeDtypeStruct(*o) for o in outs]...]
  transfers between devices with their start and end apart: 26 -> 26, of which waited for: 12 -> 11; matrix products, arithmetic and copies ran while one was open for 0% -> 0% of each run, Pallas kernels for 14% -> 16%
where the time goes in v6:
time: 95.1 us; the launch traced here: 93.7 us
  waiting for transfers between devices  38.3 us (40%)
  starting transfers between devices  34.3 us (36%)
  Pallas kernels  20 us (21%)
    ppermute x26, waiting for transfers between devices, permute(): return lax.ppermute(value, ALL, pairs)  38.3 us
    ppermute x26, starting transfers between devices, permute(): return lax.ppermute(value, ALL, pairs)  34.3 us
    pallas_call x1, Pallas kernels, own_terms(): pl.pallas_call(own_kernel, in_specs=[SMEM, HBM, VMEM], out_specs=[VMEM] *...  5.39 us
    pallas_call x15, Pallas kernels, call(): pl.pallas_call(kernel, out_shape=[jax.ShapeDtypeStruct(*o) for o in outs]...  4.35 us
    pallas_call x1, Pallas kernels, first(): pl.pallas_call(first_kernel, in_specs=[SMEM] + [HBM] * 5, out_specs=[VMEM...  3.62 us
    pallas_call x1, Pallas kernels, other_values(): pl.pallas_call(other_kernel, in_specs=[SMEM] + [VMEM] * 8, out_specs=[VME...  3.44 us
    pallas_call x1, Pallas kernels, all_terms(): pl.pallas_call(terms_kernel, in_specs=[SMEM] + [VMEM] * 4, out_specs=[VME...  3.25 us
  transfers between devices with their start and end apart: 26, of which 11 were waited for; matrix products, arithmetic and copies ran while one was open for 0% of the time, Pallas kernels for 16%

profile of v6, /device:TPU:0, one launch (start us, length us, event | category | flops | bytes accessed | tf_op | source)
XLA Modules:
  0.0 93.7 jit_solution(9273030599007803962)
XLA Ops:
  0.8 3.6 %shard_map.101 = (bf16[2,256,2048]{2,1,0:T(8,128)(2,1)S(1)}, bf16[2,256,2048]{2,1,0:T(8,128)(2,1)S(1)}, bf16[32,512]{1,0:T(8,128)(2,1)S(1)}, f32[32,512]{1,0:T(8...) custom-call(s32[4]{0:T(128)S(1)} %pad_add_fusion.me, bf16[2,256,8192]{2,1,0:T(8,128)(2,1)} %tokens.3, f32[32,512]{1,0:T(8,128)} %master.1, ...), custom_call_target="tpu_custom_call" | custom-call | tf_op jit(solution)/shard_map/pallas_call | solution.py:149
  4.4 0.1 collective-permute-start
  4.5 0.5 collective-permute-start.1
  5.0 0.1 collective-permute-start.2
  5.1 4.6 %collective-permute-start.6 = (bf16[32,512]{1,0:T(8,128)(2,1)S(1)}, bf16[32,512]{1,0:T(8,128)(2,1)S(1)}, u32[]{:S(2)}, u32[]{:S(2)}) collective-permute-start(bf16[32,512]{1,0:T(8,128)(2,1)S(1)} %get-tuple-element.67), channel_id=1, source_target_pairs={{0,6},{1,7},{2,4},{3,5},{4,2},{5,3},{6,0},{7,1},{8,14},{9,15},{10,... | collective-permute-start | bytes 98312 | tf_op jit(solution)/shard_map/ppermute | solution.py:37
  9.7 5.4 %shard_map.102 = (f32[8,512,512]{2,1,0:T(8,128)S(1)}, bf16[8,2,256,512]{3,2,1,0:T(8,128)(2,1)S(1)}) custom-call(s32[4]{0:T(128)S(1)} %pad_add_fusion.me, bf16[2,256,8192]{2,1,0:T(8,128)(2,1)} %tokens.3, bf16[2,256,512]{2,1,0:T(8,128)(2,1)S(1)} %copy-done), custom_call_target="tpu_custom_call" | custom-call | tf_op jit(solution)/shard_map/pallas_call | solution.py:183
  15.1 1.5 %collective-permute-start.7 = (bf16[2,32,512]{2,1,0:T(8,128)(2,1)S(1)}, bf16[2,32,512]{2,1,0:T(8,128)(2,1)S(1)}, u32[]{:S(2)}, u32[]{:S(2)}) collective-permute-start(bf16[2,32,512]{2,1,0:T(8,128)(2,1)S(1)} %pad_maximum_fusion.3), channel_id=1, source_target_pairs={{0,2},{1,3},{2,0},{3,1},{4,6},{5,7},{6,4},{7,5},{8,10},{9,11},{10,... | collective-permute-start | bytes 196616 | tf_op jit(solution)/shard_map/ppermute | solution.py:37
  16.6 3.3 %shard_map.103 = (bf16[65,16,384]{2,1,0:T(8,128)(2,1)S(1)}, bf16[65,16,384]{2,1,0:T(8,128)(2,1)S(1)}, bf16[97,32,128]{2,1,0:T(8,128)(2,1)S(1)}, f32[65,16,384]{2...) custom-call(s32[4]{0:T(128)S(1)} %pad_add_fusion.me, ...), custom_call_target="tpu_custom_call" | custom-call | tf_op jit(solution)/shard_map/pallas_call | solution.py:218
  19.9 1.7 %collective-permute-start.4 = (bf16[65,16,384]{2,1,0:T(8,128)(2,1)S(1)}, bf16[65,16,384]{2,1,0:T(8,128)(2,1)S(1)}, u32[]{:S(2)}, u32[]{:S(2)}) collective-permute-start(bf16[65,16,384]{2,1,0:T(8,128)(2,1)S(1)} %get-tuple-element.64), channel_id=1, source_target_pairs={{0,8},{1,9},{2,10},{3,11},{4,12},{5,13},{6,14},{7,15},{8,0},{9,1},... | collective-permute-start | bytes 2396168 | tf_op jit(solution)/shard_map/ppermute | solution.py:37
  21.6 1.5 %collective-permute-start.3 = (bf16[65,16,384]{2,1,0:T(8,128)(2,1)S(1)}, bf16[65,16,384]{2,1,0:T(8,128)(2,1)S(1)}, u32[]{:S(2)}, u32[]{:S(2)}) collective-permute-start(bf16[65,16,384]{2,1,0:T(8,128)(2,1)S(1)} %get-tuple-element.63), channel_id=1, source_target_pairs={{0,16},{1,17},{2,18},{3,19},{4,20},{5,21},{6,22},{7,23},{8,24},{9,... | collective-permute-start | bytes 2396168 | tf_op jit(solution)/shard_map/ppermute | solution.py:37
  23.1 1.0 %collective-permute-start.5 = (bf16[97,32,128]{2,1,0:T(8,128)(2,1)S(1)}, bf16[97,32,128]{2,1,0:T(8,128)(2,1)S(1)}, u32[]{:S(2)}, u32[]{:S(2)}) collective-permute-start(bf16[97,32,128]{2,1,0:T(8,128)(2,1)S(1)} %get-tuple-element.65), channel_id=1, source_target_pairs={{0,1},{1,0},{2,3},{3,2},{4,5},{5,4},{6,7},{7,6},{8,9},{9,8},{10,11... | collective-permute-start | bytes 2383880 | tf_op jit(solution)/shard_map/ppermute | solution.py:37
  24.1 2.3 %collective-permute-start.8 = (bf16[4,32,512]{2,1,0:T(8,128)(2,1)S(1)}, bf16[4,32,512]{2,1,0:T(8,128)(2,1)S(1)}, u32[]{:S(2)}, u32[]{:S(2)}) collective-permute-start(bf16[4,32,512]{2,1,0:T(8,128)(2,1)S(1)} %pad_maximum_fusion.2), channel_id=1, source_target_pairs={{0,136},{1,137},{2,138},{3,139},{4,140},{5,141},{6,142},{7,143},{8... | collective-permute-start | bytes 393224 | tf_op jit(solution)/shard_map/ppermute | solution.py:37
  26.4 5.5 %collective-permute-done.8 = bf16[4,32,512]{2,1,0:T(8,128)(2,1)S(1)} collective-permute-done((bf16[4,32,512]{2,1,0:T(8,128)(2,1)S(1)}, bf16[4,32,512]{2,1,0:T(8,128)(2,1)S(1)}, u32[]{:S(2)}, u32[]{:S(2)}) %collective-permute-start.8) | collective-permute-done | bytes 131104 | tf_op jit(solution)/shard_map/ppermute | solution.py:37
  31.9 2.2 %collective-permute-start.9 = (bf16[8,32,512]{2,1,0:T(8,128)(2,1)S(1)}, bf16[8,32,512]{2,1,0:T(8,128)(2,1)S(1)}, u32[]{:S(2)}, u32[]{:S(2)}) collective-permute-start(bf16[8,32,512]{2,1,0:T(8,128)(2,1)S(1)} %pad_maximum_fusion.1), channel_id=1, source_target_pairs={{0,48},{1,49},{2,50},{3,51},{4,52},{5,53},{6,54},{7,55},{8,56},{9,... | collective-permute-start | bytes 786440 | tf_op jit(solution)/shard_map/ppermute | solution.py:37
  34.0 5.5 %collective-permute-done.9 = bf16[8,32,512]{2,1,0:T(8,128)(2,1)S(1)} collective-permute-done((bf16[8,32,512]{2,1,0:T(8,128)(2,1)S(1)}, bf16[8,32,512]{2,1,0:T(8,128)(2,1)S(1)}, u32[]{:S(2)}, u32[]{:S(2)}) %collective-permute-start.9) | collective-permute-done | bytes 262176 | tf_op jit(solution)/shard_map/ppermute | solution.py:37
  39.6 0.1 shard_map.108
  39.7 0.1 collective-permute-start.14
  39.8 0.1 shard_map.104
  40.0 0.1 collective-permute-start.10
  40.1 0.2 shard_map.106
  40.3 1.3 %collective-permute-start.12 = (bf16[48,16,384]{2,1,0:T(8,128)(2,1)S(1)}, bf16[48,16,384]{2,1,0:T(8,128)(2,1)S(1)}, u32[]{:S(2)}, u32[]{:S(2)}) collective-permute-start(bf16[48,16,384]{2,1,0:T(8,128)(2,1)S(1)} %get-tuple-element.78.sent), channel_id=1, source_target_pairs={{0,1},{1,0},{2,3},{3,2},{4,5},{5,4},{6,7},{7,6},{8,9},{9,8},{10,11... | collective-permute-start | bytes 1769480 | tf_op jit(solution)/shard_map/ppermute | solution.py:37
  41.6 8.2 %collective-permute-done.14.got = bf16[72,32,128]{2,1,0:T(8,128)(2,1)S(1)} collective-permute-done((bf16[72,32,128]{2,1,0:T(8,128)(2,1)S(1)}, bf16[72,32,128]{2,1,0:T(8,128)(2,1)S(1)}, u32[]{:S(2)}, u32[]{:S(2)}) %collective-permute-start.14) | collective-permute-done | bytes 589856 | tf_op jit(solution)/shard_map/ppermute | solution.py:37
  49.8 0.1 collective-permute-start.15
  49.9 0.1 collective-permute-done.10.got
  50.0 0.1 shard_map.105
  50.1 1.1 %collective-permute-start.11 = (bf16[48,16,384]{2,1,0:T(8,128)(2,1)S(1)}, bf16[48,16,384]{2,1,0:T(8,128)(2,1)S(1)}, u32[]{:S(2)}, u32[]{:S(2)}) collective-permute-start(bf16[48,16,384]{2,1,0:T(8,128)(2,1)S(1)} %get-tuple-element.75.sent), channel_id=1, source_target_pairs={{0,1},{1,0},{2,3},{3,2},{4,5},{5,4},{6,7},{7,6},{8,9},{9,8},{10,11... | collective-permute-start | bytes 1769480 | tf_op jit(solution)/shard_map/ppermute | solution.py:37
  51.2 0.1 shard_map.107
  51.3 2.1 %collective-permute-start.13 = (bf16[48,16,384]{2,1,0:T(8,128)(2,1)S(1)}, bf16[48,16,384]{2,1,0:T(8,128)(2,1)S(1)}, u32[]{:S(2)}, u32[]{:S(2)}) collective-permute-start(bf16[48,16,384]{2,1,0:T(8,128)(2,1)S(1)} %get-tuple-element.80.sent), channel_id=1, source_target_pairs={{0,16},{1,17},{2,18},{3,19},{4,20},{5,21},{6,22},{7,23},{8,24},{9,... | collective-permute-start | bytes 1769480 | tf_op jit(solution)/shard_map/ppermute | solution.py:37
  53.4 6.3 %collective-permute-done.15.gz.got = bf16[72,32,128]{2,1,0:T(8,128)(2,1)S(1)} collective-permute-done((bf16[72,32,128]{2,1,0:T(8,128)(2,1)S(1)}, bf16[72,32,128]{2,1,0:T(8,128)(2,1)S(1)}, u32[]{:S(2)}, u32[]{:S(2)}) %collective-permute-start.15) | collective-permute-done | bytes 589856 | tf_op jit(solution)/shard_map/ppermute | solution.py:37
  59.8 1.1 %collective-permute-start.23 = (bf16[96,32,128]{2,1,0:T(8,128)(2,1)S(1)}, bf16[96,32,128]{2,1,0:T(8,128)(2,1)S(1)}, u32[]{:S(2)}, u32[]{:S(2)}) collective-permute-start(bf16[96,32,128]{2,1,0:T(8,128)(2,1)S(1)} %shard_map.115.sz), channel_id=1, source_target_pairs={{0,1},{1,0},{2,3},{3,2},{4,5},{5,4},{6,7},{7,6},{8,9},{9,8},{10,11... | collective-permute-start | bytes 2359304 | tf_op jit(solution)/shard_map/ppermute | solution.py:37
  61.0 1.3 %collective-permute-start.21 = (bf16[64,16,384]{2,1,0:T(8,128)(2,1)S(1)}, bf16[64,16,384]{2,1,0:T(8,128)(2,1)S(1)}, u32[]{:S(2)}, u32[]{:S(2)}) collective-permute-start(bf16[64,16,384]{2,1,0:T(8,128)(2,1)S(1)} %shard_map.113.sx), channel_id=1, source_target_pairs={{0,16},{1,17},{2,18},{3,19},{4,20},{5,21},{6,22},{7,23},{8,24},{9,... | collective-permute-start | bytes 2359304 | tf_op jit(solution)/shard_map/ppermute | solution.py:37
  62.3 1.1 %collective-permute-start.22 = (bf16[64,16,384]{2,1,0:T(8,128)(2,1)S(1)}, bf16[64,16,384]{2,1,0:T(8,128)(2,1)S(1)}, u32[]{:S(2)}, u32[]{:S(2)}) collective-permute-start(bf16[64,16,384]{2,1,0:T(8,128)(2,1)S(1)} %shard_map.114.sy), channel_id=1, source_target_pairs={{0,8},{1,9},{2,10},{3,11},{4,12},{5,13},{6,14},{7,15},{8,0},{9,1},... | collective-permute-start | bytes 2359304 | tf_op jit(solution)/shard_map/ppermute | solution.py:37
  63.4 0.1 shard_map.110
  63.5 2.2 %collective-permute-start.16 = (bf16[4,32,512]{2,1,0:T(8,128)(2,1)S(1)}, bf16[4,32,512]{2,1,0:T(8,128)(2,1)S(1)}, u32[]{:S(2)}, u32[]{:S(2)}) collective-permute-start(bf16[4,32,512]{2,1,0:T(8,128)(2,1)S(1)} %get-tuple-element.89), channel_id=1, source_target_pairs={{0,48},{1,49},{2,50},{3,51},{4,52},{5,53},{6,54},{7,55},{8,56},{9,... | collective-permute-start | bytes 393224 | tf_op jit(solution)/shard_map/ppermute | solution.py:37
  65.7 2.2 %collective-permute-start.17 = (bf16[4,32,512]{2,1,0:T(8,128)(2,1)S(1)}, bf16[4,32,512]{2,1,0:T(8,128)(2,1)S(1)}, u32[]{:S(2)}, u32[]{:S(2)}) collective-permute-start(bf16[4,32,512]{2,1,0:T(8,128)(2,1)S(1)} %get-tuple-element.90), channel_id=1, source_target_pairs={{0,136},{1,137},{2,138},{3,139},{4,140},{5,141},{6,142},{7,143},{8... | collective-permute-start | bytes 393224 | tf_op jit(solution)/shard_map/ppermute | solution.py:37
  67.9 3.3 %collective-permute-done.16.g0 = bf16[4,32,512]{2,1,0:T(8,128)(2,1)S(1)} collective-permute-done((bf16[4,32,512]{2,1,0:T(8,128)(2,1)S(1)}, bf16[4,32,512]{2,1,0:T(8,128)(2,1)S(1)}, u32[]{:S(2)}, u32[]{:S(2)}) %collective-permute-start.16) | collective-permute-done | bytes 131104 | tf_op jit(solution)/shard_map/ppermute | solution.py:37
  71.2 2.1 %collective-permute-done.17.g1 = bf16[4,32,512]{2,1,0:T(8,128)(2,1)S(1)} collective-permute-done((bf16[4,32,512]{2,1,0:T(8,128)(2,1)S(1)}, bf16[4,32,512]{2,1,0:T(8,128)(2,1)S(1)}, u32[]{:S(2)}, u32[]{:S(2)}) %collective-permute-start.17) | collective-permute-done | bytes 131104 | tf_op jit(solution)/shard_map/ppermute | solution.py:37
  73.4 2.3 %collective-permute-start.18 = (bf16[2,32,512]{2,1,0:T(8,128)(2,1)S(1)}, bf16[2,32,512]{2,1,0:T(8,128)(2,1)S(1)}, u32[]{:S(2)}, u32[]{:S(2)}) collective-permute-start(bf16[2,32,512]{2,1,0:T(8,128)(2,1)S(1)} %get-tuple-element.93), channel_id=1, source_target_pairs={{0,136},{1,137},{2,138},{3,139},{4,140},{5,141},{6,142},{7,143},{8... | collective-permute-start | bytes 196616 | tf_op jit(solution)/shard_map/ppermute | solution.py:37
  75.7 1.1 %collective-permute-start.19 = (bf16[2,32,512]{2,1,0:T(8,128)(2,1)S(1)}, bf16[2,32,512]{2,1,0:T(8,128)(2,1)S(1)}, u32[]{:S(2)}, u32[]{:S(2)}) collective-permute-start(bf16[2,32,512]{2,1,0:T(8,128)(2,1)S(1)} %get-tuple-element.94), channel_id=1, source_target_pairs={{0,48},{1,49},{2,50},{3,51},{4,52},{5,53},{6,54},{7,55},{8,56},{9,... | collective-permute-start | bytes 196616 | tf_op jit(solution)/shard_map/ppermute | solution.py:37
  76.8 2.1 %collective-permute-done.18.g0 = bf16[2,32,512]{2,1,0:T(8,128)(2,1)S(1)} collective-permute-done((bf16[2,32,512]{2,1,0:T(8,128)(2,1)S(1)}, bf16[2,32,512]{2,1,0:T(8,128)(2,1)S(1)}, u32[]{:S(2)}, u32[]{:S(2)}) %collective-permute-start.18) | collective-permute-done | bytes 65568 | tf_op jit(solution)/shard_map/ppermute | solution.py:37
  78.9 2.2 %collective-permute-done.19.g1 = bf16[2,32,512]{2,1,0:T(8,128)(2,1)S(1)} collective-permute-done((bf16[2,32,512]{2,1,0:T(8,128)(2,1)S(1)}, bf16[2,32,512]{2,1,0:T(8,128)(2,1)S(1)}, u32[]{:S(2)}, u32[]{:S(2)}) %collective-permute-start.19) | collective-permute-done | bytes 65568 | tf_op jit(solution)/shard_map/ppermute | solution.py:37
  81.2 1.7 %collective-permute-start.20 = (bf16[2,32,512]{2,1,0:T(8,128)(2,1)S(1)}, bf16[2,32,512]{2,1,0:T(8,128)(2,1)S(1)}, u32[]{:S(2)}, u32[]{:S(2)}) collective-permute-start(bf16[2,32,512]{2,1,0:T(8,128)(2,1)S(1)} %get-tuple-element.96), channel_id=1, source_target_pairs={{0,2},{1,3},{2,0},{3,1},{4,6},{5,7},{6,4},{7,5},{8,10},{9,11},{10,... | collective-permute-start | bytes 196616 | tf_op jit(solution)/shard_map/ppermute | solution.py:37
  82.9 3.4 %shard_map.116 = (f32[2,256,512]{2,1,0:T(8,128)S(1)}, bf16[4096,512]{1,0:T(8,128)(2,1)S(1)}) custom-call(s32[4]{0:T(128)S(1)} %pad_add_fusion.me, bf16[2,256,2048]{2,1,0:T(8,128)(2,1)S(1)} %collective-permute-done.r0, bf16[2,256,2048]{2,1,0:T(8,128)(2,1)S(1)} %collective-permute-done.1.r1, bf16[64,16,384]{2,1,0:T(8,128)(2,1)S(1)} %shard_map.113.sx, ...), custom_call_target="tpu_custom_call" | custom-call | tf_op jit(solution)/shard_map/pallas_call | solution.py:320
  86.4 0.1 collective-permute-start.25
  86.5 1.1 %collective-permute-start.24 = (bf16[32,512]{1,0:T(8,128)(2,1)S(1)}, bf16[32,512]{1,0:T(8,128)(2,1)S(1)}, u32[]{:S(2)}, u32[]{:S(2)}) collective-permute-start(bf16[32,512]{1,0:T(8,128)(2,1)S(1)} %get-tuple-element.101), channel_id=1, source_target_pairs={{0,6},{1,7},{2,4},{3,5},{4,2},{5,3},{6,0},{7,1},{8,14},{9,15},{10,... | collective-permute-start | bytes 98312 | tf_op jit(solution)/shard_map/ppermute | solution.py:37
  87.6 2.3 %shard_map.118.mine = f32[2,256,512]{2,1,0:T(8,128)S(1)} custom-call(bf16[8,2,256,512]{3,2,1,0:T(8,128)(2,1)S(1)} %get-tuple-element.103.own, bf16[4096,512]{1,0:T(8,128)(2,1)S(1)} %get-tuple-element.104.w), custom_call_target="tpu_custom_call" | custom-call | tf_op jit(solution)/shard_map/pallas_call | solution.py:98
  89.9 2.8 %collective-permute-done.24.got = bf16[32,512]{1,0:T(8,128)(2,1)S(1)} collective-permute-done((bf16[32,512]{1,0:T(8,128)(2,1)S(1)}, bf16[32,512]{1,0:T(8,128)(2,1)S(1)}, u32[]{:S(2)}, u32[]{:S(2)}) %collective-permute-start.24) | collective-permute-done | bytes 32800 | tf_op jit(solution)/shard_map/ppermute | solution.py:37
  92.7 0.9 shard_map.119
  (30 shorter events, 0.6 us)
Async XLA Ops:
  0.8 4.2 %copy-start = (bf16[2,256,512]{2,1,0:T(8,128)(2,1)S(1)}, bf16[2,256,512]{2,1,0:T(8,128)(2,1)}, u32[]{:S(2)}) copy-start(bf16[2,256,512]{2,1,0:T(8,128)(2,1)} %cot.1) | copy-start | bytes 1572868
  4.4 12.2 %collective-permute-start = (bf16[2,256,2048]{2,1,0:T(8,128)(2,1)S(1)}, bf16[2,256,2048]{2,1,0:T(8,128)(2,1)S(1)}, u32[]{:S(2)}, u32[]{:S(2)}) collective-permute-start(bf16[2,256,2048]{2,1,0:T(8,128)(2,1)S(1)} %get-tuple-element.60), channel_id=1, source_target_pairs={{0,64},{1,65},{2,66},{3,67},{4,68},{5,69},{6,70},{7,71},{8,72},{9,... | collective-permute-start | bytes 6291464 | tf_op jit(solution)/shard_map/ppermute | solution.py:37
  4.5 12.1 %collective-permute-start.1 = (bf16[2,256,2048]{2,1,0:T(8,128)(2,1)S(1)}, bf16[2,256,2048]{2,1,0:T(8,128)(2,1)S(1)}, u32[]{:S(2)}, u32[]{:S(2)}) collective-permute-start(bf16[2,256,2048]{2,1,0:T(8,128)(2,1)S(1)} %get-tuple-element.61), channel_id=1, source_target_pairs={{0,64},{1,65},{2,66},{3,67},{4,68},{5,69},{6,70},{7,71},{8,72},{9,... | collective-permute-start | bytes 6291464 | tf_op jit(solution)/shard_map/ppermute | solution.py:37
  5.0 11.6 %collective-permute-start.2 = (bf16[2,256,512]{2,1,0:T(8,128)(2,1)S(1)}, bf16[2,256,512]{2,1,0:T(8,128)(2,1)S(1)}, u32[]{:S(2)}, u32[]{:S(2)}) collective-permute-start(bf16[2,256,512]{2,1,0:T(8,128)(2,1)S(1)} %copy-done), channel_id=1, source_target_pairs={{0,64},{1,65},{2,66},{3,67},{4,68},{5,69},{6,70},{7,71},{8,72},{9,... | collective-permute-start | bytes 1572872 | tf_op jit(solution)/shard_map/ppermute | solution.py:37
  5.1 10.0 %collective-permute-start.6 = (bf16[32,512]{1,0:T(8,128)(2,1)S(1)}, bf16[32,512]{1,0:T(8,128)(2,1)S(1)}, u32[]{:S(2)}, u32[]{:S(2)}) collective-permute-start(bf16[32,512]{1,0:T(8,128)(2,1)S(1)} %get-tuple-element.67), channel_id=1, source_target_pairs={{0,6},{1,7},{2,4},{3,5},{4,2},{5,3},{6,0},{7,1},{8,14},{9,15},{10,... | collective-permute-start | bytes 98312 | tf_op jit(solution)/shard_map/ppermute | solution.py:37
  15.1 9.0 %collective-permute-start.7 = (bf16[2,32,512]{2,1,0:T(8,128)(2,1)S(1)}, bf16[2,32,512]{2,1,0:T(8,128)(2,1)S(1)}, u32[]{:S(2)}, u32[]{:S(2)}) collective-permute-start(bf16[2,32,512]{2,1,0:T(8,128)(2,1)S(1)} %pad_maximum_fusion.3), channel_id=1, source_target_pairs={{0,2},{1,3},{2,0},{3,1},{4,6},{5,7},{6,4},{7,5},{8,10},{9,11},{10,... | collective-permute-start | bytes 196616 | tf_op jit(solution)/shard_map/ppermute | solution.py:37
  19.9 19.7 %collective-permute-start.4 = (bf16[65,16,384]{2,1,0:T(8,128)(2,1)S(1)}, bf16[65,16,384]{2,1,0:T(8,128)(2,1)S(1)}, u32[]{:S(2)}, u32[]{:S(2)}) collective-permute-start(bf16[65,16,384]{2,1,0:T(8,128)(2,1)S(1)} %get-tuple-element.64), channel_id=1, source_target_pairs={{0,8},{1,9},{2,10},{3,11},{4,12},{5,13},{6,14},{7,15},{8,0},{9,1},... | collective-permute-start | bytes 2396168 | tf_op jit(solution)/shard_map/ppermute | solution.py:37
  21.6 18.0 %collective-permute-start.3 = (bf16[65,16,384]{2,1,0:T(8,128)(2,1)S(1)}, bf16[65,16,384]{2,1,0:T(8,128)(2,1)S(1)}, u32[]{:S(2)}, u32[]{:S(2)}) collective-permute-start(bf16[65,16,384]{2,1,0:T(8,128)(2,1)S(1)} %get-tuple-element.63), channel_id=1, source_target_pairs={{0,16},{1,17},{2,18},{3,19},{4,20},{5,21},{6,22},{7,23},{8,24},{9,... | collective-permute-start | bytes 2396168 | tf_op jit(solution)/shard_map/ppermute | solution.py:37
  23.1 16.5 %collective-permute-start.5 = (bf16[97,32,128]{2,1,0:T(8,128)(2,1)S(1)}, bf16[97,32,128]{2,1,0:T(8,128)(2,1)S(1)}, u32[]{:S(2)}, u32[]{:S(2)}) collective-permute-start(bf16[97,32,128]{2,1,0:T(8,128)(2,1)S(1)} %get-tuple-element.65), channel_id=1, source_target_pairs={{0,1},{1,0},{2,3},{3,2},{4,5},{5,4},{6,7},{7,6},{8,9},{9,8},{10,11... | collective-permute-start | bytes 2383880 | tf_op jit(solution)/shard_map/ppermute | solution.py:37
  24.1 7.7 %collective-permute-start.8 = (bf16[4,32,512]{2,1,0:T(8,128)(2,1)S(1)}, bf16[4,32,512]{2,1,0:T(8,128)(2,1)S(1)}, u32[]{:S(2)}, u32[]{:S(2)}) collective-permute-start(bf16[4,32,512]{2,1,0:T(8,128)(2,1)S(1)} %pad_maximum_fusion.2), channel_id=1, source_target_pairs={{0,136},{1,137},{2,138},{3,139},{4,140},{5,141},{6,142},{7,143},{8... | collective-permute-start | bytes 393224 | tf_op jit(solution)/shard_map/ppermute | solution.py:37
  31.9 7.7 %collective-permute-start.9 = (bf16[8,32,512]{2,1,0:T(8,128)(2,1)S(1)}, bf16[8,32,512]{2,1,0:T(8,128)(2,1)S(1)}, u32[]{:S(2)}, u32[]{:S(2)}) collective-permute-start(bf16[8,32,512]{2,1,0:T(8,128)(2,1)S(1)} %pad_maximum_fusion.1), channel_id=1, source_target_pairs={{0,48},{1,49},{2,50},{3,51},{4,52},{5,53},{6,54},{7,55},{8,56},{9,... | collective-permute-start | bytes 786440 | tf_op jit(solution)/shard_map/ppermute | solution.py:37
  39.7 10.0 %collective-permute-start.14 = (bf16[72,32,128]{2,1,0:T(8,128)(2,1)S(1)}, bf16[72,32,128]{2,1,0:T(8,128)(2,1)S(1)}, u32[]{:S(2)}, u32[]{:S(2)}) collective-permute-start(bf16[72,32,128]{2,1,0:T(8,128)(2,1)S(1)} %get-tuple-element.83.sent), channel_id=1, source_target_pairs={{0,16},{1,17},{2,18},{3,19},{4,20},{5,21},{6,22},{7,23},{8,24},{9,... | collective-permute-start | bytes 1769480 | tf_op jit(solution)/shard_map/ppermute | solution.py:37
  40.0 10.0 %collective-permute-start.10 = (bf16[48,16,384]{2,1,0:T(8,128)(2,1)S(1)}, bf16[48,16,384]{2,1,0:T(8,128)(2,1)S(1)}, u32[]{:S(2)}, u32[]{:S(2)}) collective-permute-start(bf16[48,16,384]{2,1,0:T(8,128)(2,1)S(1)} %get-tuple-element.73.sent), channel_id=1, source_target_pairs={{0,8},{1,9},{2,10},{3,11},{4,12},{5,13},{6,14},{7,15},{8,0},{9,1},... | collective-permute-start | bytes 1769480 | tf_op jit(solution)/shard_map/ppermute | solution.py:37
  40.3 10.9 %collective-permute-start.12 = (bf16[48,16,384]{2,1,0:T(8,128)(2,1)S(1)}, bf16[48,16,384]{2,1,0:T(8,128)(2,1)S(1)}, u32[]{:S(2)}, u32[]{:S(2)}) collective-permute-start(bf16[48,16,384]{2,1,0:T(8,128)(2,1)S(1)} %get-tuple-element.78.sent), channel_id=1, source_target_pairs={{0,1},{1,0},{2,3},{3,2},{4,5},{5,4},{6,7},{7,6},{8,9},{9,8},{10,11... | collective-permute-start | bytes 1769480 | tf_op jit(solution)/shard_map/ppermute | solution.py:37
  49.8 10.0 %collective-permute-start.15 = (bf16[72,32,128]{2,1,0:T(8,128)(2,1)S(1)}, bf16[72,32,128]{2,1,0:T(8,128)(2,1)S(1)}, u32[]{:S(2)}, u32[]{:S(2)}) collective-permute-start(bf16[72,32,128]{2,1,0:T(8,128)(2,1)S(1)} %get-tuple-element.85.sent), channel_id=1, source_target_pairs={{0,8},{1,9},{2,10},{3,11},{4,12},{5,13},{6,14},{7,15},{8,0},{9,1},... | collective-permute-start | bytes 1769480 | tf_op jit(solution)/shard_map/ppermute | solution.py:37
  50.1 10.8 %collective-permute-start.11 = (bf16[48,16,384]{2,1,0:T(8,128)(2,1)S(1)}, bf16[48,16,384]{2,1,0:T(8,128)(2,1)S(1)}, u32[]{:S(2)}, u32[]{:S(2)}) collective-permute-start(bf16[48,16,384]{2,1,0:T(8,128)(2,1)S(1)} %get-tuple-element.75.sent), channel_id=1, source_target_pairs={{0,1},{1,0},{2,3},{3,2},{4,5},{5,4},{6,7},{7,6},{8,9},{9,8},{10,11... | collective-permute-start | bytes 1769480 | tf_op jit(solution)/shard_map/ppermute | solution.py:37
  51.3 10.9 %collective-permute-start.13 = (bf16[48,16,384]{2,1,0:T(8,128)(2,1)S(1)}, bf16[48,16,384]{2,1,0:T(8,128)(2,1)S(1)}, u32[]{:S(2)}, u32[]{:S(2)}) collective-permute-start(bf16[48,16,384]{2,1,0:T(8,128)(2,1)S(1)} %get-tuple-element.80.sent), channel_id=1, source_target_pairs={{0,16},{1,17},{2,18},{3,19},{4,20},{5,21},{6,22},{7,23},{8,24},{9,... | collective-permute-start | bytes 1769480 | tf_op jit(solution)/shard_map/ppermute | solution.py:37
  59.8 23.1 %collective-permute-start.23 = (bf16[96,32,128]{2,1,0:T(8,128)(2,1)S(1)}, bf16[96,32,128]{2,1,0:T(8,128)(2,1)S(1)}, u32[]{:S(2)}, u32[]{:S(2)}) collective-permute-start(bf16[96,32,128]{2,1,0:T(8,128)(2,1)S(1)} %shard_map.115.sz), channel_id=1, source_target_pairs={{0,1},{1,0},{2,3},{3,2},{4,5},{5,4},{6,7},{7,6},{8,9},{9,8},{10,11... | collective-permute-start | bytes 2359304 | tf_op jit(solution)/shard_map/ppermute | solution.py:37
  61.0 21.9 %collective-permute-start.21 = (bf16[64,16,384]{2,1,0:T(8,128)(2,1)S(1)}, bf16[64,16,384]{2,1,0:T(8,128)(2,1)S(1)}, u32[]{:S(2)}, u32[]{:S(2)}) collective-permute-start(bf16[64,16,384]{2,1,0:T(8,128)(2,1)S(1)} %shard_map.113.sx), channel_id=1, source_target_pairs={{0,16},{1,17},{2,18},{3,19},{4,20},{5,21},{6,22},{7,23},{8,24},{9,... | collective-permute-start | bytes 2359304 | tf_op jit(solution)/shard_map/ppermute | solution.py:37
  62.3 20.6 %collective-permute-start.22 = (bf16[64,16,384]{2,1,0:T(8,128)(2,1)S(1)}, bf16[64,16,384]{2,1,0:T(8,128)(2,1)S(1)}, u32[]{:S(2)}, u32[]{:S(2)}) collective-permute-start(bf16[64,16,384]{2,1,0:T(8,128)(2,1)S(1)} %shard_map.114.sy), channel_id=1, source_target_pairs={{0,8},{1,9},{2,10},{3,11},{4,12},{5,13},{6,14},{7,15},{8,0},{9,1},... | collective-permute-start | bytes 2359304 | tf_op jit(solution)/shard_map/ppermute | solution.py:37
  63.5 7.7 %collective-permute-start.16 = (bf16[4,32,512]{2,1,0:T(8,128)(2,1)S(1)}, bf16[4,32,512]{2,1,0:T(8,128)(2,1)S(1)}, u32[]{:S(2)}, u32[]{:S(2)}) collective-permute-start(bf16[4,32,512]{2,1,0:T(8,128)(2,1)S(1)} %get-tuple-element.89), channel_id=1, source_target_pairs={{0,48},{1,49},{2,50},{3,51},{4,52},{5,53},{6,54},{7,55},{8,56},{9,... | collective-permute-start | bytes 393224 | tf_op jit(solution)/shard_map/ppermute | solution.py:37
  65.7 7.6 %collective-permute-start.17 = (bf16[4,32,512]{2,1,0:T(8,128)(2,1)S(1)}, bf16[4,32,512]{2,1,0:T(8,128)(2,1)S(1)}, u32[]{:S(2)}, u32[]{:S(2)}) collective-permute-start(bf16[4,32,512]{2,1,0:T(8,128)(2,1)S(1)} %get-tuple-element.90), channel_id=1, source_target_pairs={{0,136},{1,137},{2,138},{3,139},{4,140},{5,141},{6,142},{7,143},{8... | collective-permute-start | bytes 393224 | tf_op jit(solution)/shard_map/ppermute | solution.py:37
  73.4 5.6 %collective-permute-start.18 = (bf16[2,32,512]{2,1,0:T(8,128)(2,1)S(1)}, bf16[2,32,512]{2,1,0:T(8,128)(2,1)S(1)}, u32[]{:S(2)}, u32[]{:S(2)}) collective-permute-start(bf16[2,32,512]{2,1,0:T(8,128)(2,1)S(1)} %get-tuple-element.93), channel_id=1, source_target_pairs={{0,136},{1,137},{2,138},{3,139},{4,140},{5,141},{6,142},{7,143},{8... | collective-permute-start | bytes 196616 | tf_op jit(solution)/shard_map/ppermute | solution.py:37
  75.7 5.5 %collective-permute-start.19 = (bf16[2,32,512]{2,1,0:T(8,128)(2,1)S(1)}, bf16[2,32,512]{2,1,0:T(8,128)(2,1)S(1)}, u32[]{:S(2)}, u32[]{:S(2)}) collective-permute-start(bf16[2,32,512]{2,1,0:T(8,128)(2,1)S(1)} %get-tuple-element.94), channel_id=1, source_target_pairs={{0,48},{1,49},{2,50},{3,51},{4,52},{5,53},{6,54},{7,55},{8,56},{9,... | collective-permute-start | bytes 196616 | tf_op jit(solution)/shard_map/ppermute | solution.py:37
  81.2 5.3 %collective-permute-start.20 = (bf16[2,32,512]{2,1,0:T(8,128)(2,1)S(1)}, bf16[2,32,512]{2,1,0:T(8,128)(2,1)S(1)}, u32[]{:S(2)}, u32[]{:S(2)}) collective-permute-start(bf16[2,32,512]{2,1,0:T(8,128)(2,1)S(1)} %get-tuple-element.96), channel_id=1, source_target_pairs={{0,2},{1,3},{2,0},{3,1},{4,6},{5,7},{6,4},{7,5},{8,10},{9,11},{10,... | collective-permute-start | bytes 196616 | tf_op jit(solution)/shard_map/ppermute | solution.py:37
  86.4 6.3 %collective-permute-start.25 = (f32[2,256,512]{2,1,0:T(8,128)S(1)}, f32[2,256,512]{2,1,0:T(8,128)S(1)}, u32[]{:S(2)}, u32[]{:S(2)}) collective-permute-start(f32[2,256,512]{2,1,0:T(8,128)S(1)} %get-tuple-element.106), channel_id=1, source_target_pairs={{0,64},{1,65},{2,66},{3,67},{4,68},{5,69},{6,70},{7,71},{8,72},{9,... | collective-permute-start | bytes 3145736 | tf_op jit(solution)/shard_map/ppermute | solution.py:37
  86.5 6.2 %collective-permute-start.24 = (bf16[32,512]{1,0:T(8,128)(2,1)S(1)}, bf16[32,512]{1,0:T(8,128)(2,1)S(1)}, u32[]{:S(2)}, u32[]{:S(2)}) collective-permute-start(bf16[32,512]{1,0:T(8,128)(2,1)S(1)} %get-tuple-element.101), channel_id=1, source_target_pairs={{0,6},{1,7},{2,4},{3,5},{4,2},{5,3},{6,0},{7,1},{8,14},{9,15},{10,... | collective-permute-start | bytes 98312 | tf_op jit(solution)/shard_map/ppermute | solution.py:37

commit v7 on v6

--- a/solution.py
+++ b/solution.py
@@ -119,12 +119,13 @@
     ]
 
 
-def first_kernel(me, tokens, master, moment, second, gradient, r0, r1, weight, out_master, out_moment, out_second, rows, sems):
+def first_kernel(me, tokens, cot, master, moment, second, gradient, r0, r1, held, weight, out_master, out_moment, out_second, rows, sems):
     far = pl.multiple_of(2048 * (1 - me[3]), 2048)
     loads = [
         pltpu.make_async_copy(ref, rows.at[i], sems.at[i]) for i, ref in enumerate((master, moment, second, gradient))
     ]
     copies = load_half(tokens, far, (r0, r1), sems, 4)
+    copies.append(pltpu.make_async_copy(cot, held, sems.at[12]))
     for copy in loads + copies:
         copy.start()
     for copy in loads:
@@ -143,18 +144,18 @@
         copy.wait()
 
 
-def first(me, tokens, master, moment, second, gradient):
+def first(me, tokens, cot, master, moment, second, gradient):
     half = jax.ShapeDtypeStruct((*tokens.shape[:2], 2048), BF16)
     rows = jax.ShapeDtypeStruct(master.shape, F32)
     return pl.pallas_call(
         first_kernel,
-        in_specs=[SMEM] + [HBM] * 5,
-        out_specs=[VMEM] * 6,
-        out_shape=[half, half, jax.ShapeDtypeStruct(master.shape, BF16), rows, rows, rows],
-        scratch_shapes=[pltpu.VMEM((4, *master.shape), F32), pltpu.SemaphoreType.DMA((12,))],
-        compiler_params=PARAMS,
-        interpret=INTERPRET,
-    )(me, tokens, master, moment, second, gradient)
+        in_specs=[SMEM] + [HBM] * 6,
+        out_specs=[VMEM] * 7,
+        out_shape=[half, half, jax.ShapeDtypeStruct(cot.shape, BF16), jax.ShapeDtypeStruct(master.shape, BF16), rows, rows, rows],
+        scratch_shapes=[pltpu.VMEM((4, *master.shape), F32), pltpu.SemaphoreType.DMA((13,))],
+        compiler_params=PARAMS,
+        interpret=INTERPRET,
+    )(me, tokens, cot, master, moment, second, gradient)
 
 
 def product(a, b):
@@ -164,31 +165,18 @@
     )
 
 
-def own_kernel(me, tokens, cot, out, own, sems):
-    column = pl.multiple_of(2048 * me[3], 2048)
-    loads = [
-        pltpu.make_async_copy(
-            tokens.at[:, :, pl.ds(column + 4096 * (t // 4) + 512 * (t % 4), 512)], own.at[t], sems.at[t]
-        )
-        for t in range(8)
-    ]
-    for load in loads:
-        load.start()
+def own_kernel(me, tokens, cot, out):
     for t in range(8):
-        loads[t].wait()
-        out[t] = product(own[t], cot)
+        column = pl.multiple_of(2048 * me[3] + 4096 * (t // 4) + 512 * (t % 4), 512)
+        out[t] = product(tokens[:, :, pl.ds(column, 512)], cot)
 
 
 def own_terms(me, tokens, cot):
     return pl.pallas_call(
         own_kernel,
-        in_specs=[SMEM, HBM, VMEM],
-        out_specs=[VMEM] * 2,
-        out_shape=[
-            jax.ShapeDtypeStruct((8, 512, 512), F32),
-            jax.ShapeDtypeStruct((8, *tokens.shape[:2], 512), BF16),
-        ],
-        scratch_shapes=[pltpu.SemaphoreType.DMA((8,))],
+        in_specs=[SMEM, VMEM, VMEM],
+        out_specs=VMEM,
+        out_shape=jax.ShapeDtypeStruct((8, 512, 512), F32),
         compiler_params=PARAMS,
         interpret=INTERPRET,
     )(me, tokens, cot)
@@ -298,22 +286,34 @@
 def other_kernel(me, r0, r1, sx, sy, sz, gx, gy, gz, out, w):
     assemble(me, sx, sy, sz, gx, gy, gz, w)
     for m in range(out.shape[0]):
-        out[m] = jnp.dot(r0[m], w[0:2048], preferred_element_type=F32) + jnp.dot(
+        total = jnp.dot(r0[m], w[0:2048], preferred_element_type=F32) + jnp.dot(
             r1[m], w[2048:4096], preferred_element_type=F32
         )
-
-
-def mine_kernel(own, w, out):
-    flat = out.shape[0] * out.shape[1]
-    total = jnp.dot(own[0].reshape(flat, 512), w[0:512], preferred_element_type=F32)
-    for t in range(1, 8):
-        total += jnp.dot(own[t].reshape(flat, 512), w[512 * t : 512 * t + 512], preferred_element_type=F32)
-    out[...] = total.reshape(out.shape)
+        out[m] = total.astype(BF16)
+
+
+def mine_kernel(me, tokens, w, out):
+    columns = [pl.multiple_of(2048 * me[3] + 4096 * i, 2048) for i in range(2)]
+    for m in range(out.shape[0]):
+        out[m] = jnp.dot(tokens[m, :, pl.ds(columns[0], 2048)], w[0:2048], preferred_element_type=F32) + jnp.dot(
+            tokens[m, :, pl.ds(columns[1], 2048)], w[2048:4096], preferred_element_type=F32
+        )
+
+
+def my_values(me, tokens, w):
+    return pl.pallas_call(
+        mine_kernel,
+        in_specs=[SMEM, VMEM, VMEM],
+        out_specs=VMEM,
+        out_shape=jax.ShapeDtypeStruct((*tokens.shape[:2], 512), F32),
+        compiler_params=PARAMS,
+        interpret=INTERPRET,
+    )(me, tokens, w)
 
 
 def end_kernel(got, keep, mine, other, grad, values):
     grad[...] = keep[...] + got[...].astype(F32)
-    values[...] = (mine[...] + other[...]).astype(BF16)
+    values[...] = (mine[...] + other[...].astype(F32)).astype(BF16)
 
 
 def other_values(me, r0, r1, messages):
@@ -322,7 +322,7 @@
         in_specs=[SMEM] + [VMEM] * 8,
         out_specs=[VMEM] * 2,
         out_shape=[
-            jax.ShapeDtypeStruct((*r0.shape[:2], 512), F32),
+            jax.ShapeDtypeStruct((*r0.shape[:2], 512), BF16),
             jax.ShapeDtypeStruct((4096, 512), BF16),
         ],
         compiler_params=PARAMS,
@@ -338,13 +338,13 @@
     node, dp = lax.axis_index("node"), lax.axis_index("dp")
     me = jnp.stack([dp // 16, (node // 2) * 2 + (dp // 8) % 2, dp % 8, node % 2]).astype(jnp.int32)
 
-    tokens, master, moment, second, gradient = (
-        pltpu.with_memory_space_constraint(a, pltpu.HBM) for a in (tokens, master, moment, second, gradient)
+    in_hbm = (
+        pltpu.with_memory_space_constraint(a, pltpu.HBM) for a in (tokens, cotangent, master, moment, second, gradient)
     )
-    r0, r1, weight, new_master, new_moment, new_second = first(me, tokens, master, moment, second, gradient)
+    r0, r1, cotangent, weight, new_master, new_moment, new_second = first(me, *in_hbm)
     cotr, r0, r1 = swap(cotangent), swap(r0), swap(r1)
     far = far_step(weight, 2, True)
-    mine, own = own_terms(me, tokens, cotangent)
+    mine = own_terms(me, tokens, cotangent)
     line = jnp.stack(lax.optimization_barrier((weight, far, mine))[:2])
     line = jnp.concatenate([line, far_step(line, 2, False)])
     held = all_terms(me, r0, r1, cotr, mine)
@@ -390,7 +390,7 @@
     s, kept = call(last_kernel, [(block, BF16), (block, F32)], got, after(kept, w))
     got = far_step(s, 2, True)
     other = swap(after(other, kept))
-    (mine,) = call(mine_kernel, [((*r0.shape[:2], 512), F32)], own, after(w, kept))
+    mine = my_values(me, tokens, after(w, kept))
     weight_grad, values = call(
         end_kernel, [(block, F32), ((*r0.shape[:2], 512), BF16)], got, kept, mine, other
     )

time: 95.1 us -> 93.3 us (0.981)
  waiting for transfers between devices: 38.3 us -> 36.7 us
  Pallas kernels: 20 us -> 18.5 us
  starting transfers between devices: 34.3 us -> 35.8 us
    pallas_call x15 -> x14, Pallas kernels: 4.35 us -> 2.01 us  [call(): pl.pallas_call(kernel, out_shape=[jax.ShapeDtypeStruct(*o) for o in outs]...]
    ppermute x26, starting transfers between devices: 34.3 us -> 35.8 us  [permute(): return lax.ppermute(value, ALL, pairs)]
    ppermute x26, waiting for transfers between devices: 38.3 us -> 36.7 us  [permute(): return lax.ppermute(value, ALL, pairs)]
    pallas_call x2 -> x3, Pallas kernels: 9.01 us -> 9.76 us  [the longest x1 3.99 us: first(): pl.pallas_call(first_kernel, in_specs=[SMEM] + [HBM] * 6, out_specs=[VMEM...]
  transfers between devices with their start and end apart: 26 -> 26, of which waited for: 11 -> 11; matrix products, arithmetic and copies ran while one was open for 0% -> 0% of each run, Pallas kernels for 16% -> 15%
where the time goes in v7:
time: 93.3 us; the launch traced here: 92.1 us
  waiting for transfers between devices  36.7 us (39%)
  starting transfers between devices  35.8 us (38%)
  Pallas kernels  18.5 us (20%)
    ppermute x26, waiting for transfers between devices, permute(): return lax.ppermute(value, ALL, pairs)  36.7 us
    ppermute x26, starting transfers between devices, permute(): return lax.ppermute(value, ALL, pairs)  35.8 us
    pallas_call x1, Pallas kernels, first(): pl.pallas_call(first_kernel, in_specs=[SMEM] + [HBM] * 6, out_specs=[VMEM...  3.99 us
    pallas_call x1, Pallas kernels, other_values(): pl.pallas_call(other_kernel, in_specs=[SMEM] + [VMEM] * 8, out_specs=[VME...  3.44 us
    pallas_call x1, Pallas kernels, all_terms(): pl.pallas_call(terms_kernel, in_specs=[SMEM] + [VMEM] * 4, out_specs=[VME...  3.26 us
    pallas_call x1, Pallas kernels, own_terms(): pl.pallas_call(own_kernel, in_specs=[SMEM, VMEM, VMEM], out_specs=VMEM, o...  2.92 us
    pallas_call x1, Pallas kernels, my_values(): pl.pallas_call(mine_kernel, in_specs=[SMEM, VMEM, VMEM], out_specs=VMEM,...  2.85 us
    pallas_call x14, Pallas kernels, call(): pl.pallas_call(kernel, out_shape=[jax.ShapeDtypeStruct(*o) for o in outs]...  2.01 us
  transfers between devices with their start and end apart: 26, of which 11 were waited for; matrix products, arithmetic and copies ran while one was open for 0% of the time, Pallas kernels for 15%

profile of v7, /device:TPU:0, one launch (start us, length us, event | category | flops | bytes accessed | tf_op | source)
XLA Modules:
  0.0 92.1 jit_solution(17172683012309034234)
XLA Ops:
  0.8 4.0 %shard_map.101 = (bf16[2,256,2048]{2,1,0:T(8,128)(2,1)S(1)}, bf16[2,256,2048]{2,1,0:T(8,128)(2,1)S(1)}, bf16[2,256,512]{2,1,0:T(8,128)(2,1)S(1)}, bf16[32,512]{1...) custom-call(s32[4]{0:T(128)S(1)} %pad_add_fusion.me, bf16[2,256,8192]{2,1,0:T(8,128)(2,1)} %tokens.5, ...), custom_call_target="tpu_custom_call" | custom-call | tf_op jit(solution)/shard_map/pallas_call | solution.py:150
  4.8 0.1 collective-permute-start
  4.9 0.5 collective-permute-start.1
  5.4 0.1 collective-permute-start.2
  5.5 4.6 %collective-permute-start.6 = (bf16[32,512]{1,0:T(8,128)(2,1)S(1)}, bf16[32,512]{1,0:T(8,128)(2,1)S(1)}, u32[]{:S(2)}, u32[]{:S(2)}) collective-permute-start(bf16[32,512]{1,0:T(8,128)(2,1)S(1)} %get-tuple-element.66), channel_id=1, source_target_pairs={{0,6},{1,7},{2,4},{3,5},{4,2},{5,3},{6,0},{7,1},{8,14},{9,15},{10,... | collective-permute-start | bytes 98312 | tf_op jit(solution)/shard_map/ppermute | solution.py:37
  10.0 2.9 %shard_map.102.mine = f32[8,512,512]{2,1,0:T(8,128)S(1)} custom-call(s32[4]{0:T(128)S(1)} %pad_add_fusion.me, bf16[2,256,8192]{2,1,0:T(8,128)(2,1)S(1)} %copy-done, bf16[2,256,512]{2,1,0:T(8,128)(2,1)S(1)} %get-tuple-element.61.cot), custom_call_target="tpu_custom_call" | custom-call | tf_op jit(solution)/shard_map/pallas_call | solution.py:175
  13.0 1.5 %collective-permute-start.7 = (bf16[2,32,512]{2,1,0:T(8,128)(2,1)S(1)}, bf16[2,32,512]{2,1,0:T(8,128)(2,1)S(1)}, u32[]{:S(2)}, u32[]{:S(2)}) collective-permute-start(bf16[2,32,512]{2,1,0:T(8,128)(2,1)S(1)} %pad_maximum_fusion.3), channel_id=1, source_target_pairs={{0,2},{1,3},{2,0},{3,1},{4,6},{5,7},{6,4},{7,5},{8,10},{9,11},{10,... | collective-permute-start | bytes 196616 | tf_op jit(solution)/shard_map/ppermute | solution.py:37
  14.5 3.3 %shard_map.103 = (bf16[65,16,384]{2,1,0:T(8,128)(2,1)S(1)}, bf16[65,16,384]{2,1,0:T(8,128)(2,1)S(1)}, bf16[97,32,128]{2,1,0:T(8,128)(2,1)S(1)}, f32[65,16,384]{2...) custom-call(s32[4]{0:T(128)S(1)} %pad_add_fusion.me, ...), custom_call_target="tpu_custom_call" | custom-call | tf_op jit(solution)/shard_map/pallas_call | solution.py:206
  17.8 1.7 %collective-permute-start.4 = (bf16[65,16,384]{2,1,0:T(8,128)(2,1)S(1)}, bf16[65,16,384]{2,1,0:T(8,128)(2,1)S(1)}, u32[]{:S(2)}, u32[]{:S(2)}) collective-permute-start(bf16[65,16,384]{2,1,0:T(8,128)(2,1)S(1)} %get-tuple-element.63), channel_id=1, source_target_pairs={{0,8},{1,9},{2,10},{3,11},{4,12},{5,13},{6,14},{7,15},{8,0},{9,1},... | collective-permute-start | bytes 2396168 | tf_op jit(solution)/shard_map/ppermute | solution.py:37
  19.5 1.5 %collective-permute-start.3 = (bf16[65,16,384]{2,1,0:T(8,128)(2,1)S(1)}, bf16[65,16,384]{2,1,0:T(8,128)(2,1)S(1)}, u32[]{:S(2)}, u32[]{:S(2)}) collective-permute-start(bf16[65,16,384]{2,1,0:T(8,128)(2,1)S(1)} %get-tuple-element.62), channel_id=1, source_target_pairs={{0,16},{1,17},{2,18},{3,19},{4,20},{5,21},{6,22},{7,23},{8,24},{9,... | collective-permute-start | bytes 2396168 | tf_op jit(solution)/shard_map/ppermute | solution.py:37
  21.0 1.0 %collective-permute-start.5 = (bf16[97,32,128]{2,1,0:T(8,128)(2,1)S(1)}, bf16[97,32,128]{2,1,0:T(8,128)(2,1)S(1)}, u32[]{:S(2)}, u32[]{:S(2)}) collective-permute-start(bf16[97,32,128]{2,1,0:T(8,128)(2,1)S(1)} %get-tuple-element.64), channel_id=1, source_target_pairs={{0,1},{1,0},{2,3},{3,2},{4,5},{5,4},{6,7},{7,6},{8,9},{9,8},{10,11... | collective-permute-start | bytes 2383880 | tf_op jit(solution)/shard_map/ppermute | solution.py:37
  22.0 2.3 %collective-permute-start.8 = (bf16[4,32,512]{2,1,0:T(8,128)(2,1)S(1)}, bf16[4,32,512]{2,1,0:T(8,128)(2,1)S(1)}, u32[]{:S(2)}, u32[]{:S(2)}) collective-permute-start(bf16[4,32,512]{2,1,0:T(8,128)(2,1)S(1)} %pad_maximum_fusion.2), channel_id=1, source_target_pairs={{0,136},{1,137},{2,138},{3,139},{4,140},{5,141},{6,142},{7,143},{8... | collective-permute-start | bytes 393224 | tf_op jit(solution)/shard_map/ppermute | solution.py:37
  24.3 5.5 %collective-permute-done.8 = bf16[4,32,512]{2,1,0:T(8,128)(2,1)S(1)} collective-permute-done((bf16[4,32,512]{2,1,0:T(8,128)(2,1)S(1)}, bf16[4,32,512]{2,1,0:T(8,128)(2,1)S(1)}, u32[]{:S(2)}, u32[]{:S(2)}) %collective-permute-start.8) | collective-permute-done | bytes 131104 | tf_op jit(solution)/shard_map/ppermute | solution.py:37
  29.8 2.2 %collective-permute-start.9 = (bf16[8,32,512]{2,1,0:T(8,128)(2,1)S(1)}, bf16[8,32,512]{2,1,0:T(8,128)(2,1)S(1)}, u32[]{:S(2)}, u32[]{:S(2)}) collective-permute-start(bf16[8,32,512]{2,1,0:T(8,128)(2,1)S(1)} %pad_maximum_fusion.1), channel_id=1, source_target_pairs={{0,48},{1,49},{2,50},{3,51},{4,52},{5,53},{6,54},{7,55},{8,56},{9,... | collective-permute-start | bytes 786440 | tf_op jit(solution)/shard_map/ppermute | solution.py:37
  31.9 5.5 %collective-permute-done.9 = bf16[8,32,512]{2,1,0:T(8,128)(2,1)S(1)} collective-permute-done((bf16[8,32,512]{2,1,0:T(8,128)(2,1)S(1)}, bf16[8,32,512]{2,1,0:T(8,128)(2,1)S(1)}, u32[]{:S(2)}, u32[]{:S(2)}) %collective-permute-start.9) | collective-permute-done | bytes 262176 | tf_op jit(solution)/shard_map/ppermute | solution.py:37
  37.5 0.1 shard_map.108
  37.6 0.1 collective-permute-start.14
  37.7 0.1 shard_map.104
  37.9 0.1 collective-permute-start.10
  38.0 0.2 shard_map.106
  38.2 1.3 %collective-permute-start.12 = (bf16[48,16,384]{2,1,0:T(8,128)(2,1)S(1)}, bf16[48,16,384]{2,1,0:T(8,128)(2,1)S(1)}, u32[]{:S(2)}, u32[]{:S(2)}) collective-permute-start(bf16[48,16,384]{2,1,0:T(8,128)(2,1)S(1)} %get-tuple-element.77.sent), channel_id=1, source_target_pairs={{0,1},{1,0},{2,3},{3,2},{4,5},{5,4},{6,7},{7,6},{8,9},{9,8},{10,11... | collective-permute-start | bytes 1769480 | tf_op jit(solution)/shard_map/ppermute | solution.py:37
  39.5 8.2 %collective-permute-done.14.got = bf16[72,32,128]{2,1,0:T(8,128)(2,1)S(1)} collective-permute-done((bf16[72,32,128]{2,1,0:T(8,128)(2,1)S(1)}, bf16[72,32,128]{2,1,0:T(8,128)(2,1)S(1)}, u32[]{:S(2)}, u32[]{:S(2)}) %collective-permute-start.14) | collective-permute-done | bytes 589856 | tf_op jit(solution)/shard_map/ppermute | solution.py:37
  47.7 0.1 collective-permute-start.15
  47.9 0.1 shard_map.105
  48.0 1.1 %collective-permute-start.11 = (bf16[48,16,384]{2,1,0:T(8,128)(2,1)S(1)}, bf16[48,16,384]{2,1,0:T(8,128)(2,1)S(1)}, u32[]{:S(2)}, u32[]{:S(2)}) collective-permute-start(bf16[48,16,384]{2,1,0:T(8,128)(2,1)S(1)} %get-tuple-element.74.sent), channel_id=1, source_target_pairs={{0,1},{1,0},{2,3},{3,2},{4,5},{5,4},{6,7},{7,6},{8,9},{9,8},{10,11... | collective-permute-start | bytes 1769480 | tf_op jit(solution)/shard_map/ppermute | solution.py:37
  49.1 0.1 shard_map.107
  49.2 2.1 %collective-permute-start.13 = (bf16[48,16,384]{2,1,0:T(8,128)(2,1)S(1)}, bf16[48,16,384]{2,1,0:T(8,128)(2,1)S(1)}, u32[]{:S(2)}, u32[]{:S(2)}) collective-permute-start(bf16[48,16,384]{2,1,0:T(8,128)(2,1)S(1)} %get-tuple-element.79.sent), channel_id=1, source_target_pairs={{0,16},{1,17},{2,18},{3,19},{4,20},{5,21},{6,22},{7,23},{8,24},{9,... | collective-permute-start | bytes 1769480 | tf_op jit(solution)/shard_map/ppermute | solution.py:37
  51.3 6.4 %collective-permute-done.15.gz.got = bf16[72,32,128]{2,1,0:T(8,128)(2,1)S(1)} collective-permute-done((bf16[72,32,128]{2,1,0:T(8,128)(2,1)S(1)}, bf16[72,32,128]{2,1,0:T(8,128)(2,1)S(1)}, u32[]{:S(2)}, u32[]{:S(2)}) %collective-permute-start.15) | collective-permute-done | bytes 589856 | tf_op jit(solution)/shard_map/ppermute | solution.py:37
  57.7 1.1 %collective-permute-start.23 = (bf16[96,32,128]{2,1,0:T(8,128)(2,1)S(1)}, bf16[96,32,128]{2,1,0:T(8,128)(2,1)S(1)}, u32[]{:S(2)}, u32[]{:S(2)}) collective-permute-start(bf16[96,32,128]{2,1,0:T(8,128)(2,1)S(1)} %shard_map.115.sz), channel_id=1, source_target_pairs={{0,1},{1,0},{2,3},{3,2},{4,5},{5,4},{6,7},{7,6},{8,9},{9,8},{10,11... | collective-permute-start | bytes 2359304 | tf_op jit(solution)/shard_map/ppermute | solution.py:37
  58.9 1.3 %collective-permute-start.21 = (bf16[64,16,384]{2,1,0:T(8,128)(2,1)S(1)}, bf16[64,16,384]{2,1,0:T(8,128)(2,1)S(1)}, u32[]{:S(2)}, u32[]{:S(2)}) collective-permute-start(bf16[64,16,384]{2,1,0:T(8,128)(2,1)S(1)} %shard_map.113.sx), channel_id=1, source_target_pairs={{0,16},{1,17},{2,18},{3,19},{4,20},{5,21},{6,22},{7,23},{8,24},{9,... | collective-permute-start | bytes 2359304 | tf_op jit(solution)/shard_map/ppermute | solution.py:37
  60.2 1.0 %collective-permute-start.22 = (bf16[64,16,384]{2,1,0:T(8,128)(2,1)S(1)}, bf16[64,16,384]{2,1,0:T(8,128)(2,1)S(1)}, u32[]{:S(2)}, u32[]{:S(2)}) collective-permute-start(bf16[64,16,384]{2,1,0:T(8,128)(2,1)S(1)} %shard_map.114.sy), channel_id=1, source_target_pairs={{0,8},{1,9},{2,10},{3,11},{4,12},{5,13},{6,14},{7,15},{8,0},{9,1},... | collective-permute-start | bytes 2359304 | tf_op jit(solution)/shard_map/ppermute | solution.py:37
  61.2 0.1 shard_map.110
  61.3 2.2 %collective-permute-start.16 = (bf16[4,32,512]{2,1,0:T(8,128)(2,1)S(1)}, bf16[4,32,512]{2,1,0:T(8,128)(2,1)S(1)}, u32[]{:S(2)}, u32[]{:S(2)}) collective-permute-start(bf16[4,32,512]{2,1,0:T(8,128)(2,1)S(1)} %get-tuple-element.88), channel_id=1, source_target_pairs={{0,48},{1,49},{2,50},{3,51},{4,52},{5,53},{6,54},{7,55},{8,56},{9,... | collective-permute-start | bytes 393224 | tf_op jit(solution)/shard_map/ppermute | solution.py:37
  63.5 2.2 %collective-permute-start.17 = (bf16[4,32,512]{2,1,0:T(8,128)(2,1)S(1)}, bf16[4,32,512]{2,1,0:T(8,128)(2,1)S(1)}, u32[]{:S(2)}, u32[]{:S(2)}) collective-permute-start(bf16[4,32,512]{2,1,0:T(8,128)(2,1)S(1)} %get-tuple-element.89), channel_id=1, source_target_pairs={{0,136},{1,137},{2,138},{3,139},{4,140},{5,141},{6,142},{7,143},{8... | collective-permute-start | bytes 393224 | tf_op jit(solution)/shard_map/ppermute | solution.py:37
  65.7 3.4 %collective-permute-done.16.g0 = bf16[4,32,512]{2,1,0:T(8,128)(2,1)S(1)} collective-permute-done((bf16[4,32,512]{2,1,0:T(8,128)(2,1)S(1)}, bf16[4,32,512]{2,1,0:T(8,128)(2,1)S(1)}, u32[]{:S(2)}, u32[]{:S(2)}) %collective-permute-start.16) | collective-permute-done | bytes 131104 | tf_op jit(solution)/shard_map/ppermute | solution.py:37
  69.1 2.1 %collective-permute-done.17.g1 = bf16[4,32,512]{2,1,0:T(8,128)(2,1)S(1)} collective-permute-done((bf16[4,32,512]{2,1,0:T(8,128)(2,1)S(1)}, bf16[4,32,512]{2,1,0:T(8,128)(2,1)S(1)}, u32[]{:S(2)}, u32[]{:S(2)}) %collective-permute-start.17) | collective-permute-done | bytes 131104 | tf_op jit(solution)/shard_map/ppermute | solution.py:37
  71.2 2.3 %collective-permute-start.18 = (bf16[2,32,512]{2,1,0:T(8,128)(2,1)S(1)}, bf16[2,32,512]{2,1,0:T(8,128)(2,1)S(1)}, u32[]{:S(2)}, u32[]{:S(2)}) collective-permute-start(bf16[2,32,512]{2,1,0:T(8,128)(2,1)S(1)} %get-tuple-element.92), channel_id=1, source_target_pairs={{0,136},{1,137},{2,138},{3,139},{4,140},{5,141},{6,142},{7,143},{8... | collective-permute-start | bytes 196616 | tf_op jit(solution)/shard_map/ppermute | solution.py:37
  73.5 1.1 %collective-permute-start.19 = (bf16[2,32,512]{2,1,0:T(8,128)(2,1)S(1)}, bf16[2,32,512]{2,1,0:T(8,128)(2,1)S(1)}, u32[]{:S(2)}, u32[]{:S(2)}) collective-permute-start(bf16[2,32,512]{2,1,0:T(8,128)(2,1)S(1)} %get-tuple-element.93), channel_id=1, source_target_pairs={{0,48},{1,49},{2,50},{3,51},{4,52},{5,53},{6,54},{7,55},{8,56},{9,... | collective-permute-start | bytes 196616 | tf_op jit(solution)/shard_map/ppermute | solution.py:37
  74.6 2.2 %collective-permute-done.18.g0 = bf16[2,32,512]{2,1,0:T(8,128)(2,1)S(1)} collective-permute-done((bf16[2,32,512]{2,1,0:T(8,128)(2,1)S(1)}, bf16[2,32,512]{2,1,0:T(8,128)(2,1)S(1)}, u32[]{:S(2)}, u32[]{:S(2)}) %collective-permute-start.18) | collective-permute-done | bytes 65568 | tf_op jit(solution)/shard_map/ppermute | solution.py:37
  76.8 2.2 %collective-permute-done.19.g1 = bf16[2,32,512]{2,1,0:T(8,128)(2,1)S(1)} collective-permute-done((bf16[2,32,512]{2,1,0:T(8,128)(2,1)S(1)}, bf16[2,32,512]{2,1,0:T(8,128)(2,1)S(1)}, u32[]{:S(2)}, u32[]{:S(2)}) %collective-permute-start.19) | collective-permute-done | bytes 65568 | tf_op jit(solution)/shard_map/ppermute | solution.py:37
  79.0 1.5 %collective-permute-start.20 = (bf16[2,32,512]{2,1,0:T(8,128)(2,1)S(1)}, bf16[2,32,512]{2,1,0:T(8,128)(2,1)S(1)}, u32[]{:S(2)}, u32[]{:S(2)}) collective-permute-start(bf16[2,32,512]{2,1,0:T(8,128)(2,1)S(1)} %get-tuple-element.95), channel_id=1, source_target_pairs={{0,2},{1,3},{2,0},{3,1},{4,6},{5,7},{6,4},{7,5},{8,10},{9,11},{10,... | collective-permute-start | bytes 196616 | tf_op jit(solution)/shard_map/ppermute | solution.py:37
  80.6 3.4 %shard_map.116 = (bf16[2,256,512]{2,1,0:T(8,128)(2,1)S(1)}, bf16[4096,512]{1,0:T(8,128)(2,1)S(1)}) custom-call(s32[4]{0:T(128)S(1)} %pad_add_fusion.me, bf16[2,256,2048]{2,1,0:T(8,128)(2,1)S(1)} %collective-permute-done.r0, bf16[2,256,2048]{2,1,0:T(8,128)(2,1)S(1)} %collective-permute-done.1.r1, bf16[64,16,384]{2,1,0:T(8,128)(2,1)S(1)} %shard_map.113.sx, ...), custom_call_target="tpu_custom_call" | custom-call | tf_op jit(solution)/shard_map/pallas_call | solution.py:320
  84.0 0.9 %collective-permute-done.20.got = bf16[2,32,512]{2,1,0:T(8,128)(2,1)S(1)} collective-permute-done((bf16[2,32,512]{2,1,0:T(8,128)(2,1)S(1)}, bf16[2,32,512]{2,1,0:T(8,128)(2,1)S(1)}, u32[]{:S(2)}, u32[]{:S(2)}) %collective-permute-start.20) | collective-permute-done | bytes 65568 | tf_op jit(solution)/shard_map/ppermute | solution.py:37
  85.0 0.1 collective-permute-start.25
  85.1 2.9 %collective-permute-start.24 = (bf16[32,512]{1,0:T(8,128)(2,1)S(1)}, bf16[32,512]{1,0:T(8,128)(2,1)S(1)}, u32[]{:S(2)}, u32[]{:S(2)}) collective-permute-start(bf16[32,512]{1,0:T(8,128)(2,1)S(1)} %get-tuple-element.100), channel_id=1, source_target_pairs={{0,6},{1,7},{2,4},{3,5},{4,2},{5,3},{6,0},{7,1},{8,14},{9,15},{10,... | collective-permute-start | bytes 98312 | tf_op jit(solution)/shard_map/ppermute | solution.py:37
  87.9 2.9 %shard_map.118.mine = f32[2,256,512]{2,1,0:T(8,128)S(1)} custom-call(s32[4]{0:T(128)S(1)} %pad_add_fusion.me, bf16[2,256,8192]{2,1,0:T(8,128)(2,1)S(1)} %copy-done, bf16[4096,512]{1,0:T(8,128)(2,1)S(1)} %get-tuple-element.102.w), custom_call_target="tpu_custom_call" | custom-call | tf_op jit(solution)/shard_map/pallas_call | solution.py:304
  90.8 0.4 collective-permute-done.24.got
  91.2 0.9 %shard_map.119 = (f32[32,512]{1,0:T(8,128)}, bf16[2,256,512]{2,1,0:T(8,128)(2,1)}) custom-call(bf16[32,512]{1,0:T(8,128)(2,1)S(1)} %collective-permute-done.24.got, f32[32,512]{1,0:T(8,128)S(1)} %get-tuple-element.101.keep, f32[2,256,512]{2,1,0:T(8,128)S(1)} %shard_map.118.mine, bf16[2,256,512]{2,1,0:T(8,128)(2,1)S(1)} %collective-permute-done.25.other), custom_call_target="tpu_custom_call" | custom-call | tf_op jit(solution)/shard_map/pallas_call | solution.py:98
  (30 shorter events, 0.6 us)
Async XLA Ops:
  0.8 9.3 %copy-start = (bf16[2,256,8192]{2,1,0:T(8,128)(2,1)S(1)}, bf16[2,256,8192]{2,1,0:T(8,128)(2,1)}, u32[]{:S(2)}) copy-start(bf16[2,256,8192]{2,1,0:T(8,128)(2,1)} %tokens.5) | copy-start | bytes 25165828
  4.8 9.8 %collective-permute-start = (bf16[2,256,2048]{2,1,0:T(8,128)(2,1)S(1)}, bf16[2,256,2048]{2,1,0:T(8,128)(2,1)S(1)}, u32[]{:S(2)}, u32[]{:S(2)}) collective-permute-start(bf16[2,256,2048]{2,1,0:T(8,128)(2,1)S(1)} %get-tuple-element.59), channel_id=1, source_target_pairs={{0,64},{1,65},{2,66},{3,67},{4,68},{5,69},{6,70},{7,71},{8,72},{9,... | collective-permute-start | bytes 6291464 | tf_op jit(solution)/shard_map/ppermute | solution.py:37
  4.9 9.7 %collective-permute-start.1 = (bf16[2,256,2048]{2,1,0:T(8,128)(2,1)S(1)}, bf16[2,256,2048]{2,1,0:T(8,128)(2,1)S(1)}, u32[]{:S(2)}, u32[]{:S(2)}) collective-permute-start(bf16[2,256,2048]{2,1,0:T(8,128)(2,1)S(1)} %get-tuple-element.60), channel_id=1, source_target_pairs={{0,64},{1,65},{2,66},{3,67},{4,68},{5,69},{6,70},{7,71},{8,72},{9,... | collective-permute-start | bytes 6291464 | tf_op jit(solution)/shard_map/ppermute | solution.py:37
  5.4 9.2 %collective-permute-start.2 = (bf16[2,256,512]{2,1,0:T(8,128)(2,1)S(1)}, bf16[2,256,512]{2,1,0:T(8,128)(2,1)S(1)}, u32[]{:S(2)}, u32[]{:S(2)}) collective-permute-start(bf16[2,256,512]{2,1,0:T(8,128)(2,1)S(1)} %get-tuple-element.61.cot), channel_id=1, source_target_pairs={{0,64},{1,65},{2,66},{3,67},{4,68},{5,69},{6,70},{7,71},{8,72},{9,... | collective-permute-start | bytes 1572872 | tf_op jit(solution)/shard_map/ppermute | solution.py:37
  5.5 7.5 %collective-permute-start.6 = (bf16[32,512]{1,0:T(8,128)(2,1)S(1)}, bf16[32,512]{1,0:T(8,128)(2,1)S(1)}, u32[]{:S(2)}, u32[]{:S(2)}) collective-permute-start(bf16[32,512]{1,0:T(8,128)(2,1)S(1)} %get-tuple-element.66), channel_id=1, source_target_pairs={{0,6},{1,7},{2,4},{3,5},{4,2},{5,3},{6,0},{7,1},{8,14},{9,15},{10,... | collective-permute-start | bytes 98312 | tf_op jit(solution)/shard_map/ppermute | solution.py:37
  13.0 9.0 %collective-permute-start.7 = (bf16[2,32,512]{2,1,0:T(8,128)(2,1)S(1)}, bf16[2,32,512]{2,1,0:T(8,128)(2,1)S(1)}, u32[]{:S(2)}, u32[]{:S(2)}) collective-permute-start(bf16[2,32,512]{2,1,0:T(8,128)(2,1)S(1)} %pad_maximum_fusion.3), channel_id=1, source_target_pairs={{0,2},{1,3},{2,0},{3,1},{4,6},{5,7},{6,4},{7,5},{8,10},{9,11},{10,... | collective-permute-start | bytes 196616 | tf_op jit(solution)/shard_map/ppermute | solution.py:37
  17.8 19.7 %collective-permute-start.4 = (bf16[65,16,384]{2,1,0:T(8,128)(2,1)S(1)}, bf16[65,16,384]{2,1,0:T(8,128)(2,1)S(1)}, u32[]{:S(2)}, u32[]{:S(2)}) collective-permute-start(bf16[65,16,384]{2,1,0:T(8,128)(2,1)S(1)} %get-tuple-element.63), channel_id=1, source_target_pairs={{0,8},{1,9},{2,10},{3,11},{4,12},{5,13},{6,14},{7,15},{8,0},{9,1},... | collective-permute-start | bytes 2396168 | tf_op jit(solution)/shard_map/ppermute | solution.py:37
  19.5 18.0 %collective-permute-start.3 = (bf16[65,16,384]{2,1,0:T(8,128)(2,1)S(1)}, bf16[65,16,384]{2,1,0:T(8,128)(2,1)S(1)}, u32[]{:S(2)}, u32[]{:S(2)}) collective-permute-start(bf16[65,16,384]{2,1,0:T(8,128)(2,1)S(1)} %get-tuple-element.62), channel_id=1, source_target_pairs={{0,16},{1,17},{2,18},{3,19},{4,20},{5,21},{6,22},{7,23},{8,24},{9,... | collective-permute-start | bytes 2396168 | tf_op jit(solution)/shard_map/ppermute | solution.py:37
  21.0 16.5 %collective-permute-start.5 = (bf16[97,32,128]{2,1,0:T(8,128)(2,1)S(1)}, bf16[97,32,128]{2,1,0:T(8,128)(2,1)S(1)}, u32[]{:S(2)}, u32[]{:S(2)}) collective-permute-start(bf16[97,32,128]{2,1,0:T(8,128)(2,1)S(1)} %get-tuple-element.64), channel_id=1, source_target_pairs={{0,1},{1,0},{2,3},{3,2},{4,5},{5,4},{6,7},{7,6},{8,9},{9,8},{10,11... | collective-permute-start | bytes 2383880 | tf_op jit(solution)/shard_map/ppermute | solution.py:37
  22.0 7.7 %collective-permute-start.8 = (bf16[4,32,512]{2,1,0:T(8,128)(2,1)S(1)}, bf16[4,32,512]{2,1,0:T(8,128)(2,1)S(1)}, u32[]{:S(2)}, u32[]{:S(2)}) collective-permute-start(bf16[4,32,512]{2,1,0:T(8,128)(2,1)S(1)} %pad_maximum_fusion.2), channel_id=1, source_target_pairs={{0,136},{1,137},{2,138},{3,139},{4,140},{5,141},{6,142},{7,143},{8... | collective-permute-start | bytes 393224 | tf_op jit(solution)/shard_map/ppermute | solution.py:37
  29.8 7.7 %collective-permute-start.9 = (bf16[8,32,512]{2,1,0:T(8,128)(2,1)S(1)}, bf16[8,32,512]{2,1,0:T(8,128)(2,1)S(1)}, u32[]{:S(2)}, u32[]{:S(2)}) collective-permute-start(bf16[8,32,512]{2,1,0:T(8,128)(2,1)S(1)} %pad_maximum_fusion.1), channel_id=1, source_target_pairs={{0,48},{1,49},{2,50},{3,51},{4,52},{5,53},{6,54},{7,55},{8,56},{9,... | collective-permute-start | bytes 786440 | tf_op jit(solution)/shard_map/ppermute | solution.py:37
  37.6 10.0 %collective-permute-start.14 = (bf16[72,32,128]{2,1,0:T(8,128)(2,1)S(1)}, bf16[72,32,128]{2,1,0:T(8,128)(2,1)S(1)}, u32[]{:S(2)}, u32[]{:S(2)}) collective-permute-start(bf16[72,32,128]{2,1,0:T(8,128)(2,1)S(1)} %get-tuple-element.82.sent), channel_id=1, source_target_pairs={{0,16},{1,17},{2,18},{3,19},{4,20},{5,21},{6,22},{7,23},{8,24},{9,... | collective-permute-start | bytes 1769480 | tf_op jit(solution)/shard_map/ppermute | solution.py:37
  37.9 10.0 %collective-permute-start.10 = (bf16[48,16,384]{2,1,0:T(8,128)(2,1)S(1)}, bf16[48,16,384]{2,1,0:T(8,128)(2,1)S(1)}, u32[]{:S(2)}, u32[]{:S(2)}) collective-permute-start(bf16[48,16,384]{2,1,0:T(8,128)(2,1)S(1)} %get-tuple-element.72.sent), channel_id=1, source_target_pairs={{0,8},{1,9},{2,10},{3,11},{4,12},{5,13},{6,14},{7,15},{8,0},{9,1},... | collective-permute-start | bytes 1769480 | tf_op jit(solution)/shard_map/ppermute | solution.py:37
  38.2 10.9 %collective-permute-start.12 = (bf16[48,16,384]{2,1,0:T(8,128)(2,1)S(1)}, bf16[48,16,384]{2,1,0:T(8,128)(2,1)S(1)}, u32[]{:S(2)}, u32[]{:S(2)}) collective-permute-start(bf16[48,16,384]{2,1,0:T(8,128)(2,1)S(1)} %get-tuple-element.77.sent), channel_id=1, source_target_pairs={{0,1},{1,0},{2,3},{3,2},{4,5},{5,4},{6,7},{7,6},{8,9},{9,8},{10,11... | collective-permute-start | bytes 1769480 | tf_op jit(solution)/shard_map/ppermute | solution.py:37
  47.7 10.0 %collective-permute-start.15 = (bf16[72,32,128]{2,1,0:T(8,128)(2,1)S(1)}, bf16[72,32,128]{2,1,0:T(8,128)(2,1)S(1)}, u32[]{:S(2)}, u32[]{:S(2)}) collective-permute-start(bf16[72,32,128]{2,1,0:T(8,128)(2,1)S(1)} %get-tuple-element.84.sent), channel_id=1, source_target_pairs={{0,8},{1,9},{2,10},{3,11},{4,12},{5,13},{6,14},{7,15},{8,0},{9,1},... | collective-permute-start | bytes 1769480 | tf_op jit(solution)/shard_map/ppermute | solution.py:37
  48.0 10.8 %collective-permute-start.11 = (bf16[48,16,384]{2,1,0:T(8,128)(2,1)S(1)}, bf16[48,16,384]{2,1,0:T(8,128)(2,1)S(1)}, u32[]{:S(2)}, u32[]{:S(2)}) collective-permute-start(bf16[48,16,384]{2,1,0:T(8,128)(2,1)S(1)} %get-tuple-element.74.sent), channel_id=1, source_target_pairs={{0,1},{1,0},{2,3},{3,2},{4,5},{5,4},{6,7},{7,6},{8,9},{9,8},{10,11... | collective-permute-start | bytes 1769480 | tf_op jit(solution)/shard_map/ppermute | solution.py:37
  49.2 10.9 %collective-permute-start.13 = (bf16[48,16,384]{2,1,0:T(8,128)(2,1)S(1)}, bf16[48,16,384]{2,1,0:T(8,128)(2,1)S(1)}, u32[]{:S(2)}, u32[]{:S(2)}) collective-permute-start(bf16[48,16,384]{2,1,0:T(8,128)(2,1)S(1)} %get-tuple-element.79.sent), channel_id=1, source_target_pairs={{0,16},{1,17},{2,18},{3,19},{4,20},{5,21},{6,22},{7,23},{8,24},{9,... | collective-permute-start | bytes 1769480 | tf_op jit(solution)/shard_map/ppermute | solution.py:37
  57.7 22.9 %collective-permute-start.23 = (bf16[96,32,128]{2,1,0:T(8,128)(2,1)S(1)}, bf16[96,32,128]{2,1,0:T(8,128)(2,1)S(1)}, u32[]{:S(2)}, u32[]{:S(2)}) collective-permute-start(bf16[96,32,128]{2,1,0:T(8,128)(2,1)S(1)} %shard_map.115.sz), channel_id=1, source_target_pairs={{0,1},{1,0},{2,3},{3,2},{4,5},{5,4},{6,7},{7,6},{8,9},{9,8},{10,11... | collective-permute-start | bytes 2359304 | tf_op jit(solution)/shard_map/ppermute | solution.py:37
  58.9 21.7 %collective-permute-start.21 = (bf16[64,16,384]{2,1,0:T(8,128)(2,1)S(1)}, bf16[64,16,384]{2,1,0:T(8,128)(2,1)S(1)}, u32[]{:S(2)}, u32[]{:S(2)}) collective-permute-start(bf16[64,16,384]{2,1,0:T(8,128)(2,1)S(1)} %shard_map.113.sx), channel_id=1, source_target_pairs={{0,16},{1,17},{2,18},{3,19},{4,20},{5,21},{6,22},{7,23},{8,24},{9,... | collective-permute-start | bytes 2359304 | tf_op jit(solution)/shard_map/ppermute | solution.py:37
  60.2 20.4 %collective-permute-start.22 = (bf16[64,16,384]{2,1,0:T(8,128)(2,1)S(1)}, bf16[64,16,384]{2,1,0:T(8,128)(2,1)S(1)}, u32[]{:S(2)}, u32[]{:S(2)}) collective-permute-start(bf16[64,16,384]{2,1,0:T(8,128)(2,1)S(1)} %shard_map.114.sy), channel_id=1, source_target_pairs={{0,8},{1,9},{2,10},{3,11},{4,12},{5,13},{6,14},{7,15},{8,0},{9,1},... | collective-permute-start | bytes 2359304 | tf_op jit(solution)/shard_map/ppermute | solution.py:37
  61.3 7.7 %collective-permute-start.16 = (bf16[4,32,512]{2,1,0:T(8,128)(2,1)S(1)}, bf16[4,32,512]{2,1,0:T(8,128)(2,1)S(1)}, u32[]{:S(2)}, u32[]{:S(2)}) collective-permute-start(bf16[4,32,512]{2,1,0:T(8,128)(2,1)S(1)} %get-tuple-element.88), channel_id=1, source_target_pairs={{0,48},{1,49},{2,50},{3,51},{4,52},{5,53},{6,54},{7,55},{8,56},{9,... | collective-permute-start | bytes 393224 | tf_op jit(solution)/shard_map/ppermute | solution.py:37
  63.5 7.6 %collective-permute-start.17 = (bf16[4,32,512]{2,1,0:T(8,128)(2,1)S(1)}, bf16[4,32,512]{2,1,0:T(8,128)(2,1)S(1)}, u32[]{:S(2)}, u32[]{:S(2)}) collective-permute-start(bf16[4,32,512]{2,1,0:T(8,128)(2,1)S(1)} %get-tuple-element.89), channel_id=1, source_target_pairs={{0,136},{1,137},{2,138},{3,139},{4,140},{5,141},{6,142},{7,143},{8... | collective-permute-start | bytes 393224 | tf_op jit(solution)/shard_map/ppermute | solution.py:37
  71.2 5.6 %collective-permute-start.18 = (bf16[2,32,512]{2,1,0:T(8,128)(2,1)S(1)}, bf16[2,32,512]{2,1,0:T(8,128)(2,1)S(1)}, u32[]{:S(2)}, u32[]{:S(2)}) collective-permute-start(bf16[2,32,512]{2,1,0:T(8,128)(2,1)S(1)} %get-tuple-element.92), channel_id=1, source_target_pairs={{0,136},{1,137},{2,138},{3,139},{4,140},{5,141},{6,142},{7,143},{8... | collective-permute-start | bytes 196616 | tf_op jit(solution)/shard_map/ppermute | solution.py:37
  73.5 5.5 %collective-permute-start.19 = (bf16[2,32,512]{2,1,0:T(8,128)(2,1)S(1)}, bf16[2,32,512]{2,1,0:T(8,128)(2,1)S(1)}, u32[]{:S(2)}, u32[]{:S(2)}) collective-permute-start(bf16[2,32,512]{2,1,0:T(8,128)(2,1)S(1)} %get-tuple-element.93), channel_id=1, source_target_pairs={{0,48},{1,49},{2,50},{3,51},{4,52},{5,53},{6,54},{7,55},{8,56},{9,... | collective-permute-start | bytes 196616 | tf_op jit(solution)/shard_map/ppermute | solution.py:37
  79.0 6.0 %collective-permute-start.20 = (bf16[2,32,512]{2,1,0:T(8,128)(2,1)S(1)}, bf16[2,32,512]{2,1,0:T(8,128)(2,1)S(1)}, u32[]{:S(2)}, u32[]{:S(2)}) collective-permute-start(bf16[2,32,512]{2,1,0:T(8,128)(2,1)S(1)} %get-tuple-element.95), channel_id=1, source_target_pairs={{0,2},{1,3},{2,0},{3,1},{4,6},{5,7},{6,4},{7,5},{8,10},{9,11},{10,... | collective-permute-start | bytes 196616 | tf_op jit(solution)/shard_map/ppermute | solution.py:37
  85.0 6.2 %collective-permute-start.25 = (bf16[2,256,512]{2,1,0:T(8,128)(2,1)S(1)}, bf16[2,256,512]{2,1,0:T(8,128)(2,1)S(1)}, u32[]{:S(2)}, u32[]{:S(2)}) collective-permute-start(bf16[2,256,512]{2,1,0:T(8,128)(2,1)S(1)} %get-tuple-element.104), channel_id=1, source_target_pairs={{0,64},{1,65},{2,66},{3,67},{4,68},{5,69},{6,70},{7,71},{8,72},{9,... | collective-permute-start | bytes 1572872 | tf_op jit(solution)/shard_map/ppermute | solution.py:37
  85.1 6.1 %collective-permute-start.24 = (bf16[32,512]{1,0:T(8,128)(2,1)S(1)}, bf16[32,512]{1,0:T(8,128)(2,1)S(1)}, u32[]{:S(2)}, u32[]{:S(2)}) collective-permute-start(bf16[32,512]{1,0:T(8,128)(2,1)S(1)} %get-tuple-element.100), channel_id=1, source_target_pairs={{0,6},{1,7},{2,4},{3,5},{4,2},{5,3},{6,0},{7,1},{8,14},{9,15},{10,... | collective-permute-start | bytes 98312 | tf_op jit(solution)/shard_map/ppermute | solution.py:37

commit v8 on v7

--- a/solution.py
+++ b/solution.py
@@ -16,11 +16,11 @@
 
 
 STREAMS = ((16, 384), (16, 384), (32, 128))
-AXES = ((0, 1, 2), (1, 2, 0), (2, 0, 1))
+AXES = ((2, 0, 1), (1, 2, 0), (0, 1, 2))
 
 
 def message(n, stream):
-    return (n + n // 2 if stream == 2 else n, *STREAMS[stream]), BF16
+    return (n + n // 2 if stream == 2 and n == 48 else n, *STREAMS[stream]), BF16
 
 
 def place(x, y, z, c):

time: 93.3 us -> 92.5 us (level)
  waiting for transfers between devices: 36.7 us -> 35.6 us
    ppermute x26, waiting for transfers between devices: 36.7 us -> 35.6 us  [permute(): return lax.ppermute(value, ALL, pairs)]
  transfers between devices with their start and end apart: 26 -> 26, of which waited for: 11 -> 12; matrix products, arithmetic and copies ran while one was open for 0% -> 0% of each run, Pallas kernels for 15% -> 15%
where the time goes in v8:
time: 92.5 us; the launch traced here: 91.6 us
  starting transfers between devices  36.4 us (39%)
  waiting for transfers between devices  35.6 us (38%)
  Pallas kernels  18.5 us (20%)
    ppermute x26, starting transfers between devices, permute(): return lax.ppermute(value, ALL, pairs)  36.4 us
    ppermute x26, waiting for transfers between devices, permute(): return lax.ppermute(value, ALL, pairs)  35.6 us
    pallas_call x1, Pallas kernels, first(): pl.pallas_call(first_kernel, in_specs=[SMEM] + [HBM] * 6, out_specs=[VMEM...  3.99 us
    pallas_call x1, Pallas kernels, other_values(): pl.pallas_call(other_kernel, in_specs=[SMEM] + [VMEM] * 8, out_specs=[VME...  3.44 us
    pallas_call x1, Pallas kernels, all_terms(): pl.pallas_call(terms_kernel, in_specs=[SMEM] + [VMEM] * 4, out_specs=[VME...  3.26 us
    pallas_call x1, Pallas kernels, own_terms(): pl.pallas_call(own_kernel, in_specs=[SMEM, VMEM, VMEM], out_specs=VMEM, o...  2.92 us
    pallas_call x1, Pallas kernels, my_values(): pl.pallas_call(mine_kernel, in_specs=[SMEM, VMEM, VMEM], out_specs=VMEM,...  2.85 us
    pallas_call x14, Pallas kernels, call(): pl.pallas_call(kernel, out_shape=[jax.ShapeDtypeStruct(*o) for o in outs]...  2.07 us
  transfers between devices with their start and end apart: 26, of which 12 were waited for; matrix products, arithmetic and copies ran while one was open for 0% of the time, Pallas kernels for 15%

profile of v8, /device:TPU:0, one launch (start us, length us, event | category | flops | bytes accessed | tf_op | source)
XLA Modules:
  0.0 91.6 jit_solution(11872859267906157107)
XLA Ops:
  0.8 4.0 %shard_map.101 = (bf16[2,256,2048]{2,1,0:T(8,128)(2,1)S(1)}, bf16[2,256,2048]{2,1,0:T(8,128)(2,1)S(1)}, bf16[2,256,512]{2,1,0:T(8,128)(2,1)S(1)}, bf16[32,512]{1...) custom-call(s32[4]{0:T(128)S(1)} %pad_add_fusion.me, bf16[2,256,8192]{2,1,0:T(8,128)(2,1)} %tokens.5, ...), custom_call_target="tpu_custom_call" | custom-call | tf_op jit(solution)/shard_map/pallas_call | solution.py:150
  4.8 0.1 collective-permute-start
  4.9 0.5 collective-permute-start.1
  5.4 0.1 collective-permute-start.2
  5.5 4.6 %collective-permute-start.6 = (bf16[32,512]{1,0:T(8,128)(2,1)S(1)}, bf16[32,512]{1,0:T(8,128)(2,1)S(1)}, u32[]{:S(2)}, u32[]{:S(2)}) collective-permute-start(bf16[32,512]{1,0:T(8,128)(2,1)S(1)} %get-tuple-element.66), channel_id=1, source_target_pairs={{0,6},{1,7},{2,4},{3,5},{4,2},{5,3},{6,0},{7,1},{8,14},{9,15},{10,... | collective-permute-start | bytes 98312 | tf_op jit(solution)/shard_map/ppermute | solution.py:37
  10.0 2.9 %shard_map.102.mine = f32[8,512,512]{2,1,0:T(8,128)S(1)} custom-call(s32[4]{0:T(128)S(1)} %pad_add_fusion.me, bf16[2,256,8192]{2,1,0:T(8,128)(2,1)S(1)} %copy-done, bf16[2,256,512]{2,1,0:T(8,128)(2,1)S(1)} %get-tuple-element.61.cot), custom_call_target="tpu_custom_call" | custom-call | tf_op jit(solution)/shard_map/pallas_call | solution.py:175
  13.0 1.5 %collective-permute-start.7 = (bf16[2,32,512]{2,1,0:T(8,128)(2,1)S(1)}, bf16[2,32,512]{2,1,0:T(8,128)(2,1)S(1)}, u32[]{:S(2)}, u32[]{:S(2)}) collective-permute-start(bf16[2,32,512]{2,1,0:T(8,128)(2,1)S(1)} %pad_maximum_fusion.3), channel_id=1, source_target_pairs={{0,2},{1,3},{2,0},{3,1},{4,6},{5,7},{6,4},{7,5},{8,10},{9,11},{10,... | collective-permute-start | bytes 196616 | tf_op jit(solution)/shard_map/ppermute | solution.py:37
  14.5 3.3 %shard_map.103 = (bf16[65,16,384]{2,1,0:T(8,128)(2,1)S(1)}, bf16[65,16,384]{2,1,0:T(8,128)(2,1)S(1)}, bf16[65,32,128]{2,1,0:T(8,128)(2,1)S(1)}, f32[65,16,384]{2...) custom-call(s32[4]{0:T(128)S(1)} %pad_add_fusion.me, ...), custom_call_target="tpu_custom_call" | custom-call | tf_op jit(solution)/shard_map/pallas_call | solution.py:206
  17.8 1.7 %collective-permute-start.4 = (bf16[65,16,384]{2,1,0:T(8,128)(2,1)S(1)}, bf16[65,16,384]{2,1,0:T(8,128)(2,1)S(1)}, u32[]{:S(2)}, u32[]{:S(2)}) collective-permute-start(bf16[65,16,384]{2,1,0:T(8,128)(2,1)S(1)} %get-tuple-element.63), channel_id=1, source_target_pairs={{0,8},{1,9},{2,10},{3,11},{4,12},{5,13},{6,14},{7,15},{8,0},{9,1},... | collective-permute-start | bytes 2396168 | tf_op jit(solution)/shard_map/ppermute | solution.py:37
  19.5 1.0 %collective-permute-start.3 = (bf16[65,16,384]{2,1,0:T(8,128)(2,1)S(1)}, bf16[65,16,384]{2,1,0:T(8,128)(2,1)S(1)}, u32[]{:S(2)}, u32[]{:S(2)}) collective-permute-start(bf16[65,16,384]{2,1,0:T(8,128)(2,1)S(1)} %get-tuple-element.62), channel_id=1, source_target_pairs={{0,1},{1,0},{2,3},{3,2},{4,5},{5,4},{6,7},{7,6},{8,9},{9,8},{10,11... | collective-permute-start | bytes 2396168 | tf_op jit(solution)/shard_map/ppermute | solution.py:37
  20.5 2.3 %collective-permute-start.8 = (bf16[4,32,512]{2,1,0:T(8,128)(2,1)S(1)}, bf16[4,32,512]{2,1,0:T(8,128)(2,1)S(1)}, u32[]{:S(2)}, u32[]{:S(2)}) collective-permute-start(bf16[4,32,512]{2,1,0:T(8,128)(2,1)S(1)} %pad_maximum_fusion.2), channel_id=1, source_target_pairs={{0,136},{1,137},{2,138},{3,139},{4,140},{5,141},{6,142},{7,143},{8... | collective-permute-start | bytes 393224 | tf_op jit(solution)/shard_map/ppermute | solution.py:37
  22.8 1.5 %collective-permute-start.5 = (bf16[65,32,128]{2,1,0:T(8,128)(2,1)S(1)}, bf16[65,32,128]{2,1,0:T(8,128)(2,1)S(1)}, u32[]{:S(2)}, u32[]{:S(2)}) collective-permute-start(bf16[65,32,128]{2,1,0:T(8,128)(2,1)S(1)} %get-tuple-element.64), channel_id=1, source_target_pairs={{0,16},{1,17},{2,18},{3,19},{4,20},{5,21},{6,22},{7,23},{8,24},{9,... | collective-permute-start | bytes 1597448 | tf_op jit(solution)/shard_map/ppermute | solution.py:37
  24.3 4.0 %collective-permute-done.8 = bf16[4,32,512]{2,1,0:T(8,128)(2,1)S(1)} collective-permute-done((bf16[4,32,512]{2,1,0:T(8,128)(2,1)S(1)}, bf16[4,32,512]{2,1,0:T(8,128)(2,1)S(1)}, u32[]{:S(2)}, u32[]{:S(2)}) %collective-permute-start.8) | collective-permute-done | bytes 131104 | tf_op jit(solution)/shard_map/ppermute | solution.py:37
  28.3 2.8 %collective-permute-start.9 = (bf16[8,32,512]{2,1,0:T(8,128)(2,1)S(1)}, bf16[8,32,512]{2,1,0:T(8,128)(2,1)S(1)}, u32[]{:S(2)}, u32[]{:S(2)}) collective-permute-start(bf16[8,32,512]{2,1,0:T(8,128)(2,1)S(1)} %pad_maximum_fusion.1), channel_id=1, source_target_pairs={{0,48},{1,49},{2,50},{3,51},{4,52},{5,53},{6,54},{7,55},{8,56},{9,... | collective-permute-start | bytes 786440 | tf_op jit(solution)/shard_map/ppermute | solution.py:37
  31.1 4.8 %collective-permute-done.9 = bf16[8,32,512]{2,1,0:T(8,128)(2,1)S(1)} collective-permute-done((bf16[8,32,512]{2,1,0:T(8,128)(2,1)S(1)}, bf16[8,32,512]{2,1,0:T(8,128)(2,1)S(1)}, u32[]{:S(2)}, u32[]{:S(2)}) %collective-permute-start.9) | collective-permute-done | bytes 262176 | tf_op jit(solution)/shard_map/ppermute | solution.py:37
  36.0 0.2 shard_map.104
  36.2 0.4 collective-permute-start.10
  36.6 0.2 shard_map.106
  36.8 1.1 %collective-permute-start.12 = (bf16[48,16,384]{2,1,0:T(8,128)(2,1)S(1)}, bf16[48,16,384]{2,1,0:T(8,128)(2,1)S(1)}, u32[]{:S(2)}, u32[]{:S(2)}) collective-permute-start(bf16[48,16,384]{2,1,0:T(8,128)(2,1)S(1)} %get-tuple-element.77.sent), channel_id=1, source_target_pairs={{0,1},{1,0},{2,3},{3,2},{4,5},{5,4},{6,7},{7,6},{8,9},{9,8},{10,11... | collective-permute-start | bytes 1769480 | tf_op jit(solution)/shard_map/ppermute | solution.py:37
  37.9 0.1 shard_map.108
  38.0 1.0 %collective-permute-start.14 = (bf16[72,32,128]{2,1,0:T(8,128)(2,1)S(1)}, bf16[72,32,128]{2,1,0:T(8,128)(2,1)S(1)}, u32[]{:S(2)}, u32[]{:S(2)}) collective-permute-start(bf16[72,32,128]{2,1,0:T(8,128)(2,1)S(1)} %get-tuple-element.82.sent), channel_id=1, source_target_pairs={{0,8},{1,9},{2,10},{3,11},{4,12},{5,13},{6,14},{7,15},{8,0},{9,1},... | collective-permute-start | bytes 1769480 | tf_op jit(solution)/shard_map/ppermute | solution.py:37
  39.0 7.2 %collective-permute-done.10.got = bf16[48,16,384]{2,1,0:T(8,128)(2,1)S(1)} collective-permute-done((bf16[48,16,384]{2,1,0:T(8,128)(2,1)S(1)}, bf16[48,16,384]{2,1,0:T(8,128)(2,1)S(1)}, u32[]{:S(2)}, u32[]{:S(2)}) %collective-permute-start.10) | collective-permute-done | bytes 589856 | tf_op jit(solution)/shard_map/ppermute | solution.py:37
  46.2 0.1 shard_map.105
  46.3 1.1 %collective-permute-start.11 = (bf16[48,16,384]{2,1,0:T(8,128)(2,1)S(1)}, bf16[48,16,384]{2,1,0:T(8,128)(2,1)S(1)}, u32[]{:S(2)}, u32[]{:S(2)}) collective-permute-start(bf16[48,16,384]{2,1,0:T(8,128)(2,1)S(1)} %get-tuple-element.74.sent), channel_id=1, source_target_pairs={{0,8},{1,9},{2,10},{3,11},{4,12},{5,13},{6,14},{7,15},{8,0},{9,1},... | collective-permute-start | bytes 1769480 | tf_op jit(solution)/shard_map/ppermute | solution.py:37
  47.4 0.1 shard_map.107
  47.6 1.1 %collective-permute-start.13 = (bf16[48,16,384]{2,1,0:T(8,128)(2,1)S(1)}, bf16[48,16,384]{2,1,0:T(8,128)(2,1)S(1)}, u32[]{:S(2)}, u32[]{:S(2)}) collective-permute-start(bf16[48,16,384]{2,1,0:T(8,128)(2,1)S(1)} %get-tuple-element.79.sent), channel_id=1, source_target_pairs={{0,16},{1,17},{2,18},{3,19},{4,20},{5,21},{6,22},{7,23},{8,24},{9,... | collective-permute-start | bytes 1769480 | tf_op jit(solution)/shard_map/ppermute | solution.py:37
  48.8 1.1 %collective-permute-start.15 = (bf16[72,32,128]{2,1,0:T(8,128)(2,1)S(1)}, bf16[72,32,128]{2,1,0:T(8,128)(2,1)S(1)}, u32[]{:S(2)}, u32[]{:S(2)}) collective-permute-start(bf16[72,32,128]{2,1,0:T(8,128)(2,1)S(1)} %get-tuple-element.84.sent), channel_id=1, source_target_pairs={{0,1},{1,0},{2,3},{3,2},{4,5},{5,4},{6,7},{7,6},{8,9},{9,8},{10,11... | collective-permute-start | bytes 1769480 | tf_op jit(solution)/shard_map/ppermute | solution.py:37
  49.9 6.4 %collective-permute-done.11.gx.got = bf16[48,16,384]{2,1,0:T(8,128)(2,1)S(1)} collective-permute-done((bf16[48,16,384]{2,1,0:T(8,128)(2,1)S(1)}, bf16[48,16,384]{2,1,0:T(8,128)(2,1)S(1)}, u32[]{:S(2)}, u32[]{:S(2)}) %collective-permute-start.11) | collective-permute-done | bytes 589856 | tf_op jit(solution)/shard_map/ppermute | solution.py:37
  56.3 1.1 %collective-permute-start.21 = (bf16[64,16,384]{2,1,0:T(8,128)(2,1)S(1)}, bf16[64,16,384]{2,1,0:T(8,128)(2,1)S(1)}, u32[]{:S(2)}, u32[]{:S(2)}) collective-permute-start(bf16[64,16,384]{2,1,0:T(8,128)(2,1)S(1)} %shard_map.113.sx), channel_id=1, source_target_pairs={{0,1},{1,0},{2,3},{3,2},{4,5},{5,4},{6,7},{7,6},{8,9},{9,8},{10,11... | collective-permute-start | bytes 2359304 | tf_op jit(solution)/shard_map/ppermute | solution.py:37
  57.4 0.1 collective-permute-done.13.gy.got
  57.6 1.1 %collective-permute-start.22 = (bf16[64,16,384]{2,1,0:T(8,128)(2,1)S(1)}, bf16[64,16,384]{2,1,0:T(8,128)(2,1)S(1)}, u32[]{:S(2)}, u32[]{:S(2)}) collective-permute-start(bf16[64,16,384]{2,1,0:T(8,128)(2,1)S(1)} %shard_map.114.sy), channel_id=1, source_target_pairs={{0,8},{1,9},{2,10},{3,11},{4,12},{5,13},{6,14},{7,15},{8,0},{9,1},... | collective-permute-start | bytes 2359304 | tf_op jit(solution)/shard_map/ppermute | solution.py:37
  58.8 1.3 %collective-permute-start.23 = (bf16[64,32,128]{2,1,0:T(8,128)(2,1)S(1)}, bf16[64,32,128]{2,1,0:T(8,128)(2,1)S(1)}, u32[]{:S(2)}, u32[]{:S(2)}) collective-permute-start(bf16[64,32,128]{2,1,0:T(8,128)(2,1)S(1)} %shard_map.115.sz), channel_id=1, source_target_pairs={{0,16},{1,17},{2,18},{3,19},{4,20},{5,21},{6,22},{7,23},{8,24},{9,... | collective-permute-start | bytes 1572872 | tf_op jit(solution)/shard_map/ppermute | solution.py:37
  60.1 0.1 shard_map.110
  60.2 2.8 %collective-permute-start.16 = (bf16[4,32,512]{2,1,0:T(8,128)(2,1)S(1)}, bf16[4,32,512]{2,1,0:T(8,128)(2,1)S(1)}, u32[]{:S(2)}, u32[]{:S(2)}) collective-permute-start(bf16[4,32,512]{2,1,0:T(8,128)(2,1)S(1)} %get-tuple-element.88), channel_id=1, source_target_pairs={{0,48},{1,49},{2,50},{3,51},{4,52},{5,53},{6,54},{7,55},{8,56},{9,... | collective-permute-start | bytes 393224 | tf_op jit(solution)/shard_map/ppermute | solution.py:37
  63.0 2.2 %collective-permute-start.17 = (bf16[4,32,512]{2,1,0:T(8,128)(2,1)S(1)}, bf16[4,32,512]{2,1,0:T(8,128)(2,1)S(1)}, u32[]{:S(2)}, u32[]{:S(2)}) collective-permute-start(bf16[4,32,512]{2,1,0:T(8,128)(2,1)S(1)} %get-tuple-element.89), channel_id=1, source_target_pairs={{0,136},{1,137},{2,138},{3,139},{4,140},{5,141},{6,142},{7,143},{8... | collective-permute-start | bytes 393224 | tf_op jit(solution)/shard_map/ppermute | solution.py:37
  65.2 2.6 %collective-permute-done.16.g0 = bf16[4,32,512]{2,1,0:T(8,128)(2,1)S(1)} collective-permute-done((bf16[4,32,512]{2,1,0:T(8,128)(2,1)S(1)}, bf16[4,32,512]{2,1,0:T(8,128)(2,1)S(1)}, u32[]{:S(2)}, u32[]{:S(2)}) %collective-permute-start.16) | collective-permute-done | bytes 131104 | tf_op jit(solution)/shard_map/ppermute | solution.py:37
  67.8 2.8 %collective-permute-done.17.g1 = bf16[4,32,512]{2,1,0:T(8,128)(2,1)S(1)} collective-permute-done((bf16[4,32,512]{2,1,0:T(8,128)(2,1)S(1)}, bf16[4,32,512]{2,1,0:T(8,128)(2,1)S(1)}, u32[]{:S(2)}, u32[]{:S(2)}) %collective-permute-start.17) | collective-permute-done | bytes 131104 | tf_op jit(solution)/shard_map/ppermute | solution.py:37
  70.7 2.3 %collective-permute-start.18 = (bf16[2,32,512]{2,1,0:T(8,128)(2,1)S(1)}, bf16[2,32,512]{2,1,0:T(8,128)(2,1)S(1)}, u32[]{:S(2)}, u32[]{:S(2)}) collective-permute-start(bf16[2,32,512]{2,1,0:T(8,128)(2,1)S(1)} %get-tuple-element.92), channel_id=1, source_target_pairs={{0,136},{1,137},{2,138},{3,139},{4,140},{5,141},{6,142},{7,143},{8... | collective-permute-start | bytes 196616 | tf_op jit(solution)/shard_map/ppermute | solution.py:37
  73.0 0.5 collective-permute-start.19
  73.5 2.8 %collective-permute-done.18.g0 = bf16[2,32,512]{2,1,0:T(8,128)(2,1)S(1)} collective-permute-done((bf16[2,32,512]{2,1,0:T(8,128)(2,1)S(1)}, bf16[2,32,512]{2,1,0:T(8,128)(2,1)S(1)}, u32[]{:S(2)}, u32[]{:S(2)}) %collective-permute-start.18) | collective-permute-done | bytes 65568 | tf_op jit(solution)/shard_map/ppermute | solution.py:37
  76.3 2.2 %collective-permute-done.19.g1 = bf16[2,32,512]{2,1,0:T(8,128)(2,1)S(1)} collective-permute-done((bf16[2,32,512]{2,1,0:T(8,128)(2,1)S(1)}, bf16[2,32,512]{2,1,0:T(8,128)(2,1)S(1)}, u32[]{:S(2)}, u32[]{:S(2)}) %collective-permute-start.19) | collective-permute-done | bytes 65568 | tf_op jit(solution)/shard_map/ppermute | solution.py:37
  78.5 1.1 %collective-permute-start.20 = (bf16[2,32,512]{2,1,0:T(8,128)(2,1)S(1)}, bf16[2,32,512]{2,1,0:T(8,128)(2,1)S(1)}, u32[]{:S(2)}, u32[]{:S(2)}) collective-permute-start(bf16[2,32,512]{2,1,0:T(8,128)(2,1)S(1)} %get-tuple-element.95), channel_id=1, source_target_pairs={{0,2},{1,3},{2,0},{3,1},{4,6},{5,7},{6,4},{7,5},{8,10},{9,11},{10,... | collective-permute-start | bytes 196616 | tf_op jit(solution)/shard_map/ppermute | solution.py:37
  79.6 3.4 %shard_map.116 = (bf16[2,256,512]{2,1,0:T(8,128)(2,1)S(1)}, bf16[4096,512]{1,0:T(8,128)(2,1)S(1)}) custom-call(s32[4]{0:T(128)S(1)} %pad_add_fusion.me, bf16[2,256,2048]{2,1,0:T(8,128)(2,1)S(1)} %collective-permute-done.r0, bf16[2,256,2048]{2,1,0:T(8,128)(2,1)S(1)} %collective-permute-done.1.r1, bf16[64,16,384]{2,1,0:T(8,128)(2,1)S(1)} %shard_map.113.sx, ...), custom_call_target="tpu_custom_call" | custom-call | tf_op jit(solution)/shard_map/pallas_call | solution.py:320
  83.0 1.4 %collective-permute-done.20.got = bf16[2,32,512]{2,1,0:T(8,128)(2,1)S(1)} collective-permute-done((bf16[2,32,512]{2,1,0:T(8,128)(2,1)S(1)}, bf16[2,32,512]{2,1,0:T(8,128)(2,1)S(1)}, u32[]{:S(2)}, u32[]{:S(2)}) %collective-permute-start.20) | collective-permute-done | bytes 65568 | tf_op jit(solution)/shard_map/ppermute | solution.py:37
  84.5 2.1 %collective-permute-start.24 = (bf16[32,512]{1,0:T(8,128)(2,1)S(1)}, bf16[32,512]{1,0:T(8,128)(2,1)S(1)}, u32[]{:S(2)}, u32[]{:S(2)}) collective-permute-start(bf16[32,512]{1,0:T(8,128)(2,1)S(1)} %get-tuple-element.100), channel_id=1, source_target_pairs={{0,6},{1,7},{2,4},{3,5},{4,2},{5,3},{6,0},{7,1},{8,14},{9,15},{10,... | collective-permute-start | bytes 98312 | tf_op jit(solution)/shard_map/ppermute | solution.py:37
  86.7 2.9 %shard_map.118.mine = f32[2,256,512]{2,1,0:T(8,128)S(1)} custom-call(s32[4]{0:T(128)S(1)} %pad_add_fusion.me, bf16[2,256,8192]{2,1,0:T(8,128)(2,1)S(1)} %copy-done, bf16[4096,512]{1,0:T(8,128)(2,1)S(1)} %get-tuple-element.102.w), custom_call_target="tpu_custom_call" | custom-call | tf_op jit(solution)/shard_map/pallas_call | solution.py:304
  89.5 1.1 %collective-permute-done.24.got = bf16[32,512]{1,0:T(8,128)(2,1)S(1)} collective-permute-done((bf16[32,512]{1,0:T(8,128)(2,1)S(1)}, bf16[32,512]{1,0:T(8,128)(2,1)S(1)}, u32[]{:S(2)}, u32[]{:S(2)}) %collective-permute-start.24) | collective-permute-done | bytes 32800 | tf_op jit(solution)/shard_map/ppermute | solution.py:37
  90.7 0.9 %shard_map.119 = (f32[32,512]{1,0:T(8,128)}, bf16[2,256,512]{2,1,0:T(8,128)(2,1)}) custom-call(bf16[32,512]{1,0:T(8,128)(2,1)S(1)} %collective-permute-done.24.got, f32[32,512]{1,0:T(8,128)S(1)} %get-tuple-element.101.keep, f32[2,256,512]{2,1,0:T(8,128)S(1)} %shard_map.118.mine, bf16[2,256,512]{2,1,0:T(8,128)(2,1)S(1)} %collective-permute-done.25.other), custom_call_target="tpu_custom_call" | custom-call | tf_op jit(solution)/shard_map/pallas_call | solution.py:98
  (30 shorter events, 0.7 us)
Async XLA Ops:
  0.8 9.3 %copy-start = (bf16[2,256,8192]{2,1,0:T(8,128)(2,1)S(1)}, bf16[2,256,8192]{2,1,0:T(8,128)(2,1)}, u32[]{:S(2)}) copy-start(bf16[2,256,8192]{2,1,0:T(8,128)(2,1)} %tokens.5) | copy-start | bytes 25165828
  4.8 9.8 %collective-permute-start = (bf16[2,256,2048]{2,1,0:T(8,128)(2,1)S(1)}, bf16[2,256,2048]{2,1,0:T(8,128)(2,1)S(1)}, u32[]{:S(2)}, u32[]{:S(2)}) collective-permute-start(bf16[2,256,2048]{2,1,0:T(8,128)(2,1)S(1)} %get-tuple-element.59), channel_id=1, source_target_pairs={{0,64},{1,65},{2,66},{3,67},{4,68},{5,69},{6,70},{7,71},{8,72},{9,... | collective-permute-start | bytes 6291464 | tf_op jit(solution)/shard_map/ppermute | solution.py:37
  4.9 9.7 %collective-permute-start.1 = (bf16[2,256,2048]{2,1,0:T(8,128)(2,1)S(1)}, bf16[2,256,2048]{2,1,0:T(8,128)(2,1)S(1)}, u32[]{:S(2)}, u32[]{:S(2)}) collective-permute-start(bf16[2,256,2048]{2,1,0:T(8,128)(2,1)S(1)} %get-tuple-element.60), channel_id=1, source_target_pairs={{0,64},{1,65},{2,66},{3,67},{4,68},{5,69},{6,70},{7,71},{8,72},{9,... | collective-permute-start | bytes 6291464 | tf_op jit(solution)/shard_map/ppermute | solution.py:37
  5.4 9.2 %collective-permute-start.2 = (bf16[2,256,512]{2,1,0:T(8,128)(2,1)S(1)}, bf16[2,256,512]{2,1,0:T(8,128)(2,1)S(1)}, u32[]{:S(2)}, u32[]{:S(2)}) collective-permute-start(bf16[2,256,512]{2,1,0:T(8,128)(2,1)S(1)} %get-tuple-element.61.cot), channel_id=1, source_target_pairs={{0,64},{1,65},{2,66},{3,67},{4,68},{5,69},{6,70},{7,71},{8,72},{9,... | collective-permute-start | bytes 1572872 | tf_op jit(solution)/shard_map/ppermute | solution.py:37
  5.5 7.5 %collective-permute-start.6 = (bf16[32,512]{1,0:T(8,128)(2,1)S(1)}, bf16[32,512]{1,0:T(8,128)(2,1)S(1)}, u32[]{:S(2)}, u32[]{:S(2)}) collective-permute-start(bf16[32,512]{1,0:T(8,128)(2,1)S(1)} %get-tuple-element.66), channel_id=1, source_target_pairs={{0,6},{1,7},{2,4},{3,5},{4,2},{5,3},{6,0},{7,1},{8,14},{9,15},{10,... | collective-permute-start | bytes 98312 | tf_op jit(solution)/shard_map/ppermute | solution.py:37
  13.0 7.5 %collective-permute-start.7 = (bf16[2,32,512]{2,1,0:T(8,128)(2,1)S(1)}, bf16[2,32,512]{2,1,0:T(8,128)(2,1)S(1)}, u32[]{:S(2)}, u32[]{:S(2)}) collective-permute-start(bf16[2,32,512]{2,1,0:T(8,128)(2,1)S(1)} %pad_maximum_fusion.3), channel_id=1, source_target_pairs={{0,2},{1,3},{2,0},{3,1},{4,6},{5,7},{6,4},{7,5},{8,10},{9,11},{10,... | collective-permute-start | bytes 196616 | tf_op jit(solution)/shard_map/ppermute | solution.py:37
  17.8 18.2 %collective-permute-start.4 = (bf16[65,16,384]{2,1,0:T(8,128)(2,1)S(1)}, bf16[65,16,384]{2,1,0:T(8,128)(2,1)S(1)}, u32[]{:S(2)}, u32[]{:S(2)}) collective-permute-start(bf16[65,16,384]{2,1,0:T(8,128)(2,1)S(1)} %get-tuple-element.63), channel_id=1, source_target_pairs={{0,8},{1,9},{2,10},{3,11},{4,12},{5,13},{6,14},{7,15},{8,0},{9,1},... | collective-permute-start | bytes 2396168 | tf_op jit(solution)/shard_map/ppermute | solution.py:37
  19.5 16.5 %collective-permute-start.3 = (bf16[65,16,384]{2,1,0:T(8,128)(2,1)S(1)}, bf16[65,16,384]{2,1,0:T(8,128)(2,1)S(1)}, u32[]{:S(2)}, u32[]{:S(2)}) collective-permute-start(bf16[65,16,384]{2,1,0:T(8,128)(2,1)S(1)} %get-tuple-element.62), channel_id=1, source_target_pairs={{0,1},{1,0},{2,3},{3,2},{4,5},{5,4},{6,7},{7,6},{8,9},{9,8},{10,11... | collective-permute-start | bytes 2396168 | tf_op jit(solution)/shard_map/ppermute | solution.py:37
  20.5 7.7 %collective-permute-start.8 = (bf16[4,32,512]{2,1,0:T(8,128)(2,1)S(1)}, bf16[4,32,512]{2,1,0:T(8,128)(2,1)S(1)}, u32[]{:S(2)}, u32[]{:S(2)}) collective-permute-start(bf16[4,32,512]{2,1,0:T(8,128)(2,1)S(1)} %pad_maximum_fusion.2), channel_id=1, source_target_pairs={{0,136},{1,137},{2,138},{3,139},{4,140},{5,141},{6,142},{7,143},{8... | collective-permute-start | bytes 393224 | tf_op jit(solution)/shard_map/ppermute | solution.py:37
  22.8 13.2 %collective-permute-start.5 = (bf16[65,32,128]{2,1,0:T(8,128)(2,1)S(1)}, bf16[65,32,128]{2,1,0:T(8,128)(2,1)S(1)}, u32[]{:S(2)}, u32[]{:S(2)}) collective-permute-start(bf16[65,32,128]{2,1,0:T(8,128)(2,1)S(1)} %get-tuple-element.64), channel_id=1, source_target_pairs={{0,16},{1,17},{2,18},{3,19},{4,20},{5,21},{6,22},{7,23},{8,24},{9,... | collective-permute-start | bytes 1597448 | tf_op jit(solution)/shard_map/ppermute | solution.py:37
  28.3 7.7 %collective-permute-start.9 = (bf16[8,32,512]{2,1,0:T(8,128)(2,1)S(1)}, bf16[8,32,512]{2,1,0:T(8,128)(2,1)S(1)}, u32[]{:S(2)}, u32[]{:S(2)}) collective-permute-start(bf16[8,32,512]{2,1,0:T(8,128)(2,1)S(1)} %pad_maximum_fusion.1), channel_id=1, source_target_pairs={{0,48},{1,49},{2,50},{3,51},{4,52},{5,53},{6,54},{7,55},{8,56},{9,... | collective-permute-start | bytes 786440 | tf_op jit(solution)/shard_map/ppermute | solution.py:37
  36.2 10.0 %collective-permute-start.10 = (bf16[48,16,384]{2,1,0:T(8,128)(2,1)S(1)}, bf16[48,16,384]{2,1,0:T(8,128)(2,1)S(1)}, u32[]{:S(2)}, u32[]{:S(2)}) collective-permute-start(bf16[48,16,384]{2,1,0:T(8,128)(2,1)S(1)} %get-tuple-element.72.sent), channel_id=1, source_target_pairs={{0,16},{1,17},{2,18},{3,19},{4,20},{5,21},{6,22},{7,23},{8,24},{9,... | collective-permute-start | bytes 1769480 | tf_op jit(solution)/shard_map/ppermute | solution.py:37
  36.8 10.7 %collective-permute-start.12 = (bf16[48,16,384]{2,1,0:T(8,128)(2,1)S(1)}, bf16[48,16,384]{2,1,0:T(8,128)(2,1)S(1)}, u32[]{:S(2)}, u32[]{:S(2)}) collective-permute-start(bf16[48,16,384]{2,1,0:T(8,128)(2,1)S(1)} %get-tuple-element.77.sent), channel_id=1, source_target_pairs={{0,1},{1,0},{2,3},{3,2},{4,5},{5,4},{6,7},{7,6},{8,9},{9,8},{10,11... | collective-permute-start | bytes 1769480 | tf_op jit(solution)/shard_map/ppermute | solution.py:37
  38.0 10.7 %collective-permute-start.14 = (bf16[72,32,128]{2,1,0:T(8,128)(2,1)S(1)}, bf16[72,32,128]{2,1,0:T(8,128)(2,1)S(1)}, u32[]{:S(2)}, u32[]{:S(2)}) collective-permute-start(bf16[72,32,128]{2,1,0:T(8,128)(2,1)S(1)} %get-tuple-element.82.sent), channel_id=1, source_target_pairs={{0,8},{1,9},{2,10},{3,11},{4,12},{5,13},{6,14},{7,15},{8,0},{9,1},... | collective-permute-start | bytes 1769480 | tf_op jit(solution)/shard_map/ppermute | solution.py:37
  46.3 10.0 %collective-permute-start.11 = (bf16[48,16,384]{2,1,0:T(8,128)(2,1)S(1)}, bf16[48,16,384]{2,1,0:T(8,128)(2,1)S(1)}, u32[]{:S(2)}, u32[]{:S(2)}) collective-permute-start(bf16[48,16,384]{2,1,0:T(8,128)(2,1)S(1)} %get-tuple-element.74.sent), channel_id=1, source_target_pairs={{0,8},{1,9},{2,10},{3,11},{4,12},{5,13},{6,14},{7,15},{8,0},{9,1},... | collective-permute-start | bytes 1769480 | tf_op jit(solution)/shard_map/ppermute | solution.py:37
  47.6 10.0 %collective-permute-start.13 = (bf16[48,16,384]{2,1,0:T(8,128)(2,1)S(1)}, bf16[48,16,384]{2,1,0:T(8,128)(2,1)S(1)}, u32[]{:S(2)}, u32[]{:S(2)}) collective-permute-start(bf16[48,16,384]{2,1,0:T(8,128)(2,1)S(1)} %get-tuple-element.79.sent), channel_id=1, source_target_pairs={{0,16},{1,17},{2,18},{3,19},{4,20},{5,21},{6,22},{7,23},{8,24},{9,... | collective-permute-start | bytes 1769480 | tf_op jit(solution)/shard_map/ppermute | solution.py:37
  48.8 10.0 %collective-permute-start.15 = (bf16[72,32,128]{2,1,0:T(8,128)(2,1)S(1)}, bf16[72,32,128]{2,1,0:T(8,128)(2,1)S(1)}, u32[]{:S(2)}, u32[]{:S(2)}) collective-permute-start(bf16[72,32,128]{2,1,0:T(8,128)(2,1)S(1)} %get-tuple-element.84.sent), channel_id=1, source_target_pairs={{0,1},{1,0},{2,3},{3,2},{4,5},{5,4},{6,7},{7,6},{8,9},{9,8},{10,11... | collective-permute-start | bytes 1769480 | tf_op jit(solution)/shard_map/ppermute | solution.py:37
  56.3 23.2 %collective-permute-start.21 = (bf16[64,16,384]{2,1,0:T(8,128)(2,1)S(1)}, bf16[64,16,384]{2,1,0:T(8,128)(2,1)S(1)}, u32[]{:S(2)}, u32[]{:S(2)}) collective-permute-start(bf16[64,16,384]{2,1,0:T(8,128)(2,1)S(1)} %shard_map.113.sx), channel_id=1, source_target_pairs={{0,1},{1,0},{2,3},{3,2},{4,5},{5,4},{6,7},{7,6},{8,9},{9,8},{10,11... | collective-permute-start | bytes 2359304 | tf_op jit(solution)/shard_map/ppermute | solution.py:37
  57.6 22.0 %collective-permute-start.22 = (bf16[64,16,384]{2,1,0:T(8,128)(2,1)S(1)}, bf16[64,16,384]{2,1,0:T(8,128)(2,1)S(1)}, u32[]{:S(2)}, u32[]{:S(2)}) collective-permute-start(bf16[64,16,384]{2,1,0:T(8,128)(2,1)S(1)} %shard_map.114.sy), channel_id=1, source_target_pairs={{0,8},{1,9},{2,10},{3,11},{4,12},{5,13},{6,14},{7,15},{8,0},{9,1},... | collective-permute-start | bytes 2359304 | tf_op jit(solution)/shard_map/ppermute | solution.py:37
  58.8 20.8 %collective-permute-start.23 = (bf16[64,32,128]{2,1,0:T(8,128)(2,1)S(1)}, bf16[64,32,128]{2,1,0:T(8,128)(2,1)S(1)}, u32[]{:S(2)}, u32[]{:S(2)}) collective-permute-start(bf16[64,32,128]{2,1,0:T(8,128)(2,1)S(1)} %shard_map.115.sz), channel_id=1, source_target_pairs={{0,16},{1,17},{2,18},{3,19},{4,20},{5,21},{6,22},{7,23},{8,24},{9,... | collective-permute-start | bytes 1572872 | tf_op jit(solution)/shard_map/ppermute | solution.py:37
  60.2 7.7 %collective-permute-start.16 = (bf16[4,32,512]{2,1,0:T(8,128)(2,1)S(1)}, bf16[4,32,512]{2,1,0:T(8,128)(2,1)S(1)}, u32[]{:S(2)}, u32[]{:S(2)}) collective-permute-start(bf16[4,32,512]{2,1,0:T(8,128)(2,1)S(1)} %get-tuple-element.88), channel_id=1, source_target_pairs={{0,48},{1,49},{2,50},{3,51},{4,52},{5,53},{6,54},{7,55},{8,56},{9,... | collective-permute-start | bytes 393224 | tf_op jit(solution)/shard_map/ppermute | solution.py:37
  63.0 7.6 %collective-permute-start.17 = (bf16[4,32,512]{2,1,0:T(8,128)(2,1)S(1)}, bf16[4,32,512]{2,1,0:T(8,128)(2,1)S(1)}, u32[]{:S(2)}, u32[]{:S(2)}) collective-permute-start(bf16[4,32,512]{2,1,0:T(8,128)(2,1)S(1)} %get-tuple-element.89), channel_id=1, source_target_pairs={{0,136},{1,137},{2,138},{3,139},{4,140},{5,141},{6,142},{7,143},{8... | collective-permute-start | bytes 393224 | tf_op jit(solution)/shard_map/ppermute | solution.py:37
  70.7 5.6 %collective-permute-start.18 = (bf16[2,32,512]{2,1,0:T(8,128)(2,1)S(1)}, bf16[2,32,512]{2,1,0:T(8,128)(2,1)S(1)}, u32[]{:S(2)}, u32[]{:S(2)}) collective-permute-start(bf16[2,32,512]{2,1,0:T(8,128)(2,1)S(1)} %get-tuple-element.92), channel_id=1, source_target_pairs={{0,136},{1,137},{2,138},{3,139},{4,140},{5,141},{6,142},{7,143},{8... | collective-permute-start | bytes 196616 | tf_op jit(solution)/shard_map/ppermute | solution.py:37
  73.0 5.5 %collective-permute-start.19 = (bf16[2,32,512]{2,1,0:T(8,128)(2,1)S(1)}, bf16[2,32,512]{2,1,0:T(8,128)(2,1)S(1)}, u32[]{:S(2)}, u32[]{:S(2)}) collective-permute-start(bf16[2,32,512]{2,1,0:T(8,128)(2,1)S(1)} %get-tuple-element.93), channel_id=1, source_target_pairs={{0,48},{1,49},{2,50},{3,51},{4,52},{5,53},{6,54},{7,55},{8,56},{9,... | collective-permute-start | bytes 196616 | tf_op jit(solution)/shard_map/ppermute | solution.py:37
  78.5 6.0 %collective-permute-start.20 = (bf16[2,32,512]{2,1,0:T(8,128)(2,1)S(1)}, bf16[2,32,512]{2,1,0:T(8,128)(2,1)S(1)}, u32[]{:S(2)}, u32[]{:S(2)}) collective-permute-start(bf16[2,32,512]{2,1,0:T(8,128)(2,1)S(1)} %get-tuple-element.95), channel_id=1, source_target_pairs={{0,2},{1,3},{2,0},{3,1},{4,6},{5,7},{6,4},{7,5},{8,10},{9,11},{10,... | collective-permute-start | bytes 196616 | tf_op jit(solution)/shard_map/ppermute | solution.py:37
  84.4 6.2 %collective-permute-start.25 = (bf16[2,256,512]{2,1,0:T(8,128)(2,1)S(1)}, bf16[2,256,512]{2,1,0:T(8,128)(2,1)S(1)}, u32[]{:S(2)}, u32[]{:S(2)}) collective-permute-start(bf16[2,256,512]{2,1,0:T(8,128)(2,1)S(1)} %get-tuple-element.104), channel_id=1, source_target_pairs={{0,64},{1,65},{2,66},{3,67},{4,68},{5,69},{6,70},{7,71},{8,72},{9,... | collective-permute-start | bytes 1572872 | tf_op jit(solution)/shard_map/ppermute | solution.py:37
  84.5 6.1 %collective-permute-start.24 = (bf16[32,512]{1,0:T(8,128)(2,1)S(1)}, bf16[32,512]{1,0:T(8,128)(2,1)S(1)}, u32[]{:S(2)}, u32[]{:S(2)}) collective-permute-start(bf16[32,512]{1,0:T(8,128)(2,1)S(1)} %get-tuple-element.100), channel_id=1, source_target_pairs={{0,6},{1,7},{2,4},{3,5},{4,2},{5,3},{6,0},{7,1},{8,14},{9,15},{10,... | collective-permute-start | bytes 98312 | tf_op jit(solution)/shard_map/ppermute | solution.py:37
